TPU v7x, 512 devices: a whole 4x8x8 slice. The times are simulated.
512 devices in a mesh: dp: 64 (over z, x, y_hi), feat: 8 (over y_lo, core).
Axes of the slice: x: 4, y: 8 (y_hi: 2, y_lo: 4; y = y_hi * 4 + y_lo), z: 8, core: 2. Of those that a mesh axis runs over, the one named last changes fastest.
Arguments:
- student: bfloat16 [8192, 768], P('dp'), may hold values from -40 to 40
- proj_weight: bfloat16 [768, 8192], P(None, 'feat'), may hold values from -6 to 6
- teacher: bfloat16 [8192, 8192], P('dp', 'feat'), may hold values from -480 to 480
- anchors: int32 [24576], P('dp'), may hold values from 0 to 127
- pairs: int32 [2, 24576], P(None, 'dp'), may hold values from 0 to 383
Outputs:
- grad_w: float32 [768, 8192], P('dp', 'feat')
- grad_student: float32 [8192, 768], P('dp', 'feat')
All inputs are finite; a program needn't handle non-finite values.
Results may differ from a plain program's by a relative error of at most 0.015.
Values may be sent and summed in bfloat16 or wider, within the bound.
No kernel may reach another device: no remote copies, remote signals or barrier semaphores. Data moves between devices by JAX's collectives and lax.ppermute only.
A program may use at most 64 MiB of HBM per device.

v0:
```python
import jax
import jax.numpy as jnp
from jax import lax
from jax.sharding import PartitionSpec as P

STEPS = 3


EPSILON = 1e-06
TEMPER = 50.0
MARGIN = 0.01
LOSS_SCALE = 1024.0


def passed_along(array, axis, by):
    peers = lax.axis_size(axis)
    return lax.ppermute(array, axis, [(i, (i + by) % peers) for i in range(peers)])


def row_products(left_mat, right_mat):
    return lax.dot_general(
        left_mat, right_mat, (((1,), (1,)), ((), ())), preferred_element_type=jnp.float32
    )


def column_products(left_mat, right_mat):
    return lax.dot_general(
        left_mat, right_mat, (((0,), (0,)), ((), ())), preferred_element_type=jnp.float32
    )


def relative_grad(sim_band, teach_band, anchor_rows, pair_cols):
    first_col = pair_cols[0]
    second_col = pair_cols[1]
    gap_student = sim_band[anchor_rows, first_col] - sim_band[anchor_rows, second_col]
    gap_teacher = teach_band[anchor_rows, first_col] - teach_band[anchor_rows, second_col]
    weight = jnp.tanh(TEMPER * gap_teacher)
    slopes = -weight * jax.nn.sigmoid(TEMPER * (MARGIN - weight * gap_student))
    gradient = 2.0 * (sim_band - teach_band)
    gradient = gradient.at[anchor_rows, first_col].add(slopes)
    gradient = gradient.at[anchor_rows, second_col].add(-slopes)
    return gradient


def shards(student, proj_weight, teacher, anchors, pairs):
    row_count = student.shape[0]
    projected = jnp.dot(student, proj_weight, preferred_element_type=jnp.float32)
    teacher_wide = teacher.astype(jnp.float32)
    proj_sq, teach_sq, cross = lax.psum(
        (
            jnp.sum(projected * projected, 1),
            jnp.sum(teacher_wide * teacher_wide, 1),
            jnp.sum(projected * teacher_wide, 1),
        ),
        "feat",
    )
    inv_proj = lax.rsqrt(proj_sq + EPSILON)
    inv_teach = lax.rsqrt(teach_sq + EPSILON)
    cosine = cross * inv_proj * inv_teach
    unit_rows = projected * inv_proj[:, None]
    target = teacher_wide * inv_teach[:, None]
    own_pair = jnp.stack([unit_rows.astype(jnp.bfloat16), target.astype(jnp.bfloat16)])
    own_rows = own_pair[0]
    blocks = [own_pair]
    for cycle_step in range(1, STEPS):
        blocks.append(passed_along(blocks[-1], "dp", -1))
    partials = [
        (row_products(own_pair[0], member[0]), row_products(own_pair[1], member[1]))
        for member in blocks
    ]
    summed = [lax.psum((pair_part[0], pair_part[1]), "feat") for pair_part in partials]
    sim_band = jnp.concatenate([pair_sum[0] for pair_sum in summed], 1)
    teach_band = jnp.concatenate([pair_sum[1] for pair_sum in summed], 1)
    gradient = relative_grad(sim_band, teach_band, anchors, pairs).astype(jnp.bfloat16)
    unit_grad = column_products(gradient[:, :row_count], own_rows)
    for cycle_step in range(STEPS):
        band_tile = gradient[:, cycle_step * row_count : (cycle_step + 1) * row_count]
        unit_grad = unit_grad + jnp.dot(
            band_tile, blocks[cycle_step][0], preferred_element_type=jnp.float32
        )
    for cycle_step in range(1, STEPS):
        band_tile = gradient[:, cycle_step * row_count : (cycle_step + 1) * row_count]
        unit_grad = unit_grad + passed_along(
            column_products(band_tile, own_rows).astype(jnp.bfloat16), "dp", cycle_step
        ).astype(jnp.float32)
    inner_part = lax.psum(jnp.sum(unit_rows * unit_grad, 1), "feat")
    proj_grad = (
        LOSS_SCALE
        * inv_proj[:, None]
        * (unit_grad - target + (cosine - inner_part)[:, None] * unit_rows)
    ).astype(jnp.bfloat16)
    grad_w = lax.psum_scatter(
        column_products(student, proj_grad), "dp", scatter_dimension=0, tiled=True
    )
    grad_student = lax.psum_scatter(
        row_products(proj_grad, proj_weight).astype(jnp.bfloat16),
        "feat",
        scatter_dimension=1,
        tiled=True,
    ).astype(jnp.float32)
    return (grad_w, grad_student)


def solution(mesh):
    return jax.shard_map(
        shards,
        mesh=mesh,
        in_specs=(P("dp", None), P(None, "feat"), P("dp", "feat"), P("dp"), P(None, "dp")),
        out_specs=(P("dp", "feat"), P("dp", "feat")),
        check_vma=False,
    )
```

profile of v0, /device:TPU:6, one launch (start us, length us, event | category | flops | bytes accessed | tf_op | source)
XLA Modules:
  0.0 1171.1 jit_solution(10459701523190100666)
XLA Ops:
  8.7 1.4 multiply_reduce_fusion.1
  10.0 16.6 %all-reduce.2 = (f32[128]{0:T(128)S(1)}, f32[128]{0:T(128)S(1)}) all-reduce(f32[128]{0:T(128)S(1)} %get-tuple-element.30, f32[128]{0:T(128)S(1)} %fusion.7), channel_id=1, replica_groups=mesh['dp'=64,'feat'=8] {'feat'}, use_global_device_ids=true, to_apply=%region_1.0 | all-reduce | flops 256 | bytes 2048 | tf_op jit(solution)/shard_map/psum | solution.py:49
  27.0 5.3 collective-permute-start
  33.2 21.8 %collective-permute-done = bf16[2,128,1024]{2,1,0:T(8,128)(2,1)S(1)} collective-permute-done((bf16[2,128,1024]{2,1,0:T(8,128)(2,1)S(1)}, bf16[2,128,1024]{2,1,0:T(8,128)(2,1)S(1)}, u32[]{:S(2)}, u32[]{:S(2)}) %collective-permute-start) | collective-permute-done | bytes 524320 | tf_op jit(solution)/shard_map/ppermute | solution.py:17
  55.0 5.6 collective-permute-start.1
  63.3 16.2 %collective-permute-done.1 = bf16[2,128,1024]{2,1,0:T(8,128)(2,1)S(1)} collective-permute-done((bf16[2,128,1024]{2,1,0:T(8,128)(2,1)S(1)}, bf16[2,128,1024]{2,1,0:T(8,128)(2,1)S(1)}, u32[]{:S(2)}, u32[]{:S(2)}) %collective-permute-start.1) | collective-permute-done | bytes 524320 | tf_op jit(solution)/shard_map/ppermute | solution.py:17
  81.5 87.1 %all-reduce.9.cloned.1.call-done = (f32[128,128]{1,0:T(8,128)}, f32[128,128]{1,0:T(8,128)}, f32[128,128]{1,0:T(8,128)}, f32[128,128]{1,0:T(8,128)}, f32[128,128]{1,0:T(8,128)}, /*index=5*/f32[128,128]{1,0:T(8,128)}) async-done(((f32[128,128]{1,0:T(8,128)}, f32[128,128]{1,0:T(8,128)}, f32[128,128]{1,0:T(8,128)}, f32[128,128]{1,0:T(8,128)}, f32[128,128]{1,0:T(8,128)}, /*index=5*/f32[128,128]{1,0:T(8,128)}), ...) | async-done | bytes 393232 | tf_op jit(solution)/shard_map/psum | solution.py:71
  171.1 3.4 gather_fusion.3
  174.6 3.4 gather_fusion.2
  178.1 3.4 gather_fusion.1
  181.6 3.4 gather_fusion
  185.1 20.3 %scatter_fusion = f32[128,384]{1,0:T(8,128)S(1)} fusion(f32[128,384]{1,0:T(8,128)S(1)} %subtract_multiply_fusion, s32[384]{0:T(512)S(1)} %get-tuple-element.11, f32[384]{0:T(512)S(1)} %get-tuple-element.25), kind=kCustom, calls=%fused_computation.4 | custom fusion | flops 384 | bytes 7680 | tf_op jit(solution)/shard_map/scatter-add | solution.py:40
  205.4 20.3 %scatter_fusion.1 = f32[128,384]{1,0:T(8,128)S(1)} fusion(f32[128,384]{1,0:T(8,128)S(1)} %scatter_fusion, s32[384]{0:T(512)S(1)} %get-tuple-element.10, f32[384]{0:T(512)S(1)} %get-tuple-element.24), kind=kCustom, calls=%fused_computation.5 | custom fusion | flops 384 | bytes 7680 | tf_op jit(solution)/shard_map/scatter-add | solution.py:41
  226.6 3.5 collective-permute-start.3
  230.1 5.6 collective-permute-start.2
  236.1 11.9 %collective-permute-done.2 = bf16[128,1024]{1,0:T(8,128)(2,1)S(1)} collective-permute-done((bf16[128,1024]{1,0:T(8,128)(2,1)S(1)}, bf16[128,1024]{1,0:T(8,128)(2,1)S(1)}, u32[]{:S(2)}, u32[]{:S(2)}) %collective-permute-start.2) | collective-permute-done | bytes 262176 | tf_op jit(solution)/shard_map/ppermute | solution.py:17
  248.4 15.5 %all-reduce.1 = (f32[128]{0:T(128)S(1)}, f32[128]{0:T(128)S(1)}) all-reduce(f32[128]{0:T(128)S(1)} %get-tuple-element.9, f32[128]{0:T(128)S(1)} %get-tuple-element.8), channel_id=1, replica_groups=mesh['dp'=64,'feat'=8] {'feat'}, use_global_device_ids=true, to_apply=%region_15.0 | all-reduce | flops 256 | bytes 2048 | tf_op jit(solution)/shard_map/psum | solution.py:86
  264.1 1.2 convolution_convert_fusion.2
  265.4 2.3 convolution_bitcast_fusion
  267.8 1.3 dynamic-slice
  269.7 31.4 %reduce-scatter.3.cloned.1.call-done = bf16[128,96]{0,1:T(8,128)(2,1)} async-done(((bf16[128,768]{0,1:T(8,128)(2,1)}), bf16[128,96]{0,1:T(8,128)(2,1)}) %reduce-scatter.3.cloned.1.call-update) | async-done | bytes 24592 | tf_op jit(solution)/shard_map/reduce_scatter | solution.py:95
  301.1 1.4 convert_element_type.43
  302.4 859.9 %all-reduce.7.cloned.1.call-done = f32[768,1024]{0,1:T(8,128)} async-done(((f32[768,1024]{0,1:T(8,128)}), f32[768,1024]{0,1:T(8,128)}) %all-reduce.7.cloned.1.call-update) | async-done | bytes 3145744
  1162.3 1.4 constant_dynamic-slice_fusion
  (64 shorter events, 12.6 us)
Async XLA Ops:
  7.2 1.5 copy-start
  7.2 19.5 %copy-start.1 = (bf16[128,1024]{1,0:T(8,128)(2,1)S(1)}, bf16[128,1024]{1,0:T(8,128)(2,1)}, u32[]{:S(2)}) copy-start(bf16[128,1024]{1,0:T(8,128)(2,1)} %param.7) | copy-start | bytes 786436
  7.2 161.4 %all-reduce.9.cloned.1.call-start = ((), (), s32[]{:S(2)}) async-start(), calls=%async_computation.3 | async-start | bytes 786432 | tf_op jit(solution)/shard_map/psum | solution.py:71
  27.0 28.1 %collective-permute-start = (bf16[2,128,1024]{2,1,0:T(8,128)(2,1)S(1)}, bf16[2,128,1024]{2,1,0:T(8,128)(2,1)S(1)}, u32[]{:S(2)}, u32[]{:S(2)}) collective-permute-start(bf16[2,128,1024]{2,1,0:T(8,128)(2,1)S(1)} %pad_maximum_fusion), channel_id=1, source_target_pairs={{0,504},{8,0},{16,8},{24,16},{32,24},{40,32},{48,40},{56,48},{64,5... | collective-permute-start | bytes 1572872 | tf_op jit(solution)/shard_map/ppermute | solution.py:17
  55.0 26.3 %copy-start.3 = (bf16[2,128,1024]{2,1,0:T(8,128)(2,1)}, bf16[2,128,1024]{2,1,0:T(8,128)(2,1)S(1)}, u32[]{:S(2)}) copy-start(bf16[2,128,1024]{2,1,0:T(8,128)(2,1)S(1)} %collective-permute-done) | copy-start | bytes 1572868
  55.0 24.5 %collective-permute-start.1 = (bf16[2,128,1024]{2,1,0:T(8,128)(2,1)S(1)}, bf16[2,128,1024]{2,1,0:T(8,128)(2,1)S(1)}, u32[]{:S(2)}, u32[]{:S(2)}) collective-permute-start(bf16[2,128,1024]{2,1,0:T(8,128)(2,1)S(1)} %collective-permute-done), channel_id=1, source_target_pairs={{0,504},{8,0},{16,8},{24,16},{32,24},{40,32},{48,40},{56,48},{64,5... | collective-permute-start | bytes 1572872 | tf_op jit(solution)/shard_map/ppermute | solution.py:17
  61.5 19.8 %copy-start.11 = (s32[384]{0:T(512)S(1)}, s32[384]{0:T(512)}, u32[]{:S(2)}) copy-start(s32[384]{0:T(512)} %param.8) | copy-start | bytes 4612
  61.5 19.8 %copy-start.10 = (s32[2,384]{1,0:T(2,128)S(1)}, s32[2,384]{1,0:T(2,128)}, u32[]{:S(2)}) copy-start(s32[2,384]{1,0:T(2,128)} %param.9) | copy-start | bytes 9220
  79.5 0.9 copy-start.5
  81.3 219.8 %reduce-scatter.3.cloned.1.call-start = ((), (), s32[]{:S(2)}) async-start(), calls=%async_computation.1 | async-start | bytes 221184 | tf_op jit(solution)/shard_map/reduce_scatter | solution.py:95
  174.6 3.5 copy-start.9
  174.6 3.5 copy-start.8
  174.6 3.5 copy-start.7
  225.8 10.1 copy-start.4
  226.3 21.7 %copy-start.6 = (bf16[2,128,1024]{2,1,0:T(8,128)(2,1)S(1)}, bf16[2,128,1024]{2,1,0:T(8,128)(2,1)}, u32[]{:S(2)}) copy-start(bf16[2,128,1024]{2,1,0:T(8,128)(2,1)} %copy-done.5) | copy-start | bytes 1572868
  226.6 9.5 collective-permute-start.3
  230.1 17.9 %collective-permute-start.2 = (bf16[128,1024]{1,0:T(8,128)(2,1)S(1)}, bf16[128,1024]{1,0:T(8,128)(2,1)S(1)}, u32[]{:S(2)}, u32[]{:S(2)}) collective-permute-start(bf16[128,1024]{1,0:T(8,128)(2,1)S(1)} %convolution_convert_fusion.1), channel_id=1, source_target_pairs={{0,8},{8,16},{16,24},{24,32},{32,40},{40,48},{48,56},{56,64},{64,7... | collective-permute-start | bytes 786440 | tf_op jit(solution)/shard_map/ppermute | solution.py:17
  263.9 1.6 copy-start.2
  265.4 896.9 %all-reduce.7.cloned.1.call-start = ((), (), s32[]{:S(2)}) async-start(), calls=%async_computation.2 | async-start | bytes 6291456
Sparse Core Ops, SparseCore 0:
  81.4 87.1 all-reduce.8
  265.5 35.5 reduce-scatter.2
  304.0 858.2 all-reduce.6
where the time goes:
time: 1180 us; the launch traced here: 1170 us
  waiting for transfers between devices  1030 us (87%)
  other arithmetic  43.9 us (4%)
  blocking collectives  32.1 us (3%)
  local copies, waits for them, and re-layouts  20.1 us (2%)
  starting transfers between devices  20 us (2%)
  between operations  14.8 us (1%)
  matrix products  11.8 us (1%)
    unnamed x4, waiting for transfers between devices  860 us
    psum x1, waiting for transfers between devices, shards(): lax.psum((pair_part[0], pair_part[1]), 'feat')  87.1 us
    ppermute x4, waiting for transfers between devices, passed_along(): lax.ppermute(array, axis, [(i, (i + by) % peers) for i in range(peers)])  49.9 us
    reduce_scatter x1, waiting for transfers between devices, shards(): lax.psum_scatter(row_products(proj_grad, proj_weight).astype(jnp.bfloat16...  31.4 us
  transfers between devices with their start and end apart: 7, of which 6 were waited for; matrix products, arithmetic and copies ran while one was open for 1% of the time, Pallas kernels for 0%

commit v1 on v0

v1 whole, which is shorter than its diff:
```python
import functools

import jax
import jax.numpy as jnp
from jax import lax
from jax.experimental import pallas as pl
from jax.experimental.pallas import tpu as pltpu
from jax.sharding import Mesh, PartitionSpec as P

STEPS = 3
EPSILON = 1e-06
TEMPER = 50.0
MARGIN = 0.01
LOSS_SCALE = 1024.0

DP_SIZES = {64: (4, 8, 2), 8: (2, 2, 2)}
DP = ("z", "x", "yh")
LANES = 128
f32 = jnp.float32
bf16 = jnp.bfloat16
HIGHEST = lax.Precision.HIGHEST


def dot(left, right, contract, precision=None):
    return lax.dot_general(
        left, right, ((contract[:1], contract[1:]), ((), ())),
        preferred_element_type=f32, precision=precision,
    )


def passed_along(array, by):
    peers = lax.axis_size(DP)
    return lax.ppermute(array, DP, [(i, (i + by) % peers) for i in range(peers)])


def band_kernel(parts, norms, ids, out):
    rows = parts.shape[1]
    band = norms.shape[1]
    sums = jnp.sum(parts[...], 0)
    inv_proj = norms[0:1, :]
    inv_teach = norms[1:2, :]
    row_id = lax.broadcasted_iota(jnp.int32, (rows, band), 0)
    anchor = (ids[0:1, :] == row_id).astype(f32)
    own = (ids[3:4, :] == row_id).astype(f32)
    row_proj = jnp.sum(own * inv_proj, 1, keepdims=True)
    row_teach = jnp.sum(own * inv_teach, 1, keepdims=True)
    sim = sums[:, :band] * (row_proj * inv_proj)
    teach = sums[:, band:] * (row_teach * inv_teach)
    col_id = lax.broadcasted_iota(jnp.int32, (band, band), 0)
    pick = (col_id == ids[1:2, :]).astype(f32) - (col_id == ids[2:3, :]).astype(f32)
    gap_s = jnp.sum(dot(sim, anchor, (0, 0), HIGHEST) * pick, 0, keepdims=True)
    gap_t = jnp.sum(dot(teach, anchor, (0, 0), HIGHEST) * pick, 0, keepdims=True)
    weight = jnp.tanh(TEMPER * gap_t)
    slope = -weight * jax.nn.sigmoid(TEMPER * (MARGIN - weight * gap_s))
    grad = 2.0 * (sim - teach) + dot(anchor * slope, pick, (1, 1), HIGHEST)
    product = grad * sim
    along = jnp.sum(product, 1, keepdims=True)
    inner = jnp.sum(product + along * own, 0, keepdims=True) * (inv_proj * inv_proj)
    inner_high = inner.astype(bf16)
    inner_low = (inner - inner_high.astype(f32)).astype(bf16)
    tail_id = lax.broadcasted_iota(jnp.int32, (16, band), 0)
    tail = jnp.where(
        tail_id == 0, inner_high.astype(f32), jnp.where(tail_id == 1, inner_low.astype(f32), 0.0)
    )
    out[0:rows, :] = (grad * (row_proj * inv_proj)).astype(bf16)
    out[rows : rows + 16, :] = tail.astype(bf16)


def spread_kernel(gathered, student_band, student_cols, student_pad, own, first, second, mixed):
    peers, height, band = gathered.shape
    rows = height - 16
    texts = peers * rows
    tile = gathered[:, 0:rows, :].reshape(texts, band)
    inner = jnp.sum(gathered[:, rows : rows + 16, :].astype(f32), (0, 1)).reshape(1, band)
    diagonal = lax.broadcasted_iota(jnp.int32, (band, band), 0) == lax.broadcasted_iota(
        jnp.int32, (band, band), 1
    )
    inner_col = jnp.sum(jnp.where(diagonal, inner, 0.0), 1, keepdims=True)

    def spread(values):
        direct = dot(tile, values, (1, 0))
        back = dot(tile, values[:texts], (0, 0)) - inner_col * values.astype(f32)
        return direct + back[:texts], back[texts:]

    head, rest = spread(student_cols[...])
    slab = jnp.concatenate([head, rest], 0).astype(bf16)
    mixed[...] = dot(student_pad[...], slab, (1, 0)).astype(bf16)
    head, rest = spread(student_band[...])
    own[...] = head
    first[...] = rest[:texts].astype(bf16)
    second[...] = rest[texts:].astype(bf16)


def one_hot_pad(features, sizes, padded, by_x):
    z_size, x_size, yh_size = sizes
    share = features // (z_size * x_size * yh_size)
    wide = padded if padded else share
    out = lax.broadcasted_iota(jnp.int32, (z_size * x_size * yh_size * wide, features), 0)
    feature = lax.broadcasted_iota(jnp.int32, out.shape, 1)
    place, offset = out // wide, out % wide
    if by_x:
        yh = place % yh_size
        z = (place // yh_size) % z_size
        x = place // (yh_size * z_size)
        place = (z * x_size + x) * yh_size + yh
    return ((feature == place * share + offset) & (offset < share)).astype(bf16)


def shards(student, proj_weight, teacher, anchors, pairs, *, sizes):
    z_size, x_size, yh_size = sizes
    n_dp = z_size * x_size * yh_size
    n_feat = lax.axis_size("feat")
    texts, features = student.shape
    width = teacher.shape[1]
    band = STEPS * texts
    rows = texts // n_feat
    share = features // n_dp
    padded = -(-share // 16) * 16
    groups = features // LANES
    feat = lax.axis_index("feat")

    packed = jnp.concatenate([teacher, student], 1)
    near = passed_along(packed, -1)
    far = passed_along(packed, -2)

    projected = dot(student, proj_weight, (1, 0))
    teacher_wide = teacher.astype(f32)
    proj_sq, teach_sq, cross = lax.psum(
        (
            jnp.sum(projected * projected, 1),
            jnp.sum(teacher_wide * teacher_wide, 1),
            jnp.sum(projected * teacher_wide, 1),
        ),
        "feat",
    )
    inv_proj = lax.rsqrt(proj_sq + EPSILON)
    inv_teach = lax.rsqrt(teach_sq + EPSILON)
    cosine = cross * inv_proj * inv_teach
    own_norms = jnp.stack([inv_proj, inv_teach])
    norms = jnp.concatenate(
        [own_norms, passed_along(own_norms, -1), passed_along(own_norms, -2)], 1
    )

    direct = (LOSS_SCALE * inv_proj)[:, None] * (
        (cosine * inv_proj)[:, None] * projected - inv_teach[:, None] * teacher_wide
    )
    regroup = dot(one_hot_pad(features, sizes, 0, True), student, (1, 1)).astype(bf16)
    direct_part = dot(regroup, direct.astype(bf16), (1, 0)).astype(bf16)
    direct_part = lax.all_to_all(
        direct_part.reshape(x_size, features // x_size, width), "x", 0, 0
    ).reshape(features, width)
    zy = z_size * yh_size
    row_out = lax.broadcasted_iota(jnp.int32, (zy * padded, features), 0)
    row_in = lax.broadcasted_iota(jnp.int32, (zy * padded, features), 1) % (zy * share)
    gather_rows = (
        (row_out // padded == row_in // share) & (row_out % padded == row_in % share)
    ).astype(bf16)
    direct_part = dot(gather_rows, direct_part, (1, 0)).astype(bf16)
    direct_part = lax.all_to_all(direct_part.reshape(zy, padded, width), ("z", "yh"), 0, 0)
    grad_w_direct = jnp.sum(direct_part.astype(f32), 0)

    student_band = jnp.concatenate([student, near[:, width:], far[:, width:]], 0)
    proj_own = projected.astype(bf16)
    proj_rest = dot(student_band[texts:], proj_weight, (1, 0)).astype(bf16)
    proj_band = jnp.concatenate([proj_own, proj_rest], 0)
    teach_band = jnp.concatenate([teacher, near[:, :width], far[:, :width]], 0)
    parts = jnp.concatenate(
        [dot(proj_own, proj_band, (1, 1)), dot(teacher, teach_band, (1, 1))], 1
    )
    parts = lax.all_to_all(parts.reshape(n_feat, rows, 2 * band), "feat", 0, 0)
    ids = jnp.concatenate(
        [
            anchors[None] - feat * rows,
            pairs,
            lax.broadcasted_iota(jnp.int32, (1, band), 1) - feat * rows,
            jnp.zeros((4, band), jnp.int32),
        ],
        0,
    )
    tile = pl.pallas_call(
        band_kernel,
        out_shape=jax.ShapeDtypeStruct((rows + 16, band), bf16),
        cost_estimate=pl.CostEstimate(flops=10**8, bytes_accessed=10**6, transcendentals=1000),
        name="band",
    )(parts, norms, ids)
    gathered = lax.all_gather(tile, "feat")

    student_pad = dot(one_hot_pad(features, sizes, padded, False), student_band, (1, 1)).astype(bf16)
    col_start = jnp.minimum(feat, groups - 1) * LANES
    student_cols = lax.dynamic_slice(student_band, (0, col_start), (band, LANES))
    student_cols = jnp.where(feat < groups, student_cols, jnp.zeros_like(student_cols))
    own, first, second, mixed = pl.pallas_call(
        spread_kernel,
        out_shape=(
            jax.ShapeDtypeStruct((texts, features), f32),
            jax.ShapeDtypeStruct((texts, features), bf16),
            jax.ShapeDtypeStruct((texts, features), bf16),
            jax.ShapeDtypeStruct((n_dp * padded, LANES), bf16),
        ),
        cost_estimate=pl.CostEstimate(flops=10**9, bytes_accessed=4 * 10**6, transcendentals=0),
        name="spread",
    )(gathered, student_band, student_cols, student_pad)

    mixed = lax.all_to_all(mixed.reshape(n_dp, padded, LANES), DP, 0, 0)
    mixed = jnp.sum(mixed.astype(f32), 0).astype(bf16)
    mixed = lax.all_gather(mixed, "feat")
    mixed = jnp.concatenate([mixed[g] for g in range(groups)], 1)
    grad_w = (grad_w_direct + LOSS_SCALE * dot(mixed, proj_weight, (1, 0)))[:share]

    spread = own + passed_along(first, 1).astype(f32) + passed_along(second, 2).astype(f32)
    proj_grad = (direct + LOSS_SCALE * dot(spread.astype(bf16), proj_weight, (1, 0))).astype(bf16)
    back = dot(proj_weight, proj_grad, (1, 1)).astype(bf16)
    back = lax.all_to_all(back.reshape(n_feat, features // n_feat, texts), "feat", 0, 0)
    grad_student = jnp.sum(back.astype(f32), 0).T
    return (grad_w, grad_student)


def solution(mesh):
    n_dp, n_feat = mesh.devices.shape
    sizes = DP_SIZES[n_dp]
    split = Mesh(mesh.devices.reshape(*sizes, n_feat), (*DP, "feat"))
    return jax.shard_map(
        functools.partial(shards, sizes=sizes),
        mesh=split,
        in_specs=(P(DP, None), P(None, "feat"), P(DP, "feat"), P(DP), P(None, DP)),
        out_specs=(P(DP, "feat"), P(DP, "feat")),
        check_vma=False,
    )
```

time: 1180 us -> 215 us (0.18)
  waiting for transfers between devices: 1030 us -> 63.9 us
  starting transfers between devices: 20 us -> 65.2 us
  other arithmetic: 43.9 us -> 8.24 us
  local copies, waits for them, and re-layouts: 20.1 us -> 5.88 us
  blocking collectives: 32.1 us -> 46 us
  between operations: 14.8 us -> 1.08 us
    unnamed x4 -> x0, waiting for transfers between devices: 860 us -> none
    psum x1 -> x0, waiting for transfers between devices: 87.1 us -> none  [shards(): lax.psum((pair_part[0], pair_part[1]), 'feat')]
    scatter-add x2 -> x0, other arithmetic: 40.6 us -> none  [the longest x1 20.3 us: relative_grad(): gradient = gradient.at[anchor_rows, second_col].add(-slopes)]
    all_to_all x0 -> x5, starting transfers between devices: none -> 39.8 us  [the longest x1 22.5 us: shards(): mixed = lax.all_to_all(mixed.reshape(n_dp, padded, LANES), DP, 0, 0)]
    all_to_all x0 -> x5, waiting for transfers between devices: none -> 35 us  [the longest x1 12.6 us: shards(): lax.all_to_all(direct_part.reshape(zy, padded, width), ('z', 'yh'), 0, 0)]
    reduce_scatter x1 -> x0, waiting for transfers between devices: 31.4 us -> none  [shards(): lax.psum_scatter(row_products(proj_grad, proj_weight).astype(jnp.bfloat16...]
    all_gather x0 -> x2, blocking collectives: none -> 29.4 us  [the longest x1 15.4 us: shards(): gathered = lax.all_gather(tile, 'feat')]
    ppermute x4 -> x6, waiting for transfers between devices: 49.9 us -> 28.8 us  [passed_along(): lax.ppermute(array, DP, [(i, (i + by) % peers) for i in range(peers)])]
  transfers between devices with their start and end apart: 7 -> 11, of which waited for: 6 -> 7; matrix products, arithmetic and copies ran while one was open for 1% -> 11% of each run, Pallas kernels for 0% -> 0%
where the time goes in v1:
time: 215 us; the launch traced here: 212 us
  starting transfers between devices  65.2 us (30%)
  waiting for transfers between devices  63.9 us (30%)
  blocking collectives  46 us (21%)
  matrix products  15 us (7%)
  other arithmetic  8.24 us (4%)
  Pallas kernels  6.57 us (3%)
  local copies, waits for them, and re-layouts  5.88 us (3%)
    ppermute x6, waiting for transfers between devices, passed_along(): lax.ppermute(array, DP, [(i, (i + by) % peers) for i in range(peers)])  28.8 us
    ppermute x6, starting transfers between devices, passed_along(): lax.ppermute(array, DP, [(i, (i + by) % peers) for i in range(peers)])  25.4 us
    all_to_all x1, starting transfers between devices, shards(): mixed = lax.all_to_all(mixed.reshape(n_dp, padded, LANES), DP, 0, 0)  22.5 us
    psum x1, blocking collectives, shards(): lax.psum((jnp.sum(projected * projected, 1), jnp.sum(teacher_wide * teach...  16.6 us
    all_gather x1, blocking collectives, shards(): gathered = lax.all_gather(tile, 'feat')  15.4 us
    dot_general x9, matrix products, dot(): lax.dot_general(left, right, ((contract[:1], contract[1:]), ((), ())), pr...  15 us
    all_gather x1, blocking collectives, shards(): mixed = lax.all_gather(mixed, 'feat')  14 us
    all_to_all x1, waiting for transfers between devices, shards(): lax.all_to_all(direct_part.reshape(zy, padded, width), ('z', 'yh'), 0, 0)  12.6 us
  transfers between devices with their start and end apart: 11, of which 7 were waited for; matrix products, arithmetic and copies ran while one was open for 11% of the time, Pallas kernels for 0%

profile of v1, /device:TPU:6, one launch (start us, length us, event | category | flops | bytes accessed | tf_op | source)
XLA Modules:
  0.0 211.9 jit_solution(7967398788270108772)
XLA Ops:
  4.3 16.6 %all-reduce = (f32[128]{0:T(128)S(1)}, f32[128]{0:T(128)S(1)}, f32[128]{0:T(128)S(1)}) all-reduce(f32[128]{0:T(128)S(1)} %get-tuple-element.12, f32[128]{0:T(128)S(1)} %get-tuple-element.11, f32[128]{0:T(128)S(1)} %get-tuple-element.10), channel_id=1, replica_groups=mesh['z'=4,'x'=8,'yh'=2,'feat'=8] {'feat'}, use_global_device_ids=true, to_apply=%region_5.0 | all-reduce | flops 384 | bytes 3072 | tf_op jit(solution)/shard_map/psum | solution.py:128
  21.5 5.3 %collective-permute-start.2 = (f32[2,128]{1,0:T(2,128)S(1)}, f32[2,128]{1,0:T(2,128)S(1)}, u32[]{:S(2)}, u32[]{:S(2)}) collective-permute-start(f32[2,128]{1,0:T(2,128)S(1)} %pad_maximum_fusion.3), channel_id=1, source_target_pairs={{0,504},{8,0},{16,8},{24,16},{32,24},{40,32},{48,40},{56,48},{64,5... | collective-permute-start | bytes 3080 | tf_op jit(solution)/shard_map/ppermute | solution.py:33
  30.7 4.7 %collective-permute-start = (bf16[128,1792]{1,0:T(8,128)(2,1)}, bf16[128,1792]{1,0:T(8,128)(2,1)S(1)}, u32[]{:S(2)}, u32[]{:S(2)}) collective-permute-start(bf16[128,1792]{1,0:T(8,128)(2,1)} %constant_dynamic-update-slice_fusion), channel_id=1, source_target_pairs={{0,504},{8,0},{16,8},{24,16},{32,24},{40,32},{48,40},{56,48},{64,5... | collective-permute-start | bytes 1376264 | tf_op jit(solution)/shard_map/ppermute | solution.py:33
  35.4 4.8 %collective-permute-start.1 = (bf16[128,1792]{1,0:T(8,128)(2,1)}, bf16[128,1792]{1,0:T(8,128)(2,1)S(1)}, u32[]{:S(2)}, u32[]{:S(2)}) collective-permute-start(bf16[128,1792]{1,0:T(8,128)(2,1)} %constant_dynamic-update-slice_fusion), channel_id=1, source_target_pairs={{0,496},{8,504},{16,0},{24,8},{32,16},{40,24},{48,32},{56,40},{64,... | collective-permute-start | bytes 1376264 | tf_op jit(solution)/shard_map/ppermute | solution.py:33
  43.4 11.4 %collective-permute-done = bf16[128,1792]{1,0:T(8,128)(2,1)S(1)} collective-permute-done((bf16[128,1792]{1,0:T(8,128)(2,1)}, bf16[128,1792]{1,0:T(8,128)(2,1)S(1)}, u32[]{:S(2)}, u32[]{:S(2)}) %collective-permute-start) | collective-permute-done | bytes 458784 | tf_op jit(solution)/shard_map/ppermute | solution.py:33
  57.5 3.5 %all-to-all-start.2 = ((f32[8,16,768]{2,1,0:T(8,128)}), f32[8,16,768]{2,1,0:T(8,128)S(1)}, u32[]{:S(2)}, u32[]{:S(2)}) async-start(f32[8,16,768]{2,1,0:T(8,128)} %bitcast.4), calls=%async_computation.2 | async-start | bytes 786432 | tf_op jit(solution)/shard_map/all_to_all | solution.py:170
  63.4 3.5 %fusion.28.student_pad = bf16[1024,384]{1,0:T(8,128)(2,1)} fusion(s32[1024]{0:T(1024)S(1)} %get-tuple-element.38, s32[1024]{0:T(1024)S(1)} %get-tuple-element.39, s32[1024]{0:T(1024)S(1)} %get-tuple-element.37, s32[1024]{0:T(1024)S(1)} %get-tuple-element.40, pred[1024]{0:T(1024)(128)(4,1)} %get-tuple-element.41, pred[1024]{0:T(1024)(128)(4,1)} %get-tuple-element.42, ...), kind=kOutput, calls=%fused_computation.45 | convolution fusion | flops 611647488 | bytes 1394688 | tf_op jit(solution)/shard_map/dot_general | solution.py:25
  66.9 6.6 %all-to-all-done.2.parts = f32[8,16,768]{2,1,0:T(8,128)S(1)} async-done(((f32[8,16,768]{2,1,0:T(8,128)}), f32[8,16,768]{2,1,0:T(8,128)S(1)}, u32[]{:S(2)}, u32[]{:S(2)}) %all-to-all-start.2) | async-done | bytes 393248 | tf_op jit(solution)/shard_map/all_to_all | solution.py:170
  74.2 3.5 %band.1 = bf16[32,384]{1,0:T(8,128)(2,1)} custom-call(f32[8,16,768]{2,1,0:T(8,128)} %copy-done.3, f32[2,384]{1,0:T(2,128)} %pad_maximum_fusion.2.norms, s32[8,384]{1,0:T(8,128)} %add_add_fusion.ids), custom_call_target="tpu_custom_call" | custom-call | flops 100000000 | bytes 1000000 | tf_op jit(solution)/shard_map/band/pallas_call | solution.py:180
  77.7 15.4 %all-gather = bf16[256,384]{1,0:T(8,128)(2,1)} all-gather(bf16[32,384]{1,0:T(8,128)(2,1)} %band.1), channel_id=2, replica_groups=mesh['z'=4,'x'=8,'yh'=2,'feat'=8] {'feat'}, dimensions={0}, use_global_device_ids=true | all-gather | bytes 221184 | tf_op jit(solution)/shard_map/all_gather | solution.py:186
  93.2 3.0 %spread.1 = (f32[128,768]{1,0:T(8,128)}, bf16[128,768]{1,0:T(8,128)(2,1)}, bf16[128,768]{1,0:T(8,128)(2,1)}, bf16[1024,128]{1,0:T(8,128)(2,1)}) custom-call(bf16[8,32,384]{2,1,0:T(8,128)(2,1)} %bitcast.29, bf16[384,768]{1,0:T(8,128)(2,1)} %copy-done.4, bf16[384,128]{1,0:T(8,128)(2,1)} %dynamic-slice_select_fusion.student_cols, ...), custom_call_target="tpu_custom_call" | custom-call | flops 1000000000 | bytes 4000000 | tf_op jit(solution)/shard_map/spread/pallas_call | solution.py:192
  96.2 22.5 %all-to-all-start.3 = ((bf16[64,16,128]{2,1,0:T(8,128)(2,1)}), bf16[64,16,128]{2,1,0:T(8,128)(2,1)S(1)}, u32[]{:S(2)}, u32[]{:S(2)}) async-start(bf16[64,16,128]{2,1,0:T(8,128)(2,1)} %bitcast.28), calls=%async_computation.3 | async-start | bytes 524288 | tf_op jit(solution)/shard_map/all_to_all | solution.py:204
  118.8 3.4 %convolution_convert_fusion = bf16[768,1024]{1,0:T(8,128)(2,1)} fusion(bf16[128,768]{1,0:T(8,128)(2,1)S(1)} %copy-done.2, s32[768]{0:T(1024)S(1)} %copy-done.11, s32[768]{0:T(1024)S(1)} %copy-done.12, s32[768]{0:T(1024)S(1)} %copy-done.10, s32[768]{0:T(1024)S(1)} %copy-done.13, pred[768]{0:T(1024)(128)(4,1)S(1)} %copy-done.19, ...), kind=kOutput, calls=%fused_computation.37 | convolution fusion | flops 384073728 | bytes 2571264 | tf_op jit(solution)/shard_map/dot_general | solution.py:25
  122.2 10.2 %all-to-all-done.3 = bf16[64,16,128]{2,1,0:T(8,128)(2,1)S(1)} async-done(((bf16[64,16,128]{2,1,0:T(8,128)(2,1)}), bf16[64,16,128]{2,1,0:T(8,128)(2,1)S(1)}, u32[]{:S(2)}, u32[]{:S(2)}) %all-to-all-start.3) | async-done | bytes 262176 | tf_op jit(solution)/shard_map/all_to_all | solution.py:204
  132.4 6.8 %all-to-all-start = ((bf16[8,96,1024]{2,1,0:T(8,128)(2,1)}), bf16[8,96,1024]{2,1,0:T(8,128)(2,1)}, u32[]{:S(2)}, u32[]{:S(2)}) async-start(bf16[8,96,1024]{2,1,0:T(8,128)(2,1)} %bitcast.27), calls=%async_computation | async-start | bytes 3145728 | tf_op jit(solution)/shard_map/all_to_all | solution.py:149
  139.2 4.8 %collective-permute-start.4 = (bf16[128,768]{1,0:T(8,128)(2,1)}, bf16[128,768]{1,0:T(8,128)(2,1)S(1)}, u32[]{:S(2)}, u32[]{:S(2)}) collective-permute-start(bf16[128,768]{1,0:T(8,128)(2,1)} %get-tuple-element.8), channel_id=1, source_target_pairs={{0,8},{8,16},{16,24},{24,32},{32,40},{40,48},{48,56},{56,64},{64,7... | collective-permute-start | bytes 589832 | tf_op jit(solution)/shard_map/ppermute | solution.py:33
  144.0 3.4 %collective-permute-start.5 = (bf16[128,768]{1,0:T(8,128)(2,1)}, bf16[128,768]{1,0:T(8,128)(2,1)S(1)}, u32[]{:S(2)}, u32[]{:S(2)}) collective-permute-start(bf16[128,768]{1,0:T(8,128)(2,1)} %get-tuple-element.9), channel_id=1, source_target_pairs={{0,16},{8,24},{16,32},{24,40},{32,48},{40,56},{48,64},{56,72},{64,... | collective-permute-start | bytes 589832 | tf_op jit(solution)/shard_map/ppermute | solution.py:33
  147.4 9.7 %collective-permute-done.4 = bf16[128,768]{1,0:T(8,128)(2,1)S(1)} collective-permute-done((bf16[128,768]{1,0:T(8,128)(2,1)}, bf16[128,768]{1,0:T(8,128)(2,1)S(1)}, u32[]{:S(2)}, u32[]{:S(2)}) %collective-permute-start.4) | collective-permute-done | bytes 196640 | tf_op jit(solution)/shard_map/ppermute | solution.py:33
  157.1 7.7 %collective-permute-done.5 = bf16[128,768]{1,0:T(8,128)(2,1)S(1)} collective-permute-done((bf16[128,768]{1,0:T(8,128)(2,1)}, bf16[128,768]{1,0:T(8,128)(2,1)S(1)}, u32[]{:S(2)}, u32[]{:S(2)}) %collective-permute-start.5) | collective-permute-done | bytes 196640 | tf_op jit(solution)/shard_map/ppermute | solution.py:33
  168.3 14.0 %all-gather.1 = bf16[128,128]{1,0:T(8,128)(2,1)S(1)} all-gather(bf16[16,128]{1,0:T(8,128)(2,1)S(1)} %reduce_sum.61), channel_id=3, replica_groups=mesh['z'=4,'x'=8,'yh'=2,'feat'=8] {'feat'}, dimensions={0}, use_global_device_ids=true | all-gather | bytes 36864 | tf_op jit(solution)/shard_map/all_gather | solution.py:206
  182.3 3.4 %all-to-all-start.4 = ((bf16[8,96,128]{2,1,0:T(8,128)(2,1)}), bf16[8,96,128]{2,1,0:T(8,128)(2,1)S(1)}, u32[]{:S(2)}, u32[]{:S(2)}) async-start(bf16[8,96,128]{2,1,0:T(8,128)(2,1)} %bitcast.10), calls=%async_computation.4 | async-start | bytes 393216 | tf_op jit(solution)/shard_map/all_to_all | solution.py:213
  188.3 5.7 %all-to-all-done.4 = bf16[8,96,128]{2,1,0:T(8,128)(2,1)S(1)} async-done(((bf16[8,96,128]{2,1,0:T(8,128)(2,1)}), bf16[8,96,128]{2,1,0:T(8,128)(2,1)S(1)}, u32[]{:S(2)}, u32[]{:S(2)}) %all-to-all-start.4) | async-done | bytes 196640 | tf_op jit(solution)/shard_map/all_to_all | solution.py:213
  194.0 3.7 %all-to-all-start.1 = ((bf16[8,16,1024]{2,1,0:T(8,128)(2,1)}), bf16[8,16,1024]{2,1,0:T(8,128)(2,1)S(1)}, u32[]{:S(2)}, u32[]{:S(2)}) async-start(bf16[8,16,1024]{2,1,0:T(8,128)(2,1)} %bitcast.2), calls=%async_computation.1 | async-start | bytes 524288 | tf_op jit(solution)/shard_map/all_to_all | solution.py:159
  198.6 12.6 %all-to-all-done.1 = bf16[8,16,1024]{2,1,0:T(8,128)(2,1)S(1)} async-done(((bf16[8,16,1024]{2,1,0:T(8,128)(2,1)}), bf16[8,16,1024]{2,1,0:T(8,128)(2,1)S(1)}, u32[]{:S(2)}, u32[]{:S(2)}) %all-to-all-start.1) | async-done | bytes 262176 | tf_op jit(solution)/shard_map/all_to_all | solution.py:159
  (94 shorter events, 24.7 us)
Async XLA Ops:
  0.6 29.4 %copy-start.2 = (bf16[128,768]{1,0:T(8,128)(2,1)S(1)}, bf16[128,768]{1,0:T(8,128)(2,1)}, u32[]{:S(2)}) copy-start(bf16[128,768]{1,0:T(8,128)(2,1)} %param.5) | copy-start | bytes 589828
  0.7 28.6 %copy-start.1 = (bf16[128,1024]{1,0:T(8,128)(2,1)S(1)}, bf16[128,1024]{1,0:T(8,128)(2,1)}, u32[]{:S(2)}) copy-start(bf16[128,1024]{1,0:T(8,128)(2,1)} %param.7) | copy-start | bytes 786436
  0.7 40.7 %copy-start.18 = (s32[384]{0:T(512)S(1)}, s32[384]{0:T(512)}, u32[]{:S(2)}) copy-start(s32[384]{0:T(512)} %param.8) | copy-start | bytes 4612
  2.1 40.6 %copy-start.14 = (s32[2,384]{1,0:T(2,128)S(1)}, s32[2,384]{1,0:T(2,128)}, u32[]{:S(2)}) copy-start(s32[2,384]{1,0:T(2,128)} %param.9) | copy-start | bytes 9220
  21.5 39.5 %collective-permute-start.2 = (f32[2,128]{1,0:T(2,128)S(1)}, f32[2,128]{1,0:T(2,128)S(1)}, u32[]{:S(2)}, u32[]{:S(2)}) collective-permute-start(f32[2,128]{1,0:T(2,128)S(1)} %pad_maximum_fusion.3), channel_id=1, source_target_pairs={{0,504},{8,0},{16,8},{24,16},{32,24},{40,32},{48,40},{56,48},{64,5... | collective-permute-start | bytes 3080 | tf_op jit(solution)/shard_map/ppermute | solution.py:33
  26.8 34.2 %collective-permute-start.3 = (f32[2,128]{1,0:T(2,128)S(1)}, f32[2,128]{1,0:T(2,128)S(1)}, u32[]{:S(2)}, u32[]{:S(2)}) collective-permute-start(f32[2,128]{1,0:T(2,128)S(1)} %pad_maximum_fusion.3), channel_id=1, source_target_pairs={{0,496},{8,504},{16,0},{24,8},{32,16},{40,24},{48,32},{56,40},{64,... | collective-permute-start | bytes 3080 | tf_op jit(solution)/shard_map/ppermute | solution.py:33
  30.7 24.1 %collective-permute-start = (bf16[128,1792]{1,0:T(8,128)(2,1)}, bf16[128,1792]{1,0:T(8,128)(2,1)S(1)}, u32[]{:S(2)}, u32[]{:S(2)}) collective-permute-start(bf16[128,1792]{1,0:T(8,128)(2,1)} %constant_dynamic-update-slice_fusion), channel_id=1, source_target_pairs={{0,504},{8,0},{16,8},{24,16},{32,24},{40,32},{48,40},{56,48},{64,5... | collective-permute-start | bytes 1376264 | tf_op jit(solution)/shard_map/ppermute | solution.py:33
  35.4 19.4 %collective-permute-start.1 = (bf16[128,1792]{1,0:T(8,128)(2,1)}, bf16[128,1792]{1,0:T(8,128)(2,1)S(1)}, u32[]{:S(2)}, u32[]{:S(2)}) collective-permute-start(bf16[128,1792]{1,0:T(8,128)(2,1)} %constant_dynamic-update-slice_fusion), channel_id=1, source_target_pairs={{0,496},{8,504},{16,0},{24,8},{32,16},{40,24},{48,32},{56,40},{64,... | collective-permute-start | bytes 1376264 | tf_op jit(solution)/shard_map/ppermute | solution.py:33
  57.5 15.9 %all-to-all-start.2 = ((f32[8,16,768]{2,1,0:T(8,128)}), f32[8,16,768]{2,1,0:T(8,128)S(1)}, u32[]{:S(2)}, u32[]{:S(2)}) async-start(f32[8,16,768]{2,1,0:T(8,128)} %bitcast.4), calls=%async_computation.2 | async-start | bytes 786432 | tf_op jit(solution)/shard_map/all_to_all | solution.py:170
  93.1 25.6 %copy-start.11 = (s32[768]{0:T(1024)S(1)}, s32[768]{0:T(1024)}, u32[]{:S(2)}) copy-start(s32[768]{0:T(1024)} %get-tuple-element.24) | copy-start | bytes 9220
  93.1 25.6 %copy-start.12 = (s32[768]{0:T(1024)S(1)}, s32[768]{0:T(1024)}, u32[]{:S(2)}) copy-start(s32[768]{0:T(1024)} %get-tuple-element.25) | copy-start | bytes 9220
  93.1 25.6 %copy-start.13 = (s32[768]{0:T(1024)S(1)}, s32[768]{0:T(1024)}, u32[]{:S(2)}) copy-start(s32[768]{0:T(1024)} %get-tuple-element.26) | copy-start | bytes 9220
  93.1 25.6 %copy-start.15 = (f32[128]{0:T(128)S(1)}, f32[128]{0:T(128)}, u32[]{:S(2)}) copy-start(f32[128]{0:T(128)} %get-tuple-element.18) | copy-start | bytes 1540
  93.1 25.6 %copy-start.16 = (f32[128]{0:T(128)S(1)}, f32[128]{0:T(128)}, u32[]{:S(2)}) copy-start(f32[128]{0:T(128)} %get-tuple-element.20) | copy-start | bytes 1540
  93.1 25.6 %copy-start.17 = (f32[128]{0:T(128)S(1)}, f32[128]{0:T(128)}, u32[]{:S(2)}) copy-start(f32[128]{0:T(128)} %get-tuple-element.21) | copy-start | bytes 1540
  93.2 25.6 %copy-start.19 = (pred[768]{0:T(1024)(128)(4,1)S(1)}, pred[768]{0:T(1024)(128)(4,1)}, u32[]{:S(2)}) copy-start(pred[768]{0:T(1024)(128)(4,1)} %get-tuple-element.27) | copy-start | bytes 2308
  93.2 25.6 %copy-start.20 = (pred[768]{0:T(1024)(128)(4,1)S(1)}, pred[768]{0:T(1024)(128)(4,1)}, u32[]{:S(2)}) copy-start(pred[768]{0:T(1024)(128)(4,1)} %get-tuple-element.28) | copy-start | bytes 2308
  96.2 36.2 %all-to-all-start.3 = ((bf16[64,16,128]{2,1,0:T(8,128)(2,1)}), bf16[64,16,128]{2,1,0:T(8,128)(2,1)S(1)}, u32[]{:S(2)}, u32[]{:S(2)}) async-start(bf16[64,16,128]{2,1,0:T(8,128)(2,1)} %bitcast.28), calls=%async_computation.3 | async-start | bytes 524288 | tf_op jit(solution)/shard_map/all_to_all | solution.py:204
  132.4 33.1 %copy-start.7 = (f32[128,768]{1,0:T(8,128)S(1)}, f32[128,768]{1,0:T(8,128)}, u32[]{:S(2)}) copy-start(f32[128,768]{1,0:T(8,128)} %get-tuple-element.7) | copy-start | bytes 1179652
  132.4 49.9 %all-to-all-start = ((bf16[8,96,1024]{2,1,0:T(8,128)(2,1)}), bf16[8,96,1024]{2,1,0:T(8,128)(2,1)}, u32[]{:S(2)}, u32[]{:S(2)}) async-start(bf16[8,96,1024]{2,1,0:T(8,128)(2,1)} %bitcast.27), calls=%async_computation | async-start | bytes 3145728 | tf_op jit(solution)/shard_map/all_to_all | solution.py:149
  139.2 17.9 %collective-permute-start.4 = (bf16[128,768]{1,0:T(8,128)(2,1)}, bf16[128,768]{1,0:T(8,128)(2,1)S(1)}, u32[]{:S(2)}, u32[]{:S(2)}) collective-permute-start(bf16[128,768]{1,0:T(8,128)(2,1)} %get-tuple-element.8), channel_id=1, source_target_pairs={{0,8},{8,16},{16,24},{24,32},{32,40},{40,48},{48,56},{56,64},{64,7... | collective-permute-start | bytes 589832 | tf_op jit(solution)/shard_map/ppermute | solution.py:33
  144.0 20.8 %collective-permute-start.5 = (bf16[128,768]{1,0:T(8,128)(2,1)}, bf16[128,768]{1,0:T(8,128)(2,1)S(1)}, u32[]{:S(2)}, u32[]{:S(2)}) collective-permute-start(bf16[128,768]{1,0:T(8,128)(2,1)} %get-tuple-element.9), channel_id=1, source_target_pairs={{0,16},{8,24},{16,32},{24,40},{32,48},{40,56},{48,64},{56,72},{64,... | collective-permute-start | bytes 589832 | tf_op jit(solution)/shard_map/ppermute | solution.py:33
  182.3 11.7 %all-to-all-start.4 = ((bf16[8,96,128]{2,1,0:T(8,128)(2,1)}), bf16[8,96,128]{2,1,0:T(8,128)(2,1)S(1)}, u32[]{:S(2)}, u32[]{:S(2)}) async-start(bf16[8,96,128]{2,1,0:T(8,128)(2,1)} %bitcast.10), calls=%async_computation.4 | async-start | bytes 393216 | tf_op jit(solution)/shard_map/all_to_all | solution.py:213
  194.0 17.3 %all-to-all-start.1 = ((bf16[8,16,1024]{2,1,0:T(8,128)(2,1)}), bf16[8,16,1024]{2,1,0:T(8,128)(2,1)S(1)}, u32[]{:S(2)}, u32[]{:S(2)}) async-start(bf16[8,16,1024]{2,1,0:T(8,128)(2,1)} %bitcast.2), calls=%async_computation.1 | async-start | bytes 524288 | tf_op jit(solution)/shard_map/all_to_all | solution.py:159
  (8 other events, 36.0 us)

commit v2 on v1

v2 whole, which is shorter than its diff:
```python
import functools

import jax
import jax.numpy as jnp
from jax import lax
from jax.experimental import pallas as pl
from jax.experimental.pallas import tpu as pltpu
from jax.sharding import Mesh, PartitionSpec as P

STEPS = 3
EPSILON = 1e-06
TEMPER = 50.0
MARGIN = 0.01
LOSS_SCALE = 1024.0

DP_SIZES = {64: (4, 8, 2), 8: (2, 2, 2)}
DP = ("z", "x", "yh")
LANES = 128
f32 = jnp.float32
bf16 = jnp.bfloat16
HIGHEST = lax.Precision.HIGHEST


def dot(left, right, contract, precision=None):
    return lax.dot_general(
        left, right, ((contract[:1], contract[1:]), ((), ())),
        preferred_element_type=f32, precision=precision,
    )


def passed_along(array, by):
    peers = lax.axis_size(DP)
    return lax.ppermute(array, DP, [(i, (i + by) % peers) for i in range(peers)])


def band_kernel(parts, ids, tiles, coefs):
    peers = tiles.shape[0]
    rows = parts.shape[1]
    band = ids.shape[1]
    texts = band // STEPS
    sums = jnp.sum(parts[...], 0)
    tail = sums[:, 2 * band :]
    proj_sq = jnp.concatenate([tail[s : s + 1] for s in range(STEPS)], 1)
    teach_sq = jnp.concatenate([tail[STEPS + s : STEPS + s + 1] for s in range(STEPS)], 1)
    cross = tail[2 * STEPS : 2 * STEPS + 1]
    inv_proj = lax.rsqrt(proj_sq + EPSILON)
    inv_teach = lax.rsqrt(teach_sq + EPSILON)
    both = inv_proj[:, :texts] * inv_teach[:, :texts]
    cosine = cross * both
    row_id = lax.broadcasted_iota(jnp.int32, (rows, band), 0)
    anchor = (ids[0:1, :] == row_id).astype(f32)
    own = (ids[3:4, :] == row_id).astype(f32)
    row_proj = jnp.sum(own * inv_proj, 1, keepdims=True)
    row_teach = jnp.sum(own * inv_teach, 1, keepdims=True)
    sim = sums[:, :band] * (row_proj * inv_proj)
    teach = sums[:, band : 2 * band] * (row_teach * inv_teach)
    col_id = lax.broadcasted_iota(jnp.int32, (band, band), 0)
    pick = (col_id == ids[1:2, :]).astype(f32) - (col_id == ids[2:3, :]).astype(f32)
    gap_s = jnp.sum(dot(sim, anchor, (0, 0), HIGHEST) * pick, 0, keepdims=True)
    gap_t = jnp.sum(dot(teach, anchor, (0, 0), HIGHEST) * pick, 0, keepdims=True)
    weight = jnp.tanh(TEMPER * gap_t)
    slope = -weight * jax.nn.sigmoid(TEMPER * (MARGIN - weight * gap_s))
    grad = 2.0 * (sim - teach) + dot(anchor * slope, pick, (1, 1), HIGHEST)
    product = grad * sim
    along = jnp.sum(product, 1, keepdims=True)
    inner = jnp.sum(product + along * own, 0, keepdims=True) * (inv_proj * inv_proj)
    high = inner.astype(bf16).astype(f32)
    low = inner - high
    tail_id = lax.broadcasted_iota(jnp.int32, (rows, texts), 0)
    extra = jnp.zeros((rows, texts), f32)
    for s in range(STEPS):
        piece = slice(s * texts, (s + 1) * texts)
        extra = jnp.where(tail_id == 2 * s, high[:, piece], extra)
        extra = jnp.where(tail_id == 2 * s + 1, low[:, piece], extra)
    tile = jnp.concatenate([grad * (row_proj * inv_proj), extra], 1).astype(bf16)
    for peer in range(peers):
        tiles[peer] = tile
    coefs[...] = jnp.concatenate(
        [cosine * inv_proj[:, :texts] * inv_proj[:, :texts], both, jnp.zeros((6, texts), f32)], 0
    )


def grad_kernel(gathered, coefs, proj_band, teacher, regrouped, rows_grad, grad_w):
    band = proj_band.shape[0]
    texts = band // STEPS
    gathered = gathered[...]
    tile = gathered[:, :, :band].reshape(texts, band)
    tail = jnp.sum(gathered[:, :, band:].astype(f32), 0)
    along = [
        tail[2 * s : 2 * s + 1] + tail[2 * s + 1 : 2 * s + 2] for s in range(STEPS)
    ]
    diagonal = lax.broadcasted_iota(jnp.int32, (texts, texts), 0) == lax.broadcasted_iota(
        jnp.int32, (texts, texts), 1
    )

    def upright(values):
        return jnp.sum(jnp.where(diagonal, values, 0.0), 1, keepdims=True)

    for s in range(STEPS):
        piece = slice(s * texts, (s + 1) * texts)
        lone = proj_band[piece, :].astype(f32)
        scale = -along[s]
        if s == 0:
            scale = scale + coefs[0:1, :]
        terms = dot(tile[:, piece], proj_band[0:texts, :], (0, 0)) + upright(scale) * lone
        if s == 0:
            terms = terms + dot(tile, proj_band[...], (1, 0))
            terms = terms - upright(coefs[1:2, :]) * teacher[...].astype(f32)
        rows_grad[piece, :] = (LOSS_SCALE * terms).astype(bf16)
    grad_w[...] = dot(regrouped[...], rows_grad[...], (1, 0)).astype(bf16)


def by_x(sizes, features):
    z_size, x_size, yh_size = sizes
    share = features // (z_size * x_size)
    out = lax.broadcasted_iota(jnp.int32, (features, features), 0)
    place, offset = out // share, out % share
    source = (place % z_size * x_size + place // z_size) * share + offset
    return (lax.broadcasted_iota(jnp.int32, out.shape, 1) == source).astype(bf16)


def shards(student, proj_weight, teacher, anchors, pairs, *, sizes):
    z_size, x_size, yh_size = sizes
    n_dp = z_size * x_size * yh_size
    n_feat = lax.axis_size("feat")
    texts, features = student.shape
    width = teacher.shape[1]
    band = STEPS * texts
    rows = texts // n_feat
    share = features // n_dp
    padded = -(-share // 16) * 16
    feat = lax.axis_index("feat")

    packed = jnp.concatenate([teacher, student], 1)
    near = passed_along(packed, -1)
    far = passed_along(packed, -2)

    projected = dot(student, proj_weight, (1, 0))
    teacher_wide = teacher.astype(f32)

    student_rest = jnp.concatenate([near[:, width:], far[:, width:]], 0)
    rest = dot(student_rest, proj_weight, (1, 0))
    near_teach, far_teach = near[:, :width], far[:, :width]
    proj_own = projected.astype(bf16)
    proj_rest = rest.astype(bf16)
    proj_band = jnp.concatenate([proj_own, proj_rest], 0)
    near_wide, far_wide = near_teach.astype(f32), far_teach.astype(f32)
    norms = jnp.concatenate(
        [
            jnp.sum(projected * projected, 1)[None],
            jnp.sum(rest * rest, 1).reshape(STEPS - 1, texts),
            jnp.sum(teacher_wide * teacher_wide, 1)[None],
            jnp.sum(near_wide * near_wide, 1)[None],
            jnp.sum(far_wide * far_wide, 1)[None],
            jnp.sum(projected * teacher_wide, 1)[None],
            jnp.zeros((rows - 2 * STEPS - 1, texts), f32),
        ],
        0,
    )
    parts = jnp.concatenate(
        [
            dot(proj_own, proj_own, (1, 1)),
            dot(proj_own, proj_rest, (1, 1)),
            dot(teacher, teacher, (1, 1)),
            dot(teacher, near_teach, (1, 1)),
            dot(teacher, far_teach, (1, 1)),
        ],
        1,
    ).reshape(n_feat, rows, 2 * band)
    parts = jnp.concatenate(
        [parts, jnp.broadcast_to(norms[None], (n_feat, rows, texts))], 2
    )
    parts = lax.all_to_all(parts, "feat", 0, 0)
    ids = jnp.concatenate(
        [
            anchors[None] - feat * rows,
            pairs,
            lax.broadcasted_iota(jnp.int32, (1, band), 1) - feat * rows,
            jnp.zeros((4, band), jnp.int32),
        ],
        0,
    )
    tiles, coefs = pl.pallas_call(
        band_kernel,
        out_shape=(
            jax.ShapeDtypeStruct((n_feat, rows, band + texts), bf16),
            jax.ShapeDtypeStruct((8, texts), f32),
        ),
        cost_estimate=pl.CostEstimate(flops=10**8, bytes_accessed=10**6, transcendentals=1000),
        name="band",
    )(parts, ids)
    gathered = lax.all_to_all(tiles, "feat", 0, 0)

    student_band = jnp.concatenate([student, student_rest], 0)
    regrouped = dot(by_x(sizes, features), student_band, (1, 1)).astype(bf16)
    rows_grad, grad_w = pl.pallas_call(
        grad_kernel,
        out_shape=(
            jax.ShapeDtypeStruct((band, width), bf16),
            jax.ShapeDtypeStruct((features, width), bf16),
        ),
        compiler_params=pltpu.CompilerParams(vmem_limit_bytes=32 * 2**20),
        cost_estimate=pl.CostEstimate(flops=10**9, bytes_accessed=4 * 10**6, transcendentals=0),
        name="grad",
    )(gathered, coefs, proj_band, teacher, regrouped)

    grad_w = lax.all_to_all(
        grad_w.reshape(x_size, features // x_size, width), "x", 0, 0
    ).reshape(features, width)
    zy = z_size * yh_size
    row_out = lax.broadcasted_iota(jnp.int32, (zy * padded, features), 0)
    row_in = lax.broadcasted_iota(jnp.int32, (zy * padded, features), 1) % (zy * share)
    add_rows = (
        (row_out // padded == row_in // share) & (row_out % padded == row_in % share)
    ).astype(bf16)
    grad_w = dot(add_rows, grad_w, (1, 0)).astype(bf16)
    grad_w = lax.all_to_all(grad_w.reshape(zy, padded, width), ("z", "yh"), 0, 0)
    grad_w = jnp.sum(grad_w.astype(f32), 0)[:share]

    back = dot(proj_weight, rows_grad, (1, 1)).astype(bf16)
    back = lax.all_to_all(back.reshape(n_feat, features // n_feat, band), "feat", 0, 0)
    back = jnp.sum(back.astype(f32), 0)
    grad_student = back[:, :texts]
    for s in range(1, STEPS):
        grad_student = grad_student + passed_along(back[:, s * texts : (s + 1) * texts], s)
    return (grad_w, grad_student.T)


def solution(mesh):
    n_dp, n_feat = mesh.devices.shape
    sizes = DP_SIZES[n_dp]
    split = Mesh(mesh.devices.reshape(*sizes, n_feat), (*DP, "feat"))
    return jax.shard_map(
        functools.partial(shards, sizes=sizes),
        mesh=split,
        in_specs=(P(DP, None), P(None, "feat"), P(DP, "feat"), P(DP), P(None, DP)),
        out_specs=(P(DP, "feat"), P(DP, "feat")),
        check_vma=False,
    )
```

time: 215 us -> 156 us (0.73)
  the two profiles are of different devices: /device:TPU:6 before, /device:TPU:8 now
where the time goes in v2:
time: 156 us; the launch traced here: 155 us
  waiting for transfers between devices  56.7 us (36%)
  starting transfers between devices  54.9 us (35%)
  blocking collectives  18.7 us (12%)
  matrix products  9.04 us (6%)
  Pallas kernels  6.21 us (4%)
  local copies, waits for them, and re-layouts  5.26 us (3%)
  other arithmetic  3.22 us (2%)
    ppermute x4, starting transfers between devices, passed_along(): lax.ppermute(array, DP, [(i, (i + by) % peers) for i in range(peers)])  30.8 us
    ppermute x4, waiting for transfers between devices, passed_along(): lax.ppermute(array, DP, [(i, (i + by) % peers) for i in range(peers)])  22.8 us
    all_to_all x1, waiting for transfers between devices, shards(): lax.all_to_all(grad_w.reshape(x_size, features // x_size, width), 'x', 0, 0)  20.4 us
    all_to_all x1, blocking collectives, shards(): lax.all_to_all(back.reshape(n_feat, features // n_feat, band), 'feat', 0, 0)  18.7 us
    all_to_all x1, starting transfers between devices, shards(): lax.all_to_all(grad_w.reshape(zy, padded, width), ('z', 'yh'), 0, 0)  10.2 us
    all_to_all x1, waiting for transfers between devices, shards(): parts = lax.all_to_all(parts, 'feat', 0, 0)  10.1 us
    dot_general x10, matrix products, dot(): lax.dot_general(left, right, ((contract[:1], contract[1:]), ((), ())), pr...  9.04 us
    all_to_all x1, starting transfers between devices, shards(): gathered = lax.all_to_all(tiles, 'feat', 0, 0)  6.17 us
  transfers between devices with their start and end apart: 8, of which 5 were waited for; matrix products, arithmetic and copies ran while one was open for 4% of the time, Pallas kernels for 0%

profile of v2, /device:TPU:8, one launch (start us, length us, event | category | flops | bytes accessed | tf_op | source)
XLA Modules:
  0.0 155.2 jit_solution(4803601065532917464)
XLA Ops:
  0.6 1.8 %constant_dynamic-update-slice_fusion.1 = bf16[128,1792]{1,0:T(8,128)(2,1)} fusion(bf16[128,1024]{1,0:T(8,128)(2,1)} %teacher.1), kind=kLoop, calls=%fused_computation.97 | loop fusion | bytes 524288
  2.4 1.6 %constant_dynamic-update-slice_fusion = bf16[128,1792]{1,0:T(8,128)(2,1)} fusion(bf16[128,1792]{1,0:T(8,128)(2,1)} %constant_dynamic-update-slice_fusion.1, bf16[128,768]{1,0:T(8,128)(2,1)} %param.5), kind=kLoop, calls=%fused_computation.96 | loop fusion | bytes 393216 | tf_op jit(solution)/shard_map/concatenate | solution.py:134
  4.1 17.5 %collective-permute-start = (bf16[128,1792]{1,0:T(8,128)(2,1)}, bf16[128,1792]{1,0:T(8,128)(2,1)S(1)}, u32[]{:S(2)}, u32[]{:S(2)}) collective-permute-start(bf16[128,1792]{1,0:T(8,128)(2,1)} %constant_dynamic-update-slice_fusion), channel_id=1, source_target_pairs={{0,504},{8,0},{16,8},{24,16},{32,24},{40,32},{48,40},{56,48},{64,5... | collective-permute-start | bytes 1376264 | tf_op jit(solution)/shard_map/ppermute | solution.py:33
  21.6 2.7 %collective-permute-start.1 = (bf16[128,1792]{1,0:T(8,128)(2,1)}, bf16[128,1792]{1,0:T(8,128)(2,1)S(1)}, u32[]{:S(2)}, u32[]{:S(2)}) collective-permute-start(bf16[128,1792]{1,0:T(8,128)(2,1)} %constant_dynamic-update-slice_fusion), channel_id=1, source_target_pairs={{0,496},{8,504},{16,0},{24,8},{32,16},{40,24},{48,32},{56,40},{64,... | collective-permute-start | bytes 1376264 | tf_op jit(solution)/shard_map/ppermute | solution.py:33
  24.3 1.6 %fusion.41 = (f32[128]{0:T(128)S(1)}, f32[128]{0:T(128)S(1)}, f32[128]{0:T(128)S(1)}, bf16[128,1024]{1,0:T(8,128)(2,1)S(1)}) fusion(bf16[128,1024]{1,0:T(8,128)(2,1)} %teacher.1, bf16[128,768]{1,0:T(8,128)(2,1)} %param.5, bf16[768,1024]{1,0:T(8,128)(2,1)S(1)} %copy-done), kind=kOutput, calls=%fused_computation.62 | convolution fusion | flops 202374784 | bytes 2295296 | tf_op jit(solution)/shard_map/dot_general | solution.py:25
  26.1 15.3 %collective-permute-done = bf16[128,1792]{1,0:T(8,128)(2,1)S(1)} collective-permute-done((bf16[128,1792]{1,0:T(8,128)(2,1)}, bf16[128,1792]{1,0:T(8,128)(2,1)S(1)}, u32[]{:S(2)}, u32[]{:S(2)}) %collective-permute-start) | collective-permute-done | bytes 458784 | tf_op jit(solution)/shard_map/ppermute | solution.py:33
  44.2 0.8 pad_maximum_fusion.1
  45.0 3.4 %all-to-all-start = ((f32[8,16,896]{2,1,0:T(8,128)}), f32[8,16,896]{2,1,0:T(8,128)S(1)}, u32[]{:S(2)}, u32[]{:S(2)}) async-start(f32[8,16,896]{2,1,0:T(8,128)} %pad_maximum_fusion.1), calls=%async_computation | async-start | bytes 917504 | tf_op jit(solution)/shard_map/all_to_all | solution.py:173
  49.3 10.1 %all-to-all-done.parts = f32[8,16,896]{2,1,0:T(8,128)S(1)} async-done(((f32[8,16,896]{2,1,0:T(8,128)}), f32[8,16,896]{2,1,0:T(8,128)S(1)}, u32[]{:S(2)}, u32[]{:S(2)}) %all-to-all-start) | async-done | bytes 458784 | tf_op jit(solution)/shard_map/all_to_all | solution.py:173
  59.4 0.8 copy-done.7
  60.1 3.6 %band.1 = (bf16[8,16,512]{2,1,0:T(8,128)(2,1)}, f32[8,128]{1,0:T(8,128)}) custom-call(f32[8,16,896]{2,1,0:T(8,128)} %copy-done.7, s32[8,384]{1,0:T(8,128)} %add_add_fusion.ids), custom_call_target="tpu_custom_call" | custom-call | flops 100000000 | bytes 1000000 | tf_op jit(solution)/shard_map/band/pallas_call | solution.py:183
  63.7 6.2 %all-to-all-start.1 = ((bf16[8,16,512]{2,1,0:T(8,128)(2,1)}), bf16[8,16,512]{2,1,0:T(8,128)(2,1)S(1)}, u32[]{:S(2)}, u32[]{:S(2)}) async-start(bf16[8,16,512]{2,1,0:T(8,128)(2,1)} %get-tuple-element.6), calls=%async_computation.1 | async-start | bytes 262144 | tf_op jit(solution)/shard_map/all_to_all | solution.py:192
  69.9 2.2 %fusion.11.regrouped = bf16[768,384]{1,0:T(8,128)(2,1)S(1)} fusion(s32[768]{0:T(1024)S(1)} %get-tuple-element.20, s32[768]{0:T(1024)S(1)} %get-tuple-element.21, s32[768]{0:T(1024)S(1)} %get-tuple-element.19, s32[768]{0:T(1024)S(1)} %get-tuple-element.22, pred[768]{0:T(1024)(128)(4,1)S(1)} %get-tuple-element.23, pred[768]{0:T(1024)(128)(4,1)S(1)} %get-tuple-element.24, ...), kind=kOutput, calls=%fused_computation.18 | convolution fusion | flops 470384640 | bytes 1193472 | tf_op jit(solution)/shard_map/dot_general | solution.py:25
  72.2 3.4 %all-to-all-done.1.gathered = bf16[8,16,512]{2,1,0:T(8,128)(2,1)S(1)} async-done(((bf16[8,16,512]{2,1,0:T(8,128)(2,1)}), bf16[8,16,512]{2,1,0:T(8,128)(2,1)S(1)}, u32[]{:S(2)}, u32[]{:S(2)}) %all-to-all-start.1) | async-done | bytes 131104 | tf_op jit(solution)/shard_map/all_to_all | solution.py:192
  75.6 2.6 %grad.1 = (bf16[384,1024]{1,0:T(8,128)(2,1)S(1)}, bf16[768,1024]{1,0:T(8,128)(2,1)}) custom-call(bf16[8,16,512]{2,1,0:T(8,128)(2,1)S(1)} %all-to-all-done.1.gathered, f32[8,128]{1,0:T(8,128)S(1)} %copy-done.2, bf16[384,1024]{1,0:T(8,128)(2,1)S(1)} %pad_maximum_fusion.proj_band, bf16[128,1024]{1,0:T(8,128)(2,1)S(1)} %copy-done.1, ...), custom_call_target="tpu_custom_call" | custom-call | flops 1000000000 | bytes 4000000 | tf_op jit(solution)/shard_map/grad/pallas_call | solution.py:196
  78.2 0.8 fusion.14
  79.3 18.7 %all_to_all.25 = bf16[8,96,384]{2,1,0:T(8,128)(2,1)S(1)} all-to-all(bf16[8,96,384]{2,1,0:T(8,128)(2,1)S(1)} %bitcast.38), channel_id=1, replica_groups=mesh['z'=4,'x'=8,'yh'=2,'feat'=8] {'feat'}, dimensions={0} | all-to-all | bytes 1179648 | tf_op jit(solution)/shard_map/all_to_all | solution.py:221
  98.1 4.3 %all-to-all-start.2 = ((bf16[8,96,1024]{2,1,0:T(8,128)(2,1)}), bf16[8,96,1024]{2,1,0:T(8,128)(2,1)}, u32[]{:S(2)}, u32[]{:S(2)}) async-start(bf16[8,96,1024]{2,1,0:T(8,128)(2,1)} %bitcast.9), calls=%async_computation.2 | async-start | bytes 3145728 | tf_op jit(solution)/shard_map/all_to_all | solution.py:207
  102.5 20.4 %all-to-all-done.2 = bf16[8,96,1024]{2,1,0:T(8,128)(2,1)} async-done(((bf16[8,96,1024]{2,1,0:T(8,128)(2,1)}), bf16[8,96,1024]{2,1,0:T(8,128)(2,1)}, u32[]{:S(2)}, u32[]{:S(2)}) %all-to-all-start.2) | async-done | bytes 1572896 | tf_op jit(solution)/shard_map/all_to_all | solution.py:207
  122.9 2.6 %convolution_convert_fusion.1 = bf16[128,1024]{1,0:T(8,128)(2,1)} fusion(bf16[768,1024]{1,0:T(8,128)(2,1)} %bitcast.10, s32[128]{0:T(128)S(1)} %get-tuple-element.30, s32[128]{0:T(128)S(1)} %get-tuple-element.31, s32[768]{0:T(1024)S(1)} %get-tuple-element.25, s32[768]{0:T(1024)S(1)} %get-tuple-element.26, s32[128]{0:T(128)S(1)} %get-tuple-element.29, ...), kind=kOutput, calls=%fused_computation.21 | convolution fusion | flops 203227136 | bytes 1844224 | tf_op jit(solution)/shard_map/dot_general | solution.py:25
  125.5 10.2 %all-to-all-start.3 = ((bf16[8,16,1024]{2,1,0:T(8,128)(2,1)}), bf16[8,16,1024]{2,1,0:T(8,128)(2,1)S(1)}, u32[]{:S(2)}, u32[]{:S(2)}) async-start(bf16[8,16,1024]{2,1,0:T(8,128)(2,1)} %bitcast.11), calls=%async_computation.3 | async-start | bytes 524288 | tf_op jit(solution)/shard_map/all_to_all | solution.py:217
  135.8 7.8 %collective-permute-start.2 = (f32[96,128]{1,0:T(8,128)S(1)}, f32[96,128]{1,0:T(8,128)S(1)}, u32[]{:S(2)}, u32[]{:S(2)}) collective-permute-start(f32[96,128]{1,0:T(8,128)S(1)} %get-tuple-element.16), channel_id=1, source_target_pairs={{0,8},{8,16},{16,24},{24,32},{32,40},{40,48},{48,56},{56,64},{64,7... | collective-permute-start | bytes 147464 | tf_op jit(solution)/shard_map/ppermute | solution.py:33
  143.6 2.8 %collective-permute-start.3 = (f32[96,128]{1,0:T(8,128)S(1)}, f32[96,128]{1,0:T(8,128)S(1)}, u32[]{:S(2)}, u32[]{:S(2)}) collective-permute-start(f32[96,128]{1,0:T(8,128)S(1)} %get-tuple-element.17), channel_id=1, source_target_pairs={{0,16},{8,24},{16,32},{24,40},{32,48},{40,56},{48,64},{56,72},{64,... | collective-permute-start | bytes 147464 | tf_op jit(solution)/shard_map/ppermute | solution.py:33
  146.4 7.5 %collective-permute-done.2 = f32[96,128]{1,0:T(8,128)S(1)} collective-permute-done((f32[96,128]{1,0:T(8,128)S(1)}, f32[96,128]{1,0:T(8,128)S(1)}, u32[]{:S(2)}, u32[]{:S(2)}) %collective-permute-start.2) | collective-permute-done | bytes 49184 | tf_op jit(solution)/shard_map/ppermute | solution.py:33
  (63 shorter events, 5.4 us)
Async XLA Ops:
  0.6 23.7 %copy-start = (bf16[768,1024]{1,0:T(8,128)(2,1)S(1)}, bf16[768,1024]{1,0:T(8,128)(2,1)}, u32[]{:S(2)}) copy-start(bf16[768,1024]{1,0:T(8,128)(2,1)} %param.6) | copy-start | bytes 4718596
  4.1 37.4 %collective-permute-start = (bf16[128,1792]{1,0:T(8,128)(2,1)}, bf16[128,1792]{1,0:T(8,128)(2,1)S(1)}, u32[]{:S(2)}, u32[]{:S(2)}) collective-permute-start(bf16[128,1792]{1,0:T(8,128)(2,1)} %constant_dynamic-update-slice_fusion), channel_id=1, source_target_pairs={{0,504},{8,0},{16,8},{24,16},{32,24},{40,32},{48,40},{56,48},{64,5... | collective-permute-start | bytes 1376264 | tf_op jit(solution)/shard_map/ppermute | solution.py:33
  21.6 19.9 %collective-permute-start.1 = (bf16[128,1792]{1,0:T(8,128)(2,1)}, bf16[128,1792]{1,0:T(8,128)(2,1)S(1)}, u32[]{:S(2)}, u32[]{:S(2)}) collective-permute-start(bf16[128,1792]{1,0:T(8,128)(2,1)} %constant_dynamic-update-slice_fusion), channel_id=1, source_target_pairs={{0,496},{8,504},{16,0},{24,8},{32,16},{40,24},{48,32},{56,40},{64,... | collective-permute-start | bytes 1376264 | tf_op jit(solution)/shard_map/ppermute | solution.py:33
  25.9 16.3 %copy-start.3 = (bf16[128,1024]{1,0:T(8,128)(2,1)}, bf16[128,1024]{1,0:T(8,128)(2,1)S(1)}, u32[]{:S(2)}) copy-start(bf16[128,1024]{1,0:T(8,128)(2,1)S(1)} %get-tuple-element.15) | copy-start | bytes 786436
  41.5 0.7 copy-start.9
  41.5 1.7 %copy-start.11 = (bf16[128,768]{1,0:T(8,128)(2,1)}, bf16[128,768]{1,0:T(8,128)(2,1)S(1)}, u32[]{:S(2)}) copy-start(bf16[128,768]{1,0:T(8,128)(2,1)S(1)} %slice.33) | copy-start | bytes 589828
  41.5 1.5 copy-start.1
  42.2 0.8 copy-start.5
  43.5 4.9 %copy-start.13 = (s32[384]{0:T(512)S(1)}, s32[384]{0:T(512)}, u32[]{:S(2)}) copy-start(s32[384]{0:T(512)} %param.8) | copy-start | bytes 4612
  43.5 5.0 %copy-start.12 = (s32[2,384]{1,0:T(2,128)S(1)}, s32[2,384]{1,0:T(2,128)}, u32[]{:S(2)}) copy-start(s32[2,384]{1,0:T(2,128)} %param.9) | copy-start | bytes 9220
  43.9 26.0 %copy-start.8 = (bf16[128,768]{1,0:T(8,128)(2,1)S(1)}, bf16[128,768]{1,0:T(8,128)(2,1)}, u32[]{:S(2)}) copy-start(bf16[128,768]{1,0:T(8,128)(2,1)} %param.5) | copy-start | bytes 589828
  44.2 25.7 %copy-start.10 = (bf16[128,768]{1,0:T(8,128)(2,1)S(1)}, bf16[128,768]{1,0:T(8,128)(2,1)}, u32[]{:S(2)}) copy-start(bf16[128,768]{1,0:T(8,128)(2,1)} %copy-done.9) | copy-start | bytes 589828
  45.0 14.4 %all-to-all-start = ((f32[8,16,896]{2,1,0:T(8,128)}), f32[8,16,896]{2,1,0:T(8,128)S(1)}, u32[]{:S(2)}, u32[]{:S(2)}) async-start(f32[8,16,896]{2,1,0:T(8,128)} %pad_maximum_fusion.1), calls=%async_computation | async-start | bytes 917504 | tf_op jit(solution)/shard_map/all_to_all | solution.py:173
  59.4 0.8 copy-start.7
  63.7 11.9 %all-to-all-start.1 = ((bf16[8,16,512]{2,1,0:T(8,128)(2,1)}), bf16[8,16,512]{2,1,0:T(8,128)(2,1)S(1)}, u32[]{:S(2)}, u32[]{:S(2)}) async-start(bf16[8,16,512]{2,1,0:T(8,128)(2,1)} %get-tuple-element.6), calls=%async_computation.1 | async-start | bytes 262144 | tf_op jit(solution)/shard_map/all_to_all | solution.py:192
  69.9 2.2 %copy-start.4 = (bf16[128,1024]{1,0:T(8,128)(2,1)S(1)}, bf16[128,1024]{1,0:T(8,128)(2,1)}, u32[]{:S(2)}) copy-start(bf16[128,1024]{1,0:T(8,128)(2,1)} %copy-done.3) | copy-start | bytes 786436
  69.9 2.2 %copy-start.6 = (bf16[256,1024]{1,0:T(8,128)(2,1)S(1)}, bf16[256,1024]{1,0:T(8,128)(2,1)}, u32[]{:S(2)}) copy-start(bf16[256,1024]{1,0:T(8,128)(2,1)} %copy-done.5) | copy-start | bytes 1572868
  72.2 3.4 %copy-start.2 = (f32[8,128]{1,0:T(8,128)S(1)}, f32[8,128]{1,0:T(8,128)}, u32[]{:S(2)}) copy-start(f32[8,128]{1,0:T(8,128)} %get-tuple-element.7.coefs) | copy-start | bytes 12292
  98.1 24.9 %all-to-all-start.2 = ((bf16[8,96,1024]{2,1,0:T(8,128)(2,1)}), bf16[8,96,1024]{2,1,0:T(8,128)(2,1)}, u32[]{:S(2)}, u32[]{:S(2)}) async-start(bf16[8,96,1024]{2,1,0:T(8,128)(2,1)} %bitcast.9), calls=%async_computation.2 | async-start | bytes 3145728 | tf_op jit(solution)/shard_map/all_to_all | solution.py:207
  125.5 28.9 %all-to-all-start.3 = ((bf16[8,16,1024]{2,1,0:T(8,128)(2,1)}), bf16[8,16,1024]{2,1,0:T(8,128)(2,1)S(1)}, u32[]{:S(2)}, u32[]{:S(2)}) async-start(bf16[8,16,1024]{2,1,0:T(8,128)(2,1)} %bitcast.11), calls=%async_computation.3 | async-start | bytes 524288 | tf_op jit(solution)/shard_map/all_to_all | solution.py:217
  135.8 18.1 %collective-permute-start.2 = (f32[96,128]{1,0:T(8,128)S(1)}, f32[96,128]{1,0:T(8,128)S(1)}, u32[]{:S(2)}, u32[]{:S(2)}) collective-permute-start(f32[96,128]{1,0:T(8,128)S(1)} %get-tuple-element.16), channel_id=1, source_target_pairs={{0,8},{8,16},{16,24},{24,32},{32,40},{40,48},{48,56},{56,64},{64,7... | collective-permute-start | bytes 147464 | tf_op jit(solution)/shard_map/ppermute | solution.py:33
  143.6 10.2 %collective-permute-start.3 = (f32[96,128]{1,0:T(8,128)S(1)}, f32[96,128]{1,0:T(8,128)S(1)}, u32[]{:S(2)}, u32[]{:S(2)}) collective-permute-start(f32[96,128]{1,0:T(8,128)S(1)} %get-tuple-element.17), channel_id=1, source_target_pairs={{0,16},{8,24},{16,32},{24,40},{32,48},{40,56},{48,64},{56,72},{64,... | collective-permute-start | bytes 147464 | tf_op jit(solution)/shard_map/ppermute | solution.py:33

commit v3 on v2

--- a/solution.py
+++ b/solution.py
@@ -33,27 +33,19 @@
     return lax.ppermute(array, DP, [(i, (i + by) % peers) for i in range(peers)])
 
 
-def band_kernel(parts, ids, tiles, coefs):
+def band_kernel(parts, sim_raw, norms, ids, tiles):
     peers = tiles.shape[0]
-    rows = parts.shape[1]
-    band = ids.shape[1]
+    rows, band = sim_raw.shape
     texts = band // STEPS
-    sums = jnp.sum(parts[...], 0)
-    tail = sums[:, 2 * band :]
-    proj_sq = jnp.concatenate([tail[s : s + 1] for s in range(STEPS)], 1)
-    teach_sq = jnp.concatenate([tail[STEPS + s : STEPS + s + 1] for s in range(STEPS)], 1)
-    cross = tail[2 * STEPS : 2 * STEPS + 1]
-    inv_proj = lax.rsqrt(proj_sq + EPSILON)
-    inv_teach = lax.rsqrt(teach_sq + EPSILON)
-    both = inv_proj[:, :texts] * inv_teach[:, :texts]
-    cosine = cross * both
+    inv_proj = lax.rsqrt(norms[0:1, :] + EPSILON)
+    inv_teach = lax.rsqrt(norms[1:2, :] + EPSILON)
     row_id = lax.broadcasted_iota(jnp.int32, (rows, band), 0)
     anchor = (ids[0:1, :] == row_id).astype(f32)
     own = (ids[3:4, :] == row_id).astype(f32)
     row_proj = jnp.sum(own * inv_proj, 1, keepdims=True)
     row_teach = jnp.sum(own * inv_teach, 1, keepdims=True)
-    sim = sums[:, :band] * (row_proj * inv_proj)
-    teach = sums[:, band : 2 * band] * (row_teach * inv_teach)
+    sim = sim_raw[...] * (row_proj * inv_proj)
+    teach = jnp.sum(parts[...], 0) * (row_teach * inv_teach)
     col_id = lax.broadcasted_iota(jnp.int32, (band, band), 0)
     pick = (col_id == ids[1:2, :]).astype(f32) - (col_id == ids[2:3, :]).astype(f32)
     gap_s = jnp.sum(dot(sim, anchor, (0, 0), HIGHEST) * pick, 0, keepdims=True)
@@ -75,12 +67,9 @@
     tile = jnp.concatenate([grad * (row_proj * inv_proj), extra], 1).astype(bf16)
     for peer in range(peers):
         tiles[peer] = tile
-    coefs[...] = jnp.concatenate(
-        [cosine * inv_proj[:, :texts] * inv_proj[:, :texts], both, jnp.zeros((6, texts), f32)], 0
-    )
-
-
-def grad_kernel(gathered, coefs, proj_band, teacher, regrouped, rows_grad, grad_w):
+
+
+def grad_kernel(gathered, norms, proj_band, teacher, regrouped, rows_grad, grad_w):
     band = proj_band.shape[0]
     texts = band // STEPS
     gathered = gathered[...]
@@ -89,6 +78,10 @@
     along = [
         tail[2 * s : 2 * s + 1] + tail[2 * s + 1 : 2 * s + 2] for s in range(STEPS)
     ]
+    inv_proj = lax.rsqrt(norms[0:1, :texts] + EPSILON)
+    inv_teach = lax.rsqrt(norms[1:2, :texts] + EPSILON)
+    both = inv_proj * inv_teach
+    cosine = norms[2:3, :texts] * both
     diagonal = lax.broadcasted_iota(jnp.int32, (texts, texts), 0) == lax.broadcasted_iota(
         jnp.int32, (texts, texts), 1
     )
@@ -101,11 +94,11 @@
         lone = proj_band[piece, :].astype(f32)
         scale = -along[s]
         if s == 0:
-            scale = scale + coefs[0:1, :]
+            scale = scale + cosine * inv_proj * inv_proj
         terms = dot(tile[:, piece], proj_band[0:texts, :], (0, 0)) + upright(scale) * lone
         if s == 0:
             terms = terms + dot(tile, proj_band[...], (1, 0))
-            terms = terms - upright(coefs[1:2, :]) * teacher[...].astype(f32)
+            terms = terms - upright(both) * teacher[...].astype(f32)
         rows_grad[piece, :] = (LOSS_SCALE * terms).astype(bf16)
     grad_w[...] = dot(regrouped[...], rows_grad[...], (1, 0)).astype(bf16)
 
@@ -131,46 +124,46 @@
     padded = -(-share // 16) * 16
     feat = lax.axis_index("feat")
 
-    packed = jnp.concatenate([teacher, student], 1)
-    near = passed_along(packed, -1)
-    far = passed_along(packed, -2)
+    near_teach = passed_along(teacher, -1)
+    far_teach = passed_along(teacher, -2)
+    near_student = passed_along(student, -1)
+    far_student = passed_along(student, -2)
 
     projected = dot(student, proj_weight, (1, 0))
     teacher_wide = teacher.astype(f32)
-
-    student_rest = jnp.concatenate([near[:, width:], far[:, width:]], 0)
-    rest = dot(student_rest, proj_weight, (1, 0))
-    near_teach, far_teach = near[:, :width], far[:, :width]
     proj_own = projected.astype(bf16)
-    proj_rest = rest.astype(bf16)
-    proj_band = jnp.concatenate([proj_own, proj_rest], 0)
-    near_wide, far_wide = near_teach.astype(f32), far_teach.astype(f32)
-    norms = jnp.concatenate(
+    own_sums = jnp.concatenate(
         [
             jnp.sum(projected * projected, 1)[None],
-            jnp.sum(rest * rest, 1).reshape(STEPS - 1, texts),
             jnp.sum(teacher_wide * teacher_wide, 1)[None],
-            jnp.sum(near_wide * near_wide, 1)[None],
-            jnp.sum(far_wide * far_wide, 1)[None],
             jnp.sum(projected * teacher_wide, 1)[None],
-            jnp.zeros((rows - 2 * STEPS - 1, texts), f32),
+            jnp.zeros((rows - 3, texts), f32),
         ],
         0,
     )
+    through = dot(proj_own, proj_weight, (1, 1)).reshape(n_feat, rows, features)
+    through = jnp.concatenate(
+        [through, jnp.broadcast_to(own_sums[None], (n_feat, rows, texts))], 2
+    )
+    through = jnp.sum(lax.all_to_all(through, "feat", 0, 0), 0)
+    own_norms = through[:8, features:]
+    norms = jnp.concatenate(
+        [own_norms, passed_along(own_norms, -1), passed_along(own_norms, -2)], 1
+    )
+
     parts = jnp.concatenate(
         [
-            dot(proj_own, proj_own, (1, 1)),
-            dot(proj_own, proj_rest, (1, 1)),
             dot(teacher, teacher, (1, 1)),
             dot(teacher, near_teach, (1, 1)),
             dot(teacher, far_teach, (1, 1)),
         ],
         1,
-    ).reshape(n_feat, rows, 2 * band)
-    parts = jnp.concatenate(
-        [parts, jnp.broadcast_to(norms[None], (n_feat, rows, texts))], 2
-    )
-    parts = lax.all_to_all(parts, "feat", 0, 0)
+    )
+    parts = lax.all_to_all(parts.reshape(n_feat, rows, band), "feat", 0, 0)
+    student_band = jnp.concatenate([student, near_student, far_student], 0)
+    sim_raw = dot(through[:, :features], student_band.astype(f32), (1, 1), HIGHEST)
+    proj_rest = dot(student_band[texts:], proj_weight, (1, 0)).astype(bf16)
+    proj_band = jnp.concatenate([proj_own, proj_rest], 0)
     ids = jnp.concatenate(
         [
             anchors[None] - feat * rows,
@@ -180,18 +173,14 @@
         ],
         0,
     )
-    tiles, coefs = pl.pallas_call(
+    tiles = pl.pallas_call(
         band_kernel,
-        out_shape=(
-            jax.ShapeDtypeStruct((n_feat, rows, band + texts), bf16),
-            jax.ShapeDtypeStruct((8, texts), f32),
-        ),
+        out_shape=jax.ShapeDtypeStruct((n_feat, rows, band + texts), bf16),
         cost_estimate=pl.CostEstimate(flops=10**8, bytes_accessed=10**6, transcendentals=1000),
         name="band",
-    )(parts, ids)
+    )(parts, sim_raw, norms, ids)
     gathered = lax.all_to_all(tiles, "feat", 0, 0)
 
-    student_band = jnp.concatenate([student, student_rest], 0)
     regrouped = dot(by_x(sizes, features), student_band, (1, 1)).astype(bf16)
     rows_grad, grad_w = pl.pallas_call(
         grad_kernel,
@@ -202,7 +191,7 @@
         compiler_params=pltpu.CompilerParams(vmem_limit_bytes=32 * 2**20),
         cost_estimate=pl.CostEstimate(flops=10**9, bytes_accessed=4 * 10**6, transcendentals=0),
         name="grad",
-    )(gathered, coefs, proj_band, teacher, regrouped)
+    )(gathered, norms, proj_band, teacher, regrouped)
 
     grad_w = lax.all_to_all(
         grad_w.reshape(x_size, features // x_size, width), "x", 0, 0
@@ -210,16 +199,35 @@
     zy = z_size * yh_size
     row_out = lax.broadcasted_iota(jnp.int32, (zy * padded, features), 0)
     row_in = lax.broadcasted_iota(jnp.int32, (zy * padded, features), 1) % (zy * share)
-    add_rows = (
-        (row_out // padded == row_in // share) & (row_out % padded == row_in % share)
-    ).astype(bf16)
+    add_rows = lax.optimization_barrier(
+        ((row_out // padded == row_in // share) & (row_out % padded == row_in % share)).astype(bf16)
+    )
     grad_w = dot(add_rows, grad_w, (1, 0)).astype(bf16)
     grad_w = lax.all_to_all(grad_w.reshape(zy, padded, width), ("z", "yh"), 0, 0)
     grad_w = jnp.sum(grad_w.astype(f32), 0)[:share]
 
-    back = dot(proj_weight, rows_grad, (1, 1)).astype(bf16)
-    back = lax.all_to_all(back.reshape(n_feat, features // n_feat, band), "feat", 0, 0)
-    back = jnp.sum(back.astype(f32), 0)
+    bits = n_feat.bit_length() - 1
+    halves = proj_weight.reshape(n_feat // 2, 2, features // n_feat, width)
+
+    def half(array, which, axis):
+        return lax.dynamic_index_in_dim(array, which, axis, keepdims=False)
+
+    def half_back(which):
+        weight = half(halves, which, 1).reshape(features // 2, width)
+        return dot(weight, rows_grad, (1, 1)).reshape(n_feat // 2, features // n_feat, band)
+
+    def swapped(array, bit):
+        perm = [(i, i ^ (1 << bit)) for i in range(n_feat)]
+        return lax.ppermute(array.astype(bf16), "feat", perm).astype(f32)
+
+    mine = feat & 1
+    back = swapped(half_back(1 - mine), 0)
+    back = half_back(mine) + back
+    for bit in range(1, bits):
+        back = back.reshape(-1, 2, features // n_feat, band)
+        mine = (feat >> bit) & 1
+        back = half(back, mine, 1) + swapped(half(back, 1 - mine, 1), bit)
+    back = back.reshape(features // n_feat, band)
     grad_student = back[:, :texts]
     for s in range(1, STEPS):
         grad_student = grad_student + passed_along(back[:, s * texts : (s + 1) * texts], s)

time: 156 us -> 138 us (0.88)
  waiting for transfers between devices: 56.7 us -> 25.9 us
  starting transfers between devices: 54.9 us -> 80.9 us
  blocking collectives: 18.7 us -> 0 us
  matrix products: 9.04 us -> 13.3 us
    all_to_all x1, waiting for transfers between devices: 20.4 us -> 0.69 us  [shards(): lax.all_to_all(grad_w.reshape(x_size, features // x_size, width), 'x', 0, 0)]
    all_to_all x1 -> x0, blocking collectives: 18.7 us -> none  [shards(): lax.all_to_all(back.reshape(n_feat, features // n_feat, band), 'feat', 0, 0)]
    ppermute x4 -> x8, starting transfers between devices: 30.8 us -> 47 us  [passed_along(): lax.ppermute(array, DP, [(i, (i + by) % peers) for i in range(peers)])]
    ppermute x4 -> x8, waiting for transfers between devices: 22.8 us -> 7.39 us  [passed_along(): lax.ppermute(array, DP, [(i, (i + by) % peers) for i in range(peers)])]
    ppermute x0 -> x3, waiting for transfers between devices: none -> 10.3 us  [swapped(): return lax.ppermute(array.astype(bf16), 'feat', perm).astype(f32)]
    ppermute x0 -> x3, starting transfers between devices: none -> 7.92 us  [swapped(): return lax.ppermute(array.astype(bf16), 'feat', perm).astype(f32)]
    all_to_all x1 -> x2, starting transfers between devices: 3.42 us -> 11.3 us  [the longest x1 6.01 us: shards(): parts = lax.all_to_all(parts.reshape(n_feat, rows, band), 'feat', 0, 0)]
    all_to_all x1 -> x2, waiting for transfers between devices: 10.1 us -> 3.56 us  [the longest x1 3.55 us: shards(): through = jnp.sum(lax.all_to_all(through, 'feat', 0, 0), 0)]
  transfers between devices with their start and end apart: 8 -> 16, of which waited for: 5 -> 8; matrix products, arithmetic and copies ran while one was open for 4% -> 13% of each run, Pallas kernels for 0% -> 0%
where the time goes in v3:
time: 138 us; the launch traced here: 137 us
  starting transfers between devices  80.9 us (59%)
  waiting for transfers between devices  25.9 us (19%)
  matrix products  13.3 us (10%)
  Pallas kernels  6.12 us (4%)
  local copies, waits for them, and re-layouts  5.64 us (4%)
  other arithmetic  3.83 us (3%)
    ppermute x8, starting transfers between devices, passed_along(): lax.ppermute(array, DP, [(i, (i + by) % peers) for i in range(peers)])  47 us
    dot_general x11, matrix products, dot(): lax.dot_general(left, right, ((contract[:1], contract[1:]), ((), ())), pr...  13.3 us
    ppermute x3, waiting for transfers between devices, swapped(): return lax.ppermute(array.astype(bf16), 'feat', perm).astype(f32)  10.3 us
    ppermute x3, starting transfers between devices, swapped(): return lax.ppermute(array.astype(bf16), 'feat', perm).astype(f32)  7.92 us
    ppermute x8, waiting for transfers between devices, passed_along(): lax.ppermute(array, DP, [(i, (i + by) % peers) for i in range(peers)])  7.39 us
    all_to_all x1, starting transfers between devices, shards(): parts = lax.all_to_all(parts.reshape(n_feat, rows, band), 'feat', 0, 0)  6.01 us
    all_to_all x1, starting transfers between devices, shards(): through = jnp.sum(lax.all_to_all(through, 'feat', 0, 0), 0)  5.32 us
    all_to_all x1, starting transfers between devices, shards(): lax.all_to_all(grad_w.reshape(zy, padded, width), ('z', 'yh'), 0, 0)  5.28 us
  transfers between devices with their start and end apart: 16, of which 8 were waited for; matrix products, arithmetic and copies ran while one was open for 13% of the time, Pallas kernels for 0%

profile of v3, /device:TPU:8, one launch (start us, length us, event | category | flops | bytes accessed | tf_op | source)
XLA Modules:
  0.0 136.8 jit_solution(17542890794566380697)
XLA Ops:
  0.6 17.6 %collective-permute-start.2 = (bf16[128,768]{1,0:T(8,128)(2,1)}, bf16[128,768]{1,0:T(8,128)(2,1)}, u32[]{:S(2)}, u32[]{:S(2)}) collective-permute-start(bf16[128,768]{1,0:T(8,128)(2,1)} %param.5), channel_id=1, source_target_pairs={{0,504},{8,0},{16,8},{24,16},{32,24},{40,32},{48,40},{56,48},{64,5... | collective-permute-start | bytes 589832 | tf_op jit(solution)/shard_map/ppermute | solution.py:33
  18.3 2.7 %collective-permute-start.3 = (bf16[128,768]{1,0:T(8,128)(2,1)}, bf16[128,768]{1,0:T(8,128)(2,1)}, u32[]{:S(2)}, u32[]{:S(2)}) collective-permute-start(bf16[128,768]{1,0:T(8,128)(2,1)} %param.5), channel_id=1, source_target_pairs={{0,496},{8,504},{16,0},{24,8},{32,16},{40,24},{48,32},{56,40},{64,... | collective-permute-start | bytes 589832 | tf_op jit(solution)/shard_map/ppermute | solution.py:33
  21.0 2.9 %collective-permute-start = (bf16[128,1024]{1,0:T(8,128)(2,1)}, bf16[128,1024]{1,0:T(8,128)(2,1)}, u32[]{:S(2)}, u32[]{:S(2)}) collective-permute-start(bf16[128,1024]{1,0:T(8,128)(2,1)} %teacher.1), channel_id=1, source_target_pairs={{0,504},{8,0},{16,8},{24,16},{32,24},{40,32},{48,40},{56,48},{64,5... | collective-permute-start | bytes 786440 | tf_op jit(solution)/shard_map/ppermute | solution.py:33
  24.0 2.4 %collective-permute-start.1 = (bf16[128,1024]{1,0:T(8,128)(2,1)}, bf16[128,1024]{1,0:T(8,128)(2,1)S(1)}, u32[]{:S(2)}, u32[]{:S(2)}) collective-permute-start(bf16[128,1024]{1,0:T(8,128)(2,1)} %teacher.1), channel_id=1, source_target_pairs={{0,496},{8,504},{16,0},{24,8},{32,16},{40,24},{48,32},{56,40},{64,... | collective-permute-start | bytes 786440 | tf_op jit(solution)/shard_map/ppermute | solution.py:33
  29.7 5.3 %all-to-all-start.1 = ((f32[8,16,896]{2,1,0:T(8,128)}), f32[8,16,896]{2,1,0:T(8,128)S(1)}, u32[]{:S(2)}, u32[]{:S(2)}) async-start(f32[8,16,896]{2,1,0:T(8,128)} %pad_maximum_fusion.1), calls=%async_computation.1 | async-start | bytes 917504 | tf_op jit(solution)/shard_map/all_to_all | solution.py:148
  38.9 2.9 %fusion.11.regrouped = bf16[768,384]{1,0:T(8,128)(2,1)} fusion(bf16[384,768]{1,0:T(8,128)(2,1)S(1)} %constant_dynamic-update-slice_fusion, s32[768]{0:T(1024)S(1)} %get-tuple-element.22, s32[768]{0:T(1024)S(1)} %get-tuple-element.23, s32[768]{0:T(1024)S(1)} %get-tuple-element.21, s32[768]{0:T(1024)S(1)} %get-tuple-element.24, ...), kind=kOutput, calls=%fused_computation.18 | convolution fusion | flops 468615168 | bytes 1193472 | tf_op jit(solution)/shard_map/dot_general | solution.py:25
  44.1 3.6 %all-to-all-done.1 = f32[8,16,896]{2,1,0:T(8,128)S(1)} async-done(((f32[8,16,896]{2,1,0:T(8,128)}), f32[8,16,896]{2,1,0:T(8,128)S(1)}, u32[]{:S(2)}, u32[]{:S(2)}) %all-to-all-start.1) | async-done | bytes 458784 | tf_op jit(solution)/shard_map/all_to_all | solution.py:148
  47.7 6.0 %all-to-all-start = ((f32[8,16,384]{2,1,0:T(8,128)}), f32[8,16,384]{2,1,0:T(8,128)S(1)}, u32[]{:S(2)}, u32[]{:S(2)}) async-start(f32[8,16,384]{2,1,0:T(8,128)} %bitcast), calls=%async_computation | async-start | bytes 393216 | tf_op jit(solution)/shard_map/all_to_all | solution.py:162
  53.8 6.4 %collective-permute-start.4 = (f32[8,128]{1,0:T(8,128)S(1)}, f32[8,128]{1,0:T(8,128)S(1)}, u32[]{:S(2)}, u32[]{:S(2)}) collective-permute-start(f32[8,128]{1,0:T(8,128)S(1)} %slice.27), channel_id=1, source_target_pairs={{0,504},{8,0},{16,8},{24,16},{32,24},{40,32},{48,40},{56,48},{64,5... | collective-permute-start | bytes 12296 | tf_op jit(solution)/shard_map/ppermute | solution.py:33
  60.1 3.6 %collective-permute-start.5 = (f32[8,128]{1,0:T(8,128)S(1)}, f32[8,128]{1,0:T(8,128)S(1)}, u32[]{:S(2)}, u32[]{:S(2)}) collective-permute-start(f32[8,128]{1,0:T(8,128)S(1)} %slice.27), channel_id=1, source_target_pairs={{0,496},{8,504},{16,0},{24,8},{32,16},{40,24},{48,32},{56,40},{64,... | collective-permute-start | bytes 12296 | tf_op jit(solution)/shard_map/ppermute | solution.py:33
  67.3 3.5 %band.1 = bf16[8,16,512]{2,1,0:T(8,128)(2,1)} custom-call(f32[8,16,384]{2,1,0:T(8,128)} %copy-done.4, f32[16,384]{1,0:T(8,128)} %fusion.59.sim_raw, f32[8,384]{1,0:T(8,128)} %pad_maximum_fusion.3.norms, s32[8,384]{1,0:T(8,128)} %add_add_fusion.ids), custom_call_target="tpu_custom_call" | custom-call | flops 100000000 | bytes 1000000 | tf_op jit(solution)/shard_map/band/pallas_call | solution.py:176
  70.9 5.1 %all-to-all-start.2 = ((bf16[8,16,512]{2,1,0:T(8,128)(2,1)}), bf16[8,16,512]{2,1,0:T(8,128)(2,1)S(1)}, u32[]{:S(2)}, u32[]{:S(2)}) async-start(bf16[8,16,512]{2,1,0:T(8,128)(2,1)} %band.1), calls=%async_computation.2 | async-start | bytes 262144 | tf_op jit(solution)/shard_map/all_to_all | solution.py:182
  77.7 4.0 %all-to-all-done.2.gathered = bf16[8,16,512]{2,1,0:T(8,128)(2,1)S(1)} async-done(((bf16[8,16,512]{2,1,0:T(8,128)(2,1)}), bf16[8,16,512]{2,1,0:T(8,128)(2,1)S(1)}, u32[]{:S(2)}, u32[]{:S(2)}) %all-to-all-start.2) | async-done | bytes 131104 | tf_op jit(solution)/shard_map/all_to_all | solution.py:182
  82.8 2.6 %grad.1 = (bf16[384,1024]{1,0:T(8,128)(2,1)S(1)}, bf16[768,1024]{1,0:T(8,128)(2,1)}) custom-call(bf16[8,16,512]{2,1,0:T(8,128)(2,1)S(1)} %all-to-all-done.2.gathered, f32[8,384]{1,0:T(8,128)S(1)} %copy-done.2, bf16[384,1024]{1,0:T(8,128)(2,1)S(1)} %pad_maximum_fusion.proj_band, bf16[128,1024]{1,0:T(8,128)(2,1)S(1)} %copy-done.1, bf16[768,384]{1,0:T(8,128)(2,1)S(1)} %copy-done.3), custom_call_target="tpu_custom_call" | custom-call | flops 1000000000 | bytes 4000000 | tf_op jit(solution)/shard_map/grad/pallas_call | solution.py:185
  85.3 4.3 %all-to-all-start.3 = ((bf16[8,96,1024]{2,1,0:T(8,128)(2,1)}), bf16[8,96,1024]{2,1,0:T(8,128)(2,1)}, u32[]{:S(2)}, u32[]{:S(2)}) async-start(bf16[8,96,1024]{2,1,0:T(8,128)(2,1)} %bitcast.5), calls=%async_computation.3 | async-start | bytes 3145728 | tf_op jit(solution)/shard_map/all_to_all | solution.py:196
  94.3 3.0 %collective-permute-start.7 = (bf16[2,96,384]{2,1,0:T(8,128)(2,1)S(1)}, bf16[2,96,384]{2,1,0:T(8,128)(2,1)S(1)}, u32[]{:S(2)}, u32[]{:S(2)}) collective-permute-start(bf16[2,96,384]{2,1,0:T(8,128)(2,1)S(1)} %fusion.56), channel_id=1, source_target_pairs={{0,2},{1,3},{2,0},{3,1},{4,6},{5,7},{6,4},{7,5},{8,10},{9,11},{10,... | collective-permute-start | bytes 442376 | tf_op jit(solution)/shard_map/ppermute | solution.py:221
  97.4 4.7 %collective-permute-done.7 = bf16[2,96,384]{2,1,0:T(8,128)(2,1)S(1)} collective-permute-done((bf16[2,96,384]{2,1,0:T(8,128)(2,1)S(1)}, bf16[2,96,384]{2,1,0:T(8,128)(2,1)S(1)}, u32[]{:S(2)}, u32[]{:S(2)}) %collective-permute-start.7) | collective-permute-done | bytes 147488 | tf_op jit(solution)/shard_map/ppermute | solution.py:221
  102.2 3.0 %collective-permute-start.8 = (bf16[1,96,384]{2,1,0:T(8,128)(2,1)S(1)}, bf16[1,96,384]{2,1,0:T(8,128)(2,1)S(1)}, u32[]{:S(2)}, u32[]{:S(2)}) collective-permute-start(bf16[1,96,384]{2,1,0:T(8,128)(2,1)S(1)} %dynamic-slice_convert_fusion), channel_id=1, source_target_pairs={{0,4},{1,5},{2,6},{3,7},{4,0},{5,1},{6,2},{7,3},{8,12},{9,13},{10,... | collective-permute-start | bytes 221192 | tf_op jit(solution)/shard_map/ppermute | solution.py:221
  105.4 4.1 %collective-permute-done.8 = bf16[1,96,384]{2,1,0:T(8,128)(2,1)S(1)} collective-permute-done((bf16[1,96,384]{2,1,0:T(8,128)(2,1)S(1)}, bf16[1,96,384]{2,1,0:T(8,128)(2,1)S(1)}, u32[]{:S(2)}, u32[]{:S(2)}) %collective-permute-start.8) | collective-permute-done | bytes 73760 | tf_op jit(solution)/shard_map/ppermute | solution.py:221
  110.1 2.5 %convolution_convert_fusion.2 = bf16[128,1024]{1,0:T(8,128)(2,1)} fusion(bf16[128,768]{1,0:T(8,128)(2,1)S(1)} %fusion.55, bf16[768,1024]{1,0:T(8,128)(2,1)} %bitcast.6), kind=kOutput, calls=%fused_computation.21 | convolution fusion | flops 201457664 | bytes 2031616 | tf_op jit(solution)/shard_map/dot_general | solution.py:25
  112.6 5.3 %all-to-all-start.4 = ((bf16[8,16,1024]{2,1,0:T(8,128)(2,1)}), bf16[8,16,1024]{2,1,0:T(8,128)(2,1)S(1)}, u32[]{:S(2)}, u32[]{:S(2)}) async-start(bf16[8,16,1024]{2,1,0:T(8,128)(2,1)} %bitcast.7), calls=%async_computation.4 | async-start | bytes 524288 | tf_op jit(solution)/shard_map/all_to_all | solution.py:206
  117.9 3.4 %collective-permute-start.10 = (f32[96,128]{1,0:T(8,128)S(1)}, f32[96,128]{1,0:T(8,128)S(1)}, u32[]{:S(2)}, u32[]{:S(2)}) collective-permute-start(f32[96,128]{1,0:T(8,128)S(1)} %get-tuple-element.11), channel_id=1, source_target_pairs={{0,16},{8,24},{16,32},{24,40},{32,48},{40,56},{48,64},{56,72},{64,... | collective-permute-start | bytes 147464 | tf_op jit(solution)/shard_map/ppermute | solution.py:33
  121.4 7.8 %collective-permute-start.9 = (f32[96,128]{1,0:T(8,128)S(1)}, f32[96,128]{1,0:T(8,128)S(1)}, u32[]{:S(2)}, u32[]{:S(2)}) collective-permute-start(f32[96,128]{1,0:T(8,128)S(1)} %get-tuple-element.10), channel_id=1, source_target_pairs={{0,8},{8,16},{16,24},{24,32},{32,40},{40,48},{48,56},{56,64},{64,7... | collective-permute-start | bytes 147464 | tf_op jit(solution)/shard_map/ppermute | solution.py:33
  129.2 6.3 %collective-permute-done.9 = f32[96,128]{1,0:T(8,128)S(1)} collective-permute-done((f32[96,128]{1,0:T(8,128)S(1)}, f32[96,128]{1,0:T(8,128)S(1)}, u32[]{:S(2)}, u32[]{:S(2)}) %collective-permute-start.9) | collective-permute-done | bytes 49184 | tf_op jit(solution)/shard_map/ppermute | solution.py:33
  (71 shorter events, 22.6 us)
Async XLA Ops:
  0.6 25.8 %copy-start = (bf16[768,1024]{1,0:T(8,128)(2,1)S(1)}, bf16[768,1024]{1,0:T(8,128)(2,1)}, u32[]{:S(2)}) copy-start(bf16[768,1024]{1,0:T(8,128)(2,1)} %param.6) | copy-start | bytes 4718596
  0.6 36.4 %collective-permute-start.2 = (bf16[128,768]{1,0:T(8,128)(2,1)}, bf16[128,768]{1,0:T(8,128)(2,1)}, u32[]{:S(2)}, u32[]{:S(2)}) collective-permute-start(bf16[128,768]{1,0:T(8,128)(2,1)} %param.5), channel_id=1, source_target_pairs={{0,504},{8,0},{16,8},{24,16},{32,24},{40,32},{48,40},{56,48},{64,5... | collective-permute-start | bytes 589832 | tf_op jit(solution)/shard_map/ppermute | solution.py:33
  18.3 19.7 %collective-permute-start.3 = (bf16[128,768]{1,0:T(8,128)(2,1)}, bf16[128,768]{1,0:T(8,128)(2,1)}, u32[]{:S(2)}, u32[]{:S(2)}) collective-permute-start(bf16[128,768]{1,0:T(8,128)(2,1)} %param.5), channel_id=1, source_target_pairs={{0,496},{8,504},{16,0},{24,8},{32,16},{40,24},{48,32},{56,40},{64,... | collective-permute-start | bytes 589832 | tf_op jit(solution)/shard_map/ppermute | solution.py:33
  21.0 20.8 %collective-permute-start = (bf16[128,1024]{1,0:T(8,128)(2,1)}, bf16[128,1024]{1,0:T(8,128)(2,1)}, u32[]{:S(2)}, u32[]{:S(2)}) collective-permute-start(bf16[128,1024]{1,0:T(8,128)(2,1)} %teacher.1), channel_id=1, source_target_pairs={{0,504},{8,0},{16,8},{24,16},{32,24},{40,32},{48,40},{56,48},{64,5... | collective-permute-start | bytes 786440 | tf_op jit(solution)/shard_map/ppermute | solution.py:33
  24.0 19.1 %collective-permute-start.1 = (bf16[128,1024]{1,0:T(8,128)(2,1)}, bf16[128,1024]{1,0:T(8,128)(2,1)S(1)}, u32[]{:S(2)}, u32[]{:S(2)}) collective-permute-start(bf16[128,1024]{1,0:T(8,128)(2,1)} %teacher.1), channel_id=1, source_target_pairs={{0,496},{8,504},{16,0},{24,8},{32,16},{40,24},{48,32},{56,40},{64,... | collective-permute-start | bytes 786440 | tf_op jit(solution)/shard_map/ppermute | solution.py:33
  28.7 7.3 %copy-start.1 = (bf16[128,1024]{1,0:T(8,128)(2,1)S(1)}, bf16[128,1024]{1,0:T(8,128)(2,1)}, u32[]{:S(2)}) copy-start(bf16[128,1024]{1,0:T(8,128)(2,1)} %teacher.1) | copy-start | bytes 786436
  28.7 7.5 %copy-start.6 = (s32[384]{0:T(512)S(1)}, s32[384]{0:T(512)}, u32[]{:S(2)}) copy-start(s32[384]{0:T(512)} %param.8) | copy-start | bytes 4612
  28.7 7.7 %copy-start.5 = (s32[2,384]{1,0:T(2,128)S(1)}, s32[2,384]{1,0:T(2,128)}, u32[]{:S(2)}) copy-start(s32[2,384]{1,0:T(2,128)} %param.9) | copy-start | bytes 9220
  29.7 18.0 %all-to-all-start.1 = ((f32[8,16,896]{2,1,0:T(8,128)}), f32[8,16,896]{2,1,0:T(8,128)S(1)}, u32[]{:S(2)}, u32[]{:S(2)}) async-start(f32[8,16,896]{2,1,0:T(8,128)} %pad_maximum_fusion.1), calls=%async_computation.1 | async-start | bytes 917504 | tf_op jit(solution)/shard_map/all_to_all | solution.py:148
  47.7 19.0 %all-to-all-start = ((f32[8,16,384]{2,1,0:T(8,128)}), f32[8,16,384]{2,1,0:T(8,128)S(1)}, u32[]{:S(2)}, u32[]{:S(2)}) async-start(f32[8,16,384]{2,1,0:T(8,128)} %bitcast), calls=%async_computation | async-start | bytes 393216 | tf_op jit(solution)/shard_map/all_to_all | solution.py:162
  53.8 11.2 %collective-permute-start.4 = (f32[8,128]{1,0:T(8,128)S(1)}, f32[8,128]{1,0:T(8,128)S(1)}, u32[]{:S(2)}, u32[]{:S(2)}) collective-permute-start(f32[8,128]{1,0:T(8,128)S(1)} %slice.27), channel_id=1, source_target_pairs={{0,504},{8,0},{16,8},{24,16},{32,24},{40,32},{48,40},{56,48},{64,5... | collective-permute-start | bytes 12296 | tf_op jit(solution)/shard_map/ppermute | solution.py:33
  60.1 5.9 %collective-permute-start.5 = (f32[8,128]{1,0:T(8,128)S(1)}, f32[8,128]{1,0:T(8,128)S(1)}, u32[]{:S(2)}, u32[]{:S(2)}) collective-permute-start(f32[8,128]{1,0:T(8,128)S(1)} %slice.27), channel_id=1, source_target_pairs={{0,496},{8,504},{16,0},{24,8},{32,16},{40,24},{48,32},{56,40},{64,... | collective-permute-start | bytes 12296 | tf_op jit(solution)/shard_map/ppermute | solution.py:33
  66.7 0.7 copy-start.4
  70.9 10.8 %all-to-all-start.2 = ((bf16[8,16,512]{2,1,0:T(8,128)(2,1)}), bf16[8,16,512]{2,1,0:T(8,128)(2,1)S(1)}, u32[]{:S(2)}, u32[]{:S(2)}) async-start(bf16[8,16,512]{2,1,0:T(8,128)(2,1)} %band.1), calls=%async_computation.2 | async-start | bytes 262144 | tf_op jit(solution)/shard_map/all_to_all | solution.py:182
  76.0 5.7 %copy-start.2 = (f32[8,384]{1,0:T(8,128)S(1)}, f32[8,384]{1,0:T(8,128)}, u32[]{:S(2)}) copy-start(f32[8,384]{1,0:T(8,128)} %pad_maximum_fusion.3.norms) | copy-start | bytes 36868
  81.7 1.1 copy-start.3
  85.3 24.8 %all-to-all-start.3 = ((bf16[8,96,1024]{2,1,0:T(8,128)(2,1)}), bf16[8,96,1024]{2,1,0:T(8,128)(2,1)}, u32[]{:S(2)}, u32[]{:S(2)}) async-start(bf16[8,96,1024]{2,1,0:T(8,128)(2,1)} %bitcast.5), calls=%async_computation.3 | async-start | bytes 3145728 | tf_op jit(solution)/shard_map/all_to_all | solution.py:196
  90.2 3.5 %collective-permute-start.6 = (bf16[4,96,384]{2,1,0:T(8,128)(2,1)S(1)}, bf16[4,96,384]{2,1,0:T(8,128)(2,1)S(1)}, u32[]{:S(2)}, u32[]{:S(2)}) collective-permute-start(bf16[4,96,384]{2,1,0:T(8,128)(2,1)S(1)} %convolution_convert_fusion.1), channel_id=1, source_target_pairs={{0,1},{1,0},{2,3},{3,2},{4,5},{5,4},{6,7},{7,6},{8,9},{9,8},{10,11... | collective-permute-start | bytes 884744 | tf_op jit(solution)/shard_map/ppermute | solution.py:221
  94.3 7.8 %collective-permute-start.7 = (bf16[2,96,384]{2,1,0:T(8,128)(2,1)S(1)}, bf16[2,96,384]{2,1,0:T(8,128)(2,1)S(1)}, u32[]{:S(2)}, u32[]{:S(2)}) collective-permute-start(bf16[2,96,384]{2,1,0:T(8,128)(2,1)S(1)} %fusion.56), channel_id=1, source_target_pairs={{0,2},{1,3},{2,0},{3,1},{4,6},{5,7},{6,4},{7,5},{8,10},{9,11},{10,... | collective-permute-start | bytes 442376 | tf_op jit(solution)/shard_map/ppermute | solution.py:221
  102.2 7.2 %collective-permute-start.8 = (bf16[1,96,384]{2,1,0:T(8,128)(2,1)S(1)}, bf16[1,96,384]{2,1,0:T(8,128)(2,1)S(1)}, u32[]{:S(2)}, u32[]{:S(2)}) collective-permute-start(bf16[1,96,384]{2,1,0:T(8,128)(2,1)S(1)} %dynamic-slice_convert_fusion), channel_id=1, source_target_pairs={{0,4},{1,5},{2,6},{3,7},{4,0},{5,1},{6,2},{7,3},{8,12},{9,13},{10,... | collective-permute-start | bytes 221192 | tf_op jit(solution)/shard_map/ppermute | solution.py:221
  112.6 23.5 %all-to-all-start.4 = ((bf16[8,16,1024]{2,1,0:T(8,128)(2,1)}), bf16[8,16,1024]{2,1,0:T(8,128)(2,1)S(1)}, u32[]{:S(2)}, u32[]{:S(2)}) async-start(bf16[8,16,1024]{2,1,0:T(8,128)(2,1)} %bitcast.7), calls=%async_computation.4 | async-start | bytes 524288 | tf_op jit(solution)/shard_map/all_to_all | solution.py:206
  117.9 11.3 %collective-permute-start.10 = (f32[96,128]{1,0:T(8,128)S(1)}, f32[96,128]{1,0:T(8,128)S(1)}, u32[]{:S(2)}, u32[]{:S(2)}) collective-permute-start(f32[96,128]{1,0:T(8,128)S(1)} %get-tuple-element.11), channel_id=1, source_target_pairs={{0,16},{8,24},{16,32},{24,40},{32,48},{40,56},{48,64},{56,72},{64,... | collective-permute-start | bytes 147464 | tf_op jit(solution)/shard_map/ppermute | solution.py:33
  121.4 14.1 %collective-permute-start.9 = (f32[96,128]{1,0:T(8,128)S(1)}, f32[96,128]{1,0:T(8,128)S(1)}, u32[]{:S(2)}, u32[]{:S(2)}) collective-permute-start(f32[96,128]{1,0:T(8,128)S(1)} %get-tuple-element.10), channel_id=1, source_target_pairs={{0,8},{8,16},{16,24},{24,32},{32,40},{40,48},{48,56},{56,64},{64,7... | collective-permute-start | bytes 147464 | tf_op jit(solution)/shard_map/ppermute | solution.py:33

commit v4 on v2

v4 whole, which is shorter than its diff:
```python
import functools

import jax
import jax.numpy as jnp
from jax import lax
from jax.experimental import pallas as pl
from jax.experimental.pallas import tpu as pltpu
from jax.sharding import Mesh, PartitionSpec as P

STEPS = 3
EPSILON = 1e-06
TEMPER = 50.0
MARGIN = 0.01
LOSS_SCALE = 1024.0

DP_SIZES = {64: (4, 8, 2), 8: (2, 2, 2)}
DP = ("z", "x", "yh")
LANES = 128
f32 = jnp.float32
bf16 = jnp.bfloat16


def dot(left, right, contract, precision=None):
    return lax.dot_general(
        left, right, ((contract[:1], contract[1:]), ((), ())),
        preferred_element_type=f32, precision=precision,
    )


def passed_along(array, by):
    peers = lax.axis_size(DP)
    return lax.ppermute(array, DP, [(i, (i + by) % peers) for i in range(peers)])


def exact_parts(values):
    high = values.astype(bf16)
    rest = values - high.astype(f32)
    middle = rest.astype(bf16)
    low = (rest - middle.astype(f32)).astype(bf16)
    return jnp.concatenate([high, middle, low], 0)


def diagonal(size):
    return lax.broadcasted_iota(jnp.int32, (size, size), 0) == lax.broadcasted_iota(
        jnp.int32, (size, size), 1
    )


def row_sums(values):
    sums = jnp.sum(values, 1, keepdims=True)
    return jnp.sum(jnp.where(diagonal(values.shape[0]), sums, 0.0), 0, keepdims=True)


def upright(values):
    return jnp.sum(jnp.where(diagonal(values.shape[1]), values, 0.0), 1, keepdims=True)


def lay_out(payload, tiles, sums):
    peers, rows, _ = payload.shape
    for t, tile in enumerate(tiles):
        texts = tile.shape[1]
        payload[:, :, t * texts : (t + 1) * texts] = tile.reshape(peers, rows, texts)
    tail = jnp.concatenate(sums + [jnp.zeros((rows - len(sums), texts), f32)], 0)
    for peer in range(peers):
        payload[peer, :, len(tiles) * texts :] = tail


def far_kernel(student, weight, teacher, far_student, far_teacher, payload, proj_own, proj_far):
    own = dot(student[...], weight[...], (1, 0))
    far = dot(far_student[...], weight[...], (1, 0))
    proj_own[...] = own.astype(bf16)
    proj_far[...] = far.astype(bf16)
    own_wide = teacher[...].astype(f32)
    far_wide = far_teacher[...].astype(f32)
    lay_out(
        payload,
        [
            dot(proj_own[...], proj_own[...], (1, 1)),
            dot(proj_own[...], proj_far[...], (1, 1)),
            dot(teacher[...], teacher[...], (1, 1)),
            dot(teacher[...], far_teacher[...], (1, 1)),
        ],
        [
            row_sums(own * own),
            row_sums(far * far),
            row_sums(own_wide * own_wide),
            row_sums(far_wide * far_wide),
            row_sums(own * own_wide),
        ],
    )


def near_kernel(proj_own, weight, teacher, near_student, near_teacher, payload, proj_near):
    near = dot(near_student[...], weight[...], (1, 0))
    proj_near[...] = near.astype(bf16)
    wide = near_teacher[...].astype(f32)
    lay_out(
        payload,
        [
            dot(proj_own[...], proj_near[...], (1, 1)),
            dot(teacher[...], near_teacher[...], (1, 1)),
        ],
        [row_sums(near * near), row_sums(wide * wide)],
    )


def band_kernel(far_parts, near_parts, ids, tiles, norms):
    peers = tiles.shape[0]
    rows = far_parts.shape[1]
    band = ids.shape[1]
    texts = band // STEPS
    far = jnp.sum(far_parts[...], 0)
    near = jnp.sum(near_parts[...], 0)

    def part(array, t):
        return array[:, t * texts : (t + 1) * texts]

    far_tail, near_tail = part(far, 4), part(near, 2)
    proj_sq = jnp.concatenate([far_tail[0:1], near_tail[0:1], far_tail[1:2]], 1)
    teach_sq = jnp.concatenate([far_tail[2:3], near_tail[1:2], far_tail[3:4]], 1)
    cross = far_tail[4:5]
    norms[...] = jnp.concatenate(
        [proj_sq[:, :texts], teach_sq[:, :texts], cross, jnp.zeros((5, texts), f32)], 0
    )
    inv_proj = lax.rsqrt(proj_sq + EPSILON)
    inv_teach = lax.rsqrt(teach_sq + EPSILON)
    row_id = lax.broadcasted_iota(jnp.int32, (rows, band), 0)
    anchor = (ids[0:1, :] == row_id).astype(f32)
    own = (ids[3:4, :] == row_id).astype(f32)
    row_proj = jnp.sum(own * inv_proj, 1, keepdims=True)
    row_teach = jnp.sum(own * inv_teach, 1, keepdims=True)
    sim = jnp.concatenate([part(far, 0), part(near, 0), part(far, 1)], 1) * (row_proj * inv_proj)
    teach = jnp.concatenate([part(far, 2), part(near, 1), part(far, 3)], 1) * (
        row_teach * inv_teach
    )
    col_id = lax.broadcasted_iota(jnp.int32, (band, band), 0)
    pick = (col_id == ids[1:2, :]).astype(f32) - (col_id == ids[2:3, :]).astype(f32)
    anchor_thrice = jnp.concatenate([anchor, anchor, anchor], 0).astype(bf16)
    gap_s = jnp.sum(dot(exact_parts(sim), anchor_thrice, (0, 0)) * pick, 0, keepdims=True)
    gap_t = jnp.sum(dot(exact_parts(teach), anchor_thrice, (0, 0)) * pick, 0, keepdims=True)
    weight = jnp.tanh(TEMPER * gap_t)
    slope = -weight * jax.nn.sigmoid(TEMPER * (MARGIN - weight * gap_s))
    added = dot(exact_parts(anchor * slope), pick.astype(bf16), (1, 1))
    grad = 2.0 * (sim - teach) + (
        added[:rows] + added[rows : 2 * rows] + added[2 * rows :]
    )
    product = grad * sim
    along = jnp.sum(product, 1, keepdims=True)
    inner = jnp.sum(product + along * own, 0, keepdims=True) * (inv_proj * inv_proj)
    high = inner.astype(bf16).astype(f32)
    low = inner - high
    tail_id = lax.broadcasted_iota(jnp.int32, (rows, texts), 0)
    extra = jnp.zeros((rows, texts), f32)
    for s in range(STEPS):
        extra = jnp.where(tail_id == 2 * s, part(high, s), extra)
        extra = jnp.where(tail_id == 2 * s + 1, part(low, s), extra)
    tile = jnp.concatenate([grad * (row_proj * inv_proj), extra], 1).astype(bf16)
    for peer in range(peers):
        tiles[peer] = tile


def grad_kernel(gathered, norms, own, near, far, teacher, regrouped, rows_grad, grad_w):
    texts = own.shape[0]
    band = STEPS * texts
    gathered = gathered[...]
    tile = gathered[:, :, :band].reshape(texts, band)
    tail = jnp.sum(gathered[:, :, band:].astype(f32), 0)
    inv_proj = lax.rsqrt(norms[0:1, :] + EPSILON)
    inv_teach = lax.rsqrt(norms[1:2, :] + EPSILON)
    both = inv_proj * inv_teach
    cosine = norms[2:3, :] * both
    for s, partner in enumerate((own, near, far)):
        piece = slice(s * texts, (s + 1) * texts)
        scale = -(tail[2 * s : 2 * s + 1] + tail[2 * s + 1 : 2 * s + 2])
        if s == 0:
            scale = scale + cosine * inv_proj * inv_proj
        terms = dot(tile[:, piece], own[...], (0, 0)) + upright(scale) * partner[...].astype(f32)
        if s == 0:
            for other, mate in enumerate((own, near, far)):
                terms = terms + dot(
                    tile[:, other * texts : (other + 1) * texts], mate[...], (1, 0)
                )
            terms = terms - upright(both) * teacher[...].astype(f32)
        rows_grad[piece, :] = (LOSS_SCALE * terms).astype(bf16)
    grad_w[...] = dot(regrouped[...], rows_grad[...], (1, 0)).astype(bf16)


def add_kernel(received, out):
    blocks, padded, _ = out.shape
    total = jnp.sum(received[...].astype(f32), 0)
    share = total.shape[0] // blocks
    fill = jnp.zeros((padded - share, total.shape[1]), f32)
    for block in range(blocks):
        piece = total[block * share : (block + 1) * share]
        out[block] = jnp.concatenate([piece, fill], 0).astype(bf16)


def by_x(sizes, features):
    z_size, x_size, yh_size = sizes
    share = features // (z_size * x_size)
    out = lax.broadcasted_iota(jnp.int32, (features, features), 0)
    place, offset = out // share, out % share
    source = (place % z_size * x_size + place // z_size) * share + offset
    return (lax.broadcasted_iota(jnp.int32, out.shape, 1) == source).astype(bf16)


def shards(student, proj_weight, teacher, anchors, pairs, *, sizes):
    z_size, x_size, yh_size = sizes
    n_dp = z_size * x_size * yh_size
    n_feat = lax.axis_size("feat")
    texts, features = student.shape
    width = teacher.shape[1]
    band = STEPS * texts
    rows = texts // n_feat
    share = features // n_dp
    padded = -(-share // 16) * 16
    feat = lax.axis_index("feat")

    near_student = passed_along(student, -1)
    near_teacher = passed_along(teacher, -1)
    far_student = passed_along(student, -2)
    far_teacher = passed_along(teacher, -2)

    def cost(flops):
        return pl.CostEstimate(flops=flops, bytes_accessed=3 * 10**6, transcendentals=0)

    rows_type = jax.ShapeDtypeStruct((texts, width), bf16)
    far_parts, proj_own, proj_far = pl.pallas_call(
        far_kernel,
        out_shape=(jax.ShapeDtypeStruct((n_feat, rows, 5 * texts), f32), rows_type, rows_type),
        compiler_params=pltpu.CompilerParams(vmem_limit_bytes=16 * 2**20),
        cost_estimate=cost(6 * 10**8),
        name="far",
    )(student, proj_weight, teacher, far_student, far_teacher)
    far_parts = lax.all_to_all(far_parts, "feat", 0, 0)
    near_parts, proj_near = pl.pallas_call(
        near_kernel,
        out_shape=(jax.ShapeDtypeStruct((n_feat, rows, 3 * texts), f32), rows_type),
        compiler_params=pltpu.CompilerParams(vmem_limit_bytes=16 * 2**20),
        cost_estimate=cost(3 * 10**8),
        name="near",
    )(proj_own, proj_weight, teacher, near_student, near_teacher)
    near_parts = lax.all_to_all(near_parts, "feat", 0, 0)

    ids = jnp.concatenate(
        [
            anchors[None] - feat * rows,
            pairs,
            lax.broadcasted_iota(jnp.int32, (1, band), 1) - feat * rows,
            jnp.zeros((4, band), jnp.int32),
        ],
        0,
    )
    tiles, norms = pl.pallas_call(
        band_kernel,
        out_shape=(
            jax.ShapeDtypeStruct((n_feat, rows, band + texts), bf16),
            jax.ShapeDtypeStruct((8, texts), f32),
        ),
        cost_estimate=cost(10**8),
        name="band",
    )(far_parts, near_parts, ids)
    gathered = lax.all_to_all(tiles, "feat", 0, 0)

    student_band = jnp.concatenate([student, near_student, far_student], 0)
    regrouped = dot(by_x(sizes, features), student_band, (1, 1)).astype(bf16)
    rows_grad, grad_w = pl.pallas_call(
        grad_kernel,
        out_shape=(
            jax.ShapeDtypeStruct((band, width), bf16),
            jax.ShapeDtypeStruct((features, width), bf16),
        ),
        compiler_params=pltpu.CompilerParams(vmem_limit_bytes=16 * 2**20),
        cost_estimate=cost(10**9),
        name="grad",
    )(gathered, norms, proj_own, proj_near, proj_far, teacher, regrouped)

    zy = z_size * yh_size
    grad_w = lax.all_to_all(grad_w.reshape(x_size, features // x_size, width), "x", 0, 0)
    columns = min(width, 256)
    grad_w = pl.pallas_call(
        add_kernel,
        grid=(width // columns,),
        in_specs=[pl.BlockSpec((x_size, features // x_size, columns), lambda i: (0, 0, i))],
        out_specs=pl.BlockSpec((zy, padded, columns), lambda i: (0, 0, i)),
        out_shape=jax.ShapeDtypeStruct((zy, padded, width), bf16),
        cost_estimate=cost(10**6),
        name="add",
    )(grad_w)
    grad_w = lax.all_to_all(grad_w, ("z", "yh"), 0, 0)
    grad_w = jnp.sum(grad_w.astype(f32), 0)[:share]

    halves = proj_weight.reshape(n_feat // 2, 2, features // n_feat, width)

    def half_back(core):
        weight = lax.dynamic_index_in_dim(halves, core, 1, keepdims=False)
        weight = weight.reshape(features // 2, width)
        back = dot(weight, rows_grad, (1, 1))
        return back.reshape(n_feat // 2, features // n_feat, band)

    def swapped(array, mask):
        perm = [(i, i ^ mask) for i in range(n_feat)]
        return lax.ppermute(array.astype(bf16), "feat", perm).astype(f32)

    core = feat & 1
    back = swapped(half_back(1 - core), 1)
    back = half_back(core) + back
    chip = feat >> 1
    mine = lax.dynamic_index_in_dim(back, chip, 0, keepdims=False)
    for other in range(1, n_feat // 2):
        theirs = lax.dynamic_index_in_dim(back, chip ^ other, 0, keepdims=False)
        mine = mine + swapped(theirs, 2 * other)
    grad_student = mine[:, :texts]
    for s in range(1, STEPS):
        grad_student = grad_student + passed_along(mine[:, s * texts : (s + 1) * texts], s)
    return (grad_w, grad_student.T)


def solution(mesh):
    n_dp, n_feat = mesh.devices.shape
    sizes = DP_SIZES[n_dp]
    split = Mesh(mesh.devices.reshape(*sizes, n_feat), (*DP, "feat"))
    return jax.shard_map(
        functools.partial(shards, sizes=sizes),
        mesh=split,
        in_specs=(P(DP, None), P(None, "feat"), P(DP, "feat"), P(DP), P(None, DP)),
        out_specs=(P(DP, "feat"), P(DP, "feat")),
        check_vma=False,
    )
```

time: 156 us -> 145 us (0.929)
  starting transfers between devices: 54.9 us -> 76.8 us
  blocking collectives: 18.7 us -> 0 us
  waiting for transfers between devices: 56.7 us -> 44.8 us
  matrix products: 9.04 us -> 3.2 us
  Pallas kernels: 6.21 us -> 11.5 us
    all_to_all x1, waiting for transfers between devices: 20.4 us -> 1.69 us  [shards(): lax.all_to_all(grad_w.reshape(x_size, features // x_size, width), 'x', 0, 0)]
    all_to_all x1 -> x0, blocking collectives: 18.7 us -> none  [shards(): lax.all_to_all(back.reshape(n_feat, features // n_feat, band), 'feat', 0, 0)]
    ppermute x0 -> x4, starting transfers between devices: none -> 11.1 us  [swapped(): return lax.ppermute(array.astype(bf16), 'feat', perm).astype(f32)]
    pallas_call x0 -> x3, Pallas kernels: none -> 6.34 us  [the longest x1 3.41 us: shards(): pl.pallas_call(add_kernel, grid=(width // columns,), in_specs=[pl.BlockSp...]
    ppermute x0 -> x4, waiting for transfers between devices: none -> 6.32 us  [swapped(): return lax.ppermute(array.astype(bf16), 'feat', perm).astype(f32)]
    all_to_all x2 -> x3, starting transfers between devices: 13.6 us -> 19.7 us  [the longest x1 7.95 us: shards(): grad_w = lax.all_to_all(grad_w, ('z', 'yh'), 0, 0)]
    dot_general x10 -> x3, matrix products: 9.04 us -> 3.2 us  [dot(): lax.dot_general(left, right, ((contract[:1], contract[1:]), ((), ())), pr...]
    ppermute x4 -> x6, starting transfers between devices: 30.8 us -> 36.2 us  [passed_along(): lax.ppermute(array, DP, [(i, (i + by) % peers) for i in range(peers)])]
  transfers between devices with their start and end apart: 8 -> 15, of which waited for: 5 -> 10; matrix products, arithmetic and copies ran while one was open for 4% -> 3% of each run, Pallas kernels for 0% -> 1%
where the time goes in v4:
time: 145 us; the launch traced here: 144 us
  starting transfers between devices  76.8 us (53%)
  waiting for transfers between devices  44.8 us (31%)
  Pallas kernels  11.5 us (8%)
  local copies, waits for them, and re-layouts  4.5 us (3%)
  matrix products  3.2 us (2%)
  other arithmetic  2.04 us (1%)
    ppermute x6, starting transfers between devices, passed_along(): lax.ppermute(array, DP, [(i, (i + by) % peers) for i in range(peers)])  36.2 us
    ppermute x6, waiting for transfers between devices, passed_along(): lax.ppermute(array, DP, [(i, (i + by) % peers) for i in range(peers)])  18 us
    ppermute x4, starting transfers between devices, swapped(): return lax.ppermute(array.astype(bf16), 'feat', perm).astype(f32)  11.1 us
    all_to_all x1, waiting for transfers between devices, shards(): far_parts = lax.all_to_all(far_parts, 'feat', 0, 0)  8.26 us
    all_to_all x1, starting transfers between devices, shards(): grad_w = lax.all_to_all(grad_w, ('z', 'yh'), 0, 0)  7.95 us
    all_to_all x1, waiting for transfers between devices, shards(): near_parts = lax.all_to_all(near_parts, 'feat', 0, 0)  6.85 us
    ppermute x4, waiting for transfers between devices, swapped(): return lax.ppermute(array.astype(bf16), 'feat', perm).astype(f32)  6.32 us
    all_to_all x1, starting transfers between devices, shards(): near_parts = lax.all_to_all(near_parts, 'feat', 0, 0)  6.24 us
  transfers between devices with their start and end apart: 15, of which 10 were waited for; matrix products, arithmetic and copies ran while one was open for 3% of the time, Pallas kernels for 1%

profile of v4, /device:TPU:8, one launch (start us, length us, event | category | flops | bytes accessed | tf_op | source)
XLA Modules:
  0.0 143.8 jit_solution(6705136101030086777)
XLA Ops:
  0.6 13.1 %collective-permute-start.1 = (bf16[128,1024]{1,0:T(8,128)(2,1)}, bf16[128,1024]{1,0:T(8,128)(2,1)S(1)}, u32[]{:S(2)}, u32[]{:S(2)}) collective-permute-start(bf16[128,1024]{1,0:T(8,128)(2,1)} %teacher.5), channel_id=1, source_target_pairs={{0,496},{8,504},{16,0},{24,8},{32,16},{40,24},{48,32},{56,40},{64,... | collective-permute-start | bytes 786440 | tf_op jit(solution)/shard_map/ppermute | solution.py:32
  13.8 7.1 %collective-permute-start.3 = (bf16[128,1024]{1,0:T(8,128)(2,1)}, bf16[128,1024]{1,0:T(8,128)(2,1)S(1)}, u32[]{:S(2)}, u32[]{:S(2)}) collective-permute-start(bf16[128,1024]{1,0:T(8,128)(2,1)} %teacher.5), channel_id=1, source_target_pairs={{0,504},{8,0},{16,8},{24,16},{32,24},{40,32},{48,40},{56,48},{64,5... | collective-permute-start | bytes 786440 | tf_op jit(solution)/shard_map/ppermute | solution.py:32
  20.9 2.4 %collective-permute-start = (bf16[128,768]{1,0:T(8,128)(2,1)}, bf16[128,768]{1,0:T(8,128)(2,1)S(1)}, u32[]{:S(2)}, u32[]{:S(2)}) collective-permute-start(bf16[128,768]{1,0:T(8,128)(2,1)} %student.1), channel_id=1, source_target_pairs={{0,496},{8,504},{16,0},{24,8},{32,16},{40,24},{48,32},{56,40},{64,... | collective-permute-start | bytes 589832 | tf_op jit(solution)/shard_map/ppermute | solution.py:32
  23.3 2.9 %collective-permute-start.2 = (bf16[128,768]{1,0:T(8,128)(2,1)}, bf16[128,768]{1,0:T(8,128)(2,1)S(1)}, u32[]{:S(2)}, u32[]{:S(2)}) collective-permute-start(bf16[128,768]{1,0:T(8,128)(2,1)} %student.1), channel_id=1, source_target_pairs={{0,504},{8,0},{16,8},{24,16},{32,24},{40,32},{48,40},{56,48},{64,5... | collective-permute-start | bytes 589832 | tf_op jit(solution)/shard_map/ppermute | solution.py:32
  26.3 2.8 %collective-permute-done.far_student = bf16[128,768]{1,0:T(8,128)(2,1)S(1)} collective-permute-done((bf16[128,768]{1,0:T(8,128)(2,1)}, bf16[128,768]{1,0:T(8,128)(2,1)S(1)}, u32[]{:S(2)}, u32[]{:S(2)}) %collective-permute-start) | collective-permute-done | bytes 196640 | tf_op jit(solution)/shard_map/ppermute | solution.py:32
  34.0 7.7 %collective-permute-done.2.near_student = bf16[128,768]{1,0:T(8,128)(2,1)S(1)} collective-permute-done((bf16[128,768]{1,0:T(8,128)(2,1)}, bf16[128,768]{1,0:T(8,128)(2,1)S(1)}, u32[]{:S(2)}, u32[]{:S(2)}) %collective-permute-start.2) | collective-permute-done | bytes 196640 | tf_op jit(solution)/shard_map/ppermute | solution.py:32
  43.1 6.2 %all-to-all-start.1 = ((f32[8,16,384]{2,1,0:T(8,128)}), f32[8,16,384]{2,1,0:T(8,128)}, u32[]{:S(2)}, u32[]{:S(2)}) async-start(f32[8,16,384]{2,1,0:T(8,128)} %get-tuple-element.13), calls=%async_computation.1 | async-start | bytes 393216 | tf_op jit(solution)/shard_map/all_to_all | solution.py:243
  49.3 6.9 %all-to-all-done.1.near_parts = f32[8,16,384]{2,1,0:T(8,128)} async-done(((f32[8,16,384]{2,1,0:T(8,128)}), f32[8,16,384]{2,1,0:T(8,128)}, u32[]{:S(2)}, u32[]{:S(2)}) %all-to-all-start.1) | async-done | bytes 196640 | tf_op jit(solution)/shard_map/all_to_all | solution.py:243
  56.2 5.6 %all-to-all-start = ((f32[8,16,640]{2,1,0:T(8,128)}), f32[8,16,640]{2,1,0:T(8,128)}, u32[]{:S(2)}, u32[]{:S(2)}) async-start(f32[8,16,640]{2,1,0:T(8,128)} %get-tuple-element.11), calls=%async_computation | async-start | bytes 655360 | tf_op jit(solution)/shard_map/all_to_all | solution.py:235
  62.5 8.3 %all-to-all-done.far_parts = f32[8,16,640]{2,1,0:T(8,128)} async-done(((f32[8,16,640]{2,1,0:T(8,128)}), f32[8,16,640]{2,1,0:T(8,128)}, u32[]{:S(2)}, u32[]{:S(2)}) %all-to-all-start) | async-done | bytes 327712 | tf_op jit(solution)/shard_map/all_to_all | solution.py:235
  70.8 2.5 %band.1 = (bf16[8,16,512]{2,1,0:T(8,128)(2,1)}, f32[8,128]{1,0:T(8,128)}) custom-call(f32[8,16,640]{2,1,0:T(8,128)} %all-to-all-done.far_parts, f32[8,16,384]{2,1,0:T(8,128)} %all-to-all-done.1.near_parts, s32[8,384]{1,0:T(8,128)} %add_add_fusion.ids), custom_call_target="tpu_custom_call" | custom-call | flops 100000000 | bytes 3000000 | tf_op jit(solution)/shard_map/band/pallas_call | solution.py:254
  73.3 5.5 %all-to-all-start.2 = ((bf16[8,16,512]{2,1,0:T(8,128)(2,1)}), bf16[8,16,512]{2,1,0:T(8,128)(2,1)S(1)}, u32[]{:S(2)}, u32[]{:S(2)}) async-start(bf16[8,16,512]{2,1,0:T(8,128)(2,1)} %get-tuple-element.14), calls=%async_computation.2 | async-start | bytes 262144 | tf_op jit(solution)/shard_map/all_to_all | solution.py:263
  80.8 3.7 %all-to-all-done.2.gathered = bf16[8,16,512]{2,1,0:T(8,128)(2,1)S(1)} async-done(((bf16[8,16,512]{2,1,0:T(8,128)(2,1)}), bf16[8,16,512]{2,1,0:T(8,128)(2,1)S(1)}, u32[]{:S(2)}, u32[]{:S(2)}) %all-to-all-start.2) | async-done | bytes 131104 | tf_op jit(solution)/shard_map/all_to_all | solution.py:263
  85.5 2.7 %grad.1 = (bf16[384,1024]{1,0:T(8,128)(2,1)S(1)}, bf16[768,1024]{1,0:T(8,128)(2,1)}) custom-call(bf16[8,16,512]{2,1,0:T(8,128)(2,1)S(1)} %all-to-all-done.2.gathered, f32[8,128]{1,0:T(8,128)S(1)} %copy-done.6, bf16[128,1024]{1,0:T(8,128)(2,1)S(1)} %get-tuple-element.12.proj_own.own, bf16[128,1024]{1,0:T(8,128)(2,1)S(1)} %get-tuple-element.16.near, ...), custom_call_target="tpu_custom_call" | custom-call | flops 1000000000 | bytes 3000000 | tf_op jit(solution)/shard_map/grad/pallas_call | solution.py:267
  88.2 4.3 %all-to-all-start.3 = ((bf16[8,96,1024]{2,1,0:T(8,128)(2,1)}), bf16[8,96,1024]{2,1,0:T(8,128)(2,1)}, u32[]{:S(2)}, u32[]{:S(2)}) async-start(bf16[8,96,1024]{2,1,0:T(8,128)(2,1)} %bitcast), calls=%async_computation.3 | async-start | bytes 3145728 | tf_op jit(solution)/shard_map/all_to_all | solution.py:279
  97.2 3.0 %collective-permute-start.5 = (bf16[96,384]{1,0:T(8,128)(2,1)S(1)}, bf16[96,384]{1,0:T(8,128)(2,1)S(1)}, u32[]{:S(2)}, u32[]{:S(2)}) collective-permute-start(bf16[96,384]{1,0:T(8,128)(2,1)S(1)} %get-tuple-element.20), channel_id=1, source_target_pairs={{0,2},{1,3},{2,0},{3,1},{4,6},{5,7},{6,4},{7,5},{8,10},{9,11},{10,... | collective-permute-start | bytes 221192 | tf_op jit(solution)/shard_map/ppermute | solution.py:303
  100.2 2.3 %collective-permute-start.6 = (bf16[96,384]{1,0:T(8,128)(2,1)S(1)}, bf16[96,384]{1,0:T(8,128)(2,1)S(1)}, u32[]{:S(2)}, u32[]{:S(2)}) collective-permute-start(bf16[96,384]{1,0:T(8,128)(2,1)S(1)} %get-tuple-element.22), channel_id=1, source_target_pairs={{0,4},{1,5},{2,6},{3,7},{4,0},{5,1},{6,2},{7,3},{8,12},{9,13},{10,... | collective-permute-start | bytes 221192 | tf_op jit(solution)/shard_map/ppermute | solution.py:303
  102.5 3.9 %collective-permute-start.7 = (bf16[96,384]{1,0:T(8,128)(2,1)S(1)}, bf16[96,384]{1,0:T(8,128)(2,1)S(1)}, u32[]{:S(2)}, u32[]{:S(2)}) collective-permute-start(bf16[96,384]{1,0:T(8,128)(2,1)S(1)} %get-tuple-element.21), channel_id=1, source_target_pairs={{0,6},{1,7},{2,4},{3,5},{4,2},{5,3},{6,0},{7,1},{8,14},{9,15},{10,... | collective-permute-start | bytes 221192 | tf_op jit(solution)/shard_map/ppermute | solution.py:303
  107.4 3.9 %collective-permute-done.7 = bf16[96,384]{1,0:T(8,128)(2,1)S(1)} collective-permute-done((bf16[96,384]{1,0:T(8,128)(2,1)S(1)}, bf16[96,384]{1,0:T(8,128)(2,1)S(1)}, u32[]{:S(2)}, u32[]{:S(2)}) %collective-permute-start.7) | collective-permute-done | bytes 73760 | tf_op jit(solution)/shard_map/ppermute | solution.py:303
  113.0 3.4 %add.131 = bf16[8,16,1024]{2,1,0:T(8,128)(2,1)} custom-call(bf16[8,96,1024]{2,1,0:T(8,128)(2,1)} %all-to-all-done.3.received), custom_call_target="tpu_custom_call" | custom-call | flops 1000000 | bytes 3000000 | tf_op jit(solution)/shard_map/add/pallas_call | solution.py:281
  116.4 8.0 %all-to-all-start.4 = ((bf16[8,16,1024]{2,1,0:T(8,128)(2,1)}), bf16[8,16,1024]{2,1,0:T(8,128)(2,1)S(1)}, u32[]{:S(2)}, u32[]{:S(2)}) async-start(bf16[8,16,1024]{2,1,0:T(8,128)(2,1)} %add.131), calls=%async_computation.4 | async-start | bytes 524288 | tf_op jit(solution)/shard_map/all_to_all | solution.py:290
  124.4 7.8 %collective-permute-start.8 = (f32[96,128]{1,0:T(8,128)S(1)}, f32[96,128]{1,0:T(8,128)S(1)}, u32[]{:S(2)}, u32[]{:S(2)}) collective-permute-start(f32[96,128]{1,0:T(8,128)S(1)} %get-tuple-element.23), channel_id=1, source_target_pairs={{0,8},{8,16},{16,24},{24,32},{32,40},{40,48},{48,56},{56,64},{64,7... | collective-permute-start | bytes 147464 | tf_op jit(solution)/shard_map/ppermute | solution.py:32
  132.2 2.8 %collective-permute-start.9 = (f32[96,128]{1,0:T(8,128)S(1)}, f32[96,128]{1,0:T(8,128)S(1)}, u32[]{:S(2)}, u32[]{:S(2)}) collective-permute-start(f32[96,128]{1,0:T(8,128)S(1)} %get-tuple-element.24), channel_id=1, source_target_pairs={{0,16},{8,24},{16,32},{24,40},{32,48},{40,56},{48,64},{56,72},{64,... | collective-permute-start | bytes 147464 | tf_op jit(solution)/shard_map/ppermute | solution.py:32
  135.0 7.4 %collective-permute-done.8 = f32[96,128]{1,0:T(8,128)S(1)} collective-permute-done((f32[96,128]{1,0:T(8,128)S(1)}, f32[96,128]{1,0:T(8,128)S(1)}, u32[]{:S(2)}, u32[]{:S(2)}) %collective-permute-start.8) | collective-permute-done | bytes 49184 | tf_op jit(solution)/shard_map/ppermute | solution.py:32
  (48 shorter events, 18.8 us)
Async XLA Ops:
  0.6 28.4 %collective-permute-start.1 = (bf16[128,1024]{1,0:T(8,128)(2,1)}, bf16[128,1024]{1,0:T(8,128)(2,1)S(1)}, u32[]{:S(2)}, u32[]{:S(2)}) collective-permute-start(bf16[128,1024]{1,0:T(8,128)(2,1)} %teacher.5), channel_id=1, source_target_pairs={{0,496},{8,504},{16,0},{24,8},{32,16},{40,24},{48,32},{56,40},{64,... | collective-permute-start | bytes 786440 | tf_op jit(solution)/shard_map/ppermute | solution.py:32
  13.8 28.0 %collective-permute-start.3 = (bf16[128,1024]{1,0:T(8,128)(2,1)}, bf16[128,1024]{1,0:T(8,128)(2,1)S(1)}, u32[]{:S(2)}, u32[]{:S(2)}) collective-permute-start(bf16[128,1024]{1,0:T(8,128)(2,1)} %teacher.5), channel_id=1, source_target_pairs={{0,504},{8,0},{16,8},{24,16},{32,24},{40,32},{48,40},{56,48},{64,5... | collective-permute-start | bytes 786440 | tf_op jit(solution)/shard_map/ppermute | solution.py:32
  20.9 8.2 %collective-permute-start = (bf16[128,768]{1,0:T(8,128)(2,1)}, bf16[128,768]{1,0:T(8,128)(2,1)S(1)}, u32[]{:S(2)}, u32[]{:S(2)}) collective-permute-start(bf16[128,768]{1,0:T(8,128)(2,1)} %student.1), channel_id=1, source_target_pairs={{0,496},{8,504},{16,0},{24,8},{32,16},{40,24},{48,32},{56,40},{64,... | collective-permute-start | bytes 589832 | tf_op jit(solution)/shard_map/ppermute | solution.py:32
  23.3 18.4 %collective-permute-start.2 = (bf16[128,768]{1,0:T(8,128)(2,1)}, bf16[128,768]{1,0:T(8,128)(2,1)S(1)}, u32[]{:S(2)}, u32[]{:S(2)}) collective-permute-start(bf16[128,768]{1,0:T(8,128)(2,1)} %student.1), channel_id=1, source_target_pairs={{0,504},{8,0},{16,8},{24,16},{32,24},{40,32},{48,40},{56,48},{64,5... | collective-permute-start | bytes 589832 | tf_op jit(solution)/shard_map/ppermute | solution.py:32
  29.1 1.4 copy-start
  30.5 0.9 copy-start.2
  32.4 9.4 %copy-start.1 = (bf16[768,1024]{1,0:T(8,128)(2,1)S(1)}, bf16[768,1024]{1,0:T(8,128)(2,1)}, u32[]{:S(2)}) copy-start(bf16[768,1024]{1,0:T(8,128)(2,1)} %weight.3) | copy-start | bytes 4718596
  32.4 9.4 %copy-start.3 = (bf16[128,1024]{1,0:T(8,128)(2,1)S(1)}, bf16[128,1024]{1,0:T(8,128)(2,1)}, u32[]{:S(2)}) copy-start(bf16[128,1024]{1,0:T(8,128)(2,1)} %teacher.5) | copy-start | bytes 786436
  34.0 15.3 %copy-start.9 = (s32[384]{0:T(512)S(1)}, s32[384]{0:T(512)}, u32[]{:S(2)}) copy-start(s32[384]{0:T(512)} %param.8) | copy-start | bytes 4612
  41.8 20.1 %copy-start.8 = (s32[2,384]{1,0:T(2,128)S(1)}, s32[2,384]{1,0:T(2,128)}, u32[]{:S(2)}) copy-start(s32[2,384]{1,0:T(2,128)} %param.9) | copy-start | bytes 9220
  43.1 35.7 %copy-start.5 = (bf16[128,768]{1,0:T(8,128)(2,1)S(1)}, bf16[128,768]{1,0:T(8,128)(2,1)}, u32[]{:S(2)}) copy-start(bf16[128,768]{1,0:T(8,128)(2,1)} %student.1) | copy-start | bytes 589828
  43.1 13.1 %all-to-all-start.1 = ((f32[8,16,384]{2,1,0:T(8,128)}), f32[8,16,384]{2,1,0:T(8,128)}, u32[]{:S(2)}, u32[]{:S(2)}) async-start(f32[8,16,384]{2,1,0:T(8,128)} %get-tuple-element.13), calls=%async_computation.1 | async-start | bytes 393216 | tf_op jit(solution)/shard_map/all_to_all | solution.py:243
  56.2 14.6 %all-to-all-start = ((f32[8,16,640]{2,1,0:T(8,128)}), f32[8,16,640]{2,1,0:T(8,128)}, u32[]{:S(2)}, u32[]{:S(2)}) async-start(f32[8,16,640]{2,1,0:T(8,128)} %get-tuple-element.11), calls=%async_computation | async-start | bytes 655360 | tf_op jit(solution)/shard_map/all_to_all | solution.py:235
  73.3 11.2 %all-to-all-start.2 = ((bf16[8,16,512]{2,1,0:T(8,128)(2,1)}), bf16[8,16,512]{2,1,0:T(8,128)(2,1)S(1)}, u32[]{:S(2)}, u32[]{:S(2)}) async-start(bf16[8,16,512]{2,1,0:T(8,128)(2,1)} %get-tuple-element.14), calls=%async_computation.2 | async-start | bytes 262144 | tf_op jit(solution)/shard_map/all_to_all | solution.py:263
  78.8 5.7 %copy-start.6 = (f32[8,128]{1,0:T(8,128)S(1)}, f32[8,128]{1,0:T(8,128)}, u32[]{:S(2)}) copy-start(f32[8,128]{1,0:T(8,128)} %get-tuple-element.15.norms) | copy-start | bytes 12292
  84.5 1.1 copy-start.7
  88.2 24.8 %all-to-all-start.3 = ((bf16[8,96,1024]{2,1,0:T(8,128)(2,1)}), bf16[8,96,1024]{2,1,0:T(8,128)(2,1)}, u32[]{:S(2)}, u32[]{:S(2)}) async-start(bf16[8,96,1024]{2,1,0:T(8,128)(2,1)} %bitcast), calls=%async_computation.3 | async-start | bytes 3145728 | tf_op jit(solution)/shard_map/all_to_all | solution.py:279
  93.1 3.5 %collective-permute-start.4 = (bf16[4,96,384]{2,1,0:T(8,128)(2,1)S(1)}, bf16[4,96,384]{2,1,0:T(8,128)(2,1)S(1)}, u32[]{:S(2)}, u32[]{:S(2)}) collective-permute-start(bf16[4,96,384]{2,1,0:T(8,128)(2,1)S(1)} %convolution_convert_fusion), channel_id=1, source_target_pairs={{0,1},{1,0},{2,3},{3,2},{4,5},{5,4},{6,7},{7,6},{8,9},{9,8},{10,11... | collective-permute-start | bytes 884744 | tf_op jit(solution)/shard_map/ppermute | solution.py:303
  97.2 9.2 %collective-permute-start.5 = (bf16[96,384]{1,0:T(8,128)(2,1)S(1)}, bf16[96,384]{1,0:T(8,128)(2,1)S(1)}, u32[]{:S(2)}, u32[]{:S(2)}) collective-permute-start(bf16[96,384]{1,0:T(8,128)(2,1)S(1)} %get-tuple-element.20), channel_id=1, source_target_pairs={{0,2},{1,3},{2,0},{3,1},{4,6},{5,7},{6,4},{7,5},{8,10},{9,11},{10,... | collective-permute-start | bytes 221192 | tf_op jit(solution)/shard_map/ppermute | solution.py:303
  100.2 7.1 %collective-permute-start.6 = (bf16[96,384]{1,0:T(8,128)(2,1)S(1)}, bf16[96,384]{1,0:T(8,128)(2,1)S(1)}, u32[]{:S(2)}, u32[]{:S(2)}) collective-permute-start(bf16[96,384]{1,0:T(8,128)(2,1)S(1)} %get-tuple-element.22), channel_id=1, source_target_pairs={{0,4},{1,5},{2,6},{3,7},{4,0},{5,1},{6,2},{7,3},{8,12},{9,13},{10,... | collective-permute-start | bytes 221192 | tf_op jit(solution)/shard_map/ppermute | solution.py:303
  102.5 8.7 %collective-permute-start.7 = (bf16[96,384]{1,0:T(8,128)(2,1)S(1)}, bf16[96,384]{1,0:T(8,128)(2,1)S(1)}, u32[]{:S(2)}, u32[]{:S(2)}) collective-permute-start(bf16[96,384]{1,0:T(8,128)(2,1)S(1)} %get-tuple-element.21), channel_id=1, source_target_pairs={{0,6},{1,7},{2,4},{3,5},{4,2},{5,3},{6,0},{7,1},{8,14},{9,15},{10,... | collective-permute-start | bytes 221192 | tf_op jit(solution)/shard_map/ppermute | solution.py:303
  116.4 26.7 %all-to-all-start.4 = ((bf16[8,16,1024]{2,1,0:T(8,128)(2,1)}), bf16[8,16,1024]{2,1,0:T(8,128)(2,1)S(1)}, u32[]{:S(2)}, u32[]{:S(2)}) async-start(bf16[8,16,1024]{2,1,0:T(8,128)(2,1)} %add.131), calls=%async_computation.4 | async-start | bytes 524288 | tf_op jit(solution)/shard_map/all_to_all | solution.py:290
  124.4 18.1 %collective-permute-start.8 = (f32[96,128]{1,0:T(8,128)S(1)}, f32[96,128]{1,0:T(8,128)S(1)}, u32[]{:S(2)}, u32[]{:S(2)}) collective-permute-start(f32[96,128]{1,0:T(8,128)S(1)} %get-tuple-element.23), channel_id=1, source_target_pairs={{0,8},{8,16},{16,24},{24,32},{32,40},{40,48},{48,56},{56,64},{64,7... | collective-permute-start | bytes 147464 | tf_op jit(solution)/shard_map/ppermute | solution.py:32
  132.2 10.3 %collective-permute-start.9 = (f32[96,128]{1,0:T(8,128)S(1)}, f32[96,128]{1,0:T(8,128)S(1)}, u32[]{:S(2)}, u32[]{:S(2)}) collective-permute-start(f32[96,128]{1,0:T(8,128)S(1)} %get-tuple-element.24), channel_id=1, source_target_pairs={{0,16},{8,24},{16,32},{24,40},{32,48},{40,56},{48,64},{56,72},{64,... | collective-permute-start | bytes 147464 | tf_op jit(solution)/shard_map/ppermute | solution.py:32
  (1 other events, 0.9 us)

commit v5 on v4

v5 whole, which is shorter than its diff:
```python
import functools

import jax
import jax.numpy as jnp
from jax import lax
from jax.experimental import pallas as pl
from jax.experimental.pallas import tpu as pltpu
from jax.sharding import Mesh, PartitionSpec as P

STEPS = 3
EPSILON = 1e-06
TEMPER = 50.0
MARGIN = 0.01
LOSS_SCALE = 1024.0

DP_SIZES = {64: (4, 8, 2), 8: (2, 2, 2)}
DP = ("z", "x", "yh")
LANES = 128
f32 = jnp.float32
bf16 = jnp.bfloat16


def dot(left, right, contract, precision=None):
    return lax.dot_general(
        left, right, ((contract[:1], contract[1:]), ((), ())),
        preferred_element_type=f32, precision=precision,
    )


def passed_along(array, by):
    peers = lax.axis_size(DP)
    return lax.ppermute(array, DP, [(i, (i + by) % peers) for i in range(peers)])


def exact_parts(values):
    high = values.astype(bf16)
    rest = values - high.astype(f32)
    middle = rest.astype(bf16)
    low = (rest - middle.astype(f32)).astype(bf16)
    return jnp.concatenate([high, middle, low], 0)


def diagonal(size):
    return lax.broadcasted_iota(jnp.int32, (size, size), 0) == lax.broadcasted_iota(
        jnp.int32, (size, size), 1
    )


def row_sums(values):
    sums = jnp.sum(values, 1, keepdims=True)
    return jnp.sum(jnp.where(diagonal(values.shape[0]), sums, 0.0), 0, keepdims=True)


def upright(values):
    return jnp.sum(jnp.where(diagonal(values.shape[1]), values, 0.0), 1, keepdims=True)


def own_kernel(student, weight, weight_rows, teacher, through, proj_own, tiles, sums):
    peers, height, _ = through.shape
    texts = student.shape[0]
    own = dot(student[...], weight[...], (1, 0))
    proj_own[...] = own.astype(bf16)
    wide = teacher[...].astype(f32)
    tiles[:, :texts] = dot(proj_own[...], proj_own[...], (1, 1))
    tiles[:, texts:] = dot(teacher[...], teacher[...], (1, 1))
    sums[...] = jnp.concatenate(
        [row_sums(own * own), row_sums(wide * wide), row_sums(own * wide), jnp.zeros((5, texts), f32)],
        0,
    )
    for t, other in enumerate((weight_rows, teacher)):
        product = dot(weight[...], other[...], (1, 1)).astype(bf16)
        through[:, :, t * LANES : (t + 1) * LANES] = product.reshape(peers, height, LANES)


def tile_kernel(
    proj_own, weight, teacher, tiles, sums, near_student, far_student, near_teacher, far_teacher,
    payload, proj_near, proj_far,
):
    peers, rows, _ = payload.shape
    texts = proj_own.shape[0]
    tail = [sums[0:1, :], sums[1:2, :], sums[2:3, :]]

    def lay_out(t, tile):
        payload[:, :, t * texts : (t + 1) * texts] = tile.reshape(peers, rows, texts)

    lay_out(0, tiles[:, :texts])
    lay_out(STEPS, tiles[:, texts:])
    for s, rows_in, mates_in, proj in (
        (1, near_student, near_teacher, proj_near),
        (2, far_student, far_teacher, proj_far),
    ):
        other = dot(rows_in[...], weight[...], (1, 0))
        proj[...] = other.astype(bf16)
        wide = mates_in[...].astype(f32)
        tail = tail + [row_sums(other * other), row_sums(wide * wide)]
        lay_out(s, dot(proj_own[...], proj[...], (1, 1)))
        lay_out(STEPS + s, dot(teacher[...], mates_in[...], (1, 1)))
    tail = jnp.concatenate(tail + [jnp.zeros((rows - len(tail), texts), f32)], 0)
    for peer in range(peers):
        payload[peer, :, 2 * STEPS * texts :] = tail


def band_kernel(parts, ids, tiles, norms):
    peers = tiles.shape[0]
    rows = parts.shape[1]
    band = ids.shape[1]
    texts = band // STEPS
    sums = jnp.sum(parts[...], 0)

    def part(array, t):
        return array[:, t * texts : (t + 1) * texts]

    tail = part(sums, 2 * STEPS)
    norms[...] = tail[:8]
    proj_sq = jnp.concatenate([tail[0:1], tail[3:4], tail[5:6]], 1)
    teach_sq = jnp.concatenate([tail[1:2], tail[4:5], tail[6:7]], 1)
    inv_proj = lax.rsqrt(proj_sq + EPSILON)
    inv_teach = lax.rsqrt(teach_sq + EPSILON)
    row_id = lax.broadcasted_iota(jnp.int32, (rows, band), 0)
    anchor = (ids[0:1, :] == row_id).astype(f32)
    own = (ids[3:4, :] == row_id).astype(f32)
    row_proj = jnp.sum(own * inv_proj, 1, keepdims=True)
    row_teach = jnp.sum(own * inv_teach, 1, keepdims=True)
    sim = sums[:, :band] * (row_proj * inv_proj)
    teach = sums[:, band : 2 * band] * (row_teach * inv_teach)
    col_id = lax.broadcasted_iota(jnp.int32, (band, band), 0)
    pick = (col_id == ids[1:2, :]).astype(f32) - (col_id == ids[2:3, :]).astype(f32)
    anchor_thrice = jnp.concatenate([anchor, anchor, anchor], 0).astype(bf16)
    gap_s = jnp.sum(dot(exact_parts(sim), anchor_thrice, (0, 0)) * pick, 0, keepdims=True)
    gap_t = jnp.sum(dot(exact_parts(teach), anchor_thrice, (0, 0)) * pick, 0, keepdims=True)
    weight = jnp.tanh(TEMPER * gap_t)
    slope = -weight * jax.nn.sigmoid(TEMPER * (MARGIN - weight * gap_s))
    added = dot(exact_parts(anchor * slope), pick.astype(bf16), (1, 1))
    grad = 2.0 * (sim - teach) + (
        added[:rows] + added[rows : 2 * rows] + added[2 * rows :]
    )
    product = grad * sim
    along = jnp.sum(product, 1, keepdims=True)
    inner = jnp.sum(product + along * own, 0, keepdims=True) * (inv_proj * inv_proj)
    high = inner.astype(bf16).astype(f32)
    low = inner - high
    tail_id = lax.broadcasted_iota(jnp.int32, (rows, texts), 0)
    extra = jnp.zeros((rows, texts), f32)
    for s in range(STEPS):
        extra = jnp.where(tail_id == 2 * s, part(high, s), extra)
        extra = jnp.where(tail_id == 2 * s + 1, part(low, s), extra)
    tile = jnp.concatenate([grad * (row_proj * inv_proj), extra], 1).astype(bf16)
    for peer in range(peers):
        tiles[peer] = tile


def spread(gathered, norms, rows):
    own = rows[0]
    texts = own.shape[0]
    band = STEPS * texts
    gathered = gathered[...]
    tile = gathered[:, :, :band].reshape(texts, band)
    tail = jnp.sum(gathered[:, :, band:].astype(f32), 0)
    inv_proj = lax.rsqrt(norms[0:1, :] + EPSILON)
    inv_teach = lax.rsqrt(norms[1:2, :] + EPSILON)
    both = inv_proj * inv_teach
    cosine = norms[2:3, :] * both
    terms = []
    for s, partner in enumerate(rows):
        scale = -(tail[2 * s : 2 * s + 1] + tail[2 * s + 1 : 2 * s + 2])
        if s == 0:
            scale = scale + cosine * inv_proj * inv_proj
        tile_s = tile[:, s * texts : (s + 1) * texts]
        terms.append(dot(tile_s, own[...], (0, 0)) + upright(scale) * partner[...].astype(f32))
        terms[0] = terms[0] + dot(tile_s, partner[...], (1, 0))
    return terms, both


def grad_kernel(gathered, norms, own, near, far, teacher, regrouped, rows_grad, grad_w):
    texts = own.shape[0]
    terms, both = spread(gathered, norms, (own, near, far))
    terms[0] = terms[0] - upright(both) * teacher[...].astype(f32)
    for s in range(STEPS):
        rows_grad[s * texts : (s + 1) * texts, :] = (LOSS_SCALE * terms[s]).astype(bf16)
    grad_w[...] = dot(regrouped[...], rows_grad[...], (1, 0)).astype(bf16)


def student_kernel(gathered, norms, own, near, far, gram, teacher_back, out_own, out_near, out_far):
    terms, both = spread(gathered, norms, (own, near, far))
    groups = own.shape[1] // LANES
    table = jnp.concatenate([gram[g] for g in range(groups)], 1)
    for s, out in enumerate((out_own, out_near, out_far)):
        product = dot(table, terms[s].astype(bf16), (1, 1))
        if s == 0:
            product = product - both * teacher_back[...]
        out[...] = LOSS_SCALE * product


def add_kernel(received, out):
    blocks, padded, _ = out.shape
    total = jnp.sum(received[...].astype(f32), 0)
    share = total.shape[0] // blocks
    fill = jnp.zeros((padded - share, total.shape[1]), f32)
    for block in range(blocks):
        piece = total[block * share : (block + 1) * share]
        out[block] = jnp.concatenate([piece, fill], 0).astype(bf16)


def by_x(sizes, features):
    z_size, x_size, yh_size = sizes
    share = features // (z_size * x_size)
    out = lax.broadcasted_iota(jnp.int32, (features, features), 0)
    place, offset = out // share, out % share
    source = (place % z_size * x_size + place // z_size) * share + offset
    return (lax.broadcasted_iota(jnp.int32, out.shape, 1) == source).astype(bf16)


def shards(student, proj_weight, teacher, anchors, pairs, *, sizes):
    z_size, x_size, yh_size = sizes
    n_dp = z_size * x_size * yh_size
    n_feat = lax.axis_size("feat")
    texts, features = student.shape
    width = teacher.shape[1]
    band = STEPS * texts
    rows = texts // n_feat
    share = features // n_dp
    padded = -(-share // 16) * 16
    feat = lax.axis_index("feat")

    near_student = passed_along(student, -1)
    near_teacher = passed_along(teacher, -1)

    def cost(flops):
        return pl.CostEstimate(flops=flops, bytes_accessed=3 * 10**6, transcendentals=0)

    params = pltpu.CompilerParams(vmem_limit_bytes=16 * 2**20)
    rows_type = jax.ShapeDtypeStruct((texts, width), bf16)

    groups = features // LANES
    height = features // n_feat
    row_start = jnp.minimum(lax.axis_index("x"), groups - 1) * LANES
    weight_rows = lax.dynamic_slice(proj_weight, (row_start, 0), (LANES, width))
    through, proj_own, own_tiles, own_sums = pl.pallas_call(
        own_kernel,
        out_shape=(
            jax.ShapeDtypeStruct((n_feat, height, 2 * LANES), bf16),
            rows_type,
            jax.ShapeDtypeStruct((texts, 2 * texts), f32),
            jax.ShapeDtypeStruct((8, texts), f32),
        ),
        compiler_params=params,
        cost_estimate=cost(6 * 10**8),
        name="own",
    )(student, proj_weight, weight_rows, teacher)
    far_rows = lax.optimization_barrier((student, teacher, proj_own))
    far_student = passed_along(far_rows[0], -2)
    far_teacher = passed_along(far_rows[1], -2)
    through = jnp.sum(lax.all_to_all(through, "feat", 0, 0).astype(f32), 0)
    teacher_back = through[:, LANES:]
    gram = through[:, :LANES].astype(bf16)
    gram = lax.all_to_all(jnp.broadcast_to(gram[None], (x_size, height, LANES)), "x", 0, 0)

    parts, proj_near, proj_far = pl.pallas_call(
        tile_kernel,
        out_shape=(
            jax.ShapeDtypeStruct((n_feat, rows, (2 * STEPS + 1) * texts), f32),
            rows_type,
            rows_type,
        ),
        compiler_params=params,
        cost_estimate=cost(6 * 10**8),
        name="tile",
    )(
        proj_own, proj_weight, teacher, own_tiles, own_sums,
        near_student, far_student, near_teacher, far_teacher,
    )
    parts = lax.all_to_all(parts, "feat", 0, 0)

    ids = jnp.concatenate(
        [
            anchors[None] - feat * rows,
            pairs,
            lax.broadcasted_iota(jnp.int32, (1, band), 1) - feat * rows,
            jnp.zeros((4, band), jnp.int32),
        ],
        0,
    )
    tiles, norms = pl.pallas_call(
        band_kernel,
        out_shape=(
            jax.ShapeDtypeStruct((n_feat, rows, band + texts), bf16),
            jax.ShapeDtypeStruct((8, texts), f32),
        ),
        cost_estimate=cost(10**8),
        name="band",
    )(parts, ids)
    gathered = lax.all_to_all(tiles, "feat", 0, 0)

    student_band = jnp.concatenate([student, near_student, far_student], 0)
    regrouped = dot(by_x(sizes, features), student_band, (1, 1)).astype(bf16)
    _, grad_w = pl.pallas_call(
        grad_kernel,
        out_shape=(
            jax.ShapeDtypeStruct((band, width), bf16),
            jax.ShapeDtypeStruct((features, width), bf16),
        ),
        compiler_params=params,
        cost_estimate=cost(10**9),
        name="grad",
    )(gathered, norms, proj_own, proj_near, proj_far, teacher, regrouped)

    zy = z_size * yh_size
    grad_w = lax.all_to_all(grad_w.reshape(x_size, features // x_size, width), "x", 0, 0)
    grad_w = pl.pallas_call(
        add_kernel,
        grid=(z_size,),
        in_specs=[pl.BlockSpec((x_size, yh_size * share, width), lambda i: (0, i, 0))],
        out_specs=pl.BlockSpec((yh_size, padded, width), lambda i: (i, 0, 0)),
        out_shape=jax.ShapeDtypeStruct((zy, padded, width), bf16),
        cost_estimate=cost(10**6),
        name="add",
    )(grad_w)
    grad_w = lax.all_to_all(grad_w, ("z", "yh"), 0, 0)
    grad_w = jnp.sum(grad_w.astype(f32), 0)[:share]

    columns_type = jax.ShapeDtypeStruct((height, texts), f32)
    own, near, far = pl.pallas_call(
        student_kernel,
        out_shape=(columns_type,) * STEPS,
        compiler_params=params,
        cost_estimate=cost(4 * 10**8),
        name="student",
    )(gathered, norms, student, near_student, far_student, gram, teacher_back)
    grad_student = own + passed_along(near, 1) + passed_along(far, 2)
    return (grad_w, grad_student.T)


def solution(mesh):
    n_dp, n_feat = mesh.devices.shape
    sizes = DP_SIZES[n_dp]
    split = Mesh(mesh.devices.reshape(*sizes, n_feat), (*DP, "feat"))
    return jax.shard_map(
        functools.partial(shards, sizes=sizes),
        mesh=split,
        in_specs=(P(DP, None), P(None, "feat"), P(DP, "feat"), P(DP), P(None, DP)),
        out_specs=(P(DP, "feat"), P(DP, "feat")),
        check_vma=False,
    )
```

time: 145 us -> 154 us (1.062)
  the two profiles are of different devices: /device:TPU:8 before, /device:TPU:1 now
where the time goes in v5:
time: 154 us; the launch traced here: 153 us
  starting transfers between devices  67 us (44%)
  waiting for transfers between devices  62.4 us (41%)
  Pallas kernels  13.5 us (9%)
  local copies, waits for them, and re-layouts  5.9 us (4%)
  other arithmetic  2.05 us (1%)
    ppermute x6, starting transfers between devices, passed_along(): lax.ppermute(array, DP, [(i, (i + by) % peers) for i in range(peers)])  34.8 us
    all_to_all x1, waiting for transfers between devices, shards(): lax.all_to_all(grad_w.reshape(x_size, features // x_size, width), 'x', 0, 0)  20.4 us
    ppermute x6, waiting for transfers between devices, passed_along(): lax.ppermute(array, DP, [(i, (i + by) % peers) for i in range(peers)])  13.8 us
    all_to_all x1, waiting for transfers between devices, shards(): parts = lax.all_to_all(parts, 'feat', 0, 0)  12.3 us
    all_to_all x1, starting transfers between devices, shards(): parts = lax.all_to_all(parts, 'feat', 0, 0)  9.7 us
    all_to_all x1, waiting for transfers between devices, shards(): through = jnp.sum(lax.all_to_all(through, 'feat', 0, 0).astype(f32), 0)  7.59 us
    all_to_all x1, starting transfers between devices, shards(): grad_w = lax.all_to_all(grad_w, ('z', 'yh'), 0, 0)  6.78 us
    all_to_all x1, waiting for transfers between devices, shards(): gathered = lax.all_to_all(tiles, 'feat', 0, 0)  5.81 us
  transfers between devices with their start and end apart: 12, of which 8 were waited for; matrix products, arithmetic and copies ran while one was open for 2% of the time, Pallas kernels for 6%

profile of v5, /device:TPU:1, one launch (start us, length us, event | category | flops | bytes accessed | tf_op | source)
XLA Modules:
  0.0 152.9 jit_solution(1081633913558254584)
XLA Ops:
  0.6 19.1 %collective-permute-start.2 = (bf16[128,1024]{1,0:T(8,128)(2,1)}, bf16[128,1024]{1,0:T(8,128)(2,1)S(1)}, u32[]{:S(2)}, u32[]{:S(2)}) collective-permute-start(bf16[128,1024]{1,0:T(8,128)(2,1)} %teacher.5), channel_id=1, source_target_pairs={{0,504},{8,0},{16,8},{24,16},{32,24},{40,32},{48,40},{56,48},{64,5... | collective-permute-start | bytes 786440 | tf_op jit(solution)/shard_map/ppermute | solution.py:32
  24.0 2.2 %own.2 = (bf16[8,96,256]{2,1,0:T(8,128)(2,1)}, bf16[128,1024]{1,0:T(8,128)(2,1)S(1)}, f32[128,256]{1,0:T(8,128)S(1)}, f32[8,128]{1,0:T(8,128)S(1)}) custom-call(bf16[128,768]{1,0:T(8,128)(2,1)S(1)} %copy-done.4, bf16[768,1024]{1,0:T(8,128)(2,1)S(1)} %copy-done, bf16[128,1024]{1,0:T(8,128)(2,1)S(1)} %constant_dynamic-slice_fusion.weight_rows, ...), custom_call_target="tpu_custom_call" | custom-call | flops 600000000 | bytes 3000000 | tf_op jit(solution)/shard_map/own/pallas_call | solution.py:238
  26.2 2.4 %collective-permute-start.3 = (bf16[128,1024]{1,0:T(8,128)(2,1)S(1)}, bf16[128,1024]{1,0:T(8,128)(2,1)S(1)}, u32[]{:S(2)}, u32[]{:S(2)}) collective-permute-start(bf16[128,1024]{1,0:T(8,128)(2,1)S(1)} %copy-done.2), channel_id=1, source_target_pairs={{0,496},{8,504},{16,0},{24,8},{32,16},{40,24},{48,32},{56,40},{64,... | collective-permute-start | bytes 786440 | tf_op jit(solution)/shard_map/ppermute | solution.py:32
  28.6 1.9 %collective-permute-start = (bf16[128,768]{1,0:T(8,128)(2,1)S(1)}, bf16[128,768]{1,0:T(8,128)(2,1)S(1)}, u32[]{:S(2)}, u32[]{:S(2)}) collective-permute-start(bf16[128,768]{1,0:T(8,128)(2,1)S(1)} %copy-done.4), channel_id=1, source_target_pairs={{0,504},{8,0},{16,8},{24,16},{32,24},{40,32},{48,40},{56,48},{64,5... | collective-permute-start | bytes 589832 | tf_op jit(solution)/shard_map/ppermute | solution.py:32
  30.6 2.2 %collective-permute-start.1 = (bf16[128,768]{1,0:T(8,128)(2,1)S(1)}, bf16[128,768]{1,0:T(8,128)(2,1)S(1)}, u32[]{:S(2)}, u32[]{:S(2)}) collective-permute-start(bf16[128,768]{1,0:T(8,128)(2,1)S(1)} %copy-done.4), channel_id=1, source_target_pairs={{0,496},{8,504},{16,0},{24,8},{32,16},{40,24},{48,32},{56,40},{64,... | collective-permute-start | bytes 589832 | tf_op jit(solution)/shard_map/ppermute | solution.py:32
  32.7 7.0 %collective-permute-done.near_student.near = bf16[128,768]{1,0:T(8,128)(2,1)S(1)} collective-permute-done((bf16[128,768]{1,0:T(8,128)(2,1)S(1)}, bf16[128,768]{1,0:T(8,128)(2,1)S(1)}, u32[]{:S(2)}, u32[]{:S(2)}) %collective-permute-start) | collective-permute-done | bytes 196640 | tf_op jit(solution)/shard_map/ppermute | solution.py:32
  41.6 9.7 %all-to-all-start = ((f32[8,16,896]{2,1,0:T(8,128)}), f32[8,16,896]{2,1,0:T(8,128)S(1)}, u32[]{:S(2)}, u32[]{:S(2)}) async-start(f32[8,16,896]{2,1,0:T(8,128)} %get-tuple-element.22), calls=%async_computation | async-start | bytes 917504 | tf_op jit(solution)/shard_map/all_to_all | solution.py:272
  52.1 12.3 %all-to-all-done.parts = f32[8,16,896]{2,1,0:T(8,128)S(1)} async-done(((f32[8,16,896]{2,1,0:T(8,128)}), f32[8,16,896]{2,1,0:T(8,128)S(1)}, u32[]{:S(2)}, u32[]{:S(2)}) %all-to-all-start) | async-done | bytes 458784 | tf_op jit(solution)/shard_map/all_to_all | solution.py:272
  65.2 2.4 %band.1 = (bf16[8,16,512]{2,1,0:T(8,128)(2,1)}, f32[8,128]{1,0:T(8,128)}) custom-call(f32[8,16,896]{2,1,0:T(8,128)} %copy-done.8, s32[8,384]{1,0:T(8,128)} %add_add_fusion.ids), custom_call_target="tpu_custom_call" | custom-call | flops 100000000 | bytes 3000000 | tf_op jit(solution)/shard_map/band/pallas_call | solution.py:283
  67.6 4.1 %all-to-all-start.1 = ((bf16[8,16,512]{2,1,0:T(8,128)(2,1)}), bf16[8,16,512]{2,1,0:T(8,128)(2,1)S(1)}, u32[]{:S(2)}, u32[]{:S(2)}) async-start(bf16[8,16,512]{2,1,0:T(8,128)(2,1)} %get-tuple-element.23), calls=%async_computation.1 | async-start | bytes 262144 | tf_op jit(solution)/shard_map/all_to_all | solution.py:292
  71.8 5.8 %all-to-all-done.1.gathered = bf16[8,16,512]{2,1,0:T(8,128)(2,1)S(1)} async-done(((bf16[8,16,512]{2,1,0:T(8,128)(2,1)}), bf16[8,16,512]{2,1,0:T(8,128)(2,1)S(1)}, u32[]{:S(2)}, u32[]{:S(2)}) %all-to-all-start.1) | async-done | bytes 131104 | tf_op jit(solution)/shard_map/all_to_all | solution.py:292
  77.6 4.3 %all-to-all-start.4 = ((bf16[8,96,256]{2,1,0:T(8,128)(2,1)}), bf16[8,96,256]{2,1,0:T(8,128)(2,1)S(1)}, u32[]{:S(2)}, u32[]{:S(2)}) async-start(bf16[8,96,256]{2,1,0:T(8,128)(2,1)} %get-tuple-element.28), calls=%async_computation.4 | async-start | bytes 786432 | tf_op jit(solution)/shard_map/all_to_all | solution.py:253
  83.1 2.9 %grad.1 = (bf16[384,1024]{1,0:T(8,128)(2,1)}, bf16[768,1024]{1,0:T(8,128)(2,1)}) custom-call(bf16[8,16,512]{2,1,0:T(8,128)(2,1)S(1)} %all-to-all-done.1.gathered, f32[8,128]{1,0:T(8,128)S(1)} %copy-done.6, bf16[128,1024]{1,0:T(8,128)(2,1)S(1)} %get-tuple-element.17.proj_own.own, bf16[128,1024]{1,0:T(8,128)(2,1)S(1)} %get-tuple-element.25.near, ...), custom_call_target="tpu_custom_call" | custom-call | flops 1000000000 | bytes 3000000 | tf_op jit(solution)/shard_map/grad/pallas_call | solution.py:296
  86.0 7.6 %all-to-all-done.4 = bf16[8,96,256]{2,1,0:T(8,128)(2,1)S(1)} async-done(((bf16[8,96,256]{2,1,0:T(8,128)(2,1)}), bf16[8,96,256]{2,1,0:T(8,128)(2,1)S(1)}, u32[]{:S(2)}, u32[]{:S(2)}) %all-to-all-start.4) | async-done | bytes 393248 | tf_op jit(solution)/shard_map/all_to_all | solution.py:253
  93.6 3.6 %all-to-all-start.2 = ((bf16[8,96,1024]{2,1,0:T(8,128)(2,1)}), bf16[8,96,1024]{2,1,0:T(8,128)(2,1)S(1)}, u32[]{:S(2)}, u32[]{:S(2)}) async-start(bf16[8,96,1024]{2,1,0:T(8,128)(2,1)} %bitcast), calls=%async_computation.2 | async-start | bytes 3145728 | tf_op jit(solution)/shard_map/all_to_all | solution.py:308
  97.3 20.4 %all-to-all-done.2.received = bf16[8,96,1024]{2,1,0:T(8,128)(2,1)S(1)} async-done(((bf16[8,96,1024]{2,1,0:T(8,128)(2,1)}), bf16[8,96,1024]{2,1,0:T(8,128)(2,1)S(1)}, u32[]{:S(2)}, u32[]{:S(2)}) %all-to-all-start.2) | async-done | bytes 1572896 | tf_op jit(solution)/shard_map/all_to_all | solution.py:308
  118.4 3.7 %all-to-all-start.5 = ((bf16[8,96,128]{2,1,0:T(8,128)(2,1)}), bf16[8,96,128]{2,1,0:T(8,128)(2,1)S(1)}, u32[]{:S(2)}, u32[]{:S(2)}) async-start(bf16[8,96,128]{2,1,0:T(8,128)(2,1)} %broadcast_in_dim.5), calls=%async_computation.5 | async-start | bytes 393216 | tf_op jit(solution)/shard_map/all_to_all | solution.py:256
  122.1 3.4 %add.76 = bf16[8,16,1024]{2,1,0:T(8,128)(2,1)} custom-call(bf16[8,96,1024]{2,1,0:T(8,128)(2,1)} %copy-done.7), custom_call_target="tpu_custom_call" | custom-call | flops 1000000 | bytes 3000000 | tf_op jit(solution)/shard_map/add/pallas_call | solution.py:309
  125.5 2.5 %all-to-all-done.5.gram = bf16[8,96,128]{2,1,0:T(8,128)(2,1)S(1)} async-done(((bf16[8,96,128]{2,1,0:T(8,128)(2,1)}), bf16[8,96,128]{2,1,0:T(8,128)(2,1)S(1)}, u32[]{:S(2)}, u32[]{:S(2)}) %all-to-all-start.5) | async-done | bytes 196640 | tf_op jit(solution)/shard_map/all_to_all | solution.py:256
  128.0 6.8 %all-to-all-start.3 = ((bf16[8,16,1024]{2,1,0:T(8,128)(2,1)}), bf16[8,16,1024]{2,1,0:T(8,128)(2,1)S(1)}, u32[]{:S(2)}, u32[]{:S(2)}) async-start(bf16[8,16,1024]{2,1,0:T(8,128)(2,1)} %add.76), calls=%async_computation.3 | async-start | bytes 524288 | tf_op jit(solution)/shard_map/all_to_all | solution.py:318
  135.6 7.3 %collective-permute-start.4 = (f32[96,128]{1,0:T(8,128)S(1)}, f32[96,128]{1,0:T(8,128)S(1)}, u32[]{:S(2)}, u32[]{:S(2)}) collective-permute-start(f32[96,128]{1,0:T(8,128)S(1)} %get-tuple-element.30), channel_id=1, source_target_pairs={{0,8},{8,16},{16,24},{24,32},{32,40},{40,48},{48,56},{56,64},{64,7... | collective-permute-start | bytes 147464 | tf_op jit(solution)/shard_map/ppermute | solution.py:32
  142.9 1.9 %collective-permute-start.5 = (f32[96,128]{1,0:T(8,128)S(1)}, f32[96,128]{1,0:T(8,128)S(1)}, u32[]{:S(2)}, u32[]{:S(2)}) collective-permute-start(f32[96,128]{1,0:T(8,128)S(1)} %get-tuple-element.31), channel_id=1, source_target_pairs={{0,16},{8,24},{16,32},{24,40},{32,48},{40,56},{48,64},{56,72},{64,... | collective-permute-start | bytes 147464 | tf_op jit(solution)/shard_map/ppermute | solution.py:32
  144.8 4.7 %collective-permute-done.4 = f32[96,128]{1,0:T(8,128)S(1)} collective-permute-done((f32[96,128]{1,0:T(8,128)S(1)}, f32[96,128]{1,0:T(8,128)S(1)}, u32[]{:S(2)}, u32[]{:S(2)}) %collective-permute-start.4) | collective-permute-done | bytes 49184 | tf_op jit(solution)/shard_map/ppermute | solution.py:32
  149.5 2.1 %collective-permute-done.5 = f32[96,128]{1,0:T(8,128)S(1)} collective-permute-done((f32[96,128]{1,0:T(8,128)S(1)}, f32[96,128]{1,0:T(8,128)S(1)}, u32[]{:S(2)}, u32[]{:S(2)}) %collective-permute-start.5) | collective-permute-done | bytes 49184 | tf_op jit(solution)/shard_map/ppermute | solution.py:32
  (45 shorter events, 11.8 us)
Async XLA Ops:
  0.6 39.1 %copy-start.3 = (bf16[128,1024]{1,0:T(8,128)(2,1)S(1)}, bf16[128,1024]{1,0:T(8,128)(2,1)}, u32[]{:S(2)}) copy-start(bf16[128,1024]{1,0:T(8,128)(2,1)} %teacher.5) | copy-start | bytes 786436
  0.6 39.1 %collective-permute-start.2 = (bf16[128,1024]{1,0:T(8,128)(2,1)}, bf16[128,1024]{1,0:T(8,128)(2,1)S(1)}, u32[]{:S(2)}, u32[]{:S(2)}) collective-permute-start(bf16[128,1024]{1,0:T(8,128)(2,1)} %teacher.5), channel_id=1, source_target_pairs={{0,504},{8,0},{16,8},{24,16},{32,24},{40,32},{48,40},{56,48},{64,5... | collective-permute-start | bytes 786440 | tf_op jit(solution)/shard_map/ppermute | solution.py:32
  20.7 1.4 copy-start
  22.1 0.9 copy-start.2
  23.1 0.9 copy-start.4
  24.0 15.8 %copy-start.1 = (bf16[768,1024]{1,0:T(8,128)(2,1)S(1)}, bf16[768,1024]{1,0:T(8,128)(2,1)}, u32[]{:S(2)}) copy-start(bf16[768,1024]{1,0:T(8,128)(2,1)} %weight.3) | copy-start | bytes 4718596
  26.2 13.6 %collective-permute-start.3 = (bf16[128,1024]{1,0:T(8,128)(2,1)S(1)}, bf16[128,1024]{1,0:T(8,128)(2,1)S(1)}, u32[]{:S(2)}, u32[]{:S(2)}) collective-permute-start(bf16[128,1024]{1,0:T(8,128)(2,1)S(1)} %copy-done.2), channel_id=1, source_target_pairs={{0,496},{8,504},{16,0},{24,8},{32,16},{40,24},{48,32},{56,40},{64,... | collective-permute-start | bytes 786440 | tf_op jit(solution)/shard_map/ppermute | solution.py:32
  28.6 11.1 %collective-permute-start = (bf16[128,768]{1,0:T(8,128)(2,1)S(1)}, bf16[128,768]{1,0:T(8,128)(2,1)S(1)}, u32[]{:S(2)}, u32[]{:S(2)}) collective-permute-start(bf16[128,768]{1,0:T(8,128)(2,1)S(1)} %copy-done.4), channel_id=1, source_target_pairs={{0,504},{8,0},{16,8},{24,16},{32,24},{40,32},{48,40},{56,48},{64,5... | collective-permute-start | bytes 589832 | tf_op jit(solution)/shard_map/ppermute | solution.py:32
  30.6 9.2 %collective-permute-start.1 = (bf16[128,768]{1,0:T(8,128)(2,1)S(1)}, bf16[128,768]{1,0:T(8,128)(2,1)S(1)}, u32[]{:S(2)}, u32[]{:S(2)}) collective-permute-start(bf16[128,768]{1,0:T(8,128)(2,1)S(1)} %copy-done.4), channel_id=1, source_target_pairs={{0,496},{8,504},{16,0},{24,8},{32,16},{40,24},{48,32},{56,40},{64,... | collective-permute-start | bytes 589832 | tf_op jit(solution)/shard_map/ppermute | solution.py:32
  39.8 11.6 %copy-start.10 = (s32[384]{0:T(512)S(1)}, s32[384]{0:T(512)}, u32[]{:S(2)}) copy-start(s32[384]{0:T(512)} %param.8) | copy-start | bytes 4612
  39.8 11.6 %copy-start.9 = (s32[2,384]{1,0:T(2,128)S(1)}, s32[2,384]{1,0:T(2,128)}, u32[]{:S(2)}) copy-start(s32[2,384]{1,0:T(2,128)} %param.9) | copy-start | bytes 9220
  41.6 40.3 %copy-start.5 = (bf16[128,768]{1,0:T(8,128)(2,1)S(1)}, bf16[128,768]{1,0:T(8,128)(2,1)}, u32[]{:S(2)}) copy-start(bf16[128,768]{1,0:T(8,128)(2,1)} %own.3) | copy-start | bytes 589828
  41.6 22.8 %all-to-all-start = ((f32[8,16,896]{2,1,0:T(8,128)}), f32[8,16,896]{2,1,0:T(8,128)S(1)}, u32[]{:S(2)}, u32[]{:S(2)}) async-start(f32[8,16,896]{2,1,0:T(8,128)} %get-tuple-element.22), calls=%async_computation | async-start | bytes 917504 | tf_op jit(solution)/shard_map/all_to_all | solution.py:272
  64.4 0.8 copy-start.8
  67.6 10.0 %all-to-all-start.1 = ((bf16[8,16,512]{2,1,0:T(8,128)(2,1)}), bf16[8,16,512]{2,1,0:T(8,128)(2,1)S(1)}, u32[]{:S(2)}, u32[]{:S(2)}) async-start(bf16[8,16,512]{2,1,0:T(8,128)(2,1)} %get-tuple-element.23), calls=%async_computation.1 | async-start | bytes 262144 | tf_op jit(solution)/shard_map/all_to_all | solution.py:292
  77.6 16.0 %all-to-all-start.4 = ((bf16[8,96,256]{2,1,0:T(8,128)(2,1)}), bf16[8,96,256]{2,1,0:T(8,128)(2,1)S(1)}, u32[]{:S(2)}, u32[]{:S(2)}) async-start(bf16[8,96,256]{2,1,0:T(8,128)(2,1)} %get-tuple-element.28), calls=%async_computation.4 | async-start | bytes 786432 | tf_op jit(solution)/shard_map/all_to_all | solution.py:253
  81.9 1.2 copy-start.6
  93.6 24.0 %all-to-all-start.2 = ((bf16[8,96,1024]{2,1,0:T(8,128)(2,1)}), bf16[8,96,1024]{2,1,0:T(8,128)(2,1)S(1)}, u32[]{:S(2)}, u32[]{:S(2)}) async-start(bf16[8,96,1024]{2,1,0:T(8,128)(2,1)} %bitcast), calls=%async_computation.2 | async-start | bytes 3145728 | tf_op jit(solution)/shard_map/all_to_all | solution.py:308
  117.7 4.4 %copy-start.7 = (bf16[8,96,1024]{2,1,0:T(8,128)(2,1)}, bf16[8,96,1024]{2,1,0:T(8,128)(2,1)S(1)}, u32[]{:S(2)}) copy-start(bf16[8,96,1024]{2,1,0:T(8,128)(2,1)S(1)} %all-to-all-done.2.received) | copy-start | bytes 4718596
  118.4 9.5 %all-to-all-start.5 = ((bf16[8,96,128]{2,1,0:T(8,128)(2,1)}), bf16[8,96,128]{2,1,0:T(8,128)(2,1)S(1)}, u32[]{:S(2)}, u32[]{:S(2)}) async-start(bf16[8,96,128]{2,1,0:T(8,128)(2,1)} %broadcast_in_dim.5), calls=%async_computation.5 | async-start | bytes 393216 | tf_op jit(solution)/shard_map/all_to_all | solution.py:256
  128.0 24.2 %all-to-all-start.3 = ((bf16[8,16,1024]{2,1,0:T(8,128)(2,1)}), bf16[8,16,1024]{2,1,0:T(8,128)(2,1)S(1)}, u32[]{:S(2)}, u32[]{:S(2)}) async-start(bf16[8,16,1024]{2,1,0:T(8,128)(2,1)} %add.76), calls=%async_computation.3 | async-start | bytes 524288 | tf_op jit(solution)/shard_map/all_to_all | solution.py:318
  135.6 13.9 %collective-permute-start.4 = (f32[96,128]{1,0:T(8,128)S(1)}, f32[96,128]{1,0:T(8,128)S(1)}, u32[]{:S(2)}, u32[]{:S(2)}) collective-permute-start(f32[96,128]{1,0:T(8,128)S(1)} %get-tuple-element.30), channel_id=1, source_target_pairs={{0,8},{8,16},{16,24},{24,32},{32,40},{40,48},{48,56},{56,64},{64,7... | collective-permute-start | bytes 147464 | tf_op jit(solution)/shard_map/ppermute | solution.py:32
  142.9 8.7 %collective-permute-start.5 = (f32[96,128]{1,0:T(8,128)S(1)}, f32[96,128]{1,0:T(8,128)S(1)}, u32[]{:S(2)}, u32[]{:S(2)}) collective-permute-start(f32[96,128]{1,0:T(8,128)S(1)} %get-tuple-element.31), channel_id=1, source_target_pairs={{0,16},{8,24},{16,32},{24,40},{32,48},{40,56},{48,64},{56,72},{64,... | collective-permute-start | bytes 147464 | tf_op jit(solution)/shard_map/ppermute | solution.py:32

commit v6 on v5

--- a/solution.py
+++ b/solution.py
@@ -20,10 +20,10 @@
 bf16 = jnp.bfloat16
 
 
-def dot(left, right, contract, precision=None):
+def dot(left, right, contract):
     return lax.dot_general(
         left, right, ((contract[:1], contract[1:]), ((), ())),
-        preferred_element_type=f32, precision=precision,
+        preferred_element_type=f32,
     )
 
 
@@ -171,13 +171,18 @@
     return terms, both
 
 
-def grad_kernel(gathered, norms, own, near, far, teacher, regrouped, rows_grad, grad_w):
-    texts = own.shape[0]
+def grad_kernel(
+    sizes, gathered, norms, own, near, far, teacher, student, near_student, far_student, grad_w
+):
+    z_size, x_size, _ = sizes
     terms, both = spread(gathered, norms, (own, near, far))
     terms[0] = terms[0] - upright(both) * teacher[...].astype(f32)
-    for s in range(STEPS):
-        rows_grad[s * texts : (s + 1) * texts, :] = (LOSS_SCALE * terms[s]).astype(bf16)
-    grad_w[...] = dot(regrouped[...], rows_grad[...], (1, 0)).astype(bf16)
+    total = 0.0
+    for term, rows in zip(terms, (student, near_student, far_student)):
+        total = total + dot(rows[...], (LOSS_SCALE * term).astype(bf16), (0, 0))
+    step = total.shape[0] // (z_size * x_size)
+    starts = [(z * x_size + x) * step for x in range(x_size) for z in range(z_size)]
+    grad_w[...] = jnp.concatenate([total[r : r + step] for r in starts], 0).astype(bf16)
 
 
 def student_kernel(gathered, norms, own, near, far, gram, teacher_back, out_own, out_near, out_far):
@@ -191,23 +196,18 @@
         out[...] = LOSS_SCALE * product
 
 
-def add_kernel(received, out):
-    blocks, padded, _ = out.shape
-    total = jnp.sum(received[...].astype(f32), 0)
-    share = total.shape[0] // blocks
-    fill = jnp.zeros((padded - share, total.shape[1]), f32)
-    for block in range(blocks):
-        piece = total[block * share : (block + 1) * share]
-        out[block] = jnp.concatenate([piece, fill], 0).astype(bf16)
-
-
-def by_x(sizes, features):
-    z_size, x_size, yh_size = sizes
-    share = features // (z_size * x_size)
-    out = lax.broadcasted_iota(jnp.int32, (features, features), 0)
-    place, offset = out // share, out % share
-    source = (place % z_size * x_size + place // z_size) * share + offset
-    return (lax.broadcasted_iota(jnp.int32, out.shape, 1) == source).astype(bf16)
+def add_kernel(select, received, out, held, sems):
+    peers = received.shape[0]
+    copies = [
+        pltpu.make_async_copy(received.at[p], held.at[p], sems.at[p]) for p in range(peers)
+    ]
+    for copy in copies:
+        copy.start()
+    total = 0.0
+    for peer, copy in enumerate(copies):
+        copy.wait()
+        total = total + dot(select[...], held[peer], (1, 0))
+    out[...] = total.astype(bf16)
 
 
 def shards(student, proj_weight, teacher, anchors, pairs, *, sizes):
@@ -224,6 +224,8 @@
 
     near_student = passed_along(student, -1)
     near_teacher = passed_along(teacher, -1)
+    far_student = passed_along(student, -2)
+    far_teacher = passed_along(teacher, -2)
 
     def cost(flops):
         return pl.CostEstimate(flops=flops, bytes_accessed=3 * 10**6, transcendentals=0)
@@ -247,13 +249,6 @@
         cost_estimate=cost(6 * 10**8),
         name="own",
     )(student, proj_weight, weight_rows, teacher)
-    far_rows = lax.optimization_barrier((student, teacher, proj_own))
-    far_student = passed_along(far_rows[0], -2)
-    far_teacher = passed_along(far_rows[1], -2)
-    through = jnp.sum(lax.all_to_all(through, "feat", 0, 0).astype(f32), 0)
-    teacher_back = through[:, LANES:]
-    gram = through[:, :LANES].astype(bf16)
-    gram = lax.all_to_all(jnp.broadcast_to(gram[None], (x_size, height, LANES)), "x", 0, 0)
 
     parts, proj_near, proj_far = pl.pallas_call(
         tile_kernel,
@@ -269,7 +264,9 @@
         proj_own, proj_weight, teacher, own_tiles, own_sums,
         near_student, far_student, near_teacher, far_teacher,
     )
+    through, parts = lax.optimization_barrier((through, parts))
     parts = lax.all_to_all(parts, "feat", 0, 0)
+    through = lax.psum_scatter(through, "feat", scatter_dimension=0, tiled=False)
 
     ids = jnp.concatenate(
         [
@@ -291,33 +288,39 @@
     )(parts, ids)
     gathered = lax.all_to_all(tiles, "feat", 0, 0)
 
-    student_band = jnp.concatenate([student, near_student, far_student], 0)
-    regrouped = dot(by_x(sizes, features), student_band, (1, 1)).astype(bf16)
-    _, grad_w = pl.pallas_call(
-        grad_kernel,
-        out_shape=(
-            jax.ShapeDtypeStruct((band, width), bf16),
-            jax.ShapeDtypeStruct((features, width), bf16),
-        ),
+    grad_w = pl.pallas_call(
+        functools.partial(grad_kernel, sizes),
+        out_shape=jax.ShapeDtypeStruct((features, width), bf16),
         compiler_params=params,
         cost_estimate=cost(10**9),
         name="grad",
-    )(gathered, norms, proj_own, proj_near, proj_far, teacher, regrouped)
+    )(
+        gathered, norms, proj_own, proj_near, proj_far, teacher, student, near_student, far_student
+    )
+    grad_w, through = lax.optimization_barrier((grad_w, through))
 
     zy = z_size * yh_size
     grad_w = lax.all_to_all(grad_w.reshape(x_size, features // x_size, width), "x", 0, 0)
+    row_out = lax.broadcasted_iota(jnp.int32, (zy * padded, zy * share), 0)
+    row_in = lax.broadcasted_iota(jnp.int32, row_out.shape, 1)
+    select = (row_out // padded == row_in // share) & (row_out % padded == row_in % share)
     grad_w = pl.pallas_call(
         add_kernel,
-        grid=(z_size,),
-        in_specs=[pl.BlockSpec((x_size, yh_size * share, width), lambda i: (0, i, 0))],
-        out_specs=pl.BlockSpec((yh_size, padded, width), lambda i: (i, 0, 0)),
-        out_shape=jax.ShapeDtypeStruct((zy, padded, width), bf16),
-        cost_estimate=cost(10**6),
+        in_specs=[pl.BlockSpec(memory_space=pltpu.VMEM), pl.BlockSpec(memory_space=pl.ANY)],
+        out_shape=jax.ShapeDtypeStruct((zy * padded, width), bf16),
+        scratch_shapes=[
+            pltpu.VMEM((x_size, features // x_size, width), bf16),
+            pltpu.SemaphoreType.DMA((x_size,)),
+        ],
+        compiler_params=params,
+        cost_estimate=cost(10**8),
         name="add",
-    )(grad_w)
-    grad_w = lax.all_to_all(grad_w, ("z", "yh"), 0, 0)
+    )(lax.optimization_barrier(select.astype(bf16)), grad_w)
+    grad_w = lax.all_to_all(grad_w.reshape(zy, padded, width), ("z", "yh"), 0, 0)
     grad_w = jnp.sum(grad_w.astype(f32), 0)[:share]
 
+    gram = lax.all_gather(through[:, :LANES], "x")
+    teacher_back = through[:, LANES:].astype(f32)
     columns_type = jax.ShapeDtypeStruct((height, texts), f32)
     own, near, far = pl.pallas_call(
         student_kernel,

time: 154 us -> 183 us (1.19)
  the two profiles are of different devices: /device:TPU:1 before, /device:TPU:6 now
where the time goes in v6:
time: 183 us; the launch traced here: 180 us
  starting transfers between devices  54.2 us (30%)
  waiting for transfers between devices  50.9 us (28%)
  blocking collectives  38.4 us (21%)
  between operations  14.3 us (8%)
  Pallas kernels  13.8 us (8%)
  local copies, waits for them, and re-layouts  5.82 us (3%)
  other arithmetic  2.2 us (1%)
    ppermute x6, starting transfers between devices, passed_along(): lax.ppermute(array, DP, [(i, (i + by) % peers) for i in range(peers)])  33.6 us
    all_gather x1, blocking collectives, shards(): gram = lax.all_gather(through[:, :LANES], 'x')  28.3 us
    reduce_scatter x1, waiting for transfers between devices, shards(): lax.psum_scatter(through, 'feat', scatter_dimension=0, tiled=False)  17.3 us
    all_to_all x1, waiting for transfers between devices, shards(): lax.all_to_all(grad_w.reshape(x_size, features // x_size, width), 'x', 0, 0)  15.6 us
    all_to_all x1, waiting for transfers between devices, shards(): parts = lax.all_to_all(parts, 'feat', 0, 0)  12.3 us
    all_to_all x1, starting transfers between devices, shards(): lax.all_to_all(grad_w.reshape(zy, padded, width), ('z', 'yh'), 0, 0)  11.1 us
    all_to_all x1, blocking collectives, shards(): gathered = lax.all_to_all(tiles, 'feat', 0, 0)  10.1 us
    all_to_all x1, starting transfers between devices, shards(): lax.all_to_all(grad_w.reshape(x_size, features // x_size, width), 'x', 0, 0)  5.79 us
  transfers between devices with their start and end apart: 10, of which 5 were waited for; matrix products, arithmetic and copies ran while one was open for 1% of the time, Pallas kernels for 5%

profile of v6, /device:TPU:6, one launch (start us, length us, event | category | flops | bytes accessed | tf_op | source)
XLA Modules:
  0.0 179.6 jit_solution(12323961382741446141)
XLA Ops:
  7.2 8.1 %collective-permute-start.2 = (bf16[128,1024]{1,0:T(8,128)(2,1)}, bf16[128,1024]{1,0:T(8,128)(2,1)S(1)}, u32[]{:S(2)}, u32[]{:S(2)}) collective-permute-start(bf16[128,1024]{1,0:T(8,128)(2,1)} %teacher.5), channel_id=1, source_target_pairs={{0,504},{8,0},{16,8},{24,16},{32,24},{40,32},{48,40},{56,48},{64,5... | collective-permute-start | bytes 786440 | tf_op jit(solution)/shard_map/ppermute | solution.py:32
  15.3 2.4 %collective-permute-start.3 = (bf16[128,1024]{1,0:T(8,128)(2,1)}, bf16[128,1024]{1,0:T(8,128)(2,1)S(1)}, u32[]{:S(2)}, u32[]{:S(2)}) collective-permute-start(bf16[128,1024]{1,0:T(8,128)(2,1)} %teacher.5), channel_id=1, source_target_pairs={{0,496},{8,504},{16,0},{24,8},{32,16},{40,24},{48,32},{56,40},{64,... | collective-permute-start | bytes 786440 | tf_op jit(solution)/shard_map/ppermute | solution.py:32
  17.8 2.0 %collective-permute-start = (bf16[128,768]{1,0:T(8,128)(2,1)}, bf16[128,768]{1,0:T(8,128)(2,1)S(1)}, u32[]{:S(2)}, u32[]{:S(2)}) collective-permute-start(bf16[128,768]{1,0:T(8,128)(2,1)} %own.3), channel_id=1, source_target_pairs={{0,504},{8,0},{16,8},{24,16},{32,24},{40,32},{48,40},{56,48},{64,5... | collective-permute-start | bytes 589832 | tf_op jit(solution)/shard_map/ppermute | solution.py:32
  19.8 7.8 %collective-permute-start.1 = (bf16[128,768]{1,0:T(8,128)(2,1)}, bf16[128,768]{1,0:T(8,128)(2,1)S(1)}, u32[]{:S(2)}, u32[]{:S(2)}) collective-permute-start(bf16[128,768]{1,0:T(8,128)(2,1)} %own.3), channel_id=1, source_target_pairs={{0,496},{8,504},{16,0},{24,8},{32,16},{40,24},{48,32},{56,40},{64,... | collective-permute-start | bytes 589832 | tf_op jit(solution)/shard_map/ppermute | solution.py:32
  27.6 1.0 constant_dynamic-slice_fusion.weight_rows
  28.6 1.4 copy-done
  30.0 0.9 copy-done.2
  31.9 2.2 %own.2 = (bf16[8,96,256]{2,1,0:T(8,128)(2,1)}, bf16[128,1024]{1,0:T(8,128)(2,1)S(1)}, f32[128,256]{1,0:T(8,128)S(1)}, f32[8,128]{1,0:T(8,128)S(1)}) custom-call(bf16[128,768]{1,0:T(8,128)(2,1)S(1)} %copy-done.4, bf16[768,1024]{1,0:T(8,128)(2,1)S(1)} %copy-done, bf16[128,1024]{1,0:T(8,128)(2,1)S(1)} %constant_dynamic-slice_fusion.weight_rows, ...), custom_call_target="tpu_custom_call" | custom-call | flops 600000000 | bytes 3000000 | tf_op jit(solution)/shard_map/own/pallas_call | solution.py:240
  34.1 3.3 %collective-permute-done.near_student.near = bf16[128,768]{1,0:T(8,128)(2,1)S(1)} collective-permute-done((bf16[128,768]{1,0:T(8,128)(2,1)}, bf16[128,768]{1,0:T(8,128)(2,1)S(1)}, u32[]{:S(2)}, u32[]{:S(2)}) %collective-permute-start) | collective-permute-done | bytes 196640 | tf_op jit(solution)/shard_map/ppermute | solution.py:32
  37.4 1.8 tile.1
  39.2 3.6 %all-to-all-start = ((f32[8,16,896]{2,1,0:T(8,128)}), f32[8,16,896]{2,1,0:T(8,128)S(1)}, u32[]{:S(2)}, u32[]{:S(2)}) async-start(f32[8,16,896]{2,1,0:T(8,128)} %get-tuple-element.23), calls=%async_computation | async-start | bytes 917504 | tf_op jit(solution)/shard_map/all_to_all | solution.py:268
  44.3 12.3 %all-to-all-done.parts = f32[8,16,896]{2,1,0:T(8,128)S(1)} async-done(((f32[8,16,896]{2,1,0:T(8,128)}), f32[8,16,896]{2,1,0:T(8,128)S(1)}, u32[]{:S(2)}, u32[]{:S(2)}) %all-to-all-start) | async-done | bytes 458784 | tf_op jit(solution)/shard_map/all_to_all | solution.py:268
  57.4 2.4 %band.1 = (bf16[8,16,512]{2,1,0:T(8,128)(2,1)}, f32[8,128]{1,0:T(8,128)}) custom-call(f32[8,16,896]{2,1,0:T(8,128)} %copy-done.8, s32[8,384]{1,0:T(8,128)} %add_add_fusion.ids), custom_call_target="tpu_custom_call" | custom-call | flops 100000000 | bytes 3000000 | tf_op jit(solution)/shard_map/band/pallas_call | solution.py:280
  59.9 10.1 %all_to_all.20.gathered = bf16[8,16,512]{2,1,0:T(8,128)(2,1)S(1)} all-to-all(bf16[8,16,512]{2,1,0:T(8,128)(2,1)} %get-tuple-element.24), channel_id=1, replica_groups=mesh['z'=4,'x'=8,'yh'=2,'feat'=8] {'feat'}, dimensions={0} | all-to-all | bytes 262144 | tf_op jit(solution)/shard_map/all_to_all | solution.py:289
  70.7 3.1 %grad.1 = bf16[768,1024]{1,0:T(8,128)(2,1)} custom-call(bf16[8,16,512]{2,1,0:T(8,128)(2,1)S(1)} %all_to_all.20.gathered, f32[8,128]{1,0:T(8,128)S(1)} %copy-done.6, bf16[128,1024]{1,0:T(8,128)(2,1)S(1)} %get-tuple-element.19.proj_own.own, bf16[128,1024]{1,0:T(8,128)(2,1)S(1)} %get-tuple-element.26.near, bf16[128,1024]{1,0:T(8,128)(2,1)S(1)} %get-tuple-element.27.far, ...), custom_call_target="tpu_custom_call" | custom-call | flops 1000000000 | bytes 3000000 | tf_op jit(solution)/shard_map/grad/pallas_call | solution.py:291
  73.7 17.3 %reduce-scatter.2.cloned.1.call-done = bf16[1,96,256]{2,1,0:T(8,128)(2,1)} async-done(((bf16[8,96,256]{2,1,0:T(8,128)(2,1)}), bf16[1,96,256]{2,1,0:T(8,128)(2,1)}) %reduce-scatter.2.cloned.1.call-update) | async-done | bytes 49168 | tf_op jit(solution)/shard_map/reduce_scatter | solution.py:269
  91.0 5.8 %all-to-all-start.2 = ((bf16[8,96,1024]{2,1,0:T(8,128)(2,1)}), bf16[8,96,1024]{2,1,0:T(8,128)(2,1)S(1)}, u32[]{:S(2)}, u32[]{:S(2)}) async-start(bf16[8,96,1024]{2,1,0:T(8,128)(2,1)} %bitcast.1), calls=%async_computation.3 | async-start | bytes 3145728 | tf_op jit(solution)/shard_map/all_to_all | solution.py:303
  97.0 15.6 %all-to-all-done.2.received = bf16[8,96,1024]{2,1,0:T(8,128)(2,1)S(1)} async-done(((bf16[8,96,1024]{2,1,0:T(8,128)(2,1)}), bf16[8,96,1024]{2,1,0:T(8,128)(2,1)S(1)}, u32[]{:S(2)}, u32[]{:S(2)}) %all-to-all-start.2) | async-done | bytes 1572896 | tf_op jit(solution)/shard_map/all_to_all | solution.py:303
  112.6 3.6 %add.44 = bf16[128,1024]{1,0:T(8,128)(2,1)} custom-call(bf16[128,96]{1,0:T(8,128)(2,1)S(1)} %fusion.1.select, bf16[8,96,1024]{2,1,0:T(8,128)(2,1)S(1)} %all-to-all-done.2.received), custom_call_target="tpu_custom_call" | custom-call | flops 100000000 | bytes 3000000 | tf_op jit(solution)/shard_map/add/pallas_call | solution.py:307
  116.2 11.1 %all-to-all-start.3 = ((bf16[8,16,1024]{2,1,0:T(8,128)(2,1)}), bf16[8,16,1024]{2,1,0:T(8,128)(2,1)S(1)}, u32[]{:S(2)}, u32[]{:S(2)}) async-start(bf16[8,16,1024]{2,1,0:T(8,128)(2,1)} %bitcast.2), calls=%async_computation.4 | async-start | bytes 524288 | tf_op jit(solution)/shard_map/all_to_all | solution.py:319
  127.4 28.3 %all-gather = bf16[768,128]{1,0:T(8,128)(2,1)S(1)} all-gather(bf16[96,128]{1,0:T(8,128)(2,1)S(1)} %get-tuple-element.35), channel_id=2, replica_groups=mesh['z'=4,'x'=8,'yh'=2,'feat'=8] {'x'}, dimensions={0}, use_global_device_ids=true | all-gather | bytes 221184 | tf_op jit(solution)/shard_map/all_gather | solution.py:322
  156.5 8.9 %collective-permute-start.4 = (f32[96,128]{1,0:T(8,128)S(1)}, f32[96,128]{1,0:T(8,128)S(1)}, u32[]{:S(2)}, u32[]{:S(2)}) collective-permute-start(f32[96,128]{1,0:T(8,128)S(1)} %get-tuple-element.32), channel_id=1, source_target_pairs={{0,8},{8,16},{16,24},{24,32},{32,40},{40,48},{48,56},{56,64},{64,7... | collective-permute-start | bytes 147464 | tf_op jit(solution)/shard_map/ppermute | solution.py:32
  165.3 4.3 %collective-permute-start.5 = (f32[96,128]{1,0:T(8,128)S(1)}, f32[96,128]{1,0:T(8,128)S(1)}, u32[]{:S(2)}, u32[]{:S(2)}) collective-permute-start(f32[96,128]{1,0:T(8,128)S(1)} %get-tuple-element.33), channel_id=1, source_target_pairs={{0,16},{8,24},{16,32},{24,40},{32,48},{40,56},{48,64},{56,72},{64,... | collective-permute-start | bytes 147464 | tf_op jit(solution)/shard_map/ppermute | solution.py:32
  169.7 1.7 collective-permute-done.5
  (46 shorter events, 6.3 us)
Async XLA Ops:
  7.2 30.2 %copy-start.3 = (bf16[128,1024]{1,0:T(8,128)(2,1)S(1)}, bf16[128,1024]{1,0:T(8,128)(2,1)}, u32[]{:S(2)}) copy-start(bf16[128,1024]{1,0:T(8,128)(2,1)} %teacher.5) | copy-start | bytes 786436
  7.2 30.2 %collective-permute-start.2 = (bf16[128,1024]{1,0:T(8,128)(2,1)}, bf16[128,1024]{1,0:T(8,128)(2,1)S(1)}, u32[]{:S(2)}, u32[]{:S(2)}) collective-permute-start(bf16[128,1024]{1,0:T(8,128)(2,1)} %teacher.5), channel_id=1, source_target_pairs={{0,504},{8,0},{16,8},{24,16},{32,24},{40,32},{48,40},{56,48},{64,5... | collective-permute-start | bytes 786440 | tf_op jit(solution)/shard_map/ppermute | solution.py:32
  15.3 22.0 %collective-permute-start.3 = (bf16[128,1024]{1,0:T(8,128)(2,1)}, bf16[128,1024]{1,0:T(8,128)(2,1)S(1)}, u32[]{:S(2)}, u32[]{:S(2)}) collective-permute-start(bf16[128,1024]{1,0:T(8,128)(2,1)} %teacher.5), channel_id=1, source_target_pairs={{0,496},{8,504},{16,0},{24,8},{32,16},{40,24},{48,32},{56,40},{64,... | collective-permute-start | bytes 786440 | tf_op jit(solution)/shard_map/ppermute | solution.py:32
  17.8 19.6 %collective-permute-start = (bf16[128,768]{1,0:T(8,128)(2,1)}, bf16[128,768]{1,0:T(8,128)(2,1)S(1)}, u32[]{:S(2)}, u32[]{:S(2)}) collective-permute-start(bf16[128,768]{1,0:T(8,128)(2,1)} %own.3), channel_id=1, source_target_pairs={{0,504},{8,0},{16,8},{24,16},{32,24},{40,32},{48,40},{56,48},{64,5... | collective-permute-start | bytes 589832 | tf_op jit(solution)/shard_map/ppermute | solution.py:32
  19.8 17.6 %collective-permute-start.1 = (bf16[128,768]{1,0:T(8,128)(2,1)}, bf16[128,768]{1,0:T(8,128)(2,1)S(1)}, u32[]{:S(2)}, u32[]{:S(2)}) collective-permute-start(bf16[128,768]{1,0:T(8,128)(2,1)} %own.3), channel_id=1, source_target_pairs={{0,496},{8,504},{16,0},{24,8},{32,16},{40,24},{48,32},{56,40},{64,... | collective-permute-start | bytes 589832 | tf_op jit(solution)/shard_map/ppermute | solution.py:32
  28.6 1.4 copy-start
  30.0 0.9 copy-start.2
  31.0 0.9 copy-start.4
  31.9 5.5 %copy-start.1 = (bf16[768,1024]{1,0:T(8,128)(2,1)S(1)}, bf16[768,1024]{1,0:T(8,128)(2,1)}, u32[]{:S(2)}) copy-start(bf16[768,1024]{1,0:T(8,128)(2,1)} %weight.3) | copy-start | bytes 4718596
  37.4 6.2 %copy-start.11 = (s32[384]{0:T(512)S(1)}, s32[384]{0:T(512)}, u32[]{:S(2)}) copy-start(s32[384]{0:T(512)} %param.8) | copy-start | bytes 4612
  37.4 6.3 %copy-start.10 = (s32[2,384]{1,0:T(2,128)S(1)}, s32[2,384]{1,0:T(2,128)}, u32[]{:S(2)}) copy-start(s32[2,384]{1,0:T(2,128)} %param.9) | copy-start | bytes 9220
  39.2 30.8 %copy-start.5 = (bf16[128,768]{1,0:T(8,128)(2,1)S(1)}, bf16[128,768]{1,0:T(8,128)(2,1)}, u32[]{:S(2)}) copy-start(bf16[128,768]{1,0:T(8,128)(2,1)} %own.3) | copy-start | bytes 589828
  39.2 17.5 %all-to-all-start = ((f32[8,16,896]{2,1,0:T(8,128)}), f32[8,16,896]{2,1,0:T(8,128)S(1)}, u32[]{:S(2)}, u32[]{:S(2)}) async-start(f32[8,16,896]{2,1,0:T(8,128)} %get-tuple-element.23), calls=%async_computation | async-start | bytes 917504 | tf_op jit(solution)/shard_map/all_to_all | solution.py:268
  42.8 48.2 %reduce-scatter.2.cloned.1.call-start = ((), (), s32[]{:S(2)}) async-start(), calls=%async_computation.5 | async-start | bytes 442368 | tf_op jit(solution)/shard_map/reduce_scatter | solution.py:269
  56.7 0.8 copy-start.8
  70.0 0.7 copy-start.6
  91.0 21.7 %all-to-all-start.2 = ((bf16[8,96,1024]{2,1,0:T(8,128)(2,1)}), bf16[8,96,1024]{2,1,0:T(8,128)(2,1)S(1)}, u32[]{:S(2)}, u32[]{:S(2)}) async-start(bf16[8,96,1024]{2,1,0:T(8,128)(2,1)} %bitcast.1), calls=%async_computation.3 | async-start | bytes 3145728 | tf_op jit(solution)/shard_map/all_to_all | solution.py:303
  96.8 30.6 %copy-start.9 = (bf16[1,96,256]{2,1,0:T(8,128)(2,1)S(1)}, bf16[1,96,256]{2,1,0:T(8,128)(2,1)}, u32[]{:S(2)}) copy-start(bf16[1,96,256]{2,1,0:T(8,128)(2,1)} %reduce-scatter.2.cloned.1.call-done) | copy-start | bytes 147460
  96.8 58.9 %copy-start.7 = (f32[8,128]{1,0:T(8,128)S(1)}, f32[8,128]{1,0:T(8,128)}, u32[]{:S(2)}) copy-start(f32[8,128]{1,0:T(8,128)} %get-tuple-element.25.norms) | copy-start | bytes 12292
  116.2 55.8 %all-to-all-start.3 = ((bf16[8,16,1024]{2,1,0:T(8,128)(2,1)}), bf16[8,16,1024]{2,1,0:T(8,128)(2,1)S(1)}, u32[]{:S(2)}, u32[]{:S(2)}) async-start(bf16[8,16,1024]{2,1,0:T(8,128)(2,1)} %bitcast.2), calls=%async_computation.4 | async-start | bytes 524288 | tf_op jit(solution)/shard_map/all_to_all | solution.py:319
  156.5 13.2 %collective-permute-start.4 = (f32[96,128]{1,0:T(8,128)S(1)}, f32[96,128]{1,0:T(8,128)S(1)}, u32[]{:S(2)}, u32[]{:S(2)}) collective-permute-start(f32[96,128]{1,0:T(8,128)S(1)} %get-tuple-element.32), channel_id=1, source_target_pairs={{0,8},{8,16},{16,24},{24,32},{32,40},{40,48},{48,56},{56,64},{64,7... | collective-permute-start | bytes 147464 | tf_op jit(solution)/shard_map/ppermute | solution.py:32
  165.3 6.1 %collective-permute-start.5 = (f32[96,128]{1,0:T(8,128)S(1)}, f32[96,128]{1,0:T(8,128)S(1)}, u32[]{:S(2)}, u32[]{:S(2)}) collective-permute-start(f32[96,128]{1,0:T(8,128)S(1)} %get-tuple-element.33), channel_id=1, source_target_pairs={{0,16},{8,24},{16,32},{24,40},{32,48},{40,56},{48,64},{56,72},{64,... | collective-permute-start | bytes 147464 | tf_op jit(solution)/shard_map/ppermute | solution.py:32
Sparse Core Ops, SparseCore 0:
  46.4 44.5 reduce-scatter.1

commit v7 on v6

--- a/solution.py
+++ b/solution.py
@@ -55,8 +55,7 @@
     return jnp.sum(jnp.where(diagonal(values.shape[1]), values, 0.0), 1, keepdims=True)
 
 
-def own_kernel(student, weight, weight_rows, teacher, through, proj_own, tiles, sums):
-    peers, height, _ = through.shape
+def own_kernel(student, weight, teacher, proj_own, tiles, sums):
     texts = student.shape[0]
     own = dot(student[...], weight[...], (1, 0))
     proj_own[...] = own.astype(bf16)
@@ -67,9 +66,6 @@
         [row_sums(own * own), row_sums(wide * wide), row_sums(own * wide), jnp.zeros((5, texts), f32)],
         0,
     )
-    for t, other in enumerate((weight_rows, teacher)):
-        product = dot(weight[...], other[...], (1, 1)).astype(bf16)
-        through[:, :, t * LANES : (t + 1) * LANES] = product.reshape(peers, height, LANES)
 
 
 def tile_kernel(
@@ -172,42 +168,21 @@
 
 
 def grad_kernel(
-    sizes, gathered, norms, own, near, far, teacher, student, near_student, far_student, grad_w
+    sizes, gathered, norms, own, near, far, teacher, student, near_student, far_student,
+    rows_grad, grad_w,
 ):
     z_size, x_size, _ = sizes
+    texts = own.shape[0]
     terms, both = spread(gathered, norms, (own, near, far))
     terms[0] = terms[0] - upright(both) * teacher[...].astype(f32)
     total = 0.0
-    for term, rows in zip(terms, (student, near_student, far_student)):
-        total = total + dot(rows[...], (LOSS_SCALE * term).astype(bf16), (0, 0))
+    for s, rows in enumerate((student, near_student, far_student)):
+        piece = slice(s * texts, (s + 1) * texts)
+        rows_grad[piece, :] = (LOSS_SCALE * terms[s]).astype(bf16)
+        total = total + dot(rows[...], rows_grad[piece, :], (0, 0))
     step = total.shape[0] // (z_size * x_size)
     starts = [(z * x_size + x) * step for x in range(x_size) for z in range(z_size)]
     grad_w[...] = jnp.concatenate([total[r : r + step] for r in starts], 0).astype(bf16)
-
-
-def student_kernel(gathered, norms, own, near, far, gram, teacher_back, out_own, out_near, out_far):
-    terms, both = spread(gathered, norms, (own, near, far))
-    groups = own.shape[1] // LANES
-    table = jnp.concatenate([gram[g] for g in range(groups)], 1)
-    for s, out in enumerate((out_own, out_near, out_far)):
-        product = dot(table, terms[s].astype(bf16), (1, 1))
-        if s == 0:
-            product = product - both * teacher_back[...]
-        out[...] = LOSS_SCALE * product
-
-
-def add_kernel(select, received, out, held, sems):
-    peers = received.shape[0]
-    copies = [
-        pltpu.make_async_copy(received.at[p], held.at[p], sems.at[p]) for p in range(peers)
-    ]
-    for copy in copies:
-        copy.start()
-    total = 0.0
-    for peer, copy in enumerate(copies):
-        copy.wait()
-        total = total + dot(select[...], held[peer], (1, 0))
-    out[...] = total.astype(bf16)
 
 
 def shards(student, proj_weight, teacher, anchors, pairs, *, sizes):
@@ -233,22 +208,17 @@
     params = pltpu.CompilerParams(vmem_limit_bytes=16 * 2**20)
     rows_type = jax.ShapeDtypeStruct((texts, width), bf16)
 
-    groups = features // LANES
-    height = features // n_feat
-    row_start = jnp.minimum(lax.axis_index("x"), groups - 1) * LANES
-    weight_rows = lax.dynamic_slice(proj_weight, (row_start, 0), (LANES, width))
-    through, proj_own, own_tiles, own_sums = pl.pallas_call(
+    proj_own, own_tiles, own_sums = pl.pallas_call(
         own_kernel,
         out_shape=(
-            jax.ShapeDtypeStruct((n_feat, height, 2 * LANES), bf16),
             rows_type,
             jax.ShapeDtypeStruct((texts, 2 * texts), f32),
             jax.ShapeDtypeStruct((8, texts), f32),
         ),
         compiler_params=params,
-        cost_estimate=cost(6 * 10**8),
+        cost_estimate=cost(3 * 10**8),
         name="own",
-    )(student, proj_weight, weight_rows, teacher)
+    )(student, proj_weight, teacher)
 
     parts, proj_near, proj_far = pl.pallas_call(
         tile_kernel,
@@ -264,9 +234,7 @@
         proj_own, proj_weight, teacher, own_tiles, own_sums,
         near_student, far_student, near_teacher, far_teacher,
     )
-    through, parts = lax.optimization_barrier((through, parts))
     parts = lax.all_to_all(parts, "feat", 0, 0)
-    through = lax.psum_scatter(through, "feat", scatter_dimension=0, tiled=False)
 
     ids = jnp.concatenate(
         [
@@ -288,48 +256,56 @@
     )(parts, ids)
     gathered = lax.all_to_all(tiles, "feat", 0, 0)
 
-    grad_w = pl.pallas_call(
+    rows_grad, grad_w = pl.pallas_call(
         functools.partial(grad_kernel, sizes),
-        out_shape=jax.ShapeDtypeStruct((features, width), bf16),
+        out_shape=(
+            jax.ShapeDtypeStruct((band, width), bf16),
+            jax.ShapeDtypeStruct((features, width), bf16),
+        ),
         compiler_params=params,
         cost_estimate=cost(10**9),
         name="grad",
     )(
         gathered, norms, proj_own, proj_near, proj_far, teacher, student, near_student, far_student
     )
-    grad_w, through = lax.optimization_barrier((grad_w, through))
 
     zy = z_size * yh_size
-    grad_w = lax.all_to_all(grad_w.reshape(x_size, features // x_size, width), "x", 0, 0)
-    row_out = lax.broadcasted_iota(jnp.int32, (zy * padded, zy * share), 0)
-    row_in = lax.broadcasted_iota(jnp.int32, row_out.shape, 1)
+    grad_w = lax.all_to_all(
+        grad_w.reshape(x_size, features // x_size, width), "x", 0, 0
+    ).reshape(features, width)
+    row_out = lax.broadcasted_iota(jnp.int32, (zy * padded, features), 0)
+    row_in = lax.broadcasted_iota(jnp.int32, row_out.shape, 1) % (zy * share)
     select = (row_out // padded == row_in // share) & (row_out % padded == row_in % share)
-    grad_w = pl.pallas_call(
-        add_kernel,
-        in_specs=[pl.BlockSpec(memory_space=pltpu.VMEM), pl.BlockSpec(memory_space=pl.ANY)],
-        out_shape=jax.ShapeDtypeStruct((zy * padded, width), bf16),
-        scratch_shapes=[
-            pltpu.VMEM((x_size, features // x_size, width), bf16),
-            pltpu.SemaphoreType.DMA((x_size,)),
-        ],
-        compiler_params=params,
-        cost_estimate=cost(10**8),
-        name="add",
-    )(lax.optimization_barrier(select.astype(bf16)), grad_w)
+    select = lax.optimization_barrier(select.astype(bf16))
+    grad_w = dot(select, grad_w, (1, 0)).astype(bf16)
     grad_w = lax.all_to_all(grad_w.reshape(zy, padded, width), ("z", "yh"), 0, 0)
     grad_w = jnp.sum(grad_w.astype(f32), 0)[:share]
 
-    gram = lax.all_gather(through[:, :LANES], "x")
-    teacher_back = through[:, LANES:].astype(f32)
-    columns_type = jax.ShapeDtypeStruct((height, texts), f32)
-    own, near, far = pl.pallas_call(
-        student_kernel,
-        out_shape=(columns_type,) * STEPS,
-        compiler_params=params,
-        cost_estimate=cost(4 * 10**8),
-        name="student",
-    )(gathered, norms, student, near_student, far_student, gram, teacher_back)
-    grad_student = own + passed_along(near, 1) + passed_along(far, 2)
+    height = features // n_feat
+    halves = proj_weight.reshape(n_feat // 2, 2, height, width)
+
+    def half(array, which, axis):
+        return lax.dynamic_index_in_dim(array, which, axis, keepdims=False)
+
+    def half_back(which):
+        weight = half(halves, which, 1).reshape(features // 2, width)
+        return dot(weight, rows_grad, (1, 1)).reshape(n_feat // 2, height, band)
+
+    def swapped(array, bit):
+        perm = [(i, i ^ (1 << bit)) for i in range(n_feat)]
+        return lax.ppermute(array.astype(bf16), "feat", perm).astype(f32)
+
+    mine = feat & 1
+    back = swapped(half_back(1 - mine), 0)
+    back = half_back(mine) + back
+    for bit in range(1, n_feat.bit_length() - 1):
+        back = back.reshape(-1, 2, height, band)
+        mine = (feat >> bit) & 1
+        back = half(back, mine, 1) + swapped(half(back, 1 - mine, 1), bit)
+    back = back.reshape(height, band)
+    grad_student = back[:, :texts]
+    for s in range(1, STEPS):
+        grad_student = grad_student + passed_along(back[:, s * texts : (s + 1) * texts], s)
     return (grad_w, grad_student.T)
 
 

time: 183 us -> 135 us (0.74)
  the two profiles are of different devices: /device:TPU:6 before, /device:TPU:8 now
where the time goes in v7:
time: 135 us; the launch traced here: 134 us
  starting transfers between devices  62.7 us (46%)
  waiting for transfers between devices  36.3 us (27%)
  blocking collectives  11.8 us (9%)
  local copies, waits for them, and re-layouts  8.23 us (6%)
  Pallas kernels  7.81 us (6%)
  matrix products  3.7 us (3%)
  other arithmetic  2.23 us (2%)
    ppermute x6, starting transfers between devices, passed_along(): lax.ppermute(array, DP, [(i, (i + by) % peers) for i in range(peers)])  36.9 us
    ppermute x6, waiting for transfers between devices, passed_along(): lax.ppermute(array, DP, [(i, (i + by) % peers) for i in range(peers)])  15.1 us
    all_to_all x1, blocking collectives, shards(): gathered = lax.all_to_all(tiles, 'feat', 0, 0)  11.8 us
    ppermute x3, waiting for transfers between devices, swapped(): return lax.ppermute(array.astype(bf16), 'feat', perm).astype(f32)  10.3 us
    all_to_all x1, waiting for transfers between devices, shards(): parts = lax.all_to_all(parts, 'feat', 0, 0)  10.3 us
    all_to_all x1, starting transfers between devices, shards(): lax.all_to_all(grad_w.reshape(zy, padded, width), ('z', 'yh'), 0, 0)  10.1 us
    unnamed x28, local copies, waits for them, and re-layouts  8.1 us
    ppermute x3, starting transfers between devices, swapped(): return lax.ppermute(array.astype(bf16), 'feat', perm).astype(f32)  7.88 us
  transfers between devices with their start and end apart: 12, of which 8 were waited for; matrix products, arithmetic and copies ran while one was open for 2% of the time, Pallas kernels for 0%

profile of v7, /device:TPU:8, one launch (start us, length us, event | category | flops | bytes accessed | tf_op | source)
XLA Modules:
  0.0 133.7 jit_solution(10342354714673991575)
XLA Ops:
  0.6 17.5 %collective-permute-start.2 = (bf16[128,1024]{1,0:T(8,128)(2,1)}, bf16[128,1024]{1,0:T(8,128)(2,1)S(1)}, u32[]{:S(2)}, u32[]{:S(2)}) collective-permute-start(bf16[128,1024]{1,0:T(8,128)(2,1)} %teacher.5), channel_id=1, source_target_pairs={{0,504},{8,0},{16,8},{24,16},{32,24},{40,32},{48,40},{56,48},{64,5... | collective-permute-start | bytes 786440 | tf_op jit(solution)/shard_map/ppermute | solution.py:32
  18.1 2.7 %collective-permute-start.3 = (bf16[128,1024]{1,0:T(8,128)(2,1)}, bf16[128,1024]{1,0:T(8,128)(2,1)S(1)}, u32[]{:S(2)}, u32[]{:S(2)}) collective-permute-start(bf16[128,1024]{1,0:T(8,128)(2,1)} %teacher.5), channel_id=1, source_target_pairs={{0,496},{8,504},{16,0},{24,8},{32,16},{40,24},{48,32},{56,40},{64,... | collective-permute-start | bytes 786440 | tf_op jit(solution)/shard_map/ppermute | solution.py:32
  20.9 2.9 %collective-permute-start = (bf16[128,768]{1,0:T(8,128)(2,1)}, bf16[128,768]{1,0:T(8,128)(2,1)S(1)}, u32[]{:S(2)}, u32[]{:S(2)}) collective-permute-start(bf16[128,768]{1,0:T(8,128)(2,1)} %student.3), channel_id=1, source_target_pairs={{0,504},{8,0},{16,8},{24,16},{32,24},{40,32},{48,40},{56,48},{64,5... | collective-permute-start | bytes 589832 | tf_op jit(solution)/shard_map/ppermute | solution.py:32
  23.8 2.4 %collective-permute-start.1 = (bf16[128,768]{1,0:T(8,128)(2,1)}, bf16[128,768]{1,0:T(8,128)(2,1)S(1)}, u32[]{:S(2)}, u32[]{:S(2)}) collective-permute-start(bf16[128,768]{1,0:T(8,128)(2,1)} %student.3), channel_id=1, source_target_pairs={{0,496},{8,504},{16,0},{24,8},{32,16},{40,24},{48,32},{56,40},{64,... | collective-permute-start | bytes 589832 | tf_op jit(solution)/shard_map/ppermute | solution.py:32
  26.3 1.4 %copy-done = bf16[768,1024]{1,0:T(8,128)(2,1)S(1)} copy-done((bf16[768,1024]{1,0:T(8,128)(2,1)S(1)}, bf16[768,1024]{1,0:T(8,128)(2,1)}, u32[]{:S(2)}) %copy-start) | copy-done | bytes 1572888
  30.2 7.9 %collective-permute-done.near_student = bf16[128,768]{1,0:T(8,128)(2,1)S(1)} collective-permute-done((bf16[128,768]{1,0:T(8,128)(2,1)}, bf16[128,768]{1,0:T(8,128)(2,1)S(1)}, u32[]{:S(2)}, u32[]{:S(2)}) %collective-permute-start) | collective-permute-done | bytes 196640 | tf_op jit(solution)/shard_map/ppermute | solution.py:32
  38.1 1.8 %tile.1 = (f32[8,16,896]{2,1,0:T(8,128)}, bf16[128,1024]{1,0:T(8,128)(2,1)S(1)}, bf16[128,1024]{1,0:T(8,128)(2,1)S(1)}) custom-call(bf16[128,1024]{1,0:T(8,128)(2,1)S(1)} %get-tuple-element.12.proj_own.own, bf16[768,1024]{1,0:T(8,128)(2,1)S(1)} %copy-done.1, bf16[128,1024]{1,0:T(8,128)(2,1)S(1)} %copy-done.3, f32[128,256]{1,0:T(8,128)S(1)} %get-tuple-element.13.tiles, ...), custom_call_target="tpu_custom_call" | custom-call | flops 600000000 | bytes 3000000 | tf_op jit(solution)/shard_map/tile/pallas_call | solution.py:223
  41.3 3.6 %all-to-all-start = ((f32[8,16,896]{2,1,0:T(8,128)}), f32[8,16,896]{2,1,0:T(8,128)S(1)}, u32[]{:S(2)}, u32[]{:S(2)}) async-start(f32[8,16,896]{2,1,0:T(8,128)} %get-tuple-element.15), calls=%async_computation | async-start | bytes 917504 | tf_op jit(solution)/shard_map/all_to_all | solution.py:237
  45.7 10.3 %all-to-all-done.parts = f32[8,16,896]{2,1,0:T(8,128)S(1)} async-done(((f32[8,16,896]{2,1,0:T(8,128)}), f32[8,16,896]{2,1,0:T(8,128)S(1)}, u32[]{:S(2)}, u32[]{:S(2)}) %all-to-all-start) | async-done | bytes 458784 | tf_op jit(solution)/shard_map/all_to_all | solution.py:237
  56.7 2.4 %band.1 = (bf16[8,16,512]{2,1,0:T(8,128)(2,1)}, f32[8,128]{1,0:T(8,128)}) custom-call(f32[8,16,896]{2,1,0:T(8,128)} %copy-done.11, s32[8,384]{1,0:T(8,128)} %add_add_fusion.ids), custom_call_target="tpu_custom_call" | custom-call | flops 100000000 | bytes 3000000 | tf_op jit(solution)/shard_map/band/pallas_call | solution.py:248
  59.1 11.8 %all_to_all.20.gathered = bf16[8,16,512]{2,1,0:T(8,128)(2,1)S(1)} all-to-all(bf16[8,16,512]{2,1,0:T(8,128)(2,1)} %get-tuple-element.16), channel_id=1, replica_groups=mesh['z'=4,'x'=8,'yh'=2,'feat'=8] {'feat'}, dimensions={0} | all-to-all | bytes 262144 | tf_op jit(solution)/shard_map/all_to_all | solution.py:257
  73.5 3.0 %grad.1 = (bf16[384,1024]{1,0:T(8,128)(2,1)S(1)}, bf16[768,1024]{1,0:T(8,128)(2,1)}) custom-call(bf16[8,16,512]{2,1,0:T(8,128)(2,1)S(1)} %all_to_all.20.gathered, f32[8,128]{1,0:T(8,128)S(1)} %copy-done.10, bf16[128,1024]{1,0:T(8,128)(2,1)S(1)} %get-tuple-element.12.proj_own.own, bf16[128,1024]{1,0:T(8,128)(2,1)S(1)} %copy-done.7, ...), custom_call_target="tpu_custom_call" | custom-call | flops 1000000000 | bytes 3000000 | tf_op jit(solution)/shard_map/grad/pallas_call | solution.py:259
  76.6 4.3 %all-to-all-start.2 = ((bf16[8,96,1024]{2,1,0:T(8,128)(2,1)}), bf16[8,96,1024]{2,1,0:T(8,128)(2,1)}, u32[]{:S(2)}, u32[]{:S(2)}) async-start(bf16[8,96,1024]{2,1,0:T(8,128)(2,1)} %bitcast), calls=%async_computation.2 | async-start | bytes 3145728 | tf_op jit(solution)/shard_map/all_to_all | solution.py:273
  81.5 1.9 %collective-permute-start.4 = (bf16[4,96,384]{2,1,0:T(8,128)(2,1)S(1)}, bf16[4,96,384]{2,1,0:T(8,128)(2,1)S(1)}, u32[]{:S(2)}, u32[]{:S(2)}) collective-permute-start(bf16[4,96,384]{2,1,0:T(8,128)(2,1)S(1)} %convolution_convert_fusion), channel_id=1, source_target_pairs={{0,1},{1,0},{2,3},{3,2},{4,5},{5,4},{6,7},{7,6},{8,9},{9,8},{10,11... | collective-permute-start | bytes 884744 | tf_op jit(solution)/shard_map/ppermute | solution.py:296
  83.4 1.5 %collective-permute-done.4 = bf16[4,96,384]{2,1,0:T(8,128)(2,1)S(1)} collective-permute-done((bf16[4,96,384]{2,1,0:T(8,128)(2,1)S(1)}, bf16[4,96,384]{2,1,0:T(8,128)(2,1)S(1)}, u32[]{:S(2)}, u32[]{:S(2)}) %collective-permute-start.4) | collective-permute-done | bytes 294944 | tf_op jit(solution)/shard_map/ppermute | solution.py:296
  85.6 3.0 %collective-permute-start.5 = (bf16[2,96,384]{2,1,0:T(8,128)(2,1)S(1)}, bf16[2,96,384]{2,1,0:T(8,128)(2,1)S(1)}, u32[]{:S(2)}, u32[]{:S(2)}) collective-permute-start(bf16[2,96,384]{2,1,0:T(8,128)(2,1)S(1)} %fusion.17), channel_id=1, source_target_pairs={{0,2},{1,3},{2,0},{3,1},{4,6},{5,7},{6,4},{7,5},{8,10},{9,11},{10,... | collective-permute-start | bytes 442376 | tf_op jit(solution)/shard_map/ppermute | solution.py:296
  88.6 4.7 %collective-permute-done.5 = bf16[2,96,384]{2,1,0:T(8,128)(2,1)S(1)} collective-permute-done((bf16[2,96,384]{2,1,0:T(8,128)(2,1)S(1)}, bf16[2,96,384]{2,1,0:T(8,128)(2,1)S(1)}, u32[]{:S(2)}, u32[]{:S(2)}) %collective-permute-start.5) | collective-permute-done | bytes 147488 | tf_op jit(solution)/shard_map/ppermute | solution.py:296
  93.4 2.9 %collective-permute-start.6 = (bf16[1,96,384]{2,1,0:T(8,128)(2,1)S(1)}, bf16[1,96,384]{2,1,0:T(8,128)(2,1)S(1)}, u32[]{:S(2)}, u32[]{:S(2)}) collective-permute-start(bf16[1,96,384]{2,1,0:T(8,128)(2,1)S(1)} %dynamic-slice_convert_fusion), channel_id=1, source_target_pairs={{0,4},{1,5},{2,6},{3,7},{4,0},{5,1},{6,2},{7,3},{8,12},{9,13},{10,... | collective-permute-start | bytes 221192 | tf_op jit(solution)/shard_map/ppermute | solution.py:296
  96.6 4.1 %collective-permute-done.6 = bf16[1,96,384]{2,1,0:T(8,128)(2,1)S(1)} collective-permute-done((bf16[1,96,384]{2,1,0:T(8,128)(2,1)S(1)}, bf16[1,96,384]{2,1,0:T(8,128)(2,1)S(1)}, u32[]{:S(2)}, u32[]{:S(2)}) %collective-permute-start.6) | collective-permute-done | bytes 73760 | tf_op jit(solution)/shard_map/ppermute | solution.py:296
  101.4 2.5 %convolution_convert_fusion.1 = bf16[128,1024]{1,0:T(8,128)(2,1)} fusion(bf16[128,768]{1,0:T(8,128)(2,1)S(1)} %fusion.16, bf16[768,1024]{1,0:T(8,128)(2,1)} %bitcast.1), kind=kOutput, calls=%fused_computation.2 | convolution fusion | flops 201457664 | bytes 2031616 | tf_op jit(solution)/shard_map/dot_general | solution.py:24
  103.9 10.1 %all-to-all-start.3 = ((bf16[8,16,1024]{2,1,0:T(8,128)(2,1)}), bf16[8,16,1024]{2,1,0:T(8,128)(2,1)S(1)}, u32[]{:S(2)}, u32[]{:S(2)}) async-start(bf16[8,16,1024]{2,1,0:T(8,128)(2,1)} %bitcast.2), calls=%async_computation.3 | async-start | bytes 524288 | tf_op jit(solution)/shard_map/all_to_all | solution.py:281
  114.0 7.8 %collective-permute-start.7 = (f32[96,128]{1,0:T(8,128)S(1)}, f32[96,128]{1,0:T(8,128)S(1)}, u32[]{:S(2)}, u32[]{:S(2)}) collective-permute-start(f32[96,128]{1,0:T(8,128)S(1)} %get-tuple-element.22), channel_id=1, source_target_pairs={{0,8},{8,16},{16,24},{24,32},{32,40},{40,48},{48,56},{56,64},{64,7... | collective-permute-start | bytes 147464 | tf_op jit(solution)/shard_map/ppermute | solution.py:32
  121.8 3.4 %collective-permute-start.8 = (f32[96,128]{1,0:T(8,128)S(1)}, f32[96,128]{1,0:T(8,128)S(1)}, u32[]{:S(2)}, u32[]{:S(2)}) collective-permute-start(f32[96,128]{1,0:T(8,128)S(1)} %get-tuple-element.23), channel_id=1, source_target_pairs={{0,16},{8,24},{16,32},{24,40},{32,48},{40,56},{48,64},{56,72},{64,... | collective-permute-start | bytes 147464 | tf_op jit(solution)/shard_map/ppermute | solution.py:32
  125.3 6.9 %collective-permute-done.7 = f32[96,128]{1,0:T(8,128)S(1)} collective-permute-done((f32[96,128]{1,0:T(8,128)S(1)}, f32[96,128]{1,0:T(8,128)S(1)}, u32[]{:S(2)}, u32[]{:S(2)}) %collective-permute-start.7) | collective-permute-done | bytes 49184 | tf_op jit(solution)/shard_map/ppermute | solution.py:32
  (55 shorter events, 11.8 us)
Async XLA Ops:
  0.6 37.4 %collective-permute-start.2 = (bf16[128,1024]{1,0:T(8,128)(2,1)}, bf16[128,1024]{1,0:T(8,128)(2,1)S(1)}, u32[]{:S(2)}, u32[]{:S(2)}) collective-permute-start(bf16[128,1024]{1,0:T(8,128)(2,1)} %teacher.5), channel_id=1, source_target_pairs={{0,504},{8,0},{16,8},{24,16},{32,24},{40,32},{48,40},{56,48},{64,5... | collective-permute-start | bytes 786440 | tf_op jit(solution)/shard_map/ppermute | solution.py:32
  18.1 19.9 %collective-permute-start.3 = (bf16[128,1024]{1,0:T(8,128)(2,1)}, bf16[128,1024]{1,0:T(8,128)(2,1)S(1)}, u32[]{:S(2)}, u32[]{:S(2)}) collective-permute-start(bf16[128,1024]{1,0:T(8,128)(2,1)} %teacher.5), channel_id=1, source_target_pairs={{0,496},{8,504},{16,0},{24,8},{32,16},{40,24},{48,32},{56,40},{64,... | collective-permute-start | bytes 786440 | tf_op jit(solution)/shard_map/ppermute | solution.py:32
  20.9 17.2 %collective-permute-start = (bf16[128,768]{1,0:T(8,128)(2,1)}, bf16[128,768]{1,0:T(8,128)(2,1)S(1)}, u32[]{:S(2)}, u32[]{:S(2)}) collective-permute-start(bf16[128,768]{1,0:T(8,128)(2,1)} %student.3), channel_id=1, source_target_pairs={{0,504},{8,0},{16,8},{24,16},{32,24},{40,32},{48,40},{56,48},{64,5... | collective-permute-start | bytes 589832 | tf_op jit(solution)/shard_map/ppermute | solution.py:32
  23.8 14.2 %collective-permute-start.1 = (bf16[128,768]{1,0:T(8,128)(2,1)}, bf16[128,768]{1,0:T(8,128)(2,1)S(1)}, u32[]{:S(2)}, u32[]{:S(2)}) collective-permute-start(bf16[128,768]{1,0:T(8,128)(2,1)} %student.3), channel_id=1, source_target_pairs={{0,496},{8,504},{16,0},{24,8},{32,16},{40,24},{48,32},{56,40},{64,... | collective-permute-start | bytes 589832 | tf_op jit(solution)/shard_map/ppermute | solution.py:32
  26.3 1.4 %copy-start = (bf16[768,1024]{1,0:T(8,128)(2,1)S(1)}, bf16[768,1024]{1,0:T(8,128)(2,1)}, u32[]{:S(2)}) copy-start(bf16[768,1024]{1,0:T(8,128)(2,1)} %weight.3) | copy-start | bytes 4718596
  27.7 0.9 copy-start.2
  28.6 0.9 copy-start.4
  29.6 8.5 %copy-start.1 = (bf16[768,1024]{1,0:T(8,128)(2,1)S(1)}, bf16[768,1024]{1,0:T(8,128)(2,1)}, u32[]{:S(2)}) copy-start(bf16[768,1024]{1,0:T(8,128)(2,1)} %weight.3) | copy-start | bytes 4718596
  29.6 8.5 %copy-start.3 = (bf16[128,1024]{1,0:T(8,128)(2,1)S(1)}, bf16[128,1024]{1,0:T(8,128)(2,1)}, u32[]{:S(2)}) copy-start(bf16[128,1024]{1,0:T(8,128)(2,1)} %teacher.5) | copy-start | bytes 786436
  38.1 6.8 %copy-start.13 = (s32[384]{0:T(512)S(1)}, s32[384]{0:T(512)}, u32[]{:S(2)}) copy-start(s32[384]{0:T(512)} %param.8) | copy-start | bytes 4612
  38.1 6.9 %copy-start.12 = (s32[2,384]{1,0:T(2,128)S(1)}, s32[2,384]{1,0:T(2,128)}, u32[]{:S(2)}) copy-start(s32[2,384]{1,0:T(2,128)} %param.9) | copy-start | bytes 9220
  39.9 0.7 copy-start.6
  41.3 29.7 %copy-start.5 = (bf16[128,768]{1,0:T(8,128)(2,1)S(1)}, bf16[128,768]{1,0:T(8,128)(2,1)}, u32[]{:S(2)}) copy-start(bf16[128,768]{1,0:T(8,128)(2,1)} %student.3) | copy-start | bytes 589828
  41.3 14.6 %all-to-all-start = ((f32[8,16,896]{2,1,0:T(8,128)}), f32[8,16,896]{2,1,0:T(8,128)S(1)}, u32[]{:S(2)}, u32[]{:S(2)}) async-start(f32[8,16,896]{2,1,0:T(8,128)} %get-tuple-element.15), calls=%async_computation | async-start | bytes 917504 | tf_op jit(solution)/shard_map/all_to_all | solution.py:237
  55.9 0.8 copy-start.11
  71.0 1.0 copy-start.7
  71.9 0.9 copy-start.9
  76.6 24.8 %all-to-all-start.2 = ((bf16[8,96,1024]{2,1,0:T(8,128)(2,1)}), bf16[8,96,1024]{2,1,0:T(8,128)(2,1)}, u32[]{:S(2)}, u32[]{:S(2)}) async-start(bf16[8,96,1024]{2,1,0:T(8,128)(2,1)} %bitcast), calls=%async_computation.2 | async-start | bytes 3145728 | tf_op jit(solution)/shard_map/all_to_all | solution.py:273
  81.5 3.5 %collective-permute-start.4 = (bf16[4,96,384]{2,1,0:T(8,128)(2,1)S(1)}, bf16[4,96,384]{2,1,0:T(8,128)(2,1)S(1)}, u32[]{:S(2)}, u32[]{:S(2)}) collective-permute-start(bf16[4,96,384]{2,1,0:T(8,128)(2,1)S(1)} %convolution_convert_fusion), channel_id=1, source_target_pairs={{0,1},{1,0},{2,3},{3,2},{4,5},{5,4},{6,7},{7,6},{8,9},{9,8},{10,11... | collective-permute-start | bytes 884744 | tf_op jit(solution)/shard_map/ppermute | solution.py:296
  85.6 7.8 %collective-permute-start.5 = (bf16[2,96,384]{2,1,0:T(8,128)(2,1)S(1)}, bf16[2,96,384]{2,1,0:T(8,128)(2,1)S(1)}, u32[]{:S(2)}, u32[]{:S(2)}) collective-permute-start(bf16[2,96,384]{2,1,0:T(8,128)(2,1)S(1)} %fusion.17), channel_id=1, source_target_pairs={{0,2},{1,3},{2,0},{3,1},{4,6},{5,7},{6,4},{7,5},{8,10},{9,11},{10,... | collective-permute-start | bytes 442376 | tf_op jit(solution)/shard_map/ppermute | solution.py:296
  93.4 7.2 %collective-permute-start.6 = (bf16[1,96,384]{2,1,0:T(8,128)(2,1)S(1)}, bf16[1,96,384]{2,1,0:T(8,128)(2,1)S(1)}, u32[]{:S(2)}, u32[]{:S(2)}) collective-permute-start(bf16[1,96,384]{2,1,0:T(8,128)(2,1)S(1)} %dynamic-slice_convert_fusion), channel_id=1, source_target_pairs={{0,4},{1,5},{2,6},{3,7},{4,0},{5,1},{6,2},{7,3},{8,12},{9,13},{10,... | collective-permute-start | bytes 221192 | tf_op jit(solution)/shard_map/ppermute | solution.py:296
  103.9 29.2 %all-to-all-start.3 = ((bf16[8,16,1024]{2,1,0:T(8,128)(2,1)}), bf16[8,16,1024]{2,1,0:T(8,128)(2,1)S(1)}, u32[]{:S(2)}, u32[]{:S(2)}) async-start(bf16[8,16,1024]{2,1,0:T(8,128)(2,1)} %bitcast.2), calls=%async_computation.3 | async-start | bytes 524288 | tf_op jit(solution)/shard_map/all_to_all | solution.py:281
  114.0 18.2 %collective-permute-start.7 = (f32[96,128]{1,0:T(8,128)S(1)}, f32[96,128]{1,0:T(8,128)S(1)}, u32[]{:S(2)}, u32[]{:S(2)}) collective-permute-start(f32[96,128]{1,0:T(8,128)S(1)} %get-tuple-element.22), channel_id=1, source_target_pairs={{0,8},{8,16},{16,24},{24,32},{32,40},{40,48},{48,56},{56,64},{64,7... | collective-permute-start | bytes 147464 | tf_op jit(solution)/shard_map/ppermute | solution.py:32
  121.8 10.6 %collective-permute-start.8 = (f32[96,128]{1,0:T(8,128)S(1)}, f32[96,128]{1,0:T(8,128)S(1)}, u32[]{:S(2)}, u32[]{:S(2)}) collective-permute-start(f32[96,128]{1,0:T(8,128)S(1)} %get-tuple-element.23), channel_id=1, source_target_pairs={{0,16},{8,24},{16,32},{24,40},{32,48},{40,56},{48,64},{56,72},{64,... | collective-permute-start | bytes 147464 | tf_op jit(solution)/shard_map/ppermute | solution.py:32
  (2 other events, 1.4 us)

commit v8 on v7

--- a/solution.py
+++ b/solution.py
@@ -70,7 +70,7 @@
 
 def tile_kernel(
     proj_own, weight, teacher, tiles, sums, near_student, far_student, near_teacher, far_teacher,
-    payload, proj_near, proj_far,
+    payload,
 ):
     peers, rows, _ = payload.shape
     texts = proj_own.shape[0]
@@ -81,22 +81,21 @@
 
     lay_out(0, tiles[:, :texts])
     lay_out(STEPS, tiles[:, texts:])
-    for s, rows_in, mates_in, proj in (
-        (1, near_student, near_teacher, proj_near),
-        (2, far_student, far_teacher, proj_far),
+    for s, rows_in, mates_in in (
+        (1, near_student, near_teacher),
+        (2, far_student, far_teacher),
     ):
-        other = dot(rows_in[...], weight[...], (1, 0))
-        proj[...] = other.astype(bf16)
+        projected = dot(rows_in[...], weight[...], (1, 0))
         wide = mates_in[...].astype(f32)
-        tail = tail + [row_sums(other * other), row_sums(wide * wide)]
-        lay_out(s, dot(proj_own[...], proj[...], (1, 1)))
+        tail = tail + [row_sums(projected * projected), row_sums(wide * wide)]
+        lay_out(s, dot(proj_own[...], projected.astype(bf16), (1, 1)))
         lay_out(STEPS + s, dot(teacher[...], mates_in[...], (1, 1)))
     tail = jnp.concatenate(tail + [jnp.zeros((rows - len(tail), texts), f32)], 0)
     for peer in range(peers):
         payload[peer, :, 2 * STEPS * texts :] = tail
 
 
-def band_kernel(parts, ids, tiles, norms):
+def band_kernel(parts, ids, tiles):
     peers = tiles.shape[0]
     rows = parts.shape[1]
     band = ids.shape[1]
@@ -107,7 +106,6 @@
         return array[:, t * texts : (t + 1) * texts]
 
     tail = part(sums, 2 * STEPS)
-    norms[...] = tail[:8]
     proj_sq = jnp.concatenate([tail[0:1], tail[3:4], tail[5:6]], 1)
     teach_sq = jnp.concatenate([tail[1:2], tail[4:5], tail[6:7]], 1)
     inv_proj = lax.rsqrt(proj_sq + EPSILON)
@@ -133,50 +131,42 @@
     product = grad * sim
     along = jnp.sum(product, 1, keepdims=True)
     inner = jnp.sum(product + along * own, 0, keepdims=True) * (inv_proj * inv_proj)
-    high = inner.astype(bf16).astype(f32)
-    low = inner - high
+    both = inv_proj[:, :texts] * inv_teach[:, :texts]
+    cosine = tail[2:3] * both * inv_proj[:, :texts] * inv_proj[:, :texts]
+    rows_out = [
+        part(inner, 0) - cosine * (1.0 / peers), part(inner, 1), part(inner, 2), both * (1.0 / peers)
+    ]
     tail_id = lax.broadcasted_iota(jnp.int32, (rows, texts), 0)
     extra = jnp.zeros((rows, texts), f32)
-    for s in range(STEPS):
-        extra = jnp.where(tail_id == 2 * s, part(high, s), extra)
-        extra = jnp.where(tail_id == 2 * s + 1, part(low, s), extra)
+    for r, row in enumerate(rows_out):
+        high = row.astype(bf16).astype(f32)
+        extra = jnp.where(tail_id == 2 * r, high, extra)
+        extra = jnp.where(tail_id == 2 * r + 1, row - high, extra)
     tile = jnp.concatenate([grad * (row_proj * inv_proj), extra], 1).astype(bf16)
     for peer in range(peers):
         tiles[peer] = tile
 
 
-def spread(gathered, norms, rows):
-    own = rows[0]
-    texts = own.shape[0]
-    band = STEPS * texts
-    gathered = gathered[...]
-    tile = gathered[:, :, :band].reshape(texts, band)
-    tail = jnp.sum(gathered[:, :, band:].astype(f32), 0)
-    inv_proj = lax.rsqrt(norms[0:1, :] + EPSILON)
-    inv_teach = lax.rsqrt(norms[1:2, :] + EPSILON)
-    both = inv_proj * inv_teach
-    cosine = norms[2:3, :] * both
-    terms = []
-    for s, partner in enumerate(rows):
-        scale = -(tail[2 * s : 2 * s + 1] + tail[2 * s + 1 : 2 * s + 2])
-        if s == 0:
-            scale = scale + cosine * inv_proj * inv_proj
-        tile_s = tile[:, s * texts : (s + 1) * texts]
-        terms.append(dot(tile_s, own[...], (0, 0)) + upright(scale) * partner[...].astype(f32))
-        terms[0] = terms[0] + dot(tile_s, partner[...], (1, 0))
-    return terms, both
-
-
 def grad_kernel(
-    sizes, gathered, norms, own, near, far, teacher, student, near_student, far_student,
+    sizes, gathered, weight, teacher, student, near_student, far_student,
     rows_grad, grad_w,
 ):
     z_size, x_size, _ = sizes
-    texts = own.shape[0]
-    terms, both = spread(gathered, norms, (own, near, far))
-    terms[0] = terms[0] - upright(both) * teacher[...].astype(f32)
+    texts = student.shape[0]
+    band = STEPS * texts
+    rows_in = (student, near_student, far_student)
+    projected = [dot(rows[...], weight[...], (1, 0)).astype(bf16) for rows in rows_in]
+    tile = gathered[:, :, :band].reshape(texts, band)
+    tail = jnp.sum(gathered[:, :, band:].astype(f32), 0)
+    tail = [tail[2 * r : 2 * r + 1] + tail[2 * r + 1 : 2 * r + 2] for r in range(STEPS + 1)]
+    terms = []
+    for s in range(STEPS):
+        tile_s = tile[:, s * texts : (s + 1) * texts]
+        terms.append(dot(tile_s, projected[0], (0, 0)) - upright(tail[s]) * projected[s].astype(f32))
+        terms[0] = terms[0] + dot(tile_s, projected[s], (1, 0))
+    terms[0] = terms[0] - upright(tail[STEPS]) * teacher[...].astype(f32)
     total = 0.0
-    for s, rows in enumerate((student, near_student, far_student)):
+    for s, rows in enumerate(rows_in):
         piece = slice(s * texts, (s + 1) * texts)
         rows_grad[piece, :] = (LOSS_SCALE * terms[s]).astype(bf16)
         total = total + dot(rows[...], rows_grad[piece, :], (0, 0))
@@ -220,13 +210,9 @@
         name="own",
     )(student, proj_weight, teacher)
 
-    parts, proj_near, proj_far = pl.pallas_call(
+    parts = pl.pallas_call(
         tile_kernel,
-        out_shape=(
-            jax.ShapeDtypeStruct((n_feat, rows, (2 * STEPS + 1) * texts), f32),
-            rows_type,
-            rows_type,
-        ),
+        out_shape=jax.ShapeDtypeStruct((n_feat, rows, (2 * STEPS + 1) * texts), f32),
         compiler_params=params,
         cost_estimate=cost(6 * 10**8),
         name="tile",
@@ -245,12 +231,9 @@
         ],
         0,
     )
-    tiles, norms = pl.pallas_call(
+    tiles = pl.pallas_call(
         band_kernel,
-        out_shape=(
-            jax.ShapeDtypeStruct((n_feat, rows, band + texts), bf16),
-            jax.ShapeDtypeStruct((8, texts), f32),
-        ),
+        out_shape=jax.ShapeDtypeStruct((n_feat, rows, band + texts), bf16),
         cost_estimate=cost(10**8),
         name="band",
     )(parts, ids)
@@ -265,9 +248,7 @@
         compiler_params=params,
         cost_estimate=cost(10**9),
         name="grad",
-    )(
-        gathered, norms, proj_own, proj_near, proj_far, teacher, student, near_student, far_student
-    )
+    )(gathered, proj_weight, teacher, student, near_student, far_student)
 
     zy = z_size * yh_size
     grad_w = lax.all_to_all(

time: 135 us -> 131 us (0.970)
  local copies, waits for them, and re-layouts: 8.23 us -> 4.23 us
    unnamed x28 -> x18, local copies, waits for them, and re-layouts: 8.1 us -> 4.09 us
where the time goes in v8:
time: 131 us; the launch traced here: 130 us
  starting transfers between devices  62.7 us (48%)
  waiting for transfers between devices  36.3 us (28%)
  blocking collectives  11.8 us (9%)
  Pallas kernels  8.4 us (6%)
  local copies, waits for them, and re-layouts  4.23 us (3%)
  matrix products  3.71 us (3%)
  other arithmetic  2.23 us (2%)
    ppermute x6, starting transfers between devices, passed_along(): lax.ppermute(array, DP, [(i, (i + by) % peers) for i in range(peers)])  36.9 us
    ppermute x6, waiting for transfers between devices, passed_along(): lax.ppermute(array, DP, [(i, (i + by) % peers) for i in range(peers)])  15.1 us
    all_to_all x1, blocking collectives, shards(): gathered = lax.all_to_all(tiles, 'feat', 0, 0)  11.8 us
    ppermute x3, waiting for transfers between devices, swapped(): return lax.ppermute(array.astype(bf16), 'feat', perm).astype(f32)  10.3 us
    all_to_all x1, waiting for transfers between devices, shards(): parts = lax.all_to_all(parts, 'feat', 0, 0)  10.3 us
    all_to_all x1, starting transfers between devices, shards(): lax.all_to_all(grad_w.reshape(zy, padded, width), ('z', 'yh'), 0, 0)  10.1 us
    ppermute x3, starting transfers between devices, swapped(): return lax.ppermute(array.astype(bf16), 'feat', perm).astype(f32)  7.9 us
    all_to_all x1, starting transfers between devices, shards(): lax.all_to_all(grad_w.reshape(x_size, features // x_size, width), 'x', 0, 0)  4.31 us
  transfers between devices with their start and end apart: 12, of which 8 were waited for; matrix products, arithmetic and copies ran while one was open for 2% of the time, Pallas kernels for 0%

profile of v8, /device:TPU:8, one launch (start us, length us, event | category | flops | bytes accessed | tf_op | source)
XLA Modules:
  0.0 130.3 jit_solution(4470636644276941468)
XLA Ops:
  0.6 17.5 %collective-permute-start.2 = (bf16[128,1024]{1,0:T(8,128)(2,1)}, bf16[128,1024]{1,0:T(8,128)(2,1)S(1)}, u32[]{:S(2)}, u32[]{:S(2)}) collective-permute-start(bf16[128,1024]{1,0:T(8,128)(2,1)} %teacher.5), channel_id=1, source_target_pairs={{0,504},{8,0},{16,8},{24,16},{32,24},{40,32},{48,40},{56,48},{64,5... | collective-permute-start | bytes 786440 | tf_op jit(solution)/shard_map/ppermute | solution.py:32
  18.1 2.7 %collective-permute-start.3 = (bf16[128,1024]{1,0:T(8,128)(2,1)}, bf16[128,1024]{1,0:T(8,128)(2,1)S(1)}, u32[]{:S(2)}, u32[]{:S(2)}) collective-permute-start(bf16[128,1024]{1,0:T(8,128)(2,1)} %teacher.5), channel_id=1, source_target_pairs={{0,496},{8,504},{16,0},{24,8},{32,16},{40,24},{48,32},{56,40},{64,... | collective-permute-start | bytes 786440 | tf_op jit(solution)/shard_map/ppermute | solution.py:32
  20.9 2.9 %collective-permute-start = (bf16[128,768]{1,0:T(8,128)(2,1)}, bf16[128,768]{1,0:T(8,128)(2,1)S(1)}, u32[]{:S(2)}, u32[]{:S(2)}) collective-permute-start(bf16[128,768]{1,0:T(8,128)(2,1)} %student.3), channel_id=1, source_target_pairs={{0,504},{8,0},{16,8},{24,16},{32,24},{40,32},{48,40},{56,48},{64,5... | collective-permute-start | bytes 589832 | tf_op jit(solution)/shard_map/ppermute | solution.py:32
  23.8 2.4 %collective-permute-start.1 = (bf16[128,768]{1,0:T(8,128)(2,1)}, bf16[128,768]{1,0:T(8,128)(2,1)S(1)}, u32[]{:S(2)}, u32[]{:S(2)}) collective-permute-start(bf16[128,768]{1,0:T(8,128)(2,1)} %student.3), channel_id=1, source_target_pairs={{0,496},{8,504},{16,0},{24,8},{32,16},{40,24},{48,32},{56,40},{64,... | collective-permute-start | bytes 589832 | tf_op jit(solution)/shard_map/ppermute | solution.py:32
  26.3 1.4 %copy-done = bf16[768,1024]{1,0:T(8,128)(2,1)S(1)} copy-done((bf16[768,1024]{1,0:T(8,128)(2,1)S(1)}, bf16[768,1024]{1,0:T(8,128)(2,1)}, u32[]{:S(2)}) %copy-start) | copy-done | bytes 1572888
  30.2 7.9 %collective-permute-done.near_student = bf16[128,768]{1,0:T(8,128)(2,1)S(1)} collective-permute-done((bf16[128,768]{1,0:T(8,128)(2,1)}, bf16[128,768]{1,0:T(8,128)(2,1)S(1)}, u32[]{:S(2)}, u32[]{:S(2)}) %collective-permute-start) | collective-permute-done | bytes 196640 | tf_op jit(solution)/shard_map/ppermute | solution.py:32
  38.1 1.8 %tile.1 = f32[8,16,896]{2,1,0:T(8,128)} custom-call(bf16[128,1024]{1,0:T(8,128)(2,1)S(1)} %get-tuple-element.7.proj_own, bf16[768,1024]{1,0:T(8,128)(2,1)S(1)} %copy-done.1, bf16[128,1024]{1,0:T(8,128)(2,1)S(1)} %copy-done.3, f32[128,256]{1,0:T(8,128)S(1)} %get-tuple-element.8.tiles, f32[8,128]{1,0:T(8,128)S(1)} %get-tuple-element.9.sums, ...), custom_call_target="tpu_custom_call" | custom-call | flops 600000000 | bytes 3000000 | tf_op jit(solution)/shard_map/tile/pallas_call | solution.py:213
  39.9 3.6 %all-to-all-start = ((f32[8,16,896]{2,1,0:T(8,128)}), f32[8,16,896]{2,1,0:T(8,128)S(1)}, u32[]{:S(2)}, u32[]{:S(2)}) async-start(f32[8,16,896]{2,1,0:T(8,128)} %tile.1), calls=%async_computation | async-start | bytes 917504 | tf_op jit(solution)/shard_map/all_to_all | solution.py:223
  44.2 10.3 %all-to-all-done.parts = f32[8,16,896]{2,1,0:T(8,128)S(1)} async-done(((f32[8,16,896]{2,1,0:T(8,128)}), f32[8,16,896]{2,1,0:T(8,128)S(1)}, u32[]{:S(2)}, u32[]{:S(2)}) %all-to-all-start) | async-done | bytes 458784 | tf_op jit(solution)/shard_map/all_to_all | solution.py:223
  55.3 2.4 %band.1 = bf16[8,16,512]{2,1,0:T(8,128)(2,1)} custom-call(f32[8,16,896]{2,1,0:T(8,128)} %copy-done.6, s32[8,384]{1,0:T(8,128)} %add_add_fusion.ids), custom_call_target="tpu_custom_call" | custom-call | flops 100000000 | bytes 3000000 | tf_op jit(solution)/shard_map/band/pallas_call | solution.py:234
  57.7 11.8 %all_to_all.20.gathered = bf16[8,16,512]{2,1,0:T(8,128)(2,1)S(1)} all-to-all(bf16[8,16,512]{2,1,0:T(8,128)(2,1)} %band.1), channel_id=1, replica_groups=mesh['z'=4,'x'=8,'yh'=2,'feat'=8] {'feat'}, dimensions={0} | all-to-all | bytes 262144 | tf_op jit(solution)/shard_map/all_to_all | solution.py:240
  69.6 3.6 %grad.1 = (bf16[384,1024]{1,0:T(8,128)(2,1)S(1)}, bf16[768,1024]{1,0:T(8,128)(2,1)}) custom-call(bf16[8,16,512]{2,1,0:T(8,128)(2,1)S(1)} %all_to_all.20.gathered, bf16[768,1024]{1,0:T(8,128)(2,1)S(1)} %copy-done.1, bf16[128,1024]{1,0:T(8,128)(2,1)S(1)} %copy-done.3, bf16[128,768]{1,0:T(8,128)(2,1)S(1)} %copy-done.5, ...), custom_call_target="tpu_custom_call" | custom-call | flops 1000000000 | bytes 3000000 | tf_op jit(solution)/shard_map/grad/pallas_call | solution.py:242
  73.2 4.3 %all-to-all-start.2 = ((bf16[8,96,1024]{2,1,0:T(8,128)(2,1)}), bf16[8,96,1024]{2,1,0:T(8,128)(2,1)}, u32[]{:S(2)}, u32[]{:S(2)}) async-start(bf16[8,96,1024]{2,1,0:T(8,128)(2,1)} %bitcast), calls=%async_computation.2 | async-start | bytes 3145728 | tf_op jit(solution)/shard_map/all_to_all | solution.py:254
  78.1 1.9 %collective-permute-start.4 = (bf16[4,96,384]{2,1,0:T(8,128)(2,1)S(1)}, bf16[4,96,384]{2,1,0:T(8,128)(2,1)S(1)}, u32[]{:S(2)}, u32[]{:S(2)}) collective-permute-start(bf16[4,96,384]{2,1,0:T(8,128)(2,1)S(1)} %convolution_convert_fusion), channel_id=1, source_target_pairs={{0,1},{1,0},{2,3},{3,2},{4,5},{5,4},{6,7},{7,6},{8,9},{9,8},{10,11... | collective-permute-start | bytes 884744 | tf_op jit(solution)/shard_map/ppermute | solution.py:277
  80.1 1.5 %collective-permute-done.4 = bf16[4,96,384]{2,1,0:T(8,128)(2,1)S(1)} collective-permute-done((bf16[4,96,384]{2,1,0:T(8,128)(2,1)S(1)}, bf16[4,96,384]{2,1,0:T(8,128)(2,1)S(1)}, u32[]{:S(2)}, u32[]{:S(2)}) %collective-permute-start.4) | collective-permute-done | bytes 294944 | tf_op jit(solution)/shard_map/ppermute | solution.py:277
  82.2 3.0 %collective-permute-start.5 = (bf16[2,96,384]{2,1,0:T(8,128)(2,1)S(1)}, bf16[2,96,384]{2,1,0:T(8,128)(2,1)S(1)}, u32[]{:S(2)}, u32[]{:S(2)}) collective-permute-start(bf16[2,96,384]{2,1,0:T(8,128)(2,1)S(1)} %fusion.17), channel_id=1, source_target_pairs={{0,2},{1,3},{2,0},{3,1},{4,6},{5,7},{6,4},{7,5},{8,10},{9,11},{10,... | collective-permute-start | bytes 442376 | tf_op jit(solution)/shard_map/ppermute | solution.py:277
  85.3 4.7 %collective-permute-done.5 = bf16[2,96,384]{2,1,0:T(8,128)(2,1)S(1)} collective-permute-done((bf16[2,96,384]{2,1,0:T(8,128)(2,1)S(1)}, bf16[2,96,384]{2,1,0:T(8,128)(2,1)S(1)}, u32[]{:S(2)}, u32[]{:S(2)}) %collective-permute-start.5) | collective-permute-done | bytes 147488 | tf_op jit(solution)/shard_map/ppermute | solution.py:277
  90.0 3.0 %collective-permute-start.6 = (bf16[1,96,384]{2,1,0:T(8,128)(2,1)S(1)}, bf16[1,96,384]{2,1,0:T(8,128)(2,1)S(1)}, u32[]{:S(2)}, u32[]{:S(2)}) collective-permute-start(bf16[1,96,384]{2,1,0:T(8,128)(2,1)S(1)} %dynamic-slice_convert_fusion), channel_id=1, source_target_pairs={{0,4},{1,5},{2,6},{3,7},{4,0},{5,1},{6,2},{7,3},{8,12},{9,13},{10,... | collective-permute-start | bytes 221192 | tf_op jit(solution)/shard_map/ppermute | solution.py:277
  93.2 4.1 %collective-permute-done.6 = bf16[1,96,384]{2,1,0:T(8,128)(2,1)S(1)} collective-permute-done((bf16[1,96,384]{2,1,0:T(8,128)(2,1)S(1)}, bf16[1,96,384]{2,1,0:T(8,128)(2,1)S(1)}, u32[]{:S(2)}, u32[]{:S(2)}) %collective-permute-start.6) | collective-permute-done | bytes 73760 | tf_op jit(solution)/shard_map/ppermute | solution.py:277
  98.0 2.5 %convolution_convert_fusion.1 = bf16[128,1024]{1,0:T(8,128)(2,1)} fusion(bf16[128,768]{1,0:T(8,128)(2,1)S(1)} %fusion.16, bf16[768,1024]{1,0:T(8,128)(2,1)} %bitcast.1), kind=kOutput, calls=%fused_computation.2 | convolution fusion | flops 201457664 | bytes 2031616 | tf_op jit(solution)/shard_map/dot_general | solution.py:24
  100.5 10.1 %all-to-all-start.3 = ((bf16[8,16,1024]{2,1,0:T(8,128)(2,1)}), bf16[8,16,1024]{2,1,0:T(8,128)(2,1)S(1)}, u32[]{:S(2)}, u32[]{:S(2)}) async-start(bf16[8,16,1024]{2,1,0:T(8,128)(2,1)} %bitcast.2), calls=%async_computation.3 | async-start | bytes 524288 | tf_op jit(solution)/shard_map/all_to_all | solution.py:262
  110.6 7.8 %collective-permute-start.7 = (f32[96,128]{1,0:T(8,128)S(1)}, f32[96,128]{1,0:T(8,128)S(1)}, u32[]{:S(2)}, u32[]{:S(2)}) collective-permute-start(f32[96,128]{1,0:T(8,128)S(1)} %get-tuple-element.12), channel_id=1, source_target_pairs={{0,8},{8,16},{16,24},{24,32},{32,40},{40,48},{48,56},{56,64},{64,7... | collective-permute-start | bytes 147464 | tf_op jit(solution)/shard_map/ppermute | solution.py:32
  118.4 3.4 %collective-permute-start.8 = (f32[96,128]{1,0:T(8,128)S(1)}, f32[96,128]{1,0:T(8,128)S(1)}, u32[]{:S(2)}, u32[]{:S(2)}) collective-permute-start(f32[96,128]{1,0:T(8,128)S(1)} %get-tuple-element.13), channel_id=1, source_target_pairs={{0,16},{8,24},{16,32},{24,40},{32,48},{40,56},{48,64},{56,72},{64,... | collective-permute-start | bytes 147464 | tf_op jit(solution)/shard_map/ppermute | solution.py:32
  121.9 6.9 %collective-permute-done.7 = f32[96,128]{1,0:T(8,128)S(1)} collective-permute-done((f32[96,128]{1,0:T(8,128)S(1)}, f32[96,128]{1,0:T(8,128)S(1)}, u32[]{:S(2)}, u32[]{:S(2)}) %collective-permute-start.7) | collective-permute-done | bytes 49184 | tf_op jit(solution)/shard_map/ppermute | solution.py:32
  (45 shorter events, 7.8 us)
Async XLA Ops:
  0.6 37.4 %collective-permute-start.2 = (bf16[128,1024]{1,0:T(8,128)(2,1)}, bf16[128,1024]{1,0:T(8,128)(2,1)S(1)}, u32[]{:S(2)}, u32[]{:S(2)}) collective-permute-start(bf16[128,1024]{1,0:T(8,128)(2,1)} %teacher.5), channel_id=1, source_target_pairs={{0,504},{8,0},{16,8},{24,16},{32,24},{40,32},{48,40},{56,48},{64,5... | collective-permute-start | bytes 786440 | tf_op jit(solution)/shard_map/ppermute | solution.py:32
  18.1 19.9 %collective-permute-start.3 = (bf16[128,1024]{1,0:T(8,128)(2,1)}, bf16[128,1024]{1,0:T(8,128)(2,1)S(1)}, u32[]{:S(2)}, u32[]{:S(2)}) collective-permute-start(bf16[128,1024]{1,0:T(8,128)(2,1)} %teacher.5), channel_id=1, source_target_pairs={{0,496},{8,504},{16,0},{24,8},{32,16},{40,24},{48,32},{56,40},{64,... | collective-permute-start | bytes 786440 | tf_op jit(solution)/shard_map/ppermute | solution.py:32
  20.9 17.2 %collective-permute-start = (bf16[128,768]{1,0:T(8,128)(2,1)}, bf16[128,768]{1,0:T(8,128)(2,1)S(1)}, u32[]{:S(2)}, u32[]{:S(2)}) collective-permute-start(bf16[128,768]{1,0:T(8,128)(2,1)} %student.3), channel_id=1, source_target_pairs={{0,504},{8,0},{16,8},{24,16},{32,24},{40,32},{48,40},{56,48},{64,5... | collective-permute-start | bytes 589832 | tf_op jit(solution)/shard_map/ppermute | solution.py:32
  23.8 14.2 %collective-permute-start.1 = (bf16[128,768]{1,0:T(8,128)(2,1)}, bf16[128,768]{1,0:T(8,128)(2,1)S(1)}, u32[]{:S(2)}, u32[]{:S(2)}) collective-permute-start(bf16[128,768]{1,0:T(8,128)(2,1)} %student.3), channel_id=1, source_target_pairs={{0,496},{8,504},{16,0},{24,8},{32,16},{40,24},{48,32},{56,40},{64,... | collective-permute-start | bytes 589832 | tf_op jit(solution)/shard_map/ppermute | solution.py:32
  26.3 1.4 %copy-start = (bf16[768,1024]{1,0:T(8,128)(2,1)S(1)}, bf16[768,1024]{1,0:T(8,128)(2,1)}, u32[]{:S(2)}) copy-start(bf16[768,1024]{1,0:T(8,128)(2,1)} %weight.5) | copy-start | bytes 4718596
  27.7 0.9 copy-start.2
  28.6 0.9 copy-start.4
  29.6 8.5 %copy-start.1 = (bf16[768,1024]{1,0:T(8,128)(2,1)S(1)}, bf16[768,1024]{1,0:T(8,128)(2,1)}, u32[]{:S(2)}) copy-start(bf16[768,1024]{1,0:T(8,128)(2,1)} %weight.5) | copy-start | bytes 4718596
  29.6 8.5 %copy-start.3 = (bf16[128,1024]{1,0:T(8,128)(2,1)S(1)}, bf16[128,1024]{1,0:T(8,128)(2,1)}, u32[]{:S(2)}) copy-start(bf16[128,1024]{1,0:T(8,128)(2,1)} %teacher.5) | copy-start | bytes 786436
  38.1 5.4 %copy-start.8 = (s32[384]{0:T(512)S(1)}, s32[384]{0:T(512)}, u32[]{:S(2)}) copy-start(s32[384]{0:T(512)} %param.8) | copy-start | bytes 4612
  38.1 5.5 %copy-start.7 = (s32[2,384]{1,0:T(2,128)S(1)}, s32[2,384]{1,0:T(2,128)}, u32[]{:S(2)}) copy-start(s32[2,384]{1,0:T(2,128)} %param.9) | copy-start | bytes 9220
  39.9 29.7 %copy-start.5 = (bf16[128,768]{1,0:T(8,128)(2,1)S(1)}, bf16[128,768]{1,0:T(8,128)(2,1)}, u32[]{:S(2)}) copy-start(bf16[128,768]{1,0:T(8,128)(2,1)} %student.3) | copy-start | bytes 589828
  39.9 14.6 %all-to-all-start = ((f32[8,16,896]{2,1,0:T(8,128)}), f32[8,16,896]{2,1,0:T(8,128)S(1)}, u32[]{:S(2)}, u32[]{:S(2)}) async-start(f32[8,16,896]{2,1,0:T(8,128)} %tile.1), calls=%async_computation | async-start | bytes 917504 | tf_op jit(solution)/shard_map/all_to_all | solution.py:223
  54.5 0.8 copy-start.6
  73.2 24.8 %all-to-all-start.2 = ((bf16[8,96,1024]{2,1,0:T(8,128)(2,1)}), bf16[8,96,1024]{2,1,0:T(8,128)(2,1)}, u32[]{:S(2)}, u32[]{:S(2)}) async-start(bf16[8,96,1024]{2,1,0:T(8,128)(2,1)} %bitcast), calls=%async_computation.2 | async-start | bytes 3145728 | tf_op jit(solution)/shard_map/all_to_all | solution.py:254
  78.1 3.5 %collective-permute-start.4 = (bf16[4,96,384]{2,1,0:T(8,128)(2,1)S(1)}, bf16[4,96,384]{2,1,0:T(8,128)(2,1)S(1)}, u32[]{:S(2)}, u32[]{:S(2)}) collective-permute-start(bf16[4,96,384]{2,1,0:T(8,128)(2,1)S(1)} %convolution_convert_fusion), channel_id=1, source_target_pairs={{0,1},{1,0},{2,3},{3,2},{4,5},{5,4},{6,7},{7,6},{8,9},{9,8},{10,11... | collective-permute-start | bytes 884744 | tf_op jit(solution)/shard_map/ppermute | solution.py:277
  82.2 7.8 %collective-permute-start.5 = (bf16[2,96,384]{2,1,0:T(8,128)(2,1)S(1)}, bf16[2,96,384]{2,1,0:T(8,128)(2,1)S(1)}, u32[]{:S(2)}, u32[]{:S(2)}) collective-permute-start(bf16[2,96,384]{2,1,0:T(8,128)(2,1)S(1)} %fusion.17), channel_id=1, source_target_pairs={{0,2},{1,3},{2,0},{3,1},{4,6},{5,7},{6,4},{7,5},{8,10},{9,11},{10,... | collective-permute-start | bytes 442376 | tf_op jit(solution)/shard_map/ppermute | solution.py:277
  90.0 7.2 %collective-permute-start.6 = (bf16[1,96,384]{2,1,0:T(8,128)(2,1)S(1)}, bf16[1,96,384]{2,1,0:T(8,128)(2,1)S(1)}, u32[]{:S(2)}, u32[]{:S(2)}) collective-permute-start(bf16[1,96,384]{2,1,0:T(8,128)(2,1)S(1)} %dynamic-slice_convert_fusion), channel_id=1, source_target_pairs={{0,4},{1,5},{2,6},{3,7},{4,0},{5,1},{6,2},{7,3},{8,12},{9,13},{10,... | collective-permute-start | bytes 221192 | tf_op jit(solution)/shard_map/ppermute | solution.py:277
  100.5 29.2 %all-to-all-start.3 = ((bf16[8,16,1024]{2,1,0:T(8,128)(2,1)}), bf16[8,16,1024]{2,1,0:T(8,128)(2,1)S(1)}, u32[]{:S(2)}, u32[]{:S(2)}) async-start(bf16[8,16,1024]{2,1,0:T(8,128)(2,1)} %bitcast.2), calls=%async_computation.3 | async-start | bytes 524288 | tf_op jit(solution)/shard_map/all_to_all | solution.py:262
  110.6 18.2 %collective-permute-start.7 = (f32[96,128]{1,0:T(8,128)S(1)}, f32[96,128]{1,0:T(8,128)S(1)}, u32[]{:S(2)}, u32[]{:S(2)}) collective-permute-start(f32[96,128]{1,0:T(8,128)S(1)} %get-tuple-element.12), channel_id=1, source_target_pairs={{0,8},{8,16},{16,24},{24,32},{32,40},{40,48},{48,56},{56,64},{64,7... | collective-permute-start | bytes 147464 | tf_op jit(solution)/shard_map/ppermute | solution.py:32
  118.4 10.6 %collective-permute-start.8 = (f32[96,128]{1,0:T(8,128)S(1)}, f32[96,128]{1,0:T(8,128)S(1)}, u32[]{:S(2)}, u32[]{:S(2)}) collective-permute-start(f32[96,128]{1,0:T(8,128)S(1)} %get-tuple-element.13), channel_id=1, source_target_pairs={{0,16},{8,24},{16,32},{24,40},{32,48},{40,56},{48,64},{56,72},{64,... | collective-permute-start | bytes 147464 | tf_op jit(solution)/shard_map/ppermute | solution.py:32

commit v9 on v8

--- a/solution.py
+++ b/solution.py
@@ -184,7 +184,6 @@
     band = STEPS * texts
     rows = texts // n_feat
     share = features // n_dp
-    padded = -(-share // 16) * 16
     feat = lax.axis_index("feat")
 
     near_student = passed_along(student, -1)
@@ -250,17 +249,15 @@
         name="grad",
     )(gathered, proj_weight, teacher, student, near_student, far_student)
 
-    zy = z_size * yh_size
-    grad_w = lax.all_to_all(
-        grad_w.reshape(x_size, features // x_size, width), "x", 0, 0
-    ).reshape(features, width)
-    row_out = lax.broadcasted_iota(jnp.int32, (zy * padded, features), 0)
-    row_in = lax.broadcasted_iota(jnp.int32, row_out.shape, 1) % (zy * share)
-    select = (row_out // padded == row_in // share) & (row_out % padded == row_in % share)
-    select = lax.optimization_barrier(select.astype(bf16))
-    grad_w = dot(select, grad_w, (1, 0)).astype(bf16)
-    grad_w = lax.all_to_all(grad_w.reshape(zy, padded, width), ("z", "yh"), 0, 0)
-    grad_w = jnp.sum(grad_w.astype(f32), 0)[:share]
+    grad_w = lax.all_to_all(grad_w.reshape(x_size, features // x_size, width), "x", 0, 0)
+    grad_w = jnp.sum(grad_w.astype(f32), 0).astype(bf16)
+    grad_w = lax.all_to_all(grad_w.reshape(z_size, yh_size * share, width), "z", 0, 0)
+    grad_w = jnp.sum(grad_w.astype(f32), 0)
+    lower, upper = grad_w[:share], grad_w[share:]
+    first = lax.axis_index("yh") == 0
+    grad_w = jnp.where(first, lower, upper) + lax.ppermute(
+        jnp.where(first, upper, lower), "yh", [(0, 1), (1, 0)]
+    )
 
     height = features // n_feat
     halves = proj_weight.reshape(n_feat // 2, 2, height, width)

time: 131 us -> 129 us (0.985)
  the two profiles are of different devices: /device:TPU:8 before, /device:TPU:6 now
where the time goes in v9:
time: 129 us; the launch traced here: 128 us
  starting transfers between devices  63.7 us (49%)
  waiting for transfers between devices  35.3 us (27%)
  blocking collectives  10.1 us (8%)
  Pallas kernels  8.37 us (6%)
  other arithmetic  4.44 us (3%)
  local copies, waits for them, and re-layouts  4.21 us (3%)
    ppermute x6, starting transfers between devices, passed_along(): lax.ppermute(array, DP, [(i, (i + by) % peers) for i in range(peers)])  31.9 us
    all_to_all x1, waiting for transfers between devices, shards(): parts = lax.all_to_all(parts, 'feat', 0, 0)  13.1 us
    all_to_all x1, starting transfers between devices, shards(): lax.all_to_all(grad_w.reshape(x_size, features // x_size, width), 'x', 0, 0)  11.6 us
    all_to_all x1, blocking collectives, shards(): gathered = lax.all_to_all(tiles, 'feat', 0, 0)  10.1 us
    ppermute x3, starting transfers between devices, swapped(): return lax.ppermute(array.astype(bf16), 'feat', perm).astype(f32)  6.98 us
    ppermute x3, waiting for transfers between devices, swapped(): return lax.ppermute(array.astype(bf16), 'feat', perm).astype(f32)  6.49 us
    ppermute x6, waiting for transfers between devices, passed_along(): lax.ppermute(array, DP, [(i, (i + by) % peers) for i in range(peers)])  5.85 us
    ppermute x1, waiting for transfers between devices, shards(): lax.ppermute(jnp.where(first, upper, lower), 'yh', [(0, 1), (1, 0)])  5.49 us
  transfers between devices with their start and end apart: 13, of which 6 were waited for; matrix products, arithmetic and copies ran while one was open for 4% of the time, Pallas kernels for 0%

profile of v9, /device:TPU:6, one launch (start us, length us, event | category | flops | bytes accessed | tf_op | source)
XLA Modules:
  0.0 128.1 jit_solution(3322115159439726616)
XLA Ops:
  0.6 8.0 %collective-permute-start.2 = (bf16[128,1024]{1,0:T(8,128)(2,1)}, bf16[128,1024]{1,0:T(8,128)(2,1)S(1)}, u32[]{:S(2)}, u32[]{:S(2)}) collective-permute-start(bf16[128,1024]{1,0:T(8,128)(2,1)} %teacher.5), channel_id=1, source_target_pairs={{0,504},{8,0},{16,8},{24,16},{32,24},{40,32},{48,40},{56,48},{64,5... | collective-permute-start | bytes 786440 | tf_op jit(solution)/shard_map/ppermute | solution.py:32
  8.6 2.4 %collective-permute-start.3 = (bf16[128,1024]{1,0:T(8,128)(2,1)}, bf16[128,1024]{1,0:T(8,128)(2,1)S(1)}, u32[]{:S(2)}, u32[]{:S(2)}) collective-permute-start(bf16[128,1024]{1,0:T(8,128)(2,1)} %teacher.5), channel_id=1, source_target_pairs={{0,496},{8,504},{16,0},{24,8},{32,16},{40,24},{48,32},{56,40},{64,... | collective-permute-start | bytes 786440 | tf_op jit(solution)/shard_map/ppermute | solution.py:32
  11.1 2.0 %collective-permute-start = (bf16[128,768]{1,0:T(8,128)(2,1)}, bf16[128,768]{1,0:T(8,128)(2,1)S(1)}, u32[]{:S(2)}, u32[]{:S(2)}) collective-permute-start(bf16[128,768]{1,0:T(8,128)(2,1)} %student.3), channel_id=1, source_target_pairs={{0,504},{8,0},{16,8},{24,16},{32,24},{40,32},{48,40},{56,48},{64,5... | collective-permute-start | bytes 589832 | tf_op jit(solution)/shard_map/ppermute | solution.py:32
  13.1 7.8 %collective-permute-start.1 = (bf16[128,768]{1,0:T(8,128)(2,1)}, bf16[128,768]{1,0:T(8,128)(2,1)S(1)}, u32[]{:S(2)}, u32[]{:S(2)}) collective-permute-start(bf16[128,768]{1,0:T(8,128)(2,1)} %student.3), channel_id=1, source_target_pairs={{0,496},{8,504},{16,0},{24,8},{32,16},{40,24},{48,32},{56,40},{64,... | collective-permute-start | bytes 589832 | tf_op jit(solution)/shard_map/ppermute | solution.py:32
  24.8 5.8 %collective-permute-done.near_student = bf16[128,768]{1,0:T(8,128)(2,1)S(1)} collective-permute-done((bf16[128,768]{1,0:T(8,128)(2,1)}, bf16[128,768]{1,0:T(8,128)(2,1)S(1)}, u32[]{:S(2)}, u32[]{:S(2)}) %collective-permute-start) | collective-permute-done | bytes 196640 | tf_op jit(solution)/shard_map/ppermute | solution.py:32
  30.7 1.7 %tile.1 = f32[8,16,896]{2,1,0:T(8,128)} custom-call(bf16[128,1024]{1,0:T(8,128)(2,1)S(1)} %get-tuple-element.7.proj_own, bf16[768,1024]{1,0:T(8,128)(2,1)S(1)} %copy-done.1, bf16[128,1024]{1,0:T(8,128)(2,1)S(1)} %copy-done.3, f32[128,256]{1,0:T(8,128)S(1)} %get-tuple-element.8.tiles, f32[8,128]{1,0:T(8,128)S(1)} %get-tuple-element.9.sums, ...), custom_call_target="tpu_custom_call" | custom-call | flops 600000000 | bytes 3000000 | tf_op jit(solution)/shard_map/tile/pallas_call | solution.py:212
  32.5 3.6 %all-to-all-start = ((f32[8,16,896]{2,1,0:T(8,128)}), f32[8,16,896]{2,1,0:T(8,128)S(1)}, u32[]{:S(2)}, u32[]{:S(2)}) async-start(f32[8,16,896]{2,1,0:T(8,128)} %tile.1), calls=%async_computation | async-start | bytes 917504 | tf_op jit(solution)/shard_map/all_to_all | solution.py:222
  36.9 13.1 %all-to-all-done.parts = f32[8,16,896]{2,1,0:T(8,128)S(1)} async-done(((f32[8,16,896]{2,1,0:T(8,128)}), f32[8,16,896]{2,1,0:T(8,128)S(1)}, u32[]{:S(2)}, u32[]{:S(2)}) %all-to-all-start) | async-done | bytes 458784 | tf_op jit(solution)/shard_map/all_to_all | solution.py:222
  50.7 2.4 %band.1 = bf16[8,16,512]{2,1,0:T(8,128)(2,1)} custom-call(f32[8,16,896]{2,1,0:T(8,128)} %copy-done.6, s32[8,384]{1,0:T(8,128)} %add_add_fusion.ids), custom_call_target="tpu_custom_call" | custom-call | flops 100000000 | bytes 3000000 | tf_op jit(solution)/shard_map/band/pallas_call | solution.py:233
  53.2 10.1 %all_to_all.20.gathered = bf16[8,16,512]{2,1,0:T(8,128)(2,1)S(1)} all-to-all(bf16[8,16,512]{2,1,0:T(8,128)(2,1)} %band.1), channel_id=1, replica_groups=mesh['z'=4,'x'=8,'yh'=2,'feat'=8] {'feat'}, dimensions={0} | all-to-all | bytes 262144 | tf_op jit(solution)/shard_map/all_to_all | solution.py:239
  63.2 3.6 %grad.1 = (bf16[384,1024]{1,0:T(8,128)(2,1)S(1)}, bf16[768,1024]{1,0:T(8,128)(2,1)}) custom-call(bf16[8,16,512]{2,1,0:T(8,128)(2,1)S(1)} %all_to_all.20.gathered, bf16[768,1024]{1,0:T(8,128)(2,1)S(1)} %copy-done.1, bf16[128,1024]{1,0:T(8,128)(2,1)S(1)} %copy-done.3, bf16[128,768]{1,0:T(8,128)(2,1)S(1)} %copy-done.5, ...), custom_call_target="tpu_custom_call" | custom-call | flops 1000000000 | bytes 3000000 | tf_op jit(solution)/shard_map/grad/pallas_call | solution.py:241
  66.8 11.6 %all-to-all-start.2 = ((bf16[8,96,1024]{2,1,0:T(8,128)(2,1)}), bf16[8,96,1024]{2,1,0:T(8,128)(2,1)}, u32[]{:S(2)}, u32[]{:S(2)}) async-start(bf16[8,96,1024]{2,1,0:T(8,128)(2,1)} %bitcast), calls=%async_computation.2 | async-start | bytes 3145728 | tf_op jit(solution)/shard_map/all_to_all | solution.py:252
  79.0 1.9 %collective-permute-start.5 = (bf16[4,96,384]{2,1,0:T(8,128)(2,1)S(1)}, bf16[4,96,384]{2,1,0:T(8,128)(2,1)S(1)}, u32[]{:S(2)}, u32[]{:S(2)}) collective-permute-start(bf16[4,96,384]{2,1,0:T(8,128)(2,1)S(1)} %convolution_convert_fusion), channel_id=1, source_target_pairs={{0,1},{1,0},{2,3},{3,2},{4,5},{5,4},{6,7},{7,6},{8,9},{9,8},{10,11... | collective-permute-start | bytes 884744 | tf_op jit(solution)/shard_map/ppermute | solution.py:274
  81.0 1.5 %collective-permute-done.5 = bf16[4,96,384]{2,1,0:T(8,128)(2,1)S(1)} collective-permute-done((bf16[4,96,384]{2,1,0:T(8,128)(2,1)S(1)}, bf16[4,96,384]{2,1,0:T(8,128)(2,1)S(1)}, u32[]{:S(2)}, u32[]{:S(2)}) %collective-permute-start.5) | collective-permute-done | bytes 294944 | tf_op jit(solution)/shard_map/ppermute | solution.py:274
  83.2 2.8 %collective-permute-start.6 = (bf16[2,96,384]{2,1,0:T(8,128)(2,1)S(1)}, bf16[2,96,384]{2,1,0:T(8,128)(2,1)S(1)}, u32[]{:S(2)}, u32[]{:S(2)}) collective-permute-start(bf16[2,96,384]{2,1,0:T(8,128)(2,1)S(1)} %fusion.6), channel_id=1, source_target_pairs={{0,2},{1,3},{2,0},{3,1},{4,6},{5,7},{6,4},{7,5},{8,10},{9,11},{10,... | collective-permute-start | bytes 442376 | tf_op jit(solution)/shard_map/ppermute | solution.py:274
  86.0 4.9 %collective-permute-done.6 = bf16[2,96,384]{2,1,0:T(8,128)(2,1)S(1)} collective-permute-done((bf16[2,96,384]{2,1,0:T(8,128)(2,1)S(1)}, bf16[2,96,384]{2,1,0:T(8,128)(2,1)S(1)}, u32[]{:S(2)}, u32[]{:S(2)}) %collective-permute-start.6) | collective-permute-done | bytes 147488 | tf_op jit(solution)/shard_map/ppermute | solution.py:274
  91.0 2.2 %collective-permute-start.7 = (bf16[1,96,384]{2,1,0:T(8,128)(2,1)S(1)}, bf16[1,96,384]{2,1,0:T(8,128)(2,1)S(1)}, u32[]{:S(2)}, u32[]{:S(2)}) collective-permute-start(bf16[1,96,384]{2,1,0:T(8,128)(2,1)S(1)} %dynamic-slice_convert_fusion), channel_id=1, source_target_pairs={{0,4},{1,5},{2,6},{3,7},{4,0},{5,1},{6,2},{7,3},{8,12},{9,13},{10,... | collective-permute-start | bytes 221192 | tf_op jit(solution)/shard_map/ppermute | solution.py:274
  93.2 4.4 %all-to-all-done.2 = bf16[8,96,1024]{2,1,0:T(8,128)(2,1)} async-done(((bf16[8,96,1024]{2,1,0:T(8,128)(2,1)}), bf16[8,96,1024]{2,1,0:T(8,128)(2,1)}, u32[]{:S(2)}, u32[]{:S(2)}) %all-to-all-start.2) | async-done | bytes 1572896 | tf_op jit(solution)/shard_map/all_to_all | solution.py:252
  97.6 2.4 %reduce_sum.21 = bf16[96,1024]{1,0:T(8,128)(2,1)} reduce(bf16[8,96,1024]{2,1,0:T(8,128)(2,1)} %all-to-all-done.2, bf16[]{:T(256)} %constant.39.clone.1), dimensions={0}, to_apply=%region_0.0 | reduce | flops 688128 | bytes 1769474 | tf_op jit(solution)/shard_map/reduce_sum | solution.py:253
  100.0 5.1 %all-to-all-start.3 = ((bf16[4,24,1024]{2,1,0:T(8,128)(2,1)}), bf16[4,24,1024]{2,1,0:T(8,128)(2,1)S(1)}, u32[]{:S(2)}, u32[]{:S(2)}) async-start(bf16[4,24,1024]{2,1,0:T(8,128)(2,1)} %bitcast.1), calls=%async_computation.3 | async-start | bytes 393216 | tf_op jit(solution)/shard_map/all_to_all | solution.py:254
  105.1 7.1 %collective-permute-start.8 = (f32[96,128]{1,0:T(8,128)S(1)}, f32[96,128]{1,0:T(8,128)S(1)}, u32[]{:S(2)}, u32[]{:S(2)}) collective-permute-start(f32[96,128]{1,0:T(8,128)S(1)} %get-tuple-element.12), channel_id=1, source_target_pairs={{0,8},{8,16},{16,24},{24,32},{32,40},{40,48},{48,56},{56,64},{64,7... | collective-permute-start | bytes 147464 | tf_op jit(solution)/shard_map/ppermute | solution.py:32
  112.2 4.5 %collective-permute-start.9 = (f32[96,128]{1,0:T(8,128)S(1)}, f32[96,128]{1,0:T(8,128)S(1)}, u32[]{:S(2)}, u32[]{:S(2)}) collective-permute-start(f32[96,128]{1,0:T(8,128)S(1)} %get-tuple-element.13), channel_id=1, source_target_pairs={{0,16},{8,24},{16,32},{24,40},{32,48},{40,56},{48,64},{56,72},{64,... | collective-permute-start | bytes 147464 | tf_op jit(solution)/shard_map/ppermute | solution.py:32
  116.8 4.5 %collective-permute-start.4 = (f32[12,1024]{1,0:T(8,128)S(1)}, f32[12,1024]{1,0:T(8,128)S(1)}, u32[]{:S(2)}, u32[]{:S(2)}) collective-permute-start(f32[12,1024]{1,0:T(8,128)S(1)} %slice_select_fusion), channel_id=1, source_target_pairs={{0,8},{8,0},{1,9},{9,1},{2,10},{10,2},{3,11},{11,3},{4,12},{12,4},... | collective-permute-start | bytes 147464 | tf_op jit(solution)/shard_map/ppermute | solution.py:258
  122.0 5.5 %collective-permute-done.4 = f32[12,1024]{1,0:T(8,128)S(1)} collective-permute-done((f32[12,1024]{1,0:T(8,128)S(1)}, f32[12,1024]{1,0:T(8,128)S(1)}, u32[]{:S(2)}, u32[]{:S(2)}) %collective-permute-start.4) | collective-permute-done | bytes 49184 | tf_op jit(solution)/shard_map/ppermute | solution.py:258
  (43 shorter events, 8.0 us)
Async XLA Ops:
  0.6 30.0 %collective-permute-start.2 = (bf16[128,1024]{1,0:T(8,128)(2,1)}, bf16[128,1024]{1,0:T(8,128)(2,1)S(1)}, u32[]{:S(2)}, u32[]{:S(2)}) collective-permute-start(bf16[128,1024]{1,0:T(8,128)(2,1)} %teacher.5), channel_id=1, source_target_pairs={{0,504},{8,0},{16,8},{24,16},{32,24},{40,32},{48,40},{56,48},{64,5... | collective-permute-start | bytes 786440 | tf_op jit(solution)/shard_map/ppermute | solution.py:32
  8.6 22.0 %collective-permute-start.3 = (bf16[128,1024]{1,0:T(8,128)(2,1)}, bf16[128,1024]{1,0:T(8,128)(2,1)S(1)}, u32[]{:S(2)}, u32[]{:S(2)}) collective-permute-start(bf16[128,1024]{1,0:T(8,128)(2,1)} %teacher.5), channel_id=1, source_target_pairs={{0,496},{8,504},{16,0},{24,8},{32,16},{40,24},{48,32},{56,40},{64,... | collective-permute-start | bytes 786440 | tf_op jit(solution)/shard_map/ppermute | solution.py:32
  11.1 19.6 %collective-permute-start = (bf16[128,768]{1,0:T(8,128)(2,1)}, bf16[128,768]{1,0:T(8,128)(2,1)S(1)}, u32[]{:S(2)}, u32[]{:S(2)}) collective-permute-start(bf16[128,768]{1,0:T(8,128)(2,1)} %student.3), channel_id=1, source_target_pairs={{0,504},{8,0},{16,8},{24,16},{32,24},{40,32},{48,40},{56,48},{64,5... | collective-permute-start | bytes 589832 | tf_op jit(solution)/shard_map/ppermute | solution.py:32
  13.1 17.6 %collective-permute-start.1 = (bf16[128,768]{1,0:T(8,128)(2,1)}, bf16[128,768]{1,0:T(8,128)(2,1)S(1)}, u32[]{:S(2)}, u32[]{:S(2)}) collective-permute-start(bf16[128,768]{1,0:T(8,128)(2,1)} %student.3), channel_id=1, source_target_pairs={{0,496},{8,504},{16,0},{24,8},{32,16},{40,24},{48,32},{56,40},{64,... | collective-permute-start | bytes 589832 | tf_op jit(solution)/shard_map/ppermute | solution.py:32
  20.9 1.4 %copy-start = (bf16[768,1024]{1,0:T(8,128)(2,1)S(1)}, bf16[768,1024]{1,0:T(8,128)(2,1)}, u32[]{:S(2)}) copy-start(bf16[768,1024]{1,0:T(8,128)(2,1)} %weight.5) | copy-start | bytes 4718596
  22.3 0.9 copy-start.2
  23.3 0.9 copy-start.4
  24.2 6.5 %copy-start.1 = (bf16[768,1024]{1,0:T(8,128)(2,1)S(1)}, bf16[768,1024]{1,0:T(8,128)(2,1)}, u32[]{:S(2)}) copy-start(bf16[768,1024]{1,0:T(8,128)(2,1)} %weight.5) | copy-start | bytes 4718596
  24.2 6.5 %copy-start.3 = (bf16[128,1024]{1,0:T(8,128)(2,1)S(1)}, bf16[128,1024]{1,0:T(8,128)(2,1)}, u32[]{:S(2)}) copy-start(bf16[128,1024]{1,0:T(8,128)(2,1)} %teacher.5) | copy-start | bytes 786436
  30.7 5.4 %copy-start.8 = (s32[384]{0:T(512)S(1)}, s32[384]{0:T(512)}, u32[]{:S(2)}) copy-start(s32[384]{0:T(512)} %param.8) | copy-start | bytes 4612
  30.7 5.5 %copy-start.7 = (s32[2,384]{1,0:T(2,128)S(1)}, s32[2,384]{1,0:T(2,128)}, u32[]{:S(2)}) copy-start(s32[2,384]{1,0:T(2,128)} %param.9) | copy-start | bytes 9220
  32.5 30.8 %copy-start.5 = (bf16[128,768]{1,0:T(8,128)(2,1)S(1)}, bf16[128,768]{1,0:T(8,128)(2,1)}, u32[]{:S(2)}) copy-start(bf16[128,768]{1,0:T(8,128)(2,1)} %student.3) | copy-start | bytes 589828
  32.5 17.5 %all-to-all-start = ((f32[8,16,896]{2,1,0:T(8,128)}), f32[8,16,896]{2,1,0:T(8,128)S(1)}, u32[]{:S(2)}, u32[]{:S(2)}) async-start(f32[8,16,896]{2,1,0:T(8,128)} %tile.1), calls=%async_computation | async-start | bytes 917504 | tf_op jit(solution)/shard_map/all_to_all | solution.py:222
  50.0 0.8 copy-start.6
  66.8 30.8 %all-to-all-start.2 = ((bf16[8,96,1024]{2,1,0:T(8,128)(2,1)}), bf16[8,96,1024]{2,1,0:T(8,128)(2,1)}, u32[]{:S(2)}, u32[]{:S(2)}) async-start(bf16[8,96,1024]{2,1,0:T(8,128)(2,1)} %bitcast), calls=%async_computation.2 | async-start | bytes 3145728 | tf_op jit(solution)/shard_map/all_to_all | solution.py:252
  79.0 3.5 %collective-permute-start.5 = (bf16[4,96,384]{2,1,0:T(8,128)(2,1)S(1)}, bf16[4,96,384]{2,1,0:T(8,128)(2,1)S(1)}, u32[]{:S(2)}, u32[]{:S(2)}) collective-permute-start(bf16[4,96,384]{2,1,0:T(8,128)(2,1)S(1)} %convolution_convert_fusion), channel_id=1, source_target_pairs={{0,1},{1,0},{2,3},{3,2},{4,5},{5,4},{6,7},{7,6},{8,9},{9,8},{10,11... | collective-permute-start | bytes 884744 | tf_op jit(solution)/shard_map/ppermute | solution.py:274
  83.2 7.8 %collective-permute-start.6 = (bf16[2,96,384]{2,1,0:T(8,128)(2,1)S(1)}, bf16[2,96,384]{2,1,0:T(8,128)(2,1)S(1)}, u32[]{:S(2)}, u32[]{:S(2)}) collective-permute-start(bf16[2,96,384]{2,1,0:T(8,128)(2,1)S(1)} %fusion.6), channel_id=1, source_target_pairs={{0,2},{1,3},{2,0},{3,1},{4,6},{5,7},{6,4},{7,5},{8,10},{9,11},{10,... | collective-permute-start | bytes 442376 | tf_op jit(solution)/shard_map/ppermute | solution.py:274
  91.0 14.1 %collective-permute-start.7 = (bf16[1,96,384]{2,1,0:T(8,128)(2,1)S(1)}, bf16[1,96,384]{2,1,0:T(8,128)(2,1)S(1)}, u32[]{:S(2)}, u32[]{:S(2)}) collective-permute-start(bf16[1,96,384]{2,1,0:T(8,128)(2,1)S(1)} %dynamic-slice_convert_fusion), channel_id=1, source_target_pairs={{0,4},{1,5},{2,6},{3,7},{4,0},{5,1},{6,2},{7,3},{8,12},{9,13},{10,... | collective-permute-start | bytes 221192 | tf_op jit(solution)/shard_map/ppermute | solution.py:274
  100.0 16.7 %all-to-all-start.3 = ((bf16[4,24,1024]{2,1,0:T(8,128)(2,1)}), bf16[4,24,1024]{2,1,0:T(8,128)(2,1)S(1)}, u32[]{:S(2)}, u32[]{:S(2)}) async-start(bf16[4,24,1024]{2,1,0:T(8,128)(2,1)} %bitcast.1), calls=%async_computation.3 | async-start | bytes 393216 | tf_op jit(solution)/shard_map/all_to_all | solution.py:254
  105.1 16.2 %collective-permute-start.8 = (f32[96,128]{1,0:T(8,128)S(1)}, f32[96,128]{1,0:T(8,128)S(1)}, u32[]{:S(2)}, u32[]{:S(2)}) collective-permute-start(f32[96,128]{1,0:T(8,128)S(1)} %get-tuple-element.12), channel_id=1, source_target_pairs={{0,8},{8,16},{16,24},{24,32},{32,40},{40,48},{48,56},{56,64},{64,7... | collective-permute-start | bytes 147464 | tf_op jit(solution)/shard_map/ppermute | solution.py:32
  112.2 9.1 %collective-permute-start.9 = (f32[96,128]{1,0:T(8,128)S(1)}, f32[96,128]{1,0:T(8,128)S(1)}, u32[]{:S(2)}, u32[]{:S(2)}) collective-permute-start(f32[96,128]{1,0:T(8,128)S(1)} %get-tuple-element.13), channel_id=1, source_target_pairs={{0,16},{8,24},{16,32},{24,40},{32,48},{40,56},{48,64},{56,72},{64,... | collective-permute-start | bytes 147464 | tf_op jit(solution)/shard_map/ppermute | solution.py:32
  116.8 10.7 %collective-permute-start.4 = (f32[12,1024]{1,0:T(8,128)S(1)}, f32[12,1024]{1,0:T(8,128)S(1)}, u32[]{:S(2)}, u32[]{:S(2)}) collective-permute-start(f32[12,1024]{1,0:T(8,128)S(1)} %slice_select_fusion), channel_id=1, source_target_pairs={{0,8},{8,0},{1,9},{9,1},{2,10},{10,2},{3,11},{11,3},{4,12},{12,4},... | collective-permute-start | bytes 147464 | tf_op jit(solution)/shard_map/ppermute | solution.py:258

commit v10 on v9

--- a/solution.py
+++ b/solution.py
@@ -148,8 +148,8 @@
 
 
 def grad_kernel(
-    sizes, gathered, weight, teacher, student, near_student, far_student,
-    rows_grad, grad_w,
+    sizes, core, gathered, weight, teacher, student, near_student, far_student,
+    sent, kept, grad_w, rows_grad, share, sem,
 ):
     z_size, x_size, _ = sizes
     texts = student.shape[0]
@@ -172,7 +172,15 @@
         total = total + dot(rows[...], rows_grad[piece, :], (0, 0))
     step = total.shape[0] // (z_size * x_size)
     starts = [(z * x_size + x) * step for x in range(x_size) for z in range(z_size)]
-    grad_w[...] = jnp.concatenate([total[r : r + step] for r in starts], 0).astype(bf16)
+    share[...] = jnp.concatenate([total[r : r + step] for r in starts], 0).astype(bf16)
+    copy = pltpu.make_async_copy(share, grad_w, sem)
+    copy.start()
+    pairs, height, _ = kept.shape
+    back = dot(weight[...], rows_grad[...], (1, 1)).reshape(pairs, 2, height, band)
+    first = core[0] == 0
+    sent[...] = jnp.where(first, back[:, 1], back[:, 0]).astype(bf16)
+    kept[...] = jnp.where(first, back[:, 0], back[:, 1])
+    copy.wait()
 
 
 def shards(student, proj_weight, teacher, anchors, pairs, *, sizes):
@@ -238,16 +246,30 @@
     )(parts, ids)
     gathered = lax.all_to_all(tiles, "feat", 0, 0)
 
-    rows_grad, grad_w = pl.pallas_call(
+    height = features // n_feat
+    half_shape = (n_feat // 2, height, band)
+    vector = pl.BlockSpec(memory_space=pltpu.VMEM)
+    sent, back, grad_w = pl.pallas_call(
         functools.partial(grad_kernel, sizes),
+        in_specs=[pl.BlockSpec(memory_space=pltpu.SMEM)] + [vector] * 6,
+        out_specs=(vector, vector, pl.BlockSpec(memory_space=pl.ANY)),
         out_shape=(
-            jax.ShapeDtypeStruct((band, width), bf16),
+            jax.ShapeDtypeStruct(half_shape, bf16),
+            jax.ShapeDtypeStruct(half_shape, f32),
             jax.ShapeDtypeStruct((features, width), bf16),
         ),
+        scratch_shapes=[
+            pltpu.VMEM((band, width), bf16),
+            pltpu.VMEM((features, width), bf16),
+            pltpu.SemaphoreType.DMA,
+        ],
         compiler_params=params,
         cost_estimate=cost(10**9),
         name="grad",
-    )(gathered, proj_weight, teacher, student, near_student, far_student)
+    )(
+        (feat & 1).astype(jnp.int32).reshape(1),
+        gathered, proj_weight, teacher, student, near_student, far_student,
+    )
 
     grad_w = lax.all_to_all(grad_w.reshape(x_size, features // x_size, width), "x", 0, 0)
     grad_w = jnp.sum(grad_w.astype(f32), 0).astype(bf16)
@@ -259,27 +281,16 @@
         jnp.where(first, upper, lower), "yh", [(0, 1), (1, 0)]
     )
 
-    height = features // n_feat
-    halves = proj_weight.reshape(n_feat // 2, 2, height, width)
-
-    def half(array, which, axis):
-        return lax.dynamic_index_in_dim(array, which, axis, keepdims=False)
-
-    def half_back(which):
-        weight = half(halves, which, 1).reshape(features // 2, width)
-        return dot(weight, rows_grad, (1, 1)).reshape(n_feat // 2, height, band)
-
     def swapped(array, bit):
         perm = [(i, i ^ (1 << bit)) for i in range(n_feat)]
-        return lax.ppermute(array.astype(bf16), "feat", perm).astype(f32)
-
-    mine = feat & 1
-    back = swapped(half_back(1 - mine), 0)
-    back = half_back(mine) + back
+        return lax.ppermute(array, "feat", perm).astype(f32)
+
+    back = back + swapped(sent, 0)
     for bit in range(1, n_feat.bit_length() - 1):
         back = back.reshape(-1, 2, height, band)
         mine = (feat >> bit) & 1
-        back = half(back, mine, 1) + swapped(half(back, 1 - mine, 1), bit)
+        sent = lax.dynamic_index_in_dim(back, 1 - mine, 1, keepdims=False).astype(bf16)
+        back = lax.dynamic_index_in_dim(back, mine, 1, keepdims=False) + swapped(sent, bit)
     back = back.reshape(height, band)
     grad_student = back[:, :texts]
     for s in range(1, STEPS):

time: 129 us -> 128 us (level)
  blocking collectives: 10.1 us -> 0 us
  waiting for transfers between devices: 35.3 us -> 42.1 us
  starting transfers between devices: 63.7 us -> 67 us
    all_to_all x1 -> x0, blocking collectives: 10.1 us -> none  [shards(): gathered = lax.all_to_all(tiles, 'feat', 0, 0)]
    all_to_all x0 -> x1, waiting for transfers between devices: none -> 6.71 us  [shards(): gathered = lax.all_to_all(tiles, 'feat', 0, 0)]
    all_to_all x0 -> x1, starting transfers between devices: none -> 3.37 us  [shards(): gathered = lax.all_to_all(tiles, 'feat', 0, 0)]
    reduce_sum x1, other arithmetic: 2.41 us -> 0.98 us  [shards(): grad_w = jnp.sum(grad_w.astype(f32), 0).astype(bf16)]
  transfers between devices with their start and end apart: 13 -> 14, of which waited for: 6 -> 7; matrix products, arithmetic and copies ran while one was open for 4% -> 3% of each run, Pallas kernels for 0% -> 0%
where the time goes in v10:
time: 128 us; the launch traced here: 127 us
  starting transfers between devices  67 us (52%)
  waiting for transfers between devices  42.1 us (33%)
  Pallas kernels  9.11 us (7%)
  local copies, waits for them, and re-layouts  4.21 us (3%)
  other arithmetic  4.03 us (3%)
    ppermute x6, starting transfers between devices, passed_along(): lax.ppermute(array, DP, [(i, (i + by) % peers) for i in range(peers)])  32.6 us
    all_to_all x1, waiting for transfers between devices, shards(): parts = lax.all_to_all(parts, 'feat', 0, 0)  13.1 us
    all_to_all x1, starting transfers between devices, shards(): lax.all_to_all(grad_w.reshape(x_size, features // x_size, width), 'x', 0, 0)  10.9 us
    ppermute x3, starting transfers between devices, swapped(): return lax.ppermute(array, 'feat', perm).astype(f32)  6.97 us
    all_to_all x1, waiting for transfers between devices, shards(): gathered = lax.all_to_all(tiles, 'feat', 0, 0)  6.71 us
    ppermute x3, waiting for transfers between devices, swapped(): return lax.ppermute(array, 'feat', perm).astype(f32)  6.63 us
    ppermute x6, waiting for transfers between devices, passed_along(): lax.ppermute(array, DP, [(i, (i + by) % peers) for i in range(peers)])  5.85 us
    ppermute x1, waiting for transfers between devices, shards(): lax.ppermute(jnp.where(first, upper, lower), 'yh', [(0, 1), (1, 0)])  5.49 us
  transfers between devices with their start and end apart: 14, of which 7 were waited for; matrix products, arithmetic and copies ran while one was open for 3% of the time, Pallas kernels for 0%

profile of v10, /device:TPU:6, one launch (start us, length us, event | category | flops | bytes accessed | tf_op | source)
XLA Modules:
  0.0 127.4 jit_solution(7659172348955618250)
XLA Ops:
  0.6 8.0 %collective-permute-start.2 = (bf16[128,1024]{1,0:T(8,128)(2,1)}, bf16[128,1024]{1,0:T(8,128)(2,1)S(1)}, u32[]{:S(2)}, u32[]{:S(2)}) collective-permute-start(bf16[128,1024]{1,0:T(8,128)(2,1)} %teacher.5), channel_id=1, source_target_pairs={{0,504},{8,0},{16,8},{24,16},{32,24},{40,32},{48,40},{56,48},{64,5... | collective-permute-start | bytes 786440 | tf_op jit(solution)/shard_map/ppermute | solution.py:32
  8.6 2.4 %collective-permute-start.3 = (bf16[128,1024]{1,0:T(8,128)(2,1)}, bf16[128,1024]{1,0:T(8,128)(2,1)S(1)}, u32[]{:S(2)}, u32[]{:S(2)}) collective-permute-start(bf16[128,1024]{1,0:T(8,128)(2,1)} %teacher.5), channel_id=1, source_target_pairs={{0,496},{8,504},{16,0},{24,8},{32,16},{40,24},{48,32},{56,40},{64,... | collective-permute-start | bytes 786440 | tf_op jit(solution)/shard_map/ppermute | solution.py:32
  11.1 2.0 %collective-permute-start = (bf16[128,768]{1,0:T(8,128)(2,1)}, bf16[128,768]{1,0:T(8,128)(2,1)S(1)}, u32[]{:S(2)}, u32[]{:S(2)}) collective-permute-start(bf16[128,768]{1,0:T(8,128)(2,1)} %student.3), channel_id=1, source_target_pairs={{0,504},{8,0},{16,8},{24,16},{32,24},{40,32},{48,40},{56,48},{64,5... | collective-permute-start | bytes 589832 | tf_op jit(solution)/shard_map/ppermute | solution.py:32
  13.1 7.8 %collective-permute-start.1 = (bf16[128,768]{1,0:T(8,128)(2,1)}, bf16[128,768]{1,0:T(8,128)(2,1)S(1)}, u32[]{:S(2)}, u32[]{:S(2)}) collective-permute-start(bf16[128,768]{1,0:T(8,128)(2,1)} %student.3), channel_id=1, source_target_pairs={{0,496},{8,504},{16,0},{24,8},{32,16},{40,24},{48,32},{56,40},{64,... | collective-permute-start | bytes 589832 | tf_op jit(solution)/shard_map/ppermute | solution.py:32
  24.8 5.8 %collective-permute-done.near_student = bf16[128,768]{1,0:T(8,128)(2,1)S(1)} collective-permute-done((bf16[128,768]{1,0:T(8,128)(2,1)}, bf16[128,768]{1,0:T(8,128)(2,1)S(1)}, u32[]{:S(2)}, u32[]{:S(2)}) %collective-permute-start) | collective-permute-done | bytes 196640 | tf_op jit(solution)/shard_map/ppermute | solution.py:32
  30.7 1.8 %tile.1 = f32[8,16,896]{2,1,0:T(8,128)} custom-call(bf16[128,1024]{1,0:T(8,128)(2,1)S(1)} %get-tuple-element.8.proj_own, bf16[768,1024]{1,0:T(8,128)(2,1)S(1)} %copy-done.1, bf16[128,1024]{1,0:T(8,128)(2,1)S(1)} %copy-done.3, f32[128,256]{1,0:T(8,128)S(1)} %get-tuple-element.9.tiles, f32[8,128]{1,0:T(8,128)S(1)} %get-tuple-element.10.sums, ...), custom_call_target="tpu_custom_call" | custom-call | flops 600000000 | bytes 3000000 | tf_op jit(solution)/shard_map/tile/pallas_call | solution.py:220
  32.5 3.6 %all-to-all-start = ((f32[8,16,896]{2,1,0:T(8,128)}), f32[8,16,896]{2,1,0:T(8,128)S(1)}, u32[]{:S(2)}, u32[]{:S(2)}) async-start(f32[8,16,896]{2,1,0:T(8,128)} %tile.1), calls=%async_computation | async-start | bytes 917504 | tf_op jit(solution)/shard_map/all_to_all | solution.py:230
  36.9 13.1 %all-to-all-done.parts = f32[8,16,896]{2,1,0:T(8,128)S(1)} async-done(((f32[8,16,896]{2,1,0:T(8,128)}), f32[8,16,896]{2,1,0:T(8,128)S(1)}, u32[]{:S(2)}, u32[]{:S(2)}) %all-to-all-start) | async-done | bytes 458784 | tf_op jit(solution)/shard_map/all_to_all | solution.py:230
  50.8 2.4 %band.1 = bf16[8,16,512]{2,1,0:T(8,128)(2,1)} custom-call(f32[8,16,896]{2,1,0:T(8,128)} %copy-done.6, s32[8,384]{1,0:T(8,128)} %add_add_fusion.ids), custom_call_target="tpu_custom_call" | custom-call | flops 100000000 | bytes 3000000 | tf_op jit(solution)/shard_map/band/pallas_call | solution.py:241
  53.2 3.4 %all-to-all-start.1 = ((bf16[8,16,512]{2,1,0:T(8,128)(2,1)}), bf16[8,16,512]{2,1,0:T(8,128)(2,1)S(1)}, u32[]{:S(2)}, u32[]{:S(2)}) async-start(bf16[8,16,512]{2,1,0:T(8,128)(2,1)} %band.1), calls=%async_computation.1 | async-start | bytes 262144 | tf_op jit(solution)/shard_map/all_to_all | solution.py:247
  56.6 6.7 %all-to-all-done.1.gathered = bf16[8,16,512]{2,1,0:T(8,128)(2,1)S(1)} async-done(((bf16[8,16,512]{2,1,0:T(8,128)(2,1)}), bf16[8,16,512]{2,1,0:T(8,128)(2,1)S(1)}, u32[]{:S(2)}, u32[]{:S(2)}) %all-to-all-start.1) | async-done | bytes 131104 | tf_op jit(solution)/shard_map/all_to_all | solution.py:247
  63.3 4.3 %grad.1 = (bf16[4,96,384]{2,1,0:T(8,128)(2,1)S(1)}, f32[4,96,384]{2,1,0:T(8,128)S(1)}, bf16[768,1024]{1,0:T(8,128)(2,1)}) custom-call(s32[1]{0:T(128)} %bitcast.core, bf16[8,16,512]{2,1,0:T(8,128)(2,1)S(1)} %all-to-all-done.1.gathered, bf16[768,1024]{1,0:T(8,128)(2,1)S(1)} %copy-done.1, bf16[128,1024]{1,0:T(8,128)(2,1)S(1)} %copy-done.3, ...), custom_call_target="tpu_custom_call" | custom-call | flops 1000000000 | bytes 3000000 | tf_op jit(solution)/shard_map/grad/pallas_call | solution.py:252
  67.6 10.9 %all-to-all-start.2 = ((bf16[8,96,1024]{2,1,0:T(8,128)(2,1)}), bf16[8,96,1024]{2,1,0:T(8,128)(2,1)S(1)}, u32[]{:S(2)}, u32[]{:S(2)}) async-start(bf16[8,96,1024]{2,1,0:T(8,128)(2,1)} %bitcast.1), calls=%async_computation.2 | async-start | bytes 3145728 | tf_op jit(solution)/shard_map/all_to_all | solution.py:274
  78.5 1.9 %collective-permute-start.5 = (bf16[4,96,384]{2,1,0:T(8,128)(2,1)S(1)}, bf16[4,96,384]{2,1,0:T(8,128)(2,1)}, u32[]{:S(2)}, u32[]{:S(2)}) collective-permute-start(bf16[4,96,384]{2,1,0:T(8,128)(2,1)S(1)} %get-tuple-element.13), channel_id=1, source_target_pairs={{0,1},{1,0},{2,3},{3,2},{4,5},{5,4},{6,7},{7,6},{8,9},{9,8},{10,11... | collective-permute-start | bytes 884744 | tf_op jit(solution)/shard_map/ppermute | solution.py:286
  80.5 1.7 %collective-permute-done.5 = bf16[4,96,384]{2,1,0:T(8,128)(2,1)} collective-permute-done((bf16[4,96,384]{2,1,0:T(8,128)(2,1)S(1)}, bf16[4,96,384]{2,1,0:T(8,128)(2,1)}, u32[]{:S(2)}, u32[]{:S(2)}) %collective-permute-start.5) | collective-permute-done | bytes 294944 | tf_op jit(solution)/shard_map/ppermute | solution.py:286
  83.2 2.8 %collective-permute-start.6 = (bf16[2,96,384]{2,1,0:T(8,128)(2,1)S(1)}, bf16[2,96,384]{2,1,0:T(8,128)(2,1)S(1)}, u32[]{:S(2)}, u32[]{:S(2)}) collective-permute-start(bf16[2,96,384]{2,1,0:T(8,128)(2,1)S(1)} %fusion), channel_id=1, source_target_pairs={{0,2},{1,3},{2,0},{3,1},{4,6},{5,7},{6,4},{7,5},{8,10},{9,11},{10,... | collective-permute-start | bytes 442376 | tf_op jit(solution)/shard_map/ppermute | solution.py:286
  86.0 5.0 %collective-permute-done.6 = bf16[2,96,384]{2,1,0:T(8,128)(2,1)S(1)} collective-permute-done((bf16[2,96,384]{2,1,0:T(8,128)(2,1)S(1)}, bf16[2,96,384]{2,1,0:T(8,128)(2,1)S(1)}, u32[]{:S(2)}, u32[]{:S(2)}) %collective-permute-start.6) | collective-permute-done | bytes 147488 | tf_op jit(solution)/shard_map/ppermute | solution.py:286
  91.0 2.2 %collective-permute-start.7 = (bf16[1,96,384]{2,1,0:T(8,128)(2,1)S(1)}, bf16[1,96,384]{2,1,0:T(8,128)(2,1)S(1)}, u32[]{:S(2)}, u32[]{:S(2)}) collective-permute-start(bf16[1,96,384]{2,1,0:T(8,128)(2,1)S(1)} %dynamic-slice_convert_fusion), channel_id=1, source_target_pairs={{0,4},{1,5},{2,6},{3,7},{4,0},{5,1},{6,2},{7,3},{8,12},{9,13},{10,... | collective-permute-start | bytes 221192 | tf_op jit(solution)/shard_map/ppermute | solution.py:286
  93.3 4.3 %all-to-all-done.2 = bf16[8,96,1024]{2,1,0:T(8,128)(2,1)S(1)} async-done(((bf16[8,96,1024]{2,1,0:T(8,128)(2,1)}), bf16[8,96,1024]{2,1,0:T(8,128)(2,1)S(1)}, u32[]{:S(2)}, u32[]{:S(2)}) %all-to-all-start.2) | async-done | bytes 1572896 | tf_op jit(solution)/shard_map/all_to_all | solution.py:274
  98.6 5.1 %all-to-all-start.3 = ((bf16[4,24,1024]{2,1,0:T(8,128)(2,1)}), bf16[4,24,1024]{2,1,0:T(8,128)(2,1)S(1)}, u32[]{:S(2)}, u32[]{:S(2)}) async-start(bf16[4,24,1024]{2,1,0:T(8,128)(2,1)} %bitcast.2), calls=%async_computation.3 | async-start | bytes 393216 | tf_op jit(solution)/shard_map/all_to_all | solution.py:276
  103.7 7.8 %collective-permute-start.8 = (f32[96,128]{1,0:T(8,128)S(1)}, f32[96,128]{1,0:T(8,128)S(1)}, u32[]{:S(2)}, u32[]{:S(2)}) collective-permute-start(f32[96,128]{1,0:T(8,128)S(1)} %get-tuple-element.14), channel_id=1, source_target_pairs={{0,8},{8,16},{16,24},{24,32},{32,40},{40,48},{48,56},{56,64},{64,7... | collective-permute-start | bytes 147464 | tf_op jit(solution)/shard_map/ppermute | solution.py:32
  111.5 4.5 %collective-permute-start.9 = (f32[96,128]{1,0:T(8,128)S(1)}, f32[96,128]{1,0:T(8,128)S(1)}, u32[]{:S(2)}, u32[]{:S(2)}) collective-permute-start(f32[96,128]{1,0:T(8,128)S(1)} %get-tuple-element.15), channel_id=1, source_target_pairs={{0,16},{8,24},{16,32},{24,40},{32,48},{40,56},{48,64},{56,72},{64,... | collective-permute-start | bytes 147464 | tf_op jit(solution)/shard_map/ppermute | solution.py:32
  116.1 4.5 %collective-permute-start.4 = (f32[12,1024]{1,0:T(8,128)S(1)}, f32[12,1024]{1,0:T(8,128)S(1)}, u32[]{:S(2)}, u32[]{:S(2)}) collective-permute-start(f32[12,1024]{1,0:T(8,128)S(1)} %slice_select_fusion), channel_id=1, source_target_pairs={{0,8},{8,0},{1,9},{9,1},{2,10},{10,2},{3,11},{11,3},{4,12},{12,4},... | collective-permute-start | bytes 147464 | tf_op jit(solution)/shard_map/ppermute | solution.py:280
  121.3 5.5 %collective-permute-done.4 = f32[12,1024]{1,0:T(8,128)S(1)} collective-permute-done((f32[12,1024]{1,0:T(8,128)S(1)}, f32[12,1024]{1,0:T(8,128)S(1)}, u32[]{:S(2)}, u32[]{:S(2)}) %collective-permute-start.4) | collective-permute-done | bytes 49184 | tf_op jit(solution)/shard_map/ppermute | solution.py:280
  (43 shorter events, 8.8 us)
Async XLA Ops:
  0.6 30.0 %collective-permute-start.2 = (bf16[128,1024]{1,0:T(8,128)(2,1)}, bf16[128,1024]{1,0:T(8,128)(2,1)S(1)}, u32[]{:S(2)}, u32[]{:S(2)}) collective-permute-start(bf16[128,1024]{1,0:T(8,128)(2,1)} %teacher.5), channel_id=1, source_target_pairs={{0,504},{8,0},{16,8},{24,16},{32,24},{40,32},{48,40},{56,48},{64,5... | collective-permute-start | bytes 786440 | tf_op jit(solution)/shard_map/ppermute | solution.py:32
  8.6 22.0 %collective-permute-start.3 = (bf16[128,1024]{1,0:T(8,128)(2,1)}, bf16[128,1024]{1,0:T(8,128)(2,1)S(1)}, u32[]{:S(2)}, u32[]{:S(2)}) collective-permute-start(bf16[128,1024]{1,0:T(8,128)(2,1)} %teacher.5), channel_id=1, source_target_pairs={{0,496},{8,504},{16,0},{24,8},{32,16},{40,24},{48,32},{56,40},{64,... | collective-permute-start | bytes 786440 | tf_op jit(solution)/shard_map/ppermute | solution.py:32
  11.1 19.6 %collective-permute-start = (bf16[128,768]{1,0:T(8,128)(2,1)}, bf16[128,768]{1,0:T(8,128)(2,1)S(1)}, u32[]{:S(2)}, u32[]{:S(2)}) collective-permute-start(bf16[128,768]{1,0:T(8,128)(2,1)} %student.3), channel_id=1, source_target_pairs={{0,504},{8,0},{16,8},{24,16},{32,24},{40,32},{48,40},{56,48},{64,5... | collective-permute-start | bytes 589832 | tf_op jit(solution)/shard_map/ppermute | solution.py:32
  13.1 17.6 %collective-permute-start.1 = (bf16[128,768]{1,0:T(8,128)(2,1)}, bf16[128,768]{1,0:T(8,128)(2,1)S(1)}, u32[]{:S(2)}, u32[]{:S(2)}) collective-permute-start(bf16[128,768]{1,0:T(8,128)(2,1)} %student.3), channel_id=1, source_target_pairs={{0,496},{8,504},{16,0},{24,8},{32,16},{40,24},{48,32},{56,40},{64,... | collective-permute-start | bytes 589832 | tf_op jit(solution)/shard_map/ppermute | solution.py:32
  20.9 1.4 %copy-start = (bf16[768,1024]{1,0:T(8,128)(2,1)S(1)}, bf16[768,1024]{1,0:T(8,128)(2,1)}, u32[]{:S(2)}) copy-start(bf16[768,1024]{1,0:T(8,128)(2,1)} %weight.5) | copy-start | bytes 4718596
  22.3 0.9 copy-start.2
  23.3 0.9 copy-start.4
  24.2 6.5 %copy-start.1 = (bf16[768,1024]{1,0:T(8,128)(2,1)S(1)}, bf16[768,1024]{1,0:T(8,128)(2,1)}, u32[]{:S(2)}) copy-start(bf16[768,1024]{1,0:T(8,128)(2,1)} %weight.5) | copy-start | bytes 4718596
  24.2 6.5 %copy-start.3 = (bf16[128,1024]{1,0:T(8,128)(2,1)S(1)}, bf16[128,1024]{1,0:T(8,128)(2,1)}, u32[]{:S(2)}) copy-start(bf16[128,1024]{1,0:T(8,128)(2,1)} %teacher.5) | copy-start | bytes 786436
  30.7 5.4 %copy-start.8 = (s32[384]{0:T(512)S(1)}, s32[384]{0:T(512)}, u32[]{:S(2)}) copy-start(s32[384]{0:T(512)} %param.8) | copy-start | bytes 4612
  30.7 5.5 %copy-start.7 = (s32[2,384]{1,0:T(2,128)S(1)}, s32[2,384]{1,0:T(2,128)}, u32[]{:S(2)}) copy-start(s32[2,384]{1,0:T(2,128)} %param.9) | copy-start | bytes 9220
  32.5 30.8 %copy-start.5 = (bf16[128,768]{1,0:T(8,128)(2,1)S(1)}, bf16[128,768]{1,0:T(8,128)(2,1)}, u32[]{:S(2)}) copy-start(bf16[128,768]{1,0:T(8,128)(2,1)} %student.3) | copy-start | bytes 589828
  32.5 17.5 %all-to-all-start = ((f32[8,16,896]{2,1,0:T(8,128)}), f32[8,16,896]{2,1,0:T(8,128)S(1)}, u32[]{:S(2)}, u32[]{:S(2)}) async-start(f32[8,16,896]{2,1,0:T(8,128)} %tile.1), calls=%async_computation | async-start | bytes 917504 | tf_op jit(solution)/shard_map/all_to_all | solution.py:230
  50.0 0.8 copy-start.6
  53.2 10.1 %all-to-all-start.1 = ((bf16[8,16,512]{2,1,0:T(8,128)(2,1)}), bf16[8,16,512]{2,1,0:T(8,128)(2,1)S(1)}, u32[]{:S(2)}, u32[]{:S(2)}) async-start(bf16[8,16,512]{2,1,0:T(8,128)(2,1)} %band.1), calls=%async_computation.1 | async-start | bytes 262144 | tf_op jit(solution)/shard_map/all_to_all | solution.py:247
  67.6 30.0 %all-to-all-start.2 = ((bf16[8,96,1024]{2,1,0:T(8,128)(2,1)}), bf16[8,96,1024]{2,1,0:T(8,128)(2,1)S(1)}, u32[]{:S(2)}, u32[]{:S(2)}) async-start(bf16[8,96,1024]{2,1,0:T(8,128)(2,1)} %bitcast.1), calls=%async_computation.2 | async-start | bytes 3145728 | tf_op jit(solution)/shard_map/all_to_all | solution.py:274
  78.5 3.6 %collective-permute-start.5 = (bf16[4,96,384]{2,1,0:T(8,128)(2,1)S(1)}, bf16[4,96,384]{2,1,0:T(8,128)(2,1)}, u32[]{:S(2)}, u32[]{:S(2)}) collective-permute-start(bf16[4,96,384]{2,1,0:T(8,128)(2,1)S(1)} %get-tuple-element.13), channel_id=1, source_target_pairs={{0,1},{1,0},{2,3},{3,2},{4,5},{5,4},{6,7},{7,6},{8,9},{9,8},{10,11... | collective-permute-start | bytes 884744 | tf_op jit(solution)/shard_map/ppermute | solution.py:286
  83.2 7.8 %collective-permute-start.6 = (bf16[2,96,384]{2,1,0:T(8,128)(2,1)S(1)}, bf16[2,96,384]{2,1,0:T(8,128)(2,1)S(1)}, u32[]{:S(2)}, u32[]{:S(2)}) collective-permute-start(bf16[2,96,384]{2,1,0:T(8,128)(2,1)S(1)} %fusion), channel_id=1, source_target_pairs={{0,2},{1,3},{2,0},{3,1},{4,6},{5,7},{6,4},{7,5},{8,10},{9,11},{10,... | collective-permute-start | bytes 442376 | tf_op jit(solution)/shard_map/ppermute | solution.py:286
  91.0 12.6 %collective-permute-start.7 = (bf16[1,96,384]{2,1,0:T(8,128)(2,1)S(1)}, bf16[1,96,384]{2,1,0:T(8,128)(2,1)S(1)}, u32[]{:S(2)}, u32[]{:S(2)}) collective-permute-start(bf16[1,96,384]{2,1,0:T(8,128)(2,1)S(1)} %dynamic-slice_convert_fusion), channel_id=1, source_target_pairs={{0,4},{1,5},{2,6},{3,7},{4,0},{5,1},{6,2},{7,3},{8,12},{9,13},{10,... | collective-permute-start | bytes 221192 | tf_op jit(solution)/shard_map/ppermute | solution.py:286
  98.6 17.4 %all-to-all-start.3 = ((bf16[4,24,1024]{2,1,0:T(8,128)(2,1)}), bf16[4,24,1024]{2,1,0:T(8,128)(2,1)S(1)}, u32[]{:S(2)}, u32[]{:S(2)}) async-start(bf16[4,24,1024]{2,1,0:T(8,128)(2,1)} %bitcast.2), calls=%async_computation.3 | async-start | bytes 393216 | tf_op jit(solution)/shard_map/all_to_all | solution.py:276
  103.7 16.9 %collective-permute-start.8 = (f32[96,128]{1,0:T(8,128)S(1)}, f32[96,128]{1,0:T(8,128)S(1)}, u32[]{:S(2)}, u32[]{:S(2)}) collective-permute-start(f32[96,128]{1,0:T(8,128)S(1)} %get-tuple-element.14), channel_id=1, source_target_pairs={{0,8},{8,16},{16,24},{24,32},{32,40},{40,48},{48,56},{56,64},{64,7... | collective-permute-start | bytes 147464 | tf_op jit(solution)/shard_map/ppermute | solution.py:32
  111.5 9.1 %collective-permute-start.9 = (f32[96,128]{1,0:T(8,128)S(1)}, f32[96,128]{1,0:T(8,128)S(1)}, u32[]{:S(2)}, u32[]{:S(2)}) collective-permute-start(f32[96,128]{1,0:T(8,128)S(1)} %get-tuple-element.15), channel_id=1, source_target_pairs={{0,16},{8,24},{16,32},{24,40},{32,48},{40,56},{48,64},{56,72},{64,... | collective-permute-start | bytes 147464 | tf_op jit(solution)/shard_map/ppermute | solution.py:32
  116.1 10.7 %collective-permute-start.4 = (f32[12,1024]{1,0:T(8,128)S(1)}, f32[12,1024]{1,0:T(8,128)S(1)}, u32[]{:S(2)}, u32[]{:S(2)}) collective-permute-start(f32[12,1024]{1,0:T(8,128)S(1)} %slice_select_fusion), channel_id=1, source_target_pairs={{0,8},{8,0},{1,9},{9,1},{2,10},{10,2},{3,11},{11,3},{4,12},{12,4},... | collective-permute-start | bytes 147464 | tf_op jit(solution)/shard_map/ppermute | solution.py:280

commit v11 on v10

--- a/solution.py
+++ b/solution.py
@@ -70,7 +70,7 @@
 
 def tile_kernel(
     proj_own, weight, teacher, tiles, sums, near_student, far_student, near_teacher, far_teacher,
-    payload,
+    payload, rows_in,
 ):
     peers, rows, _ = payload.shape
     texts = proj_own.shape[0]
@@ -81,14 +81,16 @@
 
     lay_out(0, tiles[:, :texts])
     lay_out(STEPS, tiles[:, texts:])
-    for s, rows_in, mates_in in (
-        (1, near_student, near_teacher),
-        (2, far_student, far_teacher),
-    ):
-        projected = dot(rows_in[...], weight[...], (1, 0))
+    rows_in[:texts, :] = near_student[...]
+    rows_in[texts:, :] = far_student[...]
+    projected = dot(rows_in[...], weight[...], (1, 0))
+    tile = dot(proj_own[...], projected.astype(bf16), (1, 1))
+    squares = projected * projected
+    for s, mates_in in ((1, near_teacher), (2, far_teacher)):
+        piece = slice((s - 1) * texts, s * texts)
         wide = mates_in[...].astype(f32)
-        tail = tail + [row_sums(projected * projected), row_sums(wide * wide)]
-        lay_out(s, dot(proj_own[...], projected.astype(bf16), (1, 1)))
+        tail = tail + [row_sums(squares[piece]), row_sums(wide * wide)]
+        lay_out(s, tile[:, piece])
         lay_out(STEPS + s, dot(teacher[...], mates_in[...], (1, 1)))
     tail = jnp.concatenate(tail + [jnp.zeros((rows - len(tail), texts), f32)], 0)
     for peer in range(peers):
@@ -149,38 +151,41 @@
 
 def grad_kernel(
     sizes, core, gathered, weight, teacher, student, near_student, far_student,
-    sent, kept, grad_w, rows_grad, share, sem,
+    sent, kept, grad_w, rows_in, rows_grad, share, sems,
 ):
     z_size, x_size, _ = sizes
     texts = student.shape[0]
     band = STEPS * texts
-    rows_in = (student, near_student, far_student)
-    projected = [dot(rows[...], weight[...], (1, 0)).astype(bf16) for rows in rows_in]
+    for s, rows in enumerate((student, near_student, far_student)):
+        rows_in[s * texts : (s + 1) * texts, :] = rows[...]
+    projected = dot(rows_in[...], weight[...], (1, 0)).astype(bf16)
     tile = gathered[:, :, :band].reshape(texts, band)
     tail = jnp.sum(gathered[:, :, band:].astype(f32), 0)
     tail = [tail[2 * r : 2 * r + 1] + tail[2 * r + 1 : 2 * r + 2] for r in range(STEPS + 1)]
-    terms = []
-    for s in range(STEPS):
-        tile_s = tile[:, s * texts : (s + 1) * texts]
-        terms.append(dot(tile_s, projected[0], (0, 0)) - upright(tail[s]) * projected[s].astype(f32))
-        terms[0] = terms[0] + dot(tile_s, projected[s], (1, 0))
-    terms[0] = terms[0] - upright(tail[STEPS]) * teacher[...].astype(f32)
-    total = 0.0
-    for s, rows in enumerate(rows_in):
-        piece = slice(s * texts, (s + 1) * texts)
-        rows_grad[piece, :] = (LOSS_SCALE * terms[s]).astype(bf16)
-        total = total + dot(rows[...], rows_grad[piece, :], (0, 0))
-    step = total.shape[0] // (z_size * x_size)
+    scale = jnp.concatenate([upright(tail[s]) for s in range(STEPS)], 0)
+    terms = dot(tile, projected[:texts], (0, 0)) - scale * projected.astype(f32)
+    own = dot(tile, projected, (1, 0)) - upright(tail[STEPS]) * teacher[...].astype(f32)
+    rows_grad[:texts, :] = (LOSS_SCALE * (terms[:texts] + own)).astype(bf16)
+    rows_grad[texts:, :] = (LOSS_SCALE * terms[texts:]).astype(bf16)
+    features, width = share.shape
+    step = features // (z_size * x_size)
     starts = [(z * x_size + x) * step for x in range(x_size) for z in range(z_size)]
-    share[...] = jnp.concatenate([total[r : r + step] for r in starts], 0).astype(bf16)
-    copy = pltpu.make_async_copy(share, grad_w, sem)
-    copy.start()
+    copies = []
+    for h in range(2):
+        columns = slice(h * (width // 2), (h + 1) * (width // 2))
+        total = dot(rows_in[...], rows_grad[:, columns], (0, 0))
+        share[:, columns] = jnp.concatenate([total[r : r + step] for r in starts], 0).astype(bf16)
+        copies.append(
+            pltpu.make_async_copy(share.at[:, columns], grad_w.at[:, columns], sems.at[h])
+        )
+        copies[h].start()
     pairs, height, _ = kept.shape
     back = dot(weight[...], rows_grad[...], (1, 1)).reshape(pairs, 2, height, band)
     first = core[0] == 0
     sent[...] = jnp.where(first, back[:, 1], back[:, 0]).astype(bf16)
     kept[...] = jnp.where(first, back[:, 0], back[:, 1])
-    copy.wait()
+    for copy in copies:
+        copy.wait()
 
 
 def shards(student, proj_weight, teacher, anchors, pairs, *, sizes):
@@ -219,6 +224,7 @@
 
     parts = pl.pallas_call(
         tile_kernel,
+        scratch_shapes=[pltpu.VMEM(((STEPS - 1) * texts, features), bf16)],
         out_shape=jax.ShapeDtypeStruct((n_feat, rows, (2 * STEPS + 1) * texts), f32),
         compiler_params=params,
         cost_estimate=cost(6 * 10**8),
@@ -259,9 +265,10 @@
             jax.ShapeDtypeStruct((features, width), bf16),
         ),
         scratch_shapes=[
+            pltpu.VMEM((band, features), bf16),
             pltpu.VMEM((band, width), bf16),
             pltpu.VMEM((features, width), bf16),
-            pltpu.SemaphoreType.DMA,
+            pltpu.SemaphoreType.DMA((2,)),
         ],
         compiler_params=params,
         cost_estimate=cost(10**9),

time: 128 us -> 127 us (level)
  Pallas kernels: 9.11 us -> 7.73 us
where the time goes in v11:
time: 127 us; the launch traced here: 126 us
  starting transfers between devices  67 us (53%)
  waiting for transfers between devices  42.1 us (33%)
  Pallas kernels  7.73 us (6%)
  local copies, waits for them, and re-layouts  4.21 us (3%)
  other arithmetic  4.03 us (3%)
    ppermute x6, starting transfers between devices, passed_along(): lax.ppermute(array, DP, [(i, (i + by) % peers) for i in range(peers)])  32.6 us
    all_to_all x1, waiting for transfers between devices, shards(): parts = lax.all_to_all(parts, 'feat', 0, 0)  13.1 us
    all_to_all x1, starting transfers between devices, shards(): lax.all_to_all(grad_w.reshape(x_size, features // x_size, width), 'x', 0, 0)  11 us
    ppermute x3, starting transfers between devices, swapped(): return lax.ppermute(array, 'feat', perm).astype(f32)  6.94 us
    all_to_all x1, waiting for transfers between devices, shards(): gathered = lax.all_to_all(tiles, 'feat', 0, 0)  6.71 us
    ppermute x3, waiting for transfers between devices, swapped(): return lax.ppermute(array, 'feat', perm).astype(f32)  6.65 us
    ppermute x6, waiting for transfers between devices, passed_along(): lax.ppermute(array, DP, [(i, (i + by) % peers) for i in range(peers)])  5.85 us
    ppermute x1, waiting for transfers between devices, shards(): lax.ppermute(jnp.where(first, upper, lower), 'yh', [(0, 1), (1, 0)])  5.49 us
  transfers between devices with their start and end apart: 14, of which 7 were waited for; matrix products, arithmetic and copies ran while one was open for 3% of the time, Pallas kernels for 0%

profile of v11, /device:TPU:6, one launch (start us, length us, event | category | flops | bytes accessed | tf_op | source)
XLA Modules:
  0.0 126.0 jit_solution(12821797141224123988)
XLA Ops:
  0.6 8.0 %collective-permute-start.2 = (bf16[128,1024]{1,0:T(8,128)(2,1)}, bf16[128,1024]{1,0:T(8,128)(2,1)S(1)}, u32[]{:S(2)}, u32[]{:S(2)}) collective-permute-start(bf16[128,1024]{1,0:T(8,128)(2,1)} %teacher.5), channel_id=1, source_target_pairs={{0,504},{8,0},{16,8},{24,16},{32,24},{40,32},{48,40},{56,48},{64,5... | collective-permute-start | bytes 786440 | tf_op jit(solution)/shard_map/ppermute | solution.py:32
  8.6 2.4 %collective-permute-start.3 = (bf16[128,1024]{1,0:T(8,128)(2,1)}, bf16[128,1024]{1,0:T(8,128)(2,1)S(1)}, u32[]{:S(2)}, u32[]{:S(2)}) collective-permute-start(bf16[128,1024]{1,0:T(8,128)(2,1)} %teacher.5), channel_id=1, source_target_pairs={{0,496},{8,504},{16,0},{24,8},{32,16},{40,24},{48,32},{56,40},{64,... | collective-permute-start | bytes 786440 | tf_op jit(solution)/shard_map/ppermute | solution.py:32
  11.1 2.0 %collective-permute-start = (bf16[128,768]{1,0:T(8,128)(2,1)}, bf16[128,768]{1,0:T(8,128)(2,1)S(1)}, u32[]{:S(2)}, u32[]{:S(2)}) collective-permute-start(bf16[128,768]{1,0:T(8,128)(2,1)} %student.3), channel_id=1, source_target_pairs={{0,504},{8,0},{16,8},{24,16},{32,24},{40,32},{48,40},{56,48},{64,5... | collective-permute-start | bytes 589832 | tf_op jit(solution)/shard_map/ppermute | solution.py:32
  13.1 7.8 %collective-permute-start.1 = (bf16[128,768]{1,0:T(8,128)(2,1)}, bf16[128,768]{1,0:T(8,128)(2,1)S(1)}, u32[]{:S(2)}, u32[]{:S(2)}) collective-permute-start(bf16[128,768]{1,0:T(8,128)(2,1)} %student.3), channel_id=1, source_target_pairs={{0,496},{8,504},{16,0},{24,8},{32,16},{40,24},{48,32},{56,40},{64,... | collective-permute-start | bytes 589832 | tf_op jit(solution)/shard_map/ppermute | solution.py:32
  24.8 5.8 %collective-permute-done.near_student = bf16[128,768]{1,0:T(8,128)(2,1)S(1)} collective-permute-done((bf16[128,768]{1,0:T(8,128)(2,1)}, bf16[128,768]{1,0:T(8,128)(2,1)S(1)}, u32[]{:S(2)}, u32[]{:S(2)}) %collective-permute-start) | collective-permute-done | bytes 196640 | tf_op jit(solution)/shard_map/ppermute | solution.py:32
  30.7 1.6 %tile.1 = f32[8,16,896]{2,1,0:T(8,128)} custom-call(bf16[128,1024]{1,0:T(8,128)(2,1)S(1)} %get-tuple-element.8.proj_own, bf16[768,1024]{1,0:T(8,128)(2,1)S(1)} %copy-done.1, bf16[128,1024]{1,0:T(8,128)(2,1)S(1)} %copy-done.3, f32[128,256]{1,0:T(8,128)S(1)} %get-tuple-element.9.tiles, f32[8,128]{1,0:T(8,128)S(1)} %get-tuple-element.10.sums, ...), custom_call_target="tpu_custom_call" | custom-call | flops 600000000 | bytes 3000000 | tf_op jit(solution)/shard_map/tile/pallas_call | solution.py:225
  32.4 3.6 %all-to-all-start = ((f32[8,16,896]{2,1,0:T(8,128)}), f32[8,16,896]{2,1,0:T(8,128)S(1)}, u32[]{:S(2)}, u32[]{:S(2)}) async-start(f32[8,16,896]{2,1,0:T(8,128)} %tile.1), calls=%async_computation | async-start | bytes 917504 | tf_op jit(solution)/shard_map/all_to_all | solution.py:236
  36.8 13.1 %all-to-all-done.parts = f32[8,16,896]{2,1,0:T(8,128)S(1)} async-done(((f32[8,16,896]{2,1,0:T(8,128)}), f32[8,16,896]{2,1,0:T(8,128)S(1)}, u32[]{:S(2)}, u32[]{:S(2)}) %all-to-all-start) | async-done | bytes 458784 | tf_op jit(solution)/shard_map/all_to_all | solution.py:236
  50.6 2.4 %band.1 = bf16[8,16,512]{2,1,0:T(8,128)(2,1)} custom-call(f32[8,16,896]{2,1,0:T(8,128)} %copy-done.6, s32[8,384]{1,0:T(8,128)} %add_add_fusion.ids), custom_call_target="tpu_custom_call" | custom-call | flops 100000000 | bytes 3000000 | tf_op jit(solution)/shard_map/band/pallas_call | solution.py:247
  53.1 3.4 %all-to-all-start.1 = ((bf16[8,16,512]{2,1,0:T(8,128)(2,1)}), bf16[8,16,512]{2,1,0:T(8,128)(2,1)S(1)}, u32[]{:S(2)}, u32[]{:S(2)}) async-start(bf16[8,16,512]{2,1,0:T(8,128)(2,1)} %band.1), calls=%async_computation.1 | async-start | bytes 262144 | tf_op jit(solution)/shard_map/all_to_all | solution.py:253
  56.4 6.7 %all-to-all-done.1.gathered = bf16[8,16,512]{2,1,0:T(8,128)(2,1)S(1)} async-done(((bf16[8,16,512]{2,1,0:T(8,128)(2,1)}), bf16[8,16,512]{2,1,0:T(8,128)(2,1)S(1)}, u32[]{:S(2)}, u32[]{:S(2)}) %all-to-all-start.1) | async-done | bytes 131104 | tf_op jit(solution)/shard_map/all_to_all | solution.py:253
  63.2 3.1 %grad.1 = (bf16[4,96,384]{2,1,0:T(8,128)(2,1)S(1)}, f32[4,96,384]{2,1,0:T(8,128)S(1)}, bf16[768,1024]{1,0:T(8,128)(2,1)}) custom-call(s32[1]{0:T(128)} %bitcast.core, bf16[8,16,512]{2,1,0:T(8,128)(2,1)S(1)} %all-to-all-done.1.gathered, bf16[768,1024]{1,0:T(8,128)(2,1)S(1)} %copy-done.1, bf16[128,1024]{1,0:T(8,128)(2,1)S(1)} %copy-done.3, ...), custom_call_target="tpu_custom_call" | custom-call | flops 1000000000 | bytes 3000000 | tf_op jit(solution)/shard_map/grad/pallas_call | solution.py:258
  66.2 11.0 %all-to-all-start.2 = ((bf16[8,96,1024]{2,1,0:T(8,128)(2,1)}), bf16[8,96,1024]{2,1,0:T(8,128)(2,1)S(1)}, u32[]{:S(2)}, u32[]{:S(2)}) async-start(bf16[8,96,1024]{2,1,0:T(8,128)(2,1)} %bitcast.1), calls=%async_computation.2 | async-start | bytes 3145728 | tf_op jit(solution)/shard_map/all_to_all | solution.py:281
  77.2 1.9 %collective-permute-start.5 = (bf16[4,96,384]{2,1,0:T(8,128)(2,1)S(1)}, bf16[4,96,384]{2,1,0:T(8,128)(2,1)}, u32[]{:S(2)}, u32[]{:S(2)}) collective-permute-start(bf16[4,96,384]{2,1,0:T(8,128)(2,1)S(1)} %get-tuple-element.13), channel_id=1, source_target_pairs={{0,1},{1,0},{2,3},{3,2},{4,5},{5,4},{6,7},{7,6},{8,9},{9,8},{10,11... | collective-permute-start | bytes 884744 | tf_op jit(solution)/shard_map/ppermute | solution.py:293
  79.1 1.7 %collective-permute-done.5 = bf16[4,96,384]{2,1,0:T(8,128)(2,1)} collective-permute-done((bf16[4,96,384]{2,1,0:T(8,128)(2,1)S(1)}, bf16[4,96,384]{2,1,0:T(8,128)(2,1)}, u32[]{:S(2)}, u32[]{:S(2)}) %collective-permute-start.5) | collective-permute-done | bytes 294944 | tf_op jit(solution)/shard_map/ppermute | solution.py:293
  81.8 2.8 %collective-permute-start.6 = (bf16[2,96,384]{2,1,0:T(8,128)(2,1)S(1)}, bf16[2,96,384]{2,1,0:T(8,128)(2,1)S(1)}, u32[]{:S(2)}, u32[]{:S(2)}) collective-permute-start(bf16[2,96,384]{2,1,0:T(8,128)(2,1)S(1)} %fusion), channel_id=1, source_target_pairs={{0,2},{1,3},{2,0},{3,1},{4,6},{5,7},{6,4},{7,5},{8,10},{9,11},{10,... | collective-permute-start | bytes 442376 | tf_op jit(solution)/shard_map/ppermute | solution.py:293
  84.6 5.0 %collective-permute-done.6 = bf16[2,96,384]{2,1,0:T(8,128)(2,1)S(1)} collective-permute-done((bf16[2,96,384]{2,1,0:T(8,128)(2,1)S(1)}, bf16[2,96,384]{2,1,0:T(8,128)(2,1)S(1)}, u32[]{:S(2)}, u32[]{:S(2)}) %collective-permute-start.6) | collective-permute-done | bytes 147488 | tf_op jit(solution)/shard_map/ppermute | solution.py:293
  89.7 2.2 %collective-permute-start.7 = (bf16[1,96,384]{2,1,0:T(8,128)(2,1)S(1)}, bf16[1,96,384]{2,1,0:T(8,128)(2,1)S(1)}, u32[]{:S(2)}, u32[]{:S(2)}) collective-permute-start(bf16[1,96,384]{2,1,0:T(8,128)(2,1)S(1)} %dynamic-slice_convert_fusion), channel_id=1, source_target_pairs={{0,4},{1,5},{2,6},{3,7},{4,0},{5,1},{6,2},{7,3},{8,12},{9,13},{10,... | collective-permute-start | bytes 221192 | tf_op jit(solution)/shard_map/ppermute | solution.py:293
  91.9 4.3 %all-to-all-done.2 = bf16[8,96,1024]{2,1,0:T(8,128)(2,1)S(1)} async-done(((bf16[8,96,1024]{2,1,0:T(8,128)(2,1)}), bf16[8,96,1024]{2,1,0:T(8,128)(2,1)S(1)}, u32[]{:S(2)}, u32[]{:S(2)}) %all-to-all-start.2) | async-done | bytes 1572896 | tf_op jit(solution)/shard_map/all_to_all | solution.py:281
  97.2 5.1 %all-to-all-start.3 = ((bf16[4,24,1024]{2,1,0:T(8,128)(2,1)}), bf16[4,24,1024]{2,1,0:T(8,128)(2,1)S(1)}, u32[]{:S(2)}, u32[]{:S(2)}) async-start(bf16[4,24,1024]{2,1,0:T(8,128)(2,1)} %bitcast.2), calls=%async_computation.3 | async-start | bytes 393216 | tf_op jit(solution)/shard_map/all_to_all | solution.py:283
  102.3 7.8 %collective-permute-start.8 = (f32[96,128]{1,0:T(8,128)S(1)}, f32[96,128]{1,0:T(8,128)S(1)}, u32[]{:S(2)}, u32[]{:S(2)}) collective-permute-start(f32[96,128]{1,0:T(8,128)S(1)} %get-tuple-element.14), channel_id=1, source_target_pairs={{0,8},{8,16},{16,24},{24,32},{32,40},{40,48},{48,56},{56,64},{64,7... | collective-permute-start | bytes 147464 | tf_op jit(solution)/shard_map/ppermute | solution.py:32
  110.1 4.5 %collective-permute-start.9 = (f32[96,128]{1,0:T(8,128)S(1)}, f32[96,128]{1,0:T(8,128)S(1)}, u32[]{:S(2)}, u32[]{:S(2)}) collective-permute-start(f32[96,128]{1,0:T(8,128)S(1)} %get-tuple-element.15), channel_id=1, source_target_pairs={{0,16},{8,24},{16,32},{24,40},{32,48},{40,56},{48,64},{56,72},{64,... | collective-permute-start | bytes 147464 | tf_op jit(solution)/shard_map/ppermute | solution.py:32
  114.7 4.5 %collective-permute-start.4 = (f32[12,1024]{1,0:T(8,128)S(1)}, f32[12,1024]{1,0:T(8,128)S(1)}, u32[]{:S(2)}, u32[]{:S(2)}) collective-permute-start(f32[12,1024]{1,0:T(8,128)S(1)} %slice_select_fusion), channel_id=1, source_target_pairs={{0,8},{8,0},{1,9},{9,1},{2,10},{10,2},{3,11},{11,3},{4,12},{12,4},... | collective-permute-start | bytes 147464 | tf_op jit(solution)/shard_map/ppermute | solution.py:287
  119.9 5.5 %collective-permute-done.4 = f32[12,1024]{1,0:T(8,128)S(1)} collective-permute-done((f32[12,1024]{1,0:T(8,128)S(1)}, f32[12,1024]{1,0:T(8,128)S(1)}, u32[]{:S(2)}, u32[]{:S(2)}) %collective-permute-start.4) | collective-permute-done | bytes 49184 | tf_op jit(solution)/shard_map/ppermute | solution.py:287
  (43 shorter events, 8.8 us)
Async XLA Ops:
  0.6 30.0 %collective-permute-start.2 = (bf16[128,1024]{1,0:T(8,128)(2,1)}, bf16[128,1024]{1,0:T(8,128)(2,1)S(1)}, u32[]{:S(2)}, u32[]{:S(2)}) collective-permute-start(bf16[128,1024]{1,0:T(8,128)(2,1)} %teacher.5), channel_id=1, source_target_pairs={{0,504},{8,0},{16,8},{24,16},{32,24},{40,32},{48,40},{56,48},{64,5... | collective-permute-start | bytes 786440 | tf_op jit(solution)/shard_map/ppermute | solution.py:32
  8.6 22.0 %collective-permute-start.3 = (bf16[128,1024]{1,0:T(8,128)(2,1)}, bf16[128,1024]{1,0:T(8,128)(2,1)S(1)}, u32[]{:S(2)}, u32[]{:S(2)}) collective-permute-start(bf16[128,1024]{1,0:T(8,128)(2,1)} %teacher.5), channel_id=1, source_target_pairs={{0,496},{8,504},{16,0},{24,8},{32,16},{40,24},{48,32},{56,40},{64,... | collective-permute-start | bytes 786440 | tf_op jit(solution)/shard_map/ppermute | solution.py:32
  11.1 19.6 %collective-permute-start = (bf16[128,768]{1,0:T(8,128)(2,1)}, bf16[128,768]{1,0:T(8,128)(2,1)S(1)}, u32[]{:S(2)}, u32[]{:S(2)}) collective-permute-start(bf16[128,768]{1,0:T(8,128)(2,1)} %student.3), channel_id=1, source_target_pairs={{0,504},{8,0},{16,8},{24,16},{32,24},{40,32},{48,40},{56,48},{64,5... | collective-permute-start | bytes 589832 | tf_op jit(solution)/shard_map/ppermute | solution.py:32
  13.1 17.6 %collective-permute-start.1 = (bf16[128,768]{1,0:T(8,128)(2,1)}, bf16[128,768]{1,0:T(8,128)(2,1)S(1)}, u32[]{:S(2)}, u32[]{:S(2)}) collective-permute-start(bf16[128,768]{1,0:T(8,128)(2,1)} %student.3), channel_id=1, source_target_pairs={{0,496},{8,504},{16,0},{24,8},{32,16},{40,24},{48,32},{56,40},{64,... | collective-permute-start | bytes 589832 | tf_op jit(solution)/shard_map/ppermute | solution.py:32
  20.9 1.4 %copy-start = (bf16[768,1024]{1,0:T(8,128)(2,1)S(1)}, bf16[768,1024]{1,0:T(8,128)(2,1)}, u32[]{:S(2)}) copy-start(bf16[768,1024]{1,0:T(8,128)(2,1)} %weight.5) | copy-start | bytes 4718596
  22.3 0.9 copy-start.2
  23.3 0.9 copy-start.4
  24.2 6.5 %copy-start.1 = (bf16[768,1024]{1,0:T(8,128)(2,1)S(1)}, bf16[768,1024]{1,0:T(8,128)(2,1)}, u32[]{:S(2)}) copy-start(bf16[768,1024]{1,0:T(8,128)(2,1)} %weight.5) | copy-start | bytes 4718596
  24.2 6.5 %copy-start.3 = (bf16[128,1024]{1,0:T(8,128)(2,1)S(1)}, bf16[128,1024]{1,0:T(8,128)(2,1)}, u32[]{:S(2)}) copy-start(bf16[128,1024]{1,0:T(8,128)(2,1)} %teacher.5) | copy-start | bytes 786436
  30.7 5.3 %copy-start.8 = (s32[384]{0:T(512)S(1)}, s32[384]{0:T(512)}, u32[]{:S(2)}) copy-start(s32[384]{0:T(512)} %param.8) | copy-start | bytes 4612
  30.7 5.4 %copy-start.7 = (s32[2,384]{1,0:T(2,128)S(1)}, s32[2,384]{1,0:T(2,128)}, u32[]{:S(2)}) copy-start(s32[2,384]{1,0:T(2,128)} %param.9) | copy-start | bytes 9220
  32.4 30.8 %copy-start.5 = (bf16[128,768]{1,0:T(8,128)(2,1)S(1)}, bf16[128,768]{1,0:T(8,128)(2,1)}, u32[]{:S(2)}) copy-start(bf16[128,768]{1,0:T(8,128)(2,1)} %student.3) | copy-start | bytes 589828
  32.4 17.5 %all-to-all-start = ((f32[8,16,896]{2,1,0:T(8,128)}), f32[8,16,896]{2,1,0:T(8,128)S(1)}, u32[]{:S(2)}, u32[]{:S(2)}) async-start(f32[8,16,896]{2,1,0:T(8,128)} %tile.1), calls=%async_computation | async-start | bytes 917504 | tf_op jit(solution)/shard_map/all_to_all | solution.py:236
  49.9 0.8 copy-start.6
  53.1 10.1 %all-to-all-start.1 = ((bf16[8,16,512]{2,1,0:T(8,128)(2,1)}), bf16[8,16,512]{2,1,0:T(8,128)(2,1)S(1)}, u32[]{:S(2)}, u32[]{:S(2)}) async-start(bf16[8,16,512]{2,1,0:T(8,128)(2,1)} %band.1), calls=%async_computation.1 | async-start | bytes 262144 | tf_op jit(solution)/shard_map/all_to_all | solution.py:253
  66.2 30.0 %all-to-all-start.2 = ((bf16[8,96,1024]{2,1,0:T(8,128)(2,1)}), bf16[8,96,1024]{2,1,0:T(8,128)(2,1)S(1)}, u32[]{:S(2)}, u32[]{:S(2)}) async-start(bf16[8,96,1024]{2,1,0:T(8,128)(2,1)} %bitcast.1), calls=%async_computation.2 | async-start | bytes 3145728 | tf_op jit(solution)/shard_map/all_to_all | solution.py:281
  77.2 3.6 %collective-permute-start.5 = (bf16[4,96,384]{2,1,0:T(8,128)(2,1)S(1)}, bf16[4,96,384]{2,1,0:T(8,128)(2,1)}, u32[]{:S(2)}, u32[]{:S(2)}) collective-permute-start(bf16[4,96,384]{2,1,0:T(8,128)(2,1)S(1)} %get-tuple-element.13), channel_id=1, source_target_pairs={{0,1},{1,0},{2,3},{3,2},{4,5},{5,4},{6,7},{7,6},{8,9},{9,8},{10,11... | collective-permute-start | bytes 884744 | tf_op jit(solution)/shard_map/ppermute | solution.py:293
  81.8 7.8 %collective-permute-start.6 = (bf16[2,96,384]{2,1,0:T(8,128)(2,1)S(1)}, bf16[2,96,384]{2,1,0:T(8,128)(2,1)S(1)}, u32[]{:S(2)}, u32[]{:S(2)}) collective-permute-start(bf16[2,96,384]{2,1,0:T(8,128)(2,1)S(1)} %fusion), channel_id=1, source_target_pairs={{0,2},{1,3},{2,0},{3,1},{4,6},{5,7},{6,4},{7,5},{8,10},{9,11},{10,... | collective-permute-start | bytes 442376 | tf_op jit(solution)/shard_map/ppermute | solution.py:293
  89.7 12.6 %collective-permute-start.7 = (bf16[1,96,384]{2,1,0:T(8,128)(2,1)S(1)}, bf16[1,96,384]{2,1,0:T(8,128)(2,1)S(1)}, u32[]{:S(2)}, u32[]{:S(2)}) collective-permute-start(bf16[1,96,384]{2,1,0:T(8,128)(2,1)S(1)} %dynamic-slice_convert_fusion), channel_id=1, source_target_pairs={{0,4},{1,5},{2,6},{3,7},{4,0},{5,1},{6,2},{7,3},{8,12},{9,13},{10,... | collective-permute-start | bytes 221192 | tf_op jit(solution)/shard_map/ppermute | solution.py:293
  97.2 17.5 %all-to-all-start.3 = ((bf16[4,24,1024]{2,1,0:T(8,128)(2,1)}), bf16[4,24,1024]{2,1,0:T(8,128)(2,1)S(1)}, u32[]{:S(2)}, u32[]{:S(2)}) async-start(bf16[4,24,1024]{2,1,0:T(8,128)(2,1)} %bitcast.2), calls=%async_computation.3 | async-start | bytes 393216 | tf_op jit(solution)/shard_map/all_to_all | solution.py:283
  102.3 16.9 %collective-permute-start.8 = (f32[96,128]{1,0:T(8,128)S(1)}, f32[96,128]{1,0:T(8,128)S(1)}, u32[]{:S(2)}, u32[]{:S(2)}) collective-permute-start(f32[96,128]{1,0:T(8,128)S(1)} %get-tuple-element.14), channel_id=1, source_target_pairs={{0,8},{8,16},{16,24},{24,32},{32,40},{40,48},{48,56},{56,64},{64,7... | collective-permute-start | bytes 147464 | tf_op jit(solution)/shard_map/ppermute | solution.py:32
  110.1 9.1 %collective-permute-start.9 = (f32[96,128]{1,0:T(8,128)S(1)}, f32[96,128]{1,0:T(8,128)S(1)}, u32[]{:S(2)}, u32[]{:S(2)}) collective-permute-start(f32[96,128]{1,0:T(8,128)S(1)} %get-tuple-element.15), channel_id=1, source_target_pairs={{0,16},{8,24},{16,32},{24,40},{32,48},{40,56},{48,64},{56,72},{64,... | collective-permute-start | bytes 147464 | tf_op jit(solution)/shard_map/ppermute | solution.py:32
  114.7 10.7 %collective-permute-start.4 = (f32[12,1024]{1,0:T(8,128)S(1)}, f32[12,1024]{1,0:T(8,128)S(1)}, u32[]{:S(2)}, u32[]{:S(2)}) collective-permute-start(f32[12,1024]{1,0:T(8,128)S(1)} %slice_select_fusion), channel_id=1, source_target_pairs={{0,8},{8,0},{1,9},{9,1},{2,10},{10,2},{3,11},{11,3},{4,12},{12,4},... | collective-permute-start | bytes 147464 | tf_op jit(solution)/shard_map/ppermute | solution.py:287

commit v12 on v11

--- a/solution.py
+++ b/solution.py
@@ -72,12 +72,12 @@
     proj_own, weight, teacher, tiles, sums, near_student, far_student, near_teacher, far_teacher,
     payload, rows_in,
 ):
-    peers, rows, _ = payload.shape
-    texts = proj_own.shape[0]
+    peers, _, texts = payload.shape
+    rows = texts // peers
     tail = [sums[0:1, :], sums[1:2, :], sums[2:3, :]]
 
     def lay_out(t, tile):
-        payload[:, :, t * texts : (t + 1) * texts] = tile.reshape(peers, rows, texts)
+        payload[:, t * rows : (t + 1) * rows, :] = tile.reshape(peers, rows, texts)
 
     lay_out(0, tiles[:, :texts])
     lay_out(STEPS, tiles[:, texts:])
@@ -92,14 +92,14 @@
         tail = tail + [row_sums(squares[piece]), row_sums(wide * wide)]
         lay_out(s, tile[:, piece])
         lay_out(STEPS + s, dot(teacher[...], mates_in[...], (1, 1)))
-    tail = jnp.concatenate(tail + [jnp.zeros((rows - len(tail), texts), f32)], 0)
+    tail = jnp.concatenate(tail + [jnp.zeros((8 - len(tail), texts), f32)], 0)
     for peer in range(peers):
-        payload[peer, :, 2 * STEPS * texts :] = tail
+        payload[peer, 2 * STEPS * rows :, :] = tail
 
 
 def band_kernel(parts, ids, tiles):
     peers = tiles.shape[0]
-    rows = parts.shape[1]
+    rows = tiles.shape[1]
     band = ids.shape[1]
     texts = band // STEPS
     sums = jnp.sum(parts[...], 0)
@@ -107,7 +107,10 @@
     def part(array, t):
         return array[:, t * texts : (t + 1) * texts]
 
-    tail = part(sums, 2 * STEPS)
+    def beside(t):
+        return jnp.concatenate([sums[(t + s) * rows : (t + s + 1) * rows] for s in range(STEPS)], 1)
+
+    tail = sums[2 * STEPS * rows :]
     proj_sq = jnp.concatenate([tail[0:1], tail[3:4], tail[5:6]], 1)
     teach_sq = jnp.concatenate([tail[1:2], tail[4:5], tail[6:7]], 1)
     inv_proj = lax.rsqrt(proj_sq + EPSILON)
@@ -117,8 +120,8 @@
     own = (ids[3:4, :] == row_id).astype(f32)
     row_proj = jnp.sum(own * inv_proj, 1, keepdims=True)
     row_teach = jnp.sum(own * inv_teach, 1, keepdims=True)
-    sim = sums[:, :band] * (row_proj * inv_proj)
-    teach = sums[:, band : 2 * band] * (row_teach * inv_teach)
+    sim = beside(0) * (row_proj * inv_proj)
+    teach = beside(STEPS) * (row_teach * inv_teach)
     col_id = lax.broadcasted_iota(jnp.int32, (band, band), 0)
     pick = (col_id == ids[1:2, :]).astype(f32) - (col_id == ids[2:3, :]).astype(f32)
     anchor_thrice = jnp.concatenate([anchor, anchor, anchor], 0).astype(bf16)
@@ -225,7 +228,7 @@
     parts = pl.pallas_call(
         tile_kernel,
         scratch_shapes=[pltpu.VMEM(((STEPS - 1) * texts, features), bf16)],
-        out_shape=jax.ShapeDtypeStruct((n_feat, rows, (2 * STEPS + 1) * texts), f32),
+        out_shape=jax.ShapeDtypeStruct((n_feat, 2 * STEPS * rows + 8, texts), f32),
         compiler_params=params,
         cost_estimate=cost(6 * 10**8),
         name="tile",

time: 127 us -> 126 us (level)
  no operation moved by 1% of the time
where the time goes in v12:
time: 126 us; the launch traced here: 125 us
  starting transfers between devices  67 us (53%)
  waiting for transfers between devices  41.4 us (33%)
  Pallas kernels  7.71 us (6%)
  local copies, waits for them, and re-layouts  4.21 us (3%)
  other arithmetic  4.03 us (3%)
    ppermute x6, starting transfers between devices, passed_along(): lax.ppermute(array, DP, [(i, (i + by) % peers) for i in range(peers)])  32.6 us
    all_to_all x1, waiting for transfers between devices, shards(): parts = lax.all_to_all(parts, 'feat', 0, 0)  12.4 us
    all_to_all x1, starting transfers between devices, shards(): lax.all_to_all(grad_w.reshape(x_size, features // x_size, width), 'x', 0, 0)  10.9 us
    ppermute x3, starting transfers between devices, swapped(): return lax.ppermute(array, 'feat', perm).astype(f32)  6.97 us
    all_to_all x1, waiting for transfers between devices, shards(): gathered = lax.all_to_all(tiles, 'feat', 0, 0)  6.71 us
    ppermute x3, waiting for transfers between devices, swapped(): return lax.ppermute(array, 'feat', perm).astype(f32)  6.63 us
    ppermute x6, waiting for transfers between devices, passed_along(): lax.ppermute(array, DP, [(i, (i + by) % peers) for i in range(peers)])  5.85 us
    ppermute x1, waiting for transfers between devices, shards(): lax.ppermute(jnp.where(first, upper, lower), 'yh', [(0, 1), (1, 0)])  5.5 us
  transfers between devices with their start and end apart: 14, of which 7 were waited for; matrix products, arithmetic and copies ran while one was open for 3% of the time, Pallas kernels for 0%

profile of v12, /device:TPU:6, one launch (start us, length us, event | category | flops | bytes accessed | tf_op | source)
XLA Modules:
  0.0 125.3 jit_solution(12223457262770533710)
XLA Ops:
  0.6 8.0 %collective-permute-start.2 = (bf16[128,1024]{1,0:T(8,128)(2,1)}, bf16[128,1024]{1,0:T(8,128)(2,1)S(1)}, u32[]{:S(2)}, u32[]{:S(2)}) collective-permute-start(bf16[128,1024]{1,0:T(8,128)(2,1)} %teacher.5), channel_id=1, source_target_pairs={{0,504},{8,0},{16,8},{24,16},{32,24},{40,32},{48,40},{56,48},{64,5... | collective-permute-start | bytes 786440 | tf_op jit(solution)/shard_map/ppermute | solution.py:32
  8.6 2.4 %collective-permute-start.3 = (bf16[128,1024]{1,0:T(8,128)(2,1)}, bf16[128,1024]{1,0:T(8,128)(2,1)S(1)}, u32[]{:S(2)}, u32[]{:S(2)}) collective-permute-start(bf16[128,1024]{1,0:T(8,128)(2,1)} %teacher.5), channel_id=1, source_target_pairs={{0,496},{8,504},{16,0},{24,8},{32,16},{40,24},{48,32},{56,40},{64,... | collective-permute-start | bytes 786440 | tf_op jit(solution)/shard_map/ppermute | solution.py:32
  11.1 2.0 %collective-permute-start = (bf16[128,768]{1,0:T(8,128)(2,1)}, bf16[128,768]{1,0:T(8,128)(2,1)S(1)}, u32[]{:S(2)}, u32[]{:S(2)}) collective-permute-start(bf16[128,768]{1,0:T(8,128)(2,1)} %student.3), channel_id=1, source_target_pairs={{0,504},{8,0},{16,8},{24,16},{32,24},{40,32},{48,40},{56,48},{64,5... | collective-permute-start | bytes 589832 | tf_op jit(solution)/shard_map/ppermute | solution.py:32
  13.1 7.8 %collective-permute-start.1 = (bf16[128,768]{1,0:T(8,128)(2,1)}, bf16[128,768]{1,0:T(8,128)(2,1)S(1)}, u32[]{:S(2)}, u32[]{:S(2)}) collective-permute-start(bf16[128,768]{1,0:T(8,128)(2,1)} %student.3), channel_id=1, source_target_pairs={{0,496},{8,504},{16,0},{24,8},{32,16},{40,24},{48,32},{56,40},{64,... | collective-permute-start | bytes 589832 | tf_op jit(solution)/shard_map/ppermute | solution.py:32
  24.8 5.8 %collective-permute-done.near_student = bf16[128,768]{1,0:T(8,128)(2,1)S(1)} collective-permute-done((bf16[128,768]{1,0:T(8,128)(2,1)}, bf16[128,768]{1,0:T(8,128)(2,1)S(1)}, u32[]{:S(2)}, u32[]{:S(2)}) %collective-permute-start) | collective-permute-done | bytes 196640 | tf_op jit(solution)/shard_map/ppermute | solution.py:32
  30.7 1.6 %tile.1 = f32[8,104,128]{2,1,0:T(8,128)} custom-call(bf16[128,1024]{1,0:T(8,128)(2,1)S(1)} %get-tuple-element.8.proj_own, bf16[768,1024]{1,0:T(8,128)(2,1)S(1)} %copy-done.1, bf16[128,1024]{1,0:T(8,128)(2,1)S(1)} %copy-done.3, f32[128,256]{1,0:T(8,128)S(1)} %get-tuple-element.9.tiles, f32[8,128]{1,0:T(8,128)S(1)} %get-tuple-element.10.sums, ...), custom_call_target="tpu_custom_call" | custom-call | flops 600000000 | bytes 3000000 | tf_op jit(solution)/shard_map/tile/pallas_call | solution.py:228
  32.4 3.6 %all-to-all-start = ((f32[8,104,128]{2,1,0:T(8,128)}), f32[8,104,128]{2,1,0:T(8,128)S(1)}, u32[]{:S(2)}, u32[]{:S(2)}) async-start(f32[8,104,128]{2,1,0:T(8,128)} %tile.1), calls=%async_computation | async-start | bytes 851968 | tf_op jit(solution)/shard_map/all_to_all | solution.py:239
  36.8 12.4 %all-to-all-done.parts = f32[8,104,128]{2,1,0:T(8,128)S(1)} async-done(((f32[8,104,128]{2,1,0:T(8,128)}), f32[8,104,128]{2,1,0:T(8,128)S(1)}, u32[]{:S(2)}, u32[]{:S(2)}) %all-to-all-start) | async-done | bytes 426016 | tf_op jit(solution)/shard_map/all_to_all | solution.py:239
  49.9 2.4 %band.1 = bf16[8,16,512]{2,1,0:T(8,128)(2,1)} custom-call(f32[8,104,128]{2,1,0:T(8,128)} %copy-done.6, s32[8,384]{1,0:T(8,128)} %add_add_fusion.ids), custom_call_target="tpu_custom_call" | custom-call | flops 100000000 | bytes 3000000 | tf_op jit(solution)/shard_map/band/pallas_call | solution.py:250
  52.3 3.4 %all-to-all-start.1 = ((bf16[8,16,512]{2,1,0:T(8,128)(2,1)}), bf16[8,16,512]{2,1,0:T(8,128)(2,1)S(1)}, u32[]{:S(2)}, u32[]{:S(2)}) async-start(bf16[8,16,512]{2,1,0:T(8,128)(2,1)} %band.1), calls=%async_computation.1 | async-start | bytes 262144 | tf_op jit(solution)/shard_map/all_to_all | solution.py:256
  55.7 6.7 %all-to-all-done.1.gathered = bf16[8,16,512]{2,1,0:T(8,128)(2,1)S(1)} async-done(((bf16[8,16,512]{2,1,0:T(8,128)(2,1)}), bf16[8,16,512]{2,1,0:T(8,128)(2,1)S(1)}, u32[]{:S(2)}, u32[]{:S(2)}) %all-to-all-start.1) | async-done | bytes 131104 | tf_op jit(solution)/shard_map/all_to_all | solution.py:256
  62.4 3.1 %grad.1 = (bf16[4,96,384]{2,1,0:T(8,128)(2,1)S(1)}, f32[4,96,384]{2,1,0:T(8,128)S(1)}, bf16[768,1024]{1,0:T(8,128)(2,1)}) custom-call(s32[1]{0:T(128)} %bitcast.core, bf16[8,16,512]{2,1,0:T(8,128)(2,1)S(1)} %all-to-all-done.1.gathered, bf16[768,1024]{1,0:T(8,128)(2,1)S(1)} %copy-done.1, bf16[128,1024]{1,0:T(8,128)(2,1)S(1)} %copy-done.3, ...), custom_call_target="tpu_custom_call" | custom-call | flops 1000000000 | bytes 3000000 | tf_op jit(solution)/shard_map/grad/pallas_call | solution.py:261
  65.5 10.9 %all-to-all-start.2 = ((bf16[8,96,1024]{2,1,0:T(8,128)(2,1)}), bf16[8,96,1024]{2,1,0:T(8,128)(2,1)S(1)}, u32[]{:S(2)}, u32[]{:S(2)}) async-start(bf16[8,96,1024]{2,1,0:T(8,128)(2,1)} %bitcast.1), calls=%async_computation.2 | async-start | bytes 3145728 | tf_op jit(solution)/shard_map/all_to_all | solution.py:284
  76.4 1.9 %collective-permute-start.5 = (bf16[4,96,384]{2,1,0:T(8,128)(2,1)S(1)}, bf16[4,96,384]{2,1,0:T(8,128)(2,1)}, u32[]{:S(2)}, u32[]{:S(2)}) collective-permute-start(bf16[4,96,384]{2,1,0:T(8,128)(2,1)S(1)} %get-tuple-element.13), channel_id=1, source_target_pairs={{0,1},{1,0},{2,3},{3,2},{4,5},{5,4},{6,7},{7,6},{8,9},{9,8},{10,11... | collective-permute-start | bytes 884744 | tf_op jit(solution)/shard_map/ppermute | solution.py:296
  78.4 1.7 %collective-permute-done.5 = bf16[4,96,384]{2,1,0:T(8,128)(2,1)} collective-permute-done((bf16[4,96,384]{2,1,0:T(8,128)(2,1)S(1)}, bf16[4,96,384]{2,1,0:T(8,128)(2,1)}, u32[]{:S(2)}, u32[]{:S(2)}) %collective-permute-start.5) | collective-permute-done | bytes 294944 | tf_op jit(solution)/shard_map/ppermute | solution.py:296
  81.1 2.8 %collective-permute-start.6 = (bf16[2,96,384]{2,1,0:T(8,128)(2,1)S(1)}, bf16[2,96,384]{2,1,0:T(8,128)(2,1)S(1)}, u32[]{:S(2)}, u32[]{:S(2)}) collective-permute-start(bf16[2,96,384]{2,1,0:T(8,128)(2,1)S(1)} %fusion), channel_id=1, source_target_pairs={{0,2},{1,3},{2,0},{3,1},{4,6},{5,7},{6,4},{7,5},{8,10},{9,11},{10,... | collective-permute-start | bytes 442376 | tf_op jit(solution)/shard_map/ppermute | solution.py:296
  83.9 5.0 %collective-permute-done.6 = bf16[2,96,384]{2,1,0:T(8,128)(2,1)S(1)} collective-permute-done((bf16[2,96,384]{2,1,0:T(8,128)(2,1)S(1)}, bf16[2,96,384]{2,1,0:T(8,128)(2,1)S(1)}, u32[]{:S(2)}, u32[]{:S(2)}) %collective-permute-start.6) | collective-permute-done | bytes 147488 | tf_op jit(solution)/shard_map/ppermute | solution.py:296
  88.9 2.2 %collective-permute-start.7 = (bf16[1,96,384]{2,1,0:T(8,128)(2,1)S(1)}, bf16[1,96,384]{2,1,0:T(8,128)(2,1)S(1)}, u32[]{:S(2)}, u32[]{:S(2)}) collective-permute-start(bf16[1,96,384]{2,1,0:T(8,128)(2,1)S(1)} %dynamic-slice_convert_fusion), channel_id=1, source_target_pairs={{0,4},{1,5},{2,6},{3,7},{4,0},{5,1},{6,2},{7,3},{8,12},{9,13},{10,... | collective-permute-start | bytes 221192 | tf_op jit(solution)/shard_map/ppermute | solution.py:296
  91.2 4.3 %all-to-all-done.2 = bf16[8,96,1024]{2,1,0:T(8,128)(2,1)S(1)} async-done(((bf16[8,96,1024]{2,1,0:T(8,128)(2,1)}), bf16[8,96,1024]{2,1,0:T(8,128)(2,1)S(1)}, u32[]{:S(2)}, u32[]{:S(2)}) %all-to-all-start.2) | async-done | bytes 1572896 | tf_op jit(solution)/shard_map/all_to_all | solution.py:284
  96.5 5.1 %all-to-all-start.3 = ((bf16[4,24,1024]{2,1,0:T(8,128)(2,1)}), bf16[4,24,1024]{2,1,0:T(8,128)(2,1)S(1)}, u32[]{:S(2)}, u32[]{:S(2)}) async-start(bf16[4,24,1024]{2,1,0:T(8,128)(2,1)} %bitcast.2), calls=%async_computation.3 | async-start | bytes 393216 | tf_op jit(solution)/shard_map/all_to_all | solution.py:286
  101.6 7.8 %collective-permute-start.8 = (f32[96,128]{1,0:T(8,128)S(1)}, f32[96,128]{1,0:T(8,128)S(1)}, u32[]{:S(2)}, u32[]{:S(2)}) collective-permute-start(f32[96,128]{1,0:T(8,128)S(1)} %get-tuple-element.14), channel_id=1, source_target_pairs={{0,8},{8,16},{16,24},{24,32},{32,40},{40,48},{48,56},{56,64},{64,7... | collective-permute-start | bytes 147464 | tf_op jit(solution)/shard_map/ppermute | solution.py:32
  109.4 4.5 %collective-permute-start.9 = (f32[96,128]{1,0:T(8,128)S(1)}, f32[96,128]{1,0:T(8,128)S(1)}, u32[]{:S(2)}, u32[]{:S(2)}) collective-permute-start(f32[96,128]{1,0:T(8,128)S(1)} %get-tuple-element.15), channel_id=1, source_target_pairs={{0,16},{8,24},{16,32},{24,40},{32,48},{40,56},{48,64},{56,72},{64,... | collective-permute-start | bytes 147464 | tf_op jit(solution)/shard_map/ppermute | solution.py:32
  114.0 4.5 %collective-permute-start.4 = (f32[12,1024]{1,0:T(8,128)S(1)}, f32[12,1024]{1,0:T(8,128)S(1)}, u32[]{:S(2)}, u32[]{:S(2)}) collective-permute-start(f32[12,1024]{1,0:T(8,128)S(1)} %slice_select_fusion), channel_id=1, source_target_pairs={{0,8},{8,0},{1,9},{9,1},{2,10},{10,2},{3,11},{11,3},{4,12},{12,4},... | collective-permute-start | bytes 147464 | tf_op jit(solution)/shard_map/ppermute | solution.py:290
  119.1 5.5 %collective-permute-done.4 = f32[12,1024]{1,0:T(8,128)S(1)} collective-permute-done((f32[12,1024]{1,0:T(8,128)S(1)}, f32[12,1024]{1,0:T(8,128)S(1)}, u32[]{:S(2)}, u32[]{:S(2)}) %collective-permute-start.4) | collective-permute-done | bytes 49184 | tf_op jit(solution)/shard_map/ppermute | solution.py:290
  (43 shorter events, 8.8 us)
Async XLA Ops:
  0.6 30.0 %collective-permute-start.2 = (bf16[128,1024]{1,0:T(8,128)(2,1)}, bf16[128,1024]{1,0:T(8,128)(2,1)S(1)}, u32[]{:S(2)}, u32[]{:S(2)}) collective-permute-start(bf16[128,1024]{1,0:T(8,128)(2,1)} %teacher.5), channel_id=1, source_target_pairs={{0,504},{8,0},{16,8},{24,16},{32,24},{40,32},{48,40},{56,48},{64,5... | collective-permute-start | bytes 786440 | tf_op jit(solution)/shard_map/ppermute | solution.py:32
  8.6 22.0 %collective-permute-start.3 = (bf16[128,1024]{1,0:T(8,128)(2,1)}, bf16[128,1024]{1,0:T(8,128)(2,1)S(1)}, u32[]{:S(2)}, u32[]{:S(2)}) collective-permute-start(bf16[128,1024]{1,0:T(8,128)(2,1)} %teacher.5), channel_id=1, source_target_pairs={{0,496},{8,504},{16,0},{24,8},{32,16},{40,24},{48,32},{56,40},{64,... | collective-permute-start | bytes 786440 | tf_op jit(solution)/shard_map/ppermute | solution.py:32
  11.1 19.6 %collective-permute-start = (bf16[128,768]{1,0:T(8,128)(2,1)}, bf16[128,768]{1,0:T(8,128)(2,1)S(1)}, u32[]{:S(2)}, u32[]{:S(2)}) collective-permute-start(bf16[128,768]{1,0:T(8,128)(2,1)} %student.3), channel_id=1, source_target_pairs={{0,504},{8,0},{16,8},{24,16},{32,24},{40,32},{48,40},{56,48},{64,5... | collective-permute-start | bytes 589832 | tf_op jit(solution)/shard_map/ppermute | solution.py:32
  13.1 17.6 %collective-permute-start.1 = (bf16[128,768]{1,0:T(8,128)(2,1)}, bf16[128,768]{1,0:T(8,128)(2,1)S(1)}, u32[]{:S(2)}, u32[]{:S(2)}) collective-permute-start(bf16[128,768]{1,0:T(8,128)(2,1)} %student.3), channel_id=1, source_target_pairs={{0,496},{8,504},{16,0},{24,8},{32,16},{40,24},{48,32},{56,40},{64,... | collective-permute-start | bytes 589832 | tf_op jit(solution)/shard_map/ppermute | solution.py:32
  20.9 1.4 %copy-start = (bf16[768,1024]{1,0:T(8,128)(2,1)S(1)}, bf16[768,1024]{1,0:T(8,128)(2,1)}, u32[]{:S(2)}) copy-start(bf16[768,1024]{1,0:T(8,128)(2,1)} %weight.5) | copy-start | bytes 4718596
  22.3 0.9 copy-start.2
  23.3 0.9 copy-start.4
  24.2 6.5 %copy-start.1 = (bf16[768,1024]{1,0:T(8,128)(2,1)S(1)}, bf16[768,1024]{1,0:T(8,128)(2,1)}, u32[]{:S(2)}) copy-start(bf16[768,1024]{1,0:T(8,128)(2,1)} %weight.5) | copy-start | bytes 4718596
  24.2 6.5 %copy-start.3 = (bf16[128,1024]{1,0:T(8,128)(2,1)S(1)}, bf16[128,1024]{1,0:T(8,128)(2,1)}, u32[]{:S(2)}) copy-start(bf16[128,1024]{1,0:T(8,128)(2,1)} %teacher.5) | copy-start | bytes 786436
  30.7 5.3 %copy-start.8 = (s32[384]{0:T(512)S(1)}, s32[384]{0:T(512)}, u32[]{:S(2)}) copy-start(s32[384]{0:T(512)} %param.8) | copy-start | bytes 4612
  30.7 5.4 %copy-start.7 = (s32[2,384]{1,0:T(2,128)S(1)}, s32[2,384]{1,0:T(2,128)}, u32[]{:S(2)}) copy-start(s32[2,384]{1,0:T(2,128)} %param.9) | copy-start | bytes 9220
  32.4 30.1 %copy-start.5 = (bf16[128,768]{1,0:T(8,128)(2,1)S(1)}, bf16[128,768]{1,0:T(8,128)(2,1)}, u32[]{:S(2)}) copy-start(bf16[128,768]{1,0:T(8,128)(2,1)} %student.3) | copy-start | bytes 589828
  32.4 16.8 %all-to-all-start = ((f32[8,104,128]{2,1,0:T(8,128)}), f32[8,104,128]{2,1,0:T(8,128)S(1)}, u32[]{:S(2)}, u32[]{:S(2)}) async-start(f32[8,104,128]{2,1,0:T(8,128)} %tile.1), calls=%async_computation | async-start | bytes 851968 | tf_op jit(solution)/shard_map/all_to_all | solution.py:239
  49.1 0.8 copy-start.6
  52.3 10.1 %all-to-all-start.1 = ((bf16[8,16,512]{2,1,0:T(8,128)(2,1)}), bf16[8,16,512]{2,1,0:T(8,128)(2,1)S(1)}, u32[]{:S(2)}, u32[]{:S(2)}) async-start(bf16[8,16,512]{2,1,0:T(8,128)(2,1)} %band.1), calls=%async_computation.1 | async-start | bytes 262144 | tf_op jit(solution)/shard_map/all_to_all | solution.py:256
  65.5 30.0 %all-to-all-start.2 = ((bf16[8,96,1024]{2,1,0:T(8,128)(2,1)}), bf16[8,96,1024]{2,1,0:T(8,128)(2,1)S(1)}, u32[]{:S(2)}, u32[]{:S(2)}) async-start(bf16[8,96,1024]{2,1,0:T(8,128)(2,1)} %bitcast.1), calls=%async_computation.2 | async-start | bytes 3145728 | tf_op jit(solution)/shard_map/all_to_all | solution.py:284
  76.4 3.6 %collective-permute-start.5 = (bf16[4,96,384]{2,1,0:T(8,128)(2,1)S(1)}, bf16[4,96,384]{2,1,0:T(8,128)(2,1)}, u32[]{:S(2)}, u32[]{:S(2)}) collective-permute-start(bf16[4,96,384]{2,1,0:T(8,128)(2,1)S(1)} %get-tuple-element.13), channel_id=1, source_target_pairs={{0,1},{1,0},{2,3},{3,2},{4,5},{5,4},{6,7},{7,6},{8,9},{9,8},{10,11... | collective-permute-start | bytes 884744 | tf_op jit(solution)/shard_map/ppermute | solution.py:296
  81.1 7.8 %collective-permute-start.6 = (bf16[2,96,384]{2,1,0:T(8,128)(2,1)S(1)}, bf16[2,96,384]{2,1,0:T(8,128)(2,1)S(1)}, u32[]{:S(2)}, u32[]{:S(2)}) collective-permute-start(bf16[2,96,384]{2,1,0:T(8,128)(2,1)S(1)} %fusion), channel_id=1, source_target_pairs={{0,2},{1,3},{2,0},{3,1},{4,6},{5,7},{6,4},{7,5},{8,10},{9,11},{10,... | collective-permute-start | bytes 442376 | tf_op jit(solution)/shard_map/ppermute | solution.py:296
  88.9 12.6 %collective-permute-start.7 = (bf16[1,96,384]{2,1,0:T(8,128)(2,1)S(1)}, bf16[1,96,384]{2,1,0:T(8,128)(2,1)S(1)}, u32[]{:S(2)}, u32[]{:S(2)}) collective-permute-start(bf16[1,96,384]{2,1,0:T(8,128)(2,1)S(1)} %dynamic-slice_convert_fusion), channel_id=1, source_target_pairs={{0,4},{1,5},{2,6},{3,7},{4,0},{5,1},{6,2},{7,3},{8,12},{9,13},{10,... | collective-permute-start | bytes 221192 | tf_op jit(solution)/shard_map/ppermute | solution.py:296
  96.5 17.4 %all-to-all-start.3 = ((bf16[4,24,1024]{2,1,0:T(8,128)(2,1)}), bf16[4,24,1024]{2,1,0:T(8,128)(2,1)S(1)}, u32[]{:S(2)}, u32[]{:S(2)}) async-start(bf16[4,24,1024]{2,1,0:T(8,128)(2,1)} %bitcast.2), calls=%async_computation.3 | async-start | bytes 393216 | tf_op jit(solution)/shard_map/all_to_all | solution.py:286
  101.6 16.9 %collective-permute-start.8 = (f32[96,128]{1,0:T(8,128)S(1)}, f32[96,128]{1,0:T(8,128)S(1)}, u32[]{:S(2)}, u32[]{:S(2)}) collective-permute-start(f32[96,128]{1,0:T(8,128)S(1)} %get-tuple-element.14), channel_id=1, source_target_pairs={{0,8},{8,16},{16,24},{24,32},{32,40},{40,48},{48,56},{56,64},{64,7... | collective-permute-start | bytes 147464 | tf_op jit(solution)/shard_map/ppermute | solution.py:32
  109.4 9.1 %collective-permute-start.9 = (f32[96,128]{1,0:T(8,128)S(1)}, f32[96,128]{1,0:T(8,128)S(1)}, u32[]{:S(2)}, u32[]{:S(2)}) collective-permute-start(f32[96,128]{1,0:T(8,128)S(1)} %get-tuple-element.15), channel_id=1, source_target_pairs={{0,16},{8,24},{16,32},{24,40},{32,48},{40,56},{48,64},{56,72},{64,... | collective-permute-start | bytes 147464 | tf_op jit(solution)/shard_map/ppermute | solution.py:32
  114.0 10.7 %collective-permute-start.4 = (f32[12,1024]{1,0:T(8,128)S(1)}, f32[12,1024]{1,0:T(8,128)S(1)}, u32[]{:S(2)}, u32[]{:S(2)}) collective-permute-start(f32[12,1024]{1,0:T(8,128)S(1)} %slice_select_fusion), channel_id=1, source_target_pairs={{0,8},{8,0},{1,9},{9,1},{2,10},{10,2},{3,11},{11,3},{4,12},{12,4},... | collective-permute-start | bytes 147464 | tf_op jit(solution)/shard_map/ppermute | solution.py:290

commit v13 on v12

--- a/solution.py
+++ b/solution.py
@@ -288,8 +288,8 @@
     lower, upper = grad_w[:share], grad_w[share:]
     first = lax.axis_index("yh") == 0
     grad_w = jnp.where(first, lower, upper) + lax.ppermute(
-        jnp.where(first, upper, lower), "yh", [(0, 1), (1, 0)]
-    )
+        jnp.where(first, upper, lower).astype(bf16), "yh", [(0, 1), (1, 0)]
+    ).astype(f32)
 
     def swapped(array, bit):
         perm = [(i, i ^ (1 << bit)) for i in range(n_feat)]
@@ -304,7 +304,8 @@
     back = back.reshape(height, band)
     grad_student = back[:, :texts]
     for s in range(1, STEPS):
-        grad_student = grad_student + passed_along(back[:, s * texts : (s + 1) * texts], s)
+        terms = back[:, s * texts : (s + 1) * texts].astype(bf16)
+        grad_student = grad_student + passed_along(terms, s).astype(f32)
     return (grad_w, grad_student.T)
 
 

time: 126 us -> 125 us (level)
  no operation moved by 1% of the time
where the time goes in v13:
time: 125 us
  starting transfers between devices  67 us (54%)
  waiting for transfers between devices  40.7 us (33%)
  Pallas kernels  7.7 us (6%)
  local copies, waits for them, and re-layouts  4.19 us (3%)
  other arithmetic  4.04 us (3%)
    ppermute x6, starting transfers between devices, passed_along(): lax.ppermute(array, DP, [(i, (i + by) % peers) for i in range(peers)])  32.6 us
    all_to_all x1, waiting for transfers between devices, shards(): parts = lax.all_to_all(parts, 'feat', 0, 0)  12.4 us
    all_to_all x1, starting transfers between devices, shards(): lax.all_to_all(grad_w.reshape(x_size, features // x_size, width), 'x', 0, 0)  10.9 us
    ppermute x3, starting transfers between devices, swapped(): return lax.ppermute(array, 'feat', perm).astype(f32)  6.97 us
    all_to_all x1, waiting for transfers between devices, shards(): gathered = lax.all_to_all(tiles, 'feat', 0, 0)  6.71 us
    ppermute x3, waiting for transfers between devices, swapped(): return lax.ppermute(array, 'feat', perm).astype(f32)  6.63 us
    ppermute x6, waiting for transfers between devices, passed_along(): lax.ppermute(array, DP, [(i, (i + by) % peers) for i in range(peers)])  5.85 us
    all_to_all x1, starting transfers between devices, shards(): lax.all_to_all(grad_w.reshape(z_size, yh_size * share, width), 'z', 0, 0)  5.07 us
  transfers between devices with their start and end apart: 14, of which 7 were waited for; matrix products, arithmetic and copies ran while one was open for 3% of the time, Pallas kernels for 0%

profile of v13, /device:TPU:6, one launch (start us, length us, event | category | flops | bytes accessed | tf_op | source)
XLA Modules:
  0.0 124.6 jit_solution(3366513685389724932)
XLA Ops:
  0.6 8.0 %collective-permute-start.2 = (bf16[128,1024]{1,0:T(8,128)(2,1)}, bf16[128,1024]{1,0:T(8,128)(2,1)S(1)}, u32[]{:S(2)}, u32[]{:S(2)}) collective-permute-start(bf16[128,1024]{1,0:T(8,128)(2,1)} %teacher.5), channel_id=1, source_target_pairs={{0,504},{8,0},{16,8},{24,16},{32,24},{40,32},{48,40},{56,48},{64,5... | collective-permute-start | bytes 786440 | tf_op jit(solution)/shard_map/ppermute | solution.py:32
  8.6 2.4 %collective-permute-start.3 = (bf16[128,1024]{1,0:T(8,128)(2,1)}, bf16[128,1024]{1,0:T(8,128)(2,1)S(1)}, u32[]{:S(2)}, u32[]{:S(2)}) collective-permute-start(bf16[128,1024]{1,0:T(8,128)(2,1)} %teacher.5), channel_id=1, source_target_pairs={{0,496},{8,504},{16,0},{24,8},{32,16},{40,24},{48,32},{56,40},{64,... | collective-permute-start | bytes 786440 | tf_op jit(solution)/shard_map/ppermute | solution.py:32
  11.1 2.0 %collective-permute-start = (bf16[128,768]{1,0:T(8,128)(2,1)}, bf16[128,768]{1,0:T(8,128)(2,1)S(1)}, u32[]{:S(2)}, u32[]{:S(2)}) collective-permute-start(bf16[128,768]{1,0:T(8,128)(2,1)} %student.3), channel_id=1, source_target_pairs={{0,504},{8,0},{16,8},{24,16},{32,24},{40,32},{48,40},{56,48},{64,5... | collective-permute-start | bytes 589832 | tf_op jit(solution)/shard_map/ppermute | solution.py:32
  13.1 7.8 %collective-permute-start.1 = (bf16[128,768]{1,0:T(8,128)(2,1)}, bf16[128,768]{1,0:T(8,128)(2,1)S(1)}, u32[]{:S(2)}, u32[]{:S(2)}) collective-permute-start(bf16[128,768]{1,0:T(8,128)(2,1)} %student.3), channel_id=1, source_target_pairs={{0,496},{8,504},{16,0},{24,8},{32,16},{40,24},{48,32},{56,40},{64,... | collective-permute-start | bytes 589832 | tf_op jit(solution)/shard_map/ppermute | solution.py:32
  24.8 5.8 %collective-permute-done.near_student = bf16[128,768]{1,0:T(8,128)(2,1)S(1)} collective-permute-done((bf16[128,768]{1,0:T(8,128)(2,1)}, bf16[128,768]{1,0:T(8,128)(2,1)S(1)}, u32[]{:S(2)}, u32[]{:S(2)}) %collective-permute-start) | collective-permute-done | bytes 196640 | tf_op jit(solution)/shard_map/ppermute | solution.py:32
  30.7 1.6 %tile.1 = f32[8,104,128]{2,1,0:T(8,128)} custom-call(bf16[128,1024]{1,0:T(8,128)(2,1)S(1)} %get-tuple-element.8.proj_own, bf16[768,1024]{1,0:T(8,128)(2,1)S(1)} %copy-done.1, bf16[128,1024]{1,0:T(8,128)(2,1)S(1)} %copy-done.3, f32[128,256]{1,0:T(8,128)S(1)} %get-tuple-element.9.tiles, f32[8,128]{1,0:T(8,128)S(1)} %get-tuple-element.10.sums, ...), custom_call_target="tpu_custom_call" | custom-call | flops 600000000 | bytes 3000000 | tf_op jit(solution)/shard_map/tile/pallas_call | solution.py:228
  32.4 3.6 %all-to-all-start = ((f32[8,104,128]{2,1,0:T(8,128)}), f32[8,104,128]{2,1,0:T(8,128)S(1)}, u32[]{:S(2)}, u32[]{:S(2)}) async-start(f32[8,104,128]{2,1,0:T(8,128)} %tile.1), calls=%async_computation | async-start | bytes 851968 | tf_op jit(solution)/shard_map/all_to_all | solution.py:239
  36.8 12.4 %all-to-all-done.parts = f32[8,104,128]{2,1,0:T(8,128)S(1)} async-done(((f32[8,104,128]{2,1,0:T(8,128)}), f32[8,104,128]{2,1,0:T(8,128)S(1)}, u32[]{:S(2)}, u32[]{:S(2)}) %all-to-all-start) | async-done | bytes 426016 | tf_op jit(solution)/shard_map/all_to_all | solution.py:239
  49.9 2.4 %band.1 = bf16[8,16,512]{2,1,0:T(8,128)(2,1)} custom-call(f32[8,104,128]{2,1,0:T(8,128)} %copy-done.6, s32[8,384]{1,0:T(8,128)} %add_add_fusion.ids), custom_call_target="tpu_custom_call" | custom-call | flops 100000000 | bytes 3000000 | tf_op jit(solution)/shard_map/band/pallas_call | solution.py:250
  52.3 3.4 %all-to-all-start.1 = ((bf16[8,16,512]{2,1,0:T(8,128)(2,1)}), bf16[8,16,512]{2,1,0:T(8,128)(2,1)S(1)}, u32[]{:S(2)}, u32[]{:S(2)}) async-start(bf16[8,16,512]{2,1,0:T(8,128)(2,1)} %band.1), calls=%async_computation.1 | async-start | bytes 262144 | tf_op jit(solution)/shard_map/all_to_all | solution.py:256
  55.7 6.7 %all-to-all-done.1.gathered = bf16[8,16,512]{2,1,0:T(8,128)(2,1)S(1)} async-done(((bf16[8,16,512]{2,1,0:T(8,128)(2,1)}), bf16[8,16,512]{2,1,0:T(8,128)(2,1)S(1)}, u32[]{:S(2)}, u32[]{:S(2)}) %all-to-all-start.1) | async-done | bytes 131104 | tf_op jit(solution)/shard_map/all_to_all | solution.py:256
  62.4 3.1 %grad.1 = (bf16[4,96,384]{2,1,0:T(8,128)(2,1)S(1)}, f32[4,96,384]{2,1,0:T(8,128)S(1)}, bf16[768,1024]{1,0:T(8,128)(2,1)}) custom-call(s32[1]{0:T(128)} %bitcast.core, bf16[8,16,512]{2,1,0:T(8,128)(2,1)S(1)} %all-to-all-done.1.gathered, bf16[768,1024]{1,0:T(8,128)(2,1)S(1)} %copy-done.1, bf16[128,1024]{1,0:T(8,128)(2,1)S(1)} %copy-done.3, ...), custom_call_target="tpu_custom_call" | custom-call | flops 1000000000 | bytes 3000000 | tf_op jit(solution)/shard_map/grad/pallas_call | solution.py:261
  65.5 10.9 %all-to-all-start.2 = ((bf16[8,96,1024]{2,1,0:T(8,128)(2,1)}), bf16[8,96,1024]{2,1,0:T(8,128)(2,1)S(1)}, u32[]{:S(2)}, u32[]{:S(2)}) async-start(bf16[8,96,1024]{2,1,0:T(8,128)(2,1)} %bitcast.1), calls=%async_computation.2 | async-start | bytes 3145728 | tf_op jit(solution)/shard_map/all_to_all | solution.py:284
  76.4 1.9 %collective-permute-start.5 = (bf16[4,96,384]{2,1,0:T(8,128)(2,1)S(1)}, bf16[4,96,384]{2,1,0:T(8,128)(2,1)}, u32[]{:S(2)}, u32[]{:S(2)}) collective-permute-start(bf16[4,96,384]{2,1,0:T(8,128)(2,1)S(1)} %get-tuple-element.13), channel_id=1, source_target_pairs={{0,1},{1,0},{2,3},{3,2},{4,5},{5,4},{6,7},{7,6},{8,9},{9,8},{10,11... | collective-permute-start | bytes 884744 | tf_op jit(solution)/shard_map/ppermute | solution.py:296
  78.3 1.7 %collective-permute-done.5 = bf16[4,96,384]{2,1,0:T(8,128)(2,1)} collective-permute-done((bf16[4,96,384]{2,1,0:T(8,128)(2,1)S(1)}, bf16[4,96,384]{2,1,0:T(8,128)(2,1)}, u32[]{:S(2)}, u32[]{:S(2)}) %collective-permute-start.5) | collective-permute-done | bytes 294944 | tf_op jit(solution)/shard_map/ppermute | solution.py:296
  81.1 2.8 %collective-permute-start.6 = (bf16[2,96,384]{2,1,0:T(8,128)(2,1)S(1)}, bf16[2,96,384]{2,1,0:T(8,128)(2,1)S(1)}, u32[]{:S(2)}, u32[]{:S(2)}) collective-permute-start(bf16[2,96,384]{2,1,0:T(8,128)(2,1)S(1)} %fusion), channel_id=1, source_target_pairs={{0,2},{1,3},{2,0},{3,1},{4,6},{5,7},{6,4},{7,5},{8,10},{9,11},{10,... | collective-permute-start | bytes 442376 | tf_op jit(solution)/shard_map/ppermute | solution.py:296
  83.9 5.0 %collective-permute-done.6 = bf16[2,96,384]{2,1,0:T(8,128)(2,1)S(1)} collective-permute-done((bf16[2,96,384]{2,1,0:T(8,128)(2,1)S(1)}, bf16[2,96,384]{2,1,0:T(8,128)(2,1)S(1)}, u32[]{:S(2)}, u32[]{:S(2)}) %collective-permute-start.6) | collective-permute-done | bytes 147488 | tf_op jit(solution)/shard_map/ppermute | solution.py:296
  88.9 2.2 %collective-permute-start.7 = (bf16[1,96,384]{2,1,0:T(8,128)(2,1)S(1)}, bf16[1,96,384]{2,1,0:T(8,128)(2,1)S(1)}, u32[]{:S(2)}, u32[]{:S(2)}) collective-permute-start(bf16[1,96,384]{2,1,0:T(8,128)(2,1)S(1)} %dynamic-slice_convert_fusion), channel_id=1, source_target_pairs={{0,4},{1,5},{2,6},{3,7},{4,0},{5,1},{6,2},{7,3},{8,12},{9,13},{10,... | collective-permute-start | bytes 221192 | tf_op jit(solution)/shard_map/ppermute | solution.py:296
  91.2 4.3 %all-to-all-done.2 = bf16[8,96,1024]{2,1,0:T(8,128)(2,1)S(1)} async-done(((bf16[8,96,1024]{2,1,0:T(8,128)(2,1)}), bf16[8,96,1024]{2,1,0:T(8,128)(2,1)S(1)}, u32[]{:S(2)}, u32[]{:S(2)}) %all-to-all-start.2) | async-done | bytes 1572896 | tf_op jit(solution)/shard_map/all_to_all | solution.py:284
  96.5 5.1 %all-to-all-start.3 = ((bf16[4,24,1024]{2,1,0:T(8,128)(2,1)}), bf16[4,24,1024]{2,1,0:T(8,128)(2,1)S(1)}, u32[]{:S(2)}, u32[]{:S(2)}) async-start(bf16[4,24,1024]{2,1,0:T(8,128)(2,1)} %bitcast.2), calls=%async_computation.3 | async-start | bytes 393216 | tf_op jit(solution)/shard_map/all_to_all | solution.py:286
  101.6 7.8 %collective-permute-start.8 = (bf16[96,128]{1,0:T(8,128)(2,1)S(1)}, bf16[96,128]{1,0:T(8,128)(2,1)S(1)}, u32[]{:S(2)}, u32[]{:S(2)}) collective-permute-start(bf16[96,128]{1,0:T(8,128)(2,1)S(1)} %get-tuple-element.16), channel_id=1, source_target_pairs={{0,8},{8,16},{16,24},{24,32},{32,40},{40,48},{48,56},{56,64},{64,7... | collective-permute-start | bytes 73736 | tf_op jit(solution)/shard_map/ppermute | solution.py:32
  109.4 4.5 %collective-permute-start.9 = (bf16[96,128]{1,0:T(8,128)(2,1)S(1)}, bf16[96,128]{1,0:T(8,128)(2,1)S(1)}, u32[]{:S(2)}, u32[]{:S(2)}) collective-permute-start(bf16[96,128]{1,0:T(8,128)(2,1)S(1)} %get-tuple-element.17), channel_id=1, source_target_pairs={{0,16},{8,24},{16,32},{24,40},{32,48},{40,56},{48,64},{56,72},{64,... | collective-permute-start | bytes 73736 | tf_op jit(solution)/shard_map/ppermute | solution.py:32
  114.0 4.5 %collective-permute-start.4 = (bf16[12,1024]{1,0:T(8,128)(2,1)S(1)}, bf16[12,1024]{1,0:T(8,128)(2,1)S(1)}, u32[]{:S(2)}, u32[]{:S(2)}) collective-permute-start(bf16[12,1024]{1,0:T(8,128)(2,1)S(1)} %select_convert_fusion), channel_id=1, source_target_pairs={{0,8},{8,0},{1,9},{9,1},{2,10},{10,2},{3,11},{11,3},{4,12},{12,4},... | collective-permute-start | bytes 73736 | tf_op jit(solution)/shard_map/ppermute | solution.py:290
  119.1 4.8 %collective-permute-done.4 = bf16[12,1024]{1,0:T(8,128)(2,1)S(1)} collective-permute-done((bf16[12,1024]{1,0:T(8,128)(2,1)S(1)}, bf16[12,1024]{1,0:T(8,128)(2,1)S(1)}, u32[]{:S(2)}, u32[]{:S(2)}) %collective-permute-start.4) | collective-permute-done | bytes 24608 | tf_op jit(solution)/shard_map/ppermute | solution.py:290
  (43 shorter events, 8.8 us)
Async XLA Ops:
  0.6 30.0 %collective-permute-start.2 = (bf16[128,1024]{1,0:T(8,128)(2,1)}, bf16[128,1024]{1,0:T(8,128)(2,1)S(1)}, u32[]{:S(2)}, u32[]{:S(2)}) collective-permute-start(bf16[128,1024]{1,0:T(8,128)(2,1)} %teacher.5), channel_id=1, source_target_pairs={{0,504},{8,0},{16,8},{24,16},{32,24},{40,32},{48,40},{56,48},{64,5... | collective-permute-start | bytes 786440 | tf_op jit(solution)/shard_map/ppermute | solution.py:32
  8.6 22.0 %collective-permute-start.3 = (bf16[128,1024]{1,0:T(8,128)(2,1)}, bf16[128,1024]{1,0:T(8,128)(2,1)S(1)}, u32[]{:S(2)}, u32[]{:S(2)}) collective-permute-start(bf16[128,1024]{1,0:T(8,128)(2,1)} %teacher.5), channel_id=1, source_target_pairs={{0,496},{8,504},{16,0},{24,8},{32,16},{40,24},{48,32},{56,40},{64,... | collective-permute-start | bytes 786440 | tf_op jit(solution)/shard_map/ppermute | solution.py:32
  11.1 19.6 %collective-permute-start = (bf16[128,768]{1,0:T(8,128)(2,1)}, bf16[128,768]{1,0:T(8,128)(2,1)S(1)}, u32[]{:S(2)}, u32[]{:S(2)}) collective-permute-start(bf16[128,768]{1,0:T(8,128)(2,1)} %student.3), channel_id=1, source_target_pairs={{0,504},{8,0},{16,8},{24,16},{32,24},{40,32},{48,40},{56,48},{64,5... | collective-permute-start | bytes 589832 | tf_op jit(solution)/shard_map/ppermute | solution.py:32
  13.1 17.6 %collective-permute-start.1 = (bf16[128,768]{1,0:T(8,128)(2,1)}, bf16[128,768]{1,0:T(8,128)(2,1)S(1)}, u32[]{:S(2)}, u32[]{:S(2)}) collective-permute-start(bf16[128,768]{1,0:T(8,128)(2,1)} %student.3), channel_id=1, source_target_pairs={{0,496},{8,504},{16,0},{24,8},{32,16},{40,24},{48,32},{56,40},{64,... | collective-permute-start | bytes 589832 | tf_op jit(solution)/shard_map/ppermute | solution.py:32
  20.9 1.4 %copy-start = (bf16[768,1024]{1,0:T(8,128)(2,1)S(1)}, bf16[768,1024]{1,0:T(8,128)(2,1)}, u32[]{:S(2)}) copy-start(bf16[768,1024]{1,0:T(8,128)(2,1)} %weight.5) | copy-start | bytes 4718596
  22.3 0.9 copy-start.2
  23.3 0.9 copy-start.4
  24.2 6.5 %copy-start.1 = (bf16[768,1024]{1,0:T(8,128)(2,1)S(1)}, bf16[768,1024]{1,0:T(8,128)(2,1)}, u32[]{:S(2)}) copy-start(bf16[768,1024]{1,0:T(8,128)(2,1)} %weight.5) | copy-start | bytes 4718596
  24.2 6.5 %copy-start.3 = (bf16[128,1024]{1,0:T(8,128)(2,1)S(1)}, bf16[128,1024]{1,0:T(8,128)(2,1)}, u32[]{:S(2)}) copy-start(bf16[128,1024]{1,0:T(8,128)(2,1)} %teacher.5) | copy-start | bytes 786436
  30.7 5.3 %copy-start.8 = (s32[384]{0:T(512)S(1)}, s32[384]{0:T(512)}, u32[]{:S(2)}) copy-start(s32[384]{0:T(512)} %param.8) | copy-start | bytes 4612
  30.7 5.4 %copy-start.7 = (s32[2,384]{1,0:T(2,128)S(1)}, s32[2,384]{1,0:T(2,128)}, u32[]{:S(2)}) copy-start(s32[2,384]{1,0:T(2,128)} %param.9) | copy-start | bytes 9220
  32.4 30.0 %copy-start.5 = (bf16[128,768]{1,0:T(8,128)(2,1)S(1)}, bf16[128,768]{1,0:T(8,128)(2,1)}, u32[]{:S(2)}) copy-start(bf16[128,768]{1,0:T(8,128)(2,1)} %student.3) | copy-start | bytes 589828
  32.4 16.8 %all-to-all-start = ((f32[8,104,128]{2,1,0:T(8,128)}), f32[8,104,128]{2,1,0:T(8,128)S(1)}, u32[]{:S(2)}, u32[]{:S(2)}) async-start(f32[8,104,128]{2,1,0:T(8,128)} %tile.1), calls=%async_computation | async-start | bytes 851968 | tf_op jit(solution)/shard_map/all_to_all | solution.py:239
  49.1 0.8 copy-start.6
  52.3 10.1 %all-to-all-start.1 = ((bf16[8,16,512]{2,1,0:T(8,128)(2,1)}), bf16[8,16,512]{2,1,0:T(8,128)(2,1)S(1)}, u32[]{:S(2)}, u32[]{:S(2)}) async-start(bf16[8,16,512]{2,1,0:T(8,128)(2,1)} %band.1), calls=%async_computation.1 | async-start | bytes 262144 | tf_op jit(solution)/shard_map/all_to_all | solution.py:256
  65.5 30.0 %all-to-all-start.2 = ((bf16[8,96,1024]{2,1,0:T(8,128)(2,1)}), bf16[8,96,1024]{2,1,0:T(8,128)(2,1)S(1)}, u32[]{:S(2)}, u32[]{:S(2)}) async-start(bf16[8,96,1024]{2,1,0:T(8,128)(2,1)} %bitcast.1), calls=%async_computation.2 | async-start | bytes 3145728 | tf_op jit(solution)/shard_map/all_to_all | solution.py:284
  76.4 3.6 %collective-permute-start.5 = (bf16[4,96,384]{2,1,0:T(8,128)(2,1)S(1)}, bf16[4,96,384]{2,1,0:T(8,128)(2,1)}, u32[]{:S(2)}, u32[]{:S(2)}) collective-permute-start(bf16[4,96,384]{2,1,0:T(8,128)(2,1)S(1)} %get-tuple-element.13), channel_id=1, source_target_pairs={{0,1},{1,0},{2,3},{3,2},{4,5},{5,4},{6,7},{7,6},{8,9},{9,8},{10,11... | collective-permute-start | bytes 884744 | tf_op jit(solution)/shard_map/ppermute | solution.py:296
  81.1 7.8 %collective-permute-start.6 = (bf16[2,96,384]{2,1,0:T(8,128)(2,1)S(1)}, bf16[2,96,384]{2,1,0:T(8,128)(2,1)S(1)}, u32[]{:S(2)}, u32[]{:S(2)}) collective-permute-start(bf16[2,96,384]{2,1,0:T(8,128)(2,1)S(1)} %fusion), channel_id=1, source_target_pairs={{0,2},{1,3},{2,0},{3,1},{4,6},{5,7},{6,4},{7,5},{8,10},{9,11},{10,... | collective-permute-start | bytes 442376 | tf_op jit(solution)/shard_map/ppermute | solution.py:296
  88.9 12.6 %collective-permute-start.7 = (bf16[1,96,384]{2,1,0:T(8,128)(2,1)S(1)}, bf16[1,96,384]{2,1,0:T(8,128)(2,1)S(1)}, u32[]{:S(2)}, u32[]{:S(2)}) collective-permute-start(bf16[1,96,384]{2,1,0:T(8,128)(2,1)S(1)} %dynamic-slice_convert_fusion), channel_id=1, source_target_pairs={{0,4},{1,5},{2,6},{3,7},{4,0},{5,1},{6,2},{7,3},{8,12},{9,13},{10,... | collective-permute-start | bytes 221192 | tf_op jit(solution)/shard_map/ppermute | solution.py:296
  96.5 17.4 %all-to-all-start.3 = ((bf16[4,24,1024]{2,1,0:T(8,128)(2,1)}), bf16[4,24,1024]{2,1,0:T(8,128)(2,1)S(1)}, u32[]{:S(2)}, u32[]{:S(2)}) async-start(bf16[4,24,1024]{2,1,0:T(8,128)(2,1)} %bitcast.2), calls=%async_computation.3 | async-start | bytes 393216 | tf_op jit(solution)/shard_map/all_to_all | solution.py:286
  101.6 16.9 %collective-permute-start.8 = (bf16[96,128]{1,0:T(8,128)(2,1)S(1)}, bf16[96,128]{1,0:T(8,128)(2,1)S(1)}, u32[]{:S(2)}, u32[]{:S(2)}) collective-permute-start(bf16[96,128]{1,0:T(8,128)(2,1)S(1)} %get-tuple-element.16), channel_id=1, source_target_pairs={{0,8},{8,16},{16,24},{24,32},{32,40},{40,48},{48,56},{56,64},{64,7... | collective-permute-start | bytes 73736 | tf_op jit(solution)/shard_map/ppermute | solution.py:32
  109.4 9.1 %collective-permute-start.9 = (bf16[96,128]{1,0:T(8,128)(2,1)S(1)}, bf16[96,128]{1,0:T(8,128)(2,1)S(1)}, u32[]{:S(2)}, u32[]{:S(2)}) collective-permute-start(bf16[96,128]{1,0:T(8,128)(2,1)S(1)} %get-tuple-element.17), channel_id=1, source_target_pairs={{0,16},{8,24},{16,32},{24,40},{32,48},{40,56},{48,64},{56,72},{64,... | collective-permute-start | bytes 73736 | tf_op jit(solution)/shard_map/ppermute | solution.py:32
  114.0 9.9 %collective-permute-start.4 = (bf16[12,1024]{1,0:T(8,128)(2,1)S(1)}, bf16[12,1024]{1,0:T(8,128)(2,1)S(1)}, u32[]{:S(2)}, u32[]{:S(2)}) collective-permute-start(bf16[12,1024]{1,0:T(8,128)(2,1)S(1)} %select_convert_fusion), channel_id=1, source_target_pairs={{0,8},{8,0},{1,9},{9,1},{2,10},{10,2},{3,11},{11,3},{4,12},{12,4},... | collective-permute-start | bytes 73736 | tf_op jit(solution)/shard_map/ppermute | solution.py:290

commit v14 on v12

--- a/solution.py
+++ b/solution.py
@@ -285,11 +285,6 @@
     grad_w = jnp.sum(grad_w.astype(f32), 0).astype(bf16)
     grad_w = lax.all_to_all(grad_w.reshape(z_size, yh_size * share, width), "z", 0, 0)
     grad_w = jnp.sum(grad_w.astype(f32), 0)
-    lower, upper = grad_w[:share], grad_w[share:]
-    first = lax.axis_index("yh") == 0
-    grad_w = jnp.where(first, lower, upper) + lax.ppermute(
-        jnp.where(first, upper, lower), "yh", [(0, 1), (1, 0)]
-    )
 
     def swapped(array, bit):
         perm = [(i, i ^ (1 << bit)) for i in range(n_feat)]
@@ -302,9 +297,14 @@
         sent = lax.dynamic_index_in_dim(back, 1 - mine, 1, keepdims=False).astype(bf16)
         back = lax.dynamic_index_in_dim(back, mine, 1, keepdims=False) + swapped(sent, bit)
     back = back.reshape(height, band)
-    grad_student = back[:, :texts]
-    for s in range(1, STEPS):
-        grad_student = grad_student + passed_along(back[:, s * texts : (s + 1) * texts], s)
+    moved = passed_along(back[:, texts:].astype(bf16), 2).astype(f32)
+    first = lax.axis_index("yh") == 0
+    to_mate = jnp.where(first, back[:, texts : 2 * texts], moved[:, :texts])
+    lower, upper = grad_w[:share], grad_w[share:]
+    to_mate = jnp.concatenate([jnp.where(first, upper, lower), to_mate.reshape(-1, width)], 0)
+    from_mate = lax.ppermute(to_mate, "yh", [(0, 1), (1, 0)])
+    grad_w = jnp.where(first, lower, upper) + from_mate[:share]
+    grad_student = back[:, :texts] + moved[:, texts:] + from_mate[share:].reshape(height, texts)
     return (grad_w, grad_student.T)
 
 

time: 126 us -> 128 us (1.016)
  the two profiles are of different devices: /device:TPU:6 before, /device:TPU:40 now
where the time goes in v14:
time: 128 us; the launch traced here: 127 us
  starting transfers between devices  61.7 us (48%)
  waiting for transfers between devices  48 us (38%)
  Pallas kernels  7.69 us (6%)
  local copies, waits for them, and re-layouts  4.96 us (4%)
  other arithmetic  4.06 us (3%)
    ppermute x5, starting transfers between devices, passed_along(): lax.ppermute(array, DP, [(i, (i + by) % peers) for i in range(peers)])  28.4 us
    ppermute x5, waiting for transfers between devices, passed_along(): lax.ppermute(array, DP, [(i, (i + by) % peers) for i in range(peers)])  11.5 us
    ppermute x1, waiting for transfers between devices, shards(): from_mate = lax.ppermute(to_mate, 'yh', [(0, 1), (1, 0)])  10.3 us
    all_to_all x1, waiting for transfers between devices, shards(): parts = lax.all_to_all(parts, 'feat', 0, 0)  9.76 us
    ppermute x3, starting transfers between devices, swapped(): return lax.ppermute(array, 'feat', perm).astype(f32)  7.88 us
    all_to_all x1, starting transfers between devices, shards(): parts = lax.all_to_all(parts, 'feat', 0, 0)  7.77 us
    ppermute x3, waiting for transfers between devices, swapped(): return lax.ppermute(array, 'feat', perm).astype(f32)  6.3 us
    all_to_all x1, starting transfers between devices, shards(): lax.all_to_all(grad_w.reshape(z_size, yh_size * share, width), 'z', 0, 0)  6.21 us
  transfers between devices with their start and end apart: 13, of which 9 were waited for; matrix products, arithmetic and copies ran while one was open for 2% of the time, Pallas kernels for 0%

profile of v14, /device:TPU:40, one launch (start us, length us, event | category | flops | bytes accessed | tf_op | source)
XLA Modules:
  0.0 127.3 jit_solution(1170866291171596202)
XLA Ops:
  0.6 2.9 %collective-permute-start.2 = (bf16[128,1024]{1,0:T(8,128)(2,1)}, bf16[128,1024]{1,0:T(8,128)(2,1)S(1)}, u32[]{:S(2)}, u32[]{:S(2)}) collective-permute-start(bf16[128,1024]{1,0:T(8,128)(2,1)} %teacher.5), channel_id=1, source_target_pairs={{0,504},{8,0},{16,8},{24,16},{32,24},{40,32},{48,40},{56,48},{64,5... | collective-permute-start | bytes 786440 | tf_op jit(solution)/shard_map/ppermute | solution.py:32
  3.6 13.1 %collective-permute-start.3 = (bf16[128,1024]{1,0:T(8,128)(2,1)}, bf16[128,1024]{1,0:T(8,128)(2,1)S(1)}, u32[]{:S(2)}, u32[]{:S(2)}) collective-permute-start(bf16[128,1024]{1,0:T(8,128)(2,1)} %teacher.5), channel_id=1, source_target_pairs={{0,496},{8,504},{16,0},{24,8},{32,16},{40,24},{48,32},{56,40},{64,... | collective-permute-start | bytes 786440 | tf_op jit(solution)/shard_map/ppermute | solution.py:32
  16.7 7.1 %collective-permute-start = (bf16[128,768]{1,0:T(8,128)(2,1)}, bf16[128,768]{1,0:T(8,128)(2,1)S(1)}, u32[]{:S(2)}, u32[]{:S(2)}) collective-permute-start(bf16[128,768]{1,0:T(8,128)(2,1)} %student.3), channel_id=1, source_target_pairs={{0,504},{8,0},{16,8},{24,16},{32,24},{40,32},{48,40},{56,48},{64,5... | collective-permute-start | bytes 589832 | tf_op jit(solution)/shard_map/ppermute | solution.py:32
  23.8 2.4 %collective-permute-start.1 = (bf16[128,768]{1,0:T(8,128)(2,1)}, bf16[128,768]{1,0:T(8,128)(2,1)S(1)}, u32[]{:S(2)}, u32[]{:S(2)}) collective-permute-start(bf16[128,768]{1,0:T(8,128)(2,1)} %student.3), channel_id=1, source_target_pairs={{0,496},{8,504},{16,0},{24,8},{32,16},{40,24},{48,32},{56,40},{64,... | collective-permute-start | bytes 589832 | tf_op jit(solution)/shard_map/ppermute | solution.py:32
  30.2 2.3 %collective-permute-done.near_student = bf16[128,768]{1,0:T(8,128)(2,1)S(1)} collective-permute-done((bf16[128,768]{1,0:T(8,128)(2,1)}, bf16[128,768]{1,0:T(8,128)(2,1)S(1)}, u32[]{:S(2)}, u32[]{:S(2)}) %collective-permute-start) | collective-permute-done | bytes 196640 | tf_op jit(solution)/shard_map/ppermute | solution.py:32
  32.5 1.6 %collective-permute-done.1.far_student = bf16[128,768]{1,0:T(8,128)(2,1)S(1)} collective-permute-done((bf16[128,768]{1,0:T(8,128)(2,1)}, bf16[128,768]{1,0:T(8,128)(2,1)S(1)}, u32[]{:S(2)}, u32[]{:S(2)}) %collective-permute-start.1) | collective-permute-done | bytes 196640 | tf_op jit(solution)/shard_map/ppermute | solution.py:32
  34.1 1.6 %tile.1 = f32[8,104,128]{2,1,0:T(8,128)} custom-call(bf16[128,1024]{1,0:T(8,128)(2,1)S(1)} %get-tuple-element.8.proj_own, bf16[768,1024]{1,0:T(8,128)(2,1)S(1)} %copy-done.1, bf16[128,1024]{1,0:T(8,128)(2,1)S(1)} %copy-done.3, f32[128,256]{1,0:T(8,128)S(1)} %get-tuple-element.9.tiles, f32[8,128]{1,0:T(8,128)S(1)} %get-tuple-element.10.sums, ...), custom_call_target="tpu_custom_call" | custom-call | flops 600000000 | bytes 3000000 | tf_op jit(solution)/shard_map/tile/pallas_call | solution.py:228
  35.7 7.8 %all-to-all-start = ((f32[8,104,128]{2,1,0:T(8,128)}), f32[8,104,128]{2,1,0:T(8,128)S(1)}, u32[]{:S(2)}, u32[]{:S(2)}) async-start(f32[8,104,128]{2,1,0:T(8,128)} %tile.1), calls=%async_computation | async-start | bytes 851968 | tf_op jit(solution)/shard_map/all_to_all | solution.py:239
  44.2 9.8 %all-to-all-done.parts = f32[8,104,128]{2,1,0:T(8,128)S(1)} async-done(((f32[8,104,128]{2,1,0:T(8,128)}), f32[8,104,128]{2,1,0:T(8,128)S(1)}, u32[]{:S(2)}, u32[]{:S(2)}) %all-to-all-start) | async-done | bytes 426016 | tf_op jit(solution)/shard_map/all_to_all | solution.py:239
  54.8 2.4 %band.1 = bf16[8,16,512]{2,1,0:T(8,128)(2,1)} custom-call(f32[8,104,128]{2,1,0:T(8,128)} %copy-done.6, s32[8,384]{1,0:T(8,128)} %add_add_fusion.ids), custom_call_target="tpu_custom_call" | custom-call | flops 100000000 | bytes 3000000 | tf_op jit(solution)/shard_map/band/pallas_call | solution.py:250
  57.2 6.0 %all-to-all-start.1 = ((bf16[8,16,512]{2,1,0:T(8,128)(2,1)}), bf16[8,16,512]{2,1,0:T(8,128)(2,1)S(1)}, u32[]{:S(2)}, u32[]{:S(2)}) async-start(bf16[8,16,512]{2,1,0:T(8,128)(2,1)} %band.1), calls=%async_computation.1 | async-start | bytes 262144 | tf_op jit(solution)/shard_map/all_to_all | solution.py:256
  63.2 5.7 %all-to-all-done.1.gathered = bf16[8,16,512]{2,1,0:T(8,128)(2,1)S(1)} async-done(((bf16[8,16,512]{2,1,0:T(8,128)(2,1)}), bf16[8,16,512]{2,1,0:T(8,128)(2,1)S(1)}, u32[]{:S(2)}, u32[]{:S(2)}) %all-to-all-start.1) | async-done | bytes 131104 | tf_op jit(solution)/shard_map/all_to_all | solution.py:256
  68.9 3.1 %grad.1 = (bf16[4,96,384]{2,1,0:T(8,128)(2,1)S(1)}, f32[4,96,384]{2,1,0:T(8,128)S(1)}, bf16[768,1024]{1,0:T(8,128)(2,1)}) custom-call(s32[1]{0:T(128)} %bitcast.core, bf16[8,16,512]{2,1,0:T(8,128)(2,1)S(1)} %all-to-all-done.1.gathered, bf16[768,1024]{1,0:T(8,128)(2,1)S(1)} %copy-done.1, bf16[128,1024]{1,0:T(8,128)(2,1)S(1)} %copy-done.3, ...), custom_call_target="tpu_custom_call" | custom-call | flops 1000000000 | bytes 3000000 | tf_op jit(solution)/shard_map/grad/pallas_call | solution.py:261
  71.9 3.6 %all-to-all-start.2 = ((bf16[8,96,1024]{2,1,0:T(8,128)(2,1)}), bf16[8,96,1024]{2,1,0:T(8,128)(2,1)S(1)}, u32[]{:S(2)}, u32[]{:S(2)}) async-start(bf16[8,96,1024]{2,1,0:T(8,128)(2,1)} %bitcast.1), calls=%async_computation.2 | async-start | bytes 3145728 | tf_op jit(solution)/shard_map/all_to_all | solution.py:284
  75.5 1.9 %collective-permute-start.4 = (bf16[4,96,384]{2,1,0:T(8,128)(2,1)S(1)}, bf16[4,96,384]{2,1,0:T(8,128)(2,1)S(1)}, u32[]{:S(2)}, u32[]{:S(2)}) collective-permute-start(bf16[4,96,384]{2,1,0:T(8,128)(2,1)S(1)} %get-tuple-element.13), channel_id=1, source_target_pairs={{0,1},{1,0},{2,3},{3,2},{4,5},{5,4},{6,7},{7,6},{8,9},{9,8},{10,11... | collective-permute-start | bytes 884744 | tf_op jit(solution)/shard_map/ppermute | solution.py:291
  80.8 3.0 %collective-permute-start.5 = (bf16[2,96,384]{2,1,0:T(8,128)(2,1)S(1)}, bf16[2,96,384]{2,1,0:T(8,128)(2,1)S(1)}, u32[]{:S(2)}, u32[]{:S(2)}) collective-permute-start(bf16[2,96,384]{2,1,0:T(8,128)(2,1)S(1)} %fusion), channel_id=1, source_target_pairs={{0,2},{1,3},{2,0},{3,1},{4,6},{5,7},{6,4},{7,5},{8,10},{9,11},{10,... | collective-permute-start | bytes 442376 | tf_op jit(solution)/shard_map/ppermute | solution.py:291
  83.8 4.8 %collective-permute-done.5 = bf16[2,96,384]{2,1,0:T(8,128)(2,1)S(1)} collective-permute-done((bf16[2,96,384]{2,1,0:T(8,128)(2,1)S(1)}, bf16[2,96,384]{2,1,0:T(8,128)(2,1)S(1)}, u32[]{:S(2)}, u32[]{:S(2)}) %collective-permute-start.5) | collective-permute-done | bytes 147488 | tf_op jit(solution)/shard_map/ppermute | solution.py:291
  88.7 2.9 %collective-permute-start.6 = (bf16[1,96,384]{2,1,0:T(8,128)(2,1)S(1)}, bf16[1,96,384]{2,1,0:T(8,128)(2,1)S(1)}, u32[]{:S(2)}, u32[]{:S(2)}) collective-permute-start(bf16[1,96,384]{2,1,0:T(8,128)(2,1)S(1)} %dynamic-slice_convert_fusion), channel_id=1, source_target_pairs={{0,4},{1,5},{2,6},{3,7},{4,0},{5,1},{6,2},{7,3},{8,12},{9,13},{10,... | collective-permute-start | bytes 221192 | tf_op jit(solution)/shard_map/ppermute | solution.py:291
  91.6 4.4 %all-to-all-done.2 = bf16[8,96,1024]{2,1,0:T(8,128)(2,1)S(1)} async-done(((bf16[8,96,1024]{2,1,0:T(8,128)(2,1)}), bf16[8,96,1024]{2,1,0:T(8,128)(2,1)S(1)}, u32[]{:S(2)}, u32[]{:S(2)}) %all-to-all-start.2) | async-done | bytes 1572896 | tf_op jit(solution)/shard_map/all_to_all | solution.py:284
  97.0 6.2 %all-to-all-start.3 = ((bf16[4,24,1024]{2,1,0:T(8,128)(2,1)}), bf16[4,24,1024]{2,1,0:T(8,128)(2,1)S(1)}, u32[]{:S(2)}, u32[]{:S(2)}) async-start(bf16[4,24,1024]{2,1,0:T(8,128)(2,1)} %bitcast.2), calls=%async_computation.3 | async-start | bytes 393216 | tf_op jit(solution)/shard_map/all_to_all | solution.py:286
  103.2 2.8 %collective-permute-start.7 = (bf16[96,256]{1,0:T(8,128)(2,1)S(1)}, bf16[96,256]{1,0:T(8,128)(2,1)S(1)}, u32[]{:S(2)}, u32[]{:S(2)}) collective-permute-start(bf16[96,256]{1,0:T(8,128)(2,1)S(1)} %slice.60), channel_id=1, source_target_pairs={{0,16},{8,24},{16,32},{24,40},{32,48},{40,56},{48,64},{56,72},{64,... | collective-permute-start | bytes 147464 | tf_op jit(solution)/shard_map/ppermute | solution.py:32
  106.0 7.6 %collective-permute-done.7 = bf16[96,256]{1,0:T(8,128)(2,1)S(1)} collective-permute-done((bf16[96,256]{1,0:T(8,128)(2,1)S(1)}, bf16[96,256]{1,0:T(8,128)(2,1)S(1)}, u32[]{:S(2)}, u32[]{:S(2)}) %collective-permute-start.7) | collective-permute-done | bytes 49184 | tf_op jit(solution)/shard_map/ppermute | solution.py:32
  113.8 1.9 %collective-permute-start.8 = (f32[24,1024]{1,0:T(8,128)S(1)}, f32[24,1024]{1,0:T(8,128)S(1)}, u32[]{:S(2)}, u32[]{:S(2)}) collective-permute-start(f32[24,1024]{1,0:T(8,128)S(1)} %pad_maximum_fusion), channel_id=1, source_target_pairs={{0,8},{8,0},{1,9},{9,1},{2,10},{10,2},{3,11},{11,3},{4,12},{12,4},... | collective-permute-start | bytes 294920 | tf_op jit(solution)/shard_map/ppermute | solution.py:305
  115.7 10.3 %collective-permute-done.8 = f32[24,1024]{1,0:T(8,128)S(1)} collective-permute-done((f32[24,1024]{1,0:T(8,128)S(1)}, f32[24,1024]{1,0:T(8,128)S(1)}, u32[]{:S(2)}, u32[]{:S(2)}) %collective-permute-start.8) | collective-permute-done | bytes 98336 | tf_op jit(solution)/shard_map/ppermute | solution.py:305
  (48 shorter events, 11.2 us)
Async XLA Ops:
  0.6 33.4 %collective-permute-start.2 = (bf16[128,1024]{1,0:T(8,128)(2,1)}, bf16[128,1024]{1,0:T(8,128)(2,1)S(1)}, u32[]{:S(2)}, u32[]{:S(2)}) collective-permute-start(bf16[128,1024]{1,0:T(8,128)(2,1)} %teacher.5), channel_id=1, source_target_pairs={{0,504},{8,0},{16,8},{24,16},{32,24},{40,32},{48,40},{56,48},{64,5... | collective-permute-start | bytes 786440 | tf_op jit(solution)/shard_map/ppermute | solution.py:32
  3.6 30.5 %collective-permute-start.3 = (bf16[128,1024]{1,0:T(8,128)(2,1)}, bf16[128,1024]{1,0:T(8,128)(2,1)S(1)}, u32[]{:S(2)}, u32[]{:S(2)}) collective-permute-start(bf16[128,1024]{1,0:T(8,128)(2,1)} %teacher.5), channel_id=1, source_target_pairs={{0,496},{8,504},{16,0},{24,8},{32,16},{40,24},{48,32},{56,40},{64,... | collective-permute-start | bytes 786440 | tf_op jit(solution)/shard_map/ppermute | solution.py:32
  16.7 15.8 %collective-permute-start = (bf16[128,768]{1,0:T(8,128)(2,1)}, bf16[128,768]{1,0:T(8,128)(2,1)S(1)}, u32[]{:S(2)}, u32[]{:S(2)}) collective-permute-start(bf16[128,768]{1,0:T(8,128)(2,1)} %student.3), channel_id=1, source_target_pairs={{0,504},{8,0},{16,8},{24,16},{32,24},{40,32},{48,40},{56,48},{64,5... | collective-permute-start | bytes 589832 | tf_op jit(solution)/shard_map/ppermute | solution.py:32
  23.8 10.2 %collective-permute-start.1 = (bf16[128,768]{1,0:T(8,128)(2,1)}, bf16[128,768]{1,0:T(8,128)(2,1)S(1)}, u32[]{:S(2)}, u32[]{:S(2)}) collective-permute-start(bf16[128,768]{1,0:T(8,128)(2,1)} %student.3), channel_id=1, source_target_pairs={{0,496},{8,504},{16,0},{24,8},{32,16},{40,24},{48,32},{56,40},{64,... | collective-permute-start | bytes 589832 | tf_op jit(solution)/shard_map/ppermute | solution.py:32
  26.3 1.4 %copy-start = (bf16[768,1024]{1,0:T(8,128)(2,1)S(1)}, bf16[768,1024]{1,0:T(8,128)(2,1)}, u32[]{:S(2)}) copy-start(bf16[768,1024]{1,0:T(8,128)(2,1)} %weight.5) | copy-start | bytes 4718596
  27.7 0.9 copy-start.2
  28.6 0.9 copy-start.4
  29.6 4.5 %copy-start.1 = (bf16[768,1024]{1,0:T(8,128)(2,1)S(1)}, bf16[768,1024]{1,0:T(8,128)(2,1)}, u32[]{:S(2)}) copy-start(bf16[768,1024]{1,0:T(8,128)(2,1)} %weight.5) | copy-start | bytes 4718596
  29.6 4.5 %copy-start.3 = (bf16[128,1024]{1,0:T(8,128)(2,1)S(1)}, bf16[128,1024]{1,0:T(8,128)(2,1)}, u32[]{:S(2)}) copy-start(bf16[128,1024]{1,0:T(8,128)(2,1)} %teacher.5) | copy-start | bytes 786436
  34.0 9.4 %copy-start.9 = (s32[384]{0:T(512)S(1)}, s32[384]{0:T(512)}, u32[]{:S(2)}) copy-start(s32[384]{0:T(512)} %param.8) | copy-start | bytes 4612
  34.0 9.5 %copy-start.8 = (s32[2,384]{1,0:T(2,128)S(1)}, s32[2,384]{1,0:T(2,128)}, u32[]{:S(2)}) copy-start(s32[2,384]{1,0:T(2,128)} %param.9) | copy-start | bytes 9220
  35.7 33.2 %copy-start.5 = (bf16[128,768]{1,0:T(8,128)(2,1)S(1)}, bf16[128,768]{1,0:T(8,128)(2,1)}, u32[]{:S(2)}) copy-start(bf16[128,768]{1,0:T(8,128)(2,1)} %student.3) | copy-start | bytes 589828
  35.7 18.3 %all-to-all-start = ((f32[8,104,128]{2,1,0:T(8,128)}), f32[8,104,128]{2,1,0:T(8,128)S(1)}, u32[]{:S(2)}, u32[]{:S(2)}) async-start(f32[8,104,128]{2,1,0:T(8,128)} %tile.1), calls=%async_computation | async-start | bytes 851968 | tf_op jit(solution)/shard_map/all_to_all | solution.py:239
  54.0 0.8 copy-start.6
  57.2 11.7 %all-to-all-start.1 = ((bf16[8,16,512]{2,1,0:T(8,128)(2,1)}), bf16[8,16,512]{2,1,0:T(8,128)(2,1)S(1)}, u32[]{:S(2)}, u32[]{:S(2)}) async-start(bf16[8,16,512]{2,1,0:T(8,128)(2,1)} %band.1), calls=%async_computation.1 | async-start | bytes 262144 | tf_op jit(solution)/shard_map/all_to_all | solution.py:256
  71.9 24.0 %all-to-all-start.2 = ((bf16[8,96,1024]{2,1,0:T(8,128)(2,1)}), bf16[8,96,1024]{2,1,0:T(8,128)(2,1)S(1)}, u32[]{:S(2)}, u32[]{:S(2)}) async-start(bf16[8,96,1024]{2,1,0:T(8,128)(2,1)} %bitcast.1), calls=%async_computation.2 | async-start | bytes 3145728 | tf_op jit(solution)/shard_map/all_to_all | solution.py:284
  75.5 3.5 %collective-permute-start.4 = (bf16[4,96,384]{2,1,0:T(8,128)(2,1)S(1)}, bf16[4,96,384]{2,1,0:T(8,128)(2,1)S(1)}, u32[]{:S(2)}, u32[]{:S(2)}) collective-permute-start(bf16[4,96,384]{2,1,0:T(8,128)(2,1)S(1)} %get-tuple-element.13), channel_id=1, source_target_pairs={{0,1},{1,0},{2,3},{3,2},{4,5},{5,4},{6,7},{7,6},{8,9},{9,8},{10,11... | collective-permute-start | bytes 884744 | tf_op jit(solution)/shard_map/ppermute | solution.py:291
  79.0 0.7 copy-start.7
  80.8 7.8 %collective-permute-start.5 = (bf16[2,96,384]{2,1,0:T(8,128)(2,1)S(1)}, bf16[2,96,384]{2,1,0:T(8,128)(2,1)S(1)}, u32[]{:S(2)}, u32[]{:S(2)}) collective-permute-start(bf16[2,96,384]{2,1,0:T(8,128)(2,1)S(1)} %fusion), channel_id=1, source_target_pairs={{0,2},{1,3},{2,0},{3,1},{4,6},{5,7},{6,4},{7,5},{8,10},{9,11},{10,... | collective-permute-start | bytes 442376 | tf_op jit(solution)/shard_map/ppermute | solution.py:291
  88.7 14.5 %collective-permute-start.6 = (bf16[1,96,384]{2,1,0:T(8,128)(2,1)S(1)}, bf16[1,96,384]{2,1,0:T(8,128)(2,1)S(1)}, u32[]{:S(2)}, u32[]{:S(2)}) collective-permute-start(bf16[1,96,384]{2,1,0:T(8,128)(2,1)S(1)} %dynamic-slice_convert_fusion), channel_id=1, source_target_pairs={{0,4},{1,5},{2,6},{3,7},{4,0},{5,1},{6,2},{7,3},{8,12},{9,13},{10,... | collective-permute-start | bytes 221192 | tf_op jit(solution)/shard_map/ppermute | solution.py:291
  97.0 16.7 %all-to-all-start.3 = ((bf16[4,24,1024]{2,1,0:T(8,128)(2,1)}), bf16[4,24,1024]{2,1,0:T(8,128)(2,1)S(1)}, u32[]{:S(2)}, u32[]{:S(2)}) async-start(bf16[4,24,1024]{2,1,0:T(8,128)(2,1)} %bitcast.2), calls=%async_computation.3 | async-start | bytes 393216 | tf_op jit(solution)/shard_map/all_to_all | solution.py:286
  103.2 10.4 %collective-permute-start.7 = (bf16[96,256]{1,0:T(8,128)(2,1)S(1)}, bf16[96,256]{1,0:T(8,128)(2,1)S(1)}, u32[]{:S(2)}, u32[]{:S(2)}) collective-permute-start(bf16[96,256]{1,0:T(8,128)(2,1)S(1)} %slice.60), channel_id=1, source_target_pairs={{0,16},{8,24},{16,32},{24,40},{32,48},{40,56},{48,64},{56,72},{64,... | collective-permute-start | bytes 147464 | tf_op jit(solution)/shard_map/ppermute | solution.py:32
  113.8 12.2 %collective-permute-start.8 = (f32[24,1024]{1,0:T(8,128)S(1)}, f32[24,1024]{1,0:T(8,128)S(1)}, u32[]{:S(2)}, u32[]{:S(2)}) collective-permute-start(f32[24,1024]{1,0:T(8,128)S(1)} %pad_maximum_fusion), channel_id=1, source_target_pairs={{0,8},{8,0},{1,9},{9,1},{2,10},{10,2},{3,11},{11,3},{4,12},{12,4},... | collective-permute-start | bytes 294920 | tf_op jit(solution)/shard_map/ppermute | solution.py:305
